TPU v7x, 32 devices: a whole 2x2x4 slice. The times are simulated.
32 devices in a mesh: dp: 8 (over z, x), mp: 4 (over y, core).
Axes of the slice: x: 2, y: 2, z: 4, core: 2. Of those that a mesh axis runs over, the one named last changes fastest.
Arguments:
- tokens: bfloat16 [64, 256, 512], P('dp', 'mp'), may hold values from -6 to 6
- lengths: int32 [64], P('dp'), may hold values from 0 to 250, as said below
- order_mask: int32 [64, 256], P('dp'), may hold values from 0 to 1, as said below
- norm_scale_pair: float32 [2, 512], replicated, may hold values from 0.5 to 1.5
- norm_offset_pair: float32 [2, 512], replicated, may hold values from -1.75 to 1.75
- w_qkv: bfloat16 [3, 512, 512], P(None, None, 'mp'), may hold values from -0.25 to 0.25
- qv_bias: float32 [2, 512], P(None, 'mp'), may hold values from -1.75 to 1.75
- order_bias: float32 [8], P('mp'), may hold values from -2 to 2
- w_out: bfloat16 [512, 512], P('mp'), may hold values from -2 to 2
- out_bias: float32 [2, 512], replicated, may hold values from -1.75 to 1.75
- w_up: bfloat16 [512, 2048], P(None, 'mp'), may hold values from -0.25 to 0.25
- up_bias: float32 [2048], P('mp'), may hold values from -1.75 to 1.75
- w_down: bfloat16 [2048, 512], P('mp'), may hold values from -0.125 to 0.125
- cotangent: bfloat16 [64, 256, 512], P('dp', 'mp'), may hold values from -6 to 6
Outputs:
- output: bfloat16 [64, 256, 512], P('dp', 'mp')
- token_gradient: float32 [64, 256, 512], P('dp', 'mp')
- grad_norm_gain: float32 [2, 512], replicated
- grad_norm_shift: float32 [2, 512], replicated
- grad_qkv: float32 [3, 512, 512], P(None, None, 'mp')
- grad_qv_bias: float32 [2, 512], P(None, 'mp')
- grad_order_bias: float32 [8], P('mp')
- grad_out: float32 [512, 512], P('mp')
- grad_out_bias: float32 [2, 512], replicated
- grad_up: float32 [512, 2048], P(None, 'mp')
- grad_up_bias: float32 [2048], P('mp')
- grad_down: float32 [2048, 512], P('mp')
Inputs may be any that keep to these rules, and one draw needn't show every extreme that they name: `lengths`: each length is 0, 64, 128 or 250; within the rows of one device the rows of length 0 come last, and their number may differ from device to device. `order_mask`: in each row the slots that come first in a random order are marked, their number random.
All inputs are finite; a program needn't handle non-finite values.
Results may differ from a plain program's by a relative error of at most 0.03.
Values may be sent and summed in bfloat16 or wider, within the bound.
No kernel may reach another device: no remote copies, remote signals or barrier semaphores. Data moves between devices by JAX's collectives and lax.ppermute only.
A program may use at most 128 MiB of HBM per device.

v0:
```python
import jax
import jax.numpy as jnp
from jax import lax
from jax.sharding import PartitionSpec as P

HD = 64


def layer_normalizer(v):
    centre = v - jnp.mean(v, -1, keepdims=True)
    scale_factor = lax.rsqrt(jnp.mean(centre * centre, -1, keepdims=True) + 1e-05)
    return (centre * scale_factor, scale_factor)


def norm_backward_pass(output_gradient, normalized_input, scale_factor, norm_scale):
    scaled_result = output_gradient * norm_scale
    return scale_factor * (
        scaled_result
        - jnp.mean(scaled_result, -1, keepdims=True)
        - normalized_input * jnp.mean(scaled_result * normalized_input, -1, keepdims=True)
    )


def gelu_fn(v):
    return jax.nn.gelu(v, approximate=True)


def heads_layer(
    tokens,
    lengths,
    order_mask,
    norm_scale_pair,
    norm_offset_pair,
    w_qkv,
    qv_bias,
    order_bias,
    w_out,
    out_bias,
    w_up,
    up_bias,
    w_down,
    cotangent,
):
    single_float_type = jnp.float32
    brain_float_half = jnp.bfloat16
    rows, share, width = tokens.shape
    slots = order_mask.shape[1]
    offset = lax.axis_index("mp") * share
    heads = w_out.shape[0] // HD
    factor_q = HD ** (-0.5)

    def local_share(v):
        return lax.dynamic_slice_in_dim(v, offset, share, 1)

    whole_x = lax.all_gather(tokens, "mp", axis=1, tiled=True)
    input_single_float = whole_x.astype(single_float_type)
    keep = jnp.arange(slots, dtype=jnp.int32)[None, :] < lengths[:, None]
    keep_f = keep.astype(single_float_type)
    order_f = order_mask.astype(single_float_type)
    first_normalized, first_inverse_deviation = layer_normalizer(input_single_float)
    first_attention = (first_normalized * norm_scale_pair[0] + norm_offset_pair[0]).astype(
        brain_float_half
    )
    proj = jnp.einsum(
        "rsd,tde->trse", first_attention, w_qkv, preferred_element_type=single_float_type
    )
    query = (proj[0] + qv_bias[0]).astype(brain_float_half).reshape(rows, slots, heads, HD)
    keyed = proj[1].astype(brain_float_half).reshape(rows, slots, heads, HD)
    value = (proj[2] + qv_bias[1]).astype(brain_float_half).reshape(rows, slots, heads, HD)

    def scores_of():
        raw = (
            jnp.einsum("rqhe,rkhe->rhqk", query, keyed, preferred_element_type=single_float_type)
            * factor_q
        )
        raw = raw + order_bias[None, :, None, None] * order_f[:, None, None, :]
        return jnp.where(keep[:, None, None, :], raw, -1e30)

    scores = scores_of()
    top = jnp.max(scores, -1, keepdims=True)
    expo = jnp.exp(scores - top)
    total = jnp.sum(expo, -1, keepdims=True)
    lse = top + jnp.log(total)
    probs = expo / total
    attended = jnp.einsum(
        "rhqk,rkhe->rqhe",
        probs.astype(brain_float_half),
        value,
        preferred_element_type=single_float_type,
    )
    attended = (attended.reshape(rows, slots, heads * HD) * keep_f[:, :, None]).astype(
        brain_float_half
    )
    attn_terms = jnp.dot(attended, w_out, preferred_element_type=single_float_type)
    x1_own = tokens.astype(single_float_type) + (
        lax.psum_scatter(attn_terms, "mp", scatter_dimension=1, tiled=True) + out_bias[0]
    )
    second_normalized, rstd2 = layer_normalizer(x1_own)
    second_activation = lax.all_gather(
        (second_normalized * norm_scale_pair[1] + norm_offset_pair[1]).astype(brain_float_half),
        "mp",
        axis=1,
        tiled=True,
    )
    pre = jnp.dot(second_activation, w_up, preferred_element_type=single_float_type) + up_bias
    gelu_out, gelu_pull = jax.vjp(gelu_fn, pre)
    hidden = gelu_out.astype(brain_float_half)
    mlp_terms = jnp.dot(hidden, w_down, preferred_element_type=single_float_type)
    output = (
        x1_own
        + (
            lax.psum_scatter(
                mlp_terms.astype(jnp.bfloat16), "mp", scatter_dimension=1, tiled=True
            ).astype(jnp.float32)
            + out_bias[1]
        )
    ).astype(brain_float_half)
    output_gradient_whole = lax.all_gather(cotangent, "mp", axis=1, tiled=True)
    dy_own = cotangent.astype(single_float_type)
    g_down = jnp.einsum(
        "rsf,rsd->fd", hidden, output_gradient_whole, preferred_element_type=single_float_type
    )
    d_hidden = jnp.dot(output_gradient_whole, w_down.T, preferred_element_type=single_float_type)
    d_pre = gelu_pull(d_hidden)[0].astype(brain_float_half)
    g_up = jnp.einsum(
        "rsd,rsf->df", second_activation, d_pre, preferred_element_type=single_float_type
    )
    g_up_bias = jnp.sum(d_pre.astype(single_float_type), (0, 1))
    mid_terms = jnp.dot(d_pre, w_up.T, preferred_element_type=single_float_type)
    middle_local_rows = lax.psum_scatter(mid_terms, "mp", scatter_dimension=1, tiled=True)
    first_input_gradient_local = dy_own + norm_backward_pass(
        middle_local_rows, second_normalized, rstd2, norm_scale_pair[1]
    )
    d_att = lax.all_gather(
        first_input_gradient_local.astype(brain_float_half), "mp", axis=1, tiled=True
    )
    second_norm_scale = jnp.sum(middle_local_rows * second_normalized, (0, 1))
    shift_two = jnp.sum(middle_local_rows, (0, 1))
    bias_zero = jnp.sum(local_share(d_att).astype(single_float_type), (0, 1))
    bias_one = jnp.sum(dy_own, (0, 1))
    g_out = jnp.einsum("rse,rsd->ed", attended, d_att, preferred_element_type=single_float_type)
    d_o = jnp.dot(d_att, w_out.T, preferred_element_type=single_float_type).astype(
        brain_float_half
    ) * keep_f[:, :, None].astype(brain_float_half)
    d_o = d_o.reshape(rows, slots, heads, HD)
    again = jnp.exp(scores_of() - lse)
    d_value = jnp.einsum(
        "rhqk,rqhe->rkhe",
        again.astype(brain_float_half),
        d_o,
        preferred_element_type=single_float_type,
    ).astype(brain_float_half)
    d_probs = jnp.einsum("rqhe,rkhe->rhqk", d_o, value, preferred_element_type=single_float_type)
    d_scores = again * (d_probs - jnp.sum(again * d_probs, -1, keepdims=True))
    d_scores = jnp.where(keep[:, None, None, :], d_scores, 0.0).astype(brain_float_half)
    g_order = jnp.einsum(
        "rhqk,rk->h",
        d_scores,
        order_mask.astype(brain_float_half),
        preferred_element_type=single_float_type,
    )
    d_query = (
        jnp.einsum("rhqk,rkhe->rqhe", d_scores, keyed, preferred_element_type=single_float_type)
        * factor_q
    ).astype(brain_float_half)
    d_key = (
        jnp.einsum("rhqk,rqhe->rkhe", d_scores, query, preferred_element_type=single_float_type)
        * factor_q
    ).astype(brain_float_half)
    stacked = jnp.stack([d_query, d_key, d_value]).reshape(3, rows, slots, heads * HD)
    g_qkv = jnp.einsum(
        "rsd,trse->tde", first_attention, stacked, preferred_element_type=single_float_type
    )
    g_qv_bias = jnp.stack(
        [
            jnp.sum(stacked[0].astype(single_float_type), (0, 1)),
            jnp.sum(stacked[2].astype(single_float_type), (0, 1)),
        ]
    )
    in_terms = jnp.einsum("trse,tde->rsd", stacked, w_qkv, preferred_element_type=single_float_type)
    input_local_rows = lax.psum_scatter(
        in_terms.astype(jnp.bfloat16), "mp", scatter_dimension=1, tiled=True
    ).astype(jnp.float32)
    first_normalized_local = local_share(first_normalized)
    token_gradient = first_input_gradient_local + norm_backward_pass(
        input_local_rows,
        first_normalized_local,
        local_share(first_inverse_deviation),
        norm_scale_pair[0],
    )
    first_norm_scale = jnp.sum(input_local_rows * first_normalized_local, (0, 1))
    shift_one = jnp.sum(input_local_rows, (0, 1))
    vector_terms = (
        jnp.stack([first_norm_scale, second_norm_scale]),
        jnp.stack([shift_one, shift_two]),
        jnp.stack([bias_zero, bias_one]),
    )
    return (
        output,
        token_gradient,
        vector_terms,
        (g_qkv, g_qv_bias, g_order, g_out, g_up, g_up_bias, g_down),
    )


def body(
    tokens,
    lengths,
    order_mask,
    norm_scale_pair,
    norm_offset_pair,
    w_qkv,
    qv_bias,
    order_bias,
    w_out,
    out_bias,
    w_up,
    up_bias,
    w_down,
    cotangent,
):
    output, token_gradient, vector_terms, weight_terms = heads_layer(
        tokens,
        lengths,
        order_mask,
        norm_scale_pair,
        norm_offset_pair,
        w_qkv,
        qv_bias,
        order_bias,
        w_out,
        out_bias,
        w_up,
        up_bias,
        w_down,
        cotangent,
    )
    vectors = lax.psum((vector_terms[0], vector_terms[1], vector_terms[2]), ("dp", "mp"))
    weights = (
        lax.psum(weight_terms[0].astype(jnp.bfloat16), "dp").astype(jnp.float32),
        lax.psum(weight_terms[1].astype(jnp.bfloat16), "dp").astype(jnp.float32),
        lax.psum(weight_terms[2].astype(jnp.bfloat16), "dp").astype(jnp.float32),
        lax.psum(weight_terms[3].astype(jnp.bfloat16), "dp").astype(jnp.float32),
        lax.psum(weight_terms[4].astype(jnp.bfloat16), "dp").astype(jnp.float32),
        lax.psum(weight_terms[5].astype(jnp.bfloat16), "dp").astype(jnp.float32),
        lax.psum(weight_terms[6].astype(jnp.bfloat16), "dp").astype(jnp.float32),
    )
    return (
        output,
        token_gradient,
        vectors[0],
        vectors[1],
        weights[0],
        weights[1],
        weights[2],
        weights[3],
        vectors[2],
        weights[4],
        weights[5],
        weights[6],
    )


def solution(mesh):
    return jax.shard_map(
        body,
        mesh=mesh,
        in_specs=(
            P("dp", "mp", None),
            P("dp"),
            P("dp", None),
            P(),
            P(),
            P(None, None, "mp"),
            P(None, "mp"),
            P("mp"),
            P("mp", None),
            P(),
            P(None, "mp"),
            P("mp"),
            P("mp", None),
            P("dp", "mp", None),
        ),
        out_specs=(
            P("dp", "mp", None),
            P("dp", "mp", None),
            P(),
            P(),
            P(None, None, "mp"),
            P(None, "mp"),
            P("mp"),
            P("mp", None),
            P(),
            P(None, "mp"),
            P("mp"),
            P("mp", None),
        ),
        check_vma=False,
    )
```

profile of v0, /device:TPU:0, one launch (start us, length us, event | category | flops | bytes accessed | tf_op | source)
XLA Modules:
  0.0 463.2 jit_solution(3877018538895806028)
XLA Ops:
  12.7 22.2 %all-gather.5.cloned.1.call-done = bf16[8,256,512]{2,1,0:T(8,128)(2,1)} async-done(((bf16[8,64,512]{2,1,0:T(8,128)(2,1)}), bf16[8,256,512]{2,1,0:T(8,128)(2,1)}) %all-gather.5.cloned.1.call-update) | async-done | bytes 2097168 | tf_op jit(solution)/shard_map/all_gather | solution.py:55
  34.9 2.1 convert_reduce_fusion
  37.0 2.4 fusion.3
  39.5 1.6 convolution_bitcast_fusion
  41.3 1.3 fusion.68
  43.3 0.9 fusion.21
  44.8 2.7 fusion.56
  47.5 44.6 %reduce-scatter.5.cloned.1.call-done = f32[8,64,512]{2,1,0:T(8,128)} async-done(((f32[8,256,512]{2,1,0:T(8,128)}), f32[8,64,512]{2,1,0:T(8,128)}) %reduce-scatter.5.cloned.1.call-update) | async-done | bytes 1048592 | tf_op jit(solution)/shard_map/reduce_scatter | solution.py:96
  92.1 1.4 fusion.63
  93.8 1.0 add_convert_fusion.2
  95.5 22.1 %all-gather.7.cloned.1.call-done = bf16[8,256,512]{2,1,0:T(8,128)(2,1)} async-done(((bf16[8,64,512]{2,1,0:T(8,128)(2,1)}), bf16[8,256,512]{2,1,0:T(8,128)(2,1)}) %all-gather.7.cloned.1.call-update) | async-done | bytes 2097168 | tf_op jit(solution)/shard_map/all_gather | solution.py:99
  117.7 4.8 %fusion.49 = f32[8,256,512]{2,1,0:T(8,128)} fusion(bf16[8,256,512]{2,1,0:T(8,128)(2,1)} %all-gather.7.cloned.1.call-done, bf16[512,512]{1,0:T(8,128)(2,1)S(1)} %copy-done.13), kind=kOutput, calls=%fused_computation.87 | convolution fusion | flops 1073741824 | bytes 6815744 | tf_op jit(solution)/shard_map/dot_general | solution.py:105
  122.4 19.3 %all-gather.9.cloned.1.call-done = bf16[8,256,512]{2,1,0:T(8,128)(2,1)} async-done(((bf16[8,64,512]{2,1,0:T(8,128)(2,1)}), bf16[8,256,512]{2,1,0:T(8,128)(2,1)}) %all-gather.9.cloned.1.call-update) | async-done | bytes 2097168 | tf_op jit(solution)/shard_map/all_gather | solution.py:118
  141.8 5.8 %fusion.69 = (bf16[512]{0:T(512)(128)(2,1)S(1)}, bf16[8,256,512]{2,1,0:T(8,128)(2,1)S(1)}) fusion(f32[8,256,512]{2,1,0:T(8,128)} %fusion.49, f32[512]{0:T(512)S(1)} %copy-done.19, bf16[8,256,512]{2,1,0:T(8,128)(2,1)} %all-gather.9.cloned.1.call-done, bf16[512,512]{1,0:T(8,128)(2,1)S(1)} %copy-done), kind=kOutput, calls=%fused_computation.126 | convolution fusion | flops 1096809984 | bytes 8915968 | tf_op jit(solution)/shard_map/dot_general | solution.py:123
  147.6 1.3 copy-done.4
  148.9 3.3 fusion.47
  152.5 44.4 %reduce-scatter.9.cloned.1.call-done = f32[8,64,512]{2,1,0:T(8,128)} async-done(((f32[8,256,512]{2,1,0:T(8,128)}), f32[8,64,512]{2,1,0:T(8,128)}) %reduce-scatter.9.cloned.1.call-update) | async-done | bytes 1048592 | tf_op jit(solution)/shard_map/reduce_scatter | solution.py:130
  197.0 1.8 multiply_reduce_fusion.1
  198.7 2.4 fusion.62
  201.3 4.5 fusion.25
  205.7 4.3 fusion.26
  210.0 13.9 %all-gather.11.cloned.1.call-done = bf16[8,256,512]{2,1,0:T(8,128)(2,1)} async-done(((bf16[8,64,512]{2,1,0:T(8,128)(2,1)}), bf16[8,256,512]{2,1,0:T(8,128)(2,1)}) %all-gather.11.cloned.1.call-update) | async-done | bytes 2097168 | tf_op jit(solution)/shard_map/all_gather | solution.py:134
  223.9 2.4 fusion.33
  226.3 0.8 copy-done.12
  227.1 3.8 bitcast_reduce_fusion
  230.9 8.1 %convert_reduce_fusion.1 = (bf16[8,2,256]{2,1,0:T(2,128)(2,1)S(1)}, bf16[8,2,256,256]{2,3,1,0:T(8,128)(2,1)}) fusion(f32[8,2,256,256]{2,3,1,0:T(8,128)} %copy-done.2, f32[8,2,256]{2,1,0:T(2,128)S(1)} %bitcast.128, bf16[8,256,2,64]{1,3,2,0:T(8,128)(2,1)} %bitcast.122, pred[8,256]{1,0:T(8,128)(4,1)S(1)} %get-tuple-element.61, ...), kind=kOutput, calls=%fused_computation.16 | convolution fusion | flops 278921472 | bytes 7891456 | tf_op jit(solution)/shard_map/sub | solution.py:154
  239.0 3.6 fusion.31
  242.6 1.3 bitcast_reduce_fusion.1
  243.9 1.3 copy.35
  245.2 2.0 copy.36
  247.3 2.0 copy.34
  249.3 2.7 fusion.35
  252.0 4.2 fusion.34
  256.3 3.7 bitcast_convert_fusion
  260.4 5.6 %convolution_convert_fusion = bf16[8,256,512]{2,1,0:T(8,128)(2,1)} fusion(bf16[512,512]{1,0:T(8,128)(2,1)S(1)} %copy-done, f32[8,256,512]{2,1,0:T(8,128)} %fusion.49, f32[512]{0:T(512)S(1)} %copy-done.19), kind=kOutput, calls=%fused_computation.34 | convolution fusion | flops 1085276160 | bytes 6817792 | tf_op jit(solution)/shard_map/dot_general | solution.py:108
  266.1 3.6 fusion.1
  270.0 21.9 %all-reduce.1 = (bf16[2,128]{1,0:T(2,128)(2,1)S(1)}, bf16[2]{0:T(256)(128)(2,1)S(1)}, bf16[512]{0:T(512)(128)(2,1)S(1)}) all-reduce(bf16[2,128]{1,0:T(2,128)(2,1)S(1)} %pad_maximum_fusion.6, bf16[2]{0:T(256)(128)(2,1)S(1)} %fusion.36, bf16[512]{0:T(512)(128)(2,1)S(1)} %get-tuple-element.70), channel_id=1, replica_groups=mesh['dp'=8,'mp'=4] {'dp'}, use_global_device_ids=true, to_apply=%region_24.25 | all-reduce | flops 770 | bytes 3080 | tf_op jit(solution)/shard_map/psum | solution.py:241
  293.5 1.2 convert_reduce_fusion.4
  294.6 52.0 %all-reduce.5.cloned.1.call-done = (bf16[3,512,128]{1,2,0:T(8,128)(2,1)}, bf16[128,512]{1,0:T(8,128)(2,1)}, bf16[512,512]{1,0:T(8,128)(2,1)}, bf16[512,512]{1,0:T(8,128)(2,1)}) async-done(((bf16[3,512,128]{1,2,0:T(8,128)(2,1)}, bf16[128,512]{1,0:T(8,128)(2,1)}, bf16[512,512]{1,0:T(8,128)(2,1)}, bf16[512,512]{1,0:T(8,128)(2,1)}), (bf16[3,512,128]{1,2,0:T(8,128)(2,1)}, bf16[128,512]{1,0:T(8,128)(2,1)}, ...) | async-done | bytes 1572880 | tf_op jit(solution)/shard_map/psum | solution.py:240
  346.6 1.6 convert_element_type.208
  348.2 2.0 copy.39
  350.3 2.1 convert_element_type.211
  352.4 2.1 convert_element_type.214
  354.6 25.4 %reduce-scatter.11.cloned.1.call-done = bf16[8,64,512]{2,1,0:T(8,128)(2,1)} async-done(((bf16[8,256,512]{2,1,0:T(8,128)(2,1)}), bf16[8,64,512]{2,1,0:T(8,128)(2,1)}) %reduce-scatter.11.cloned.1.call-update) | async-done | bytes 524304 | tf_op jit(solution)/shard_map/reduce_scatter | solution.py:181
  380.0 1.8 fusion.41
  381.9 32.2 %reduce-scatter.7.cloned.1.call-done = bf16[8,64,512]{2,1,0:T(8,128)(2,1)} async-done(((bf16[8,256,512]{2,1,0:T(8,128)(2,1)}), bf16[8,64,512]{2,1,0:T(8,128)(2,1)}) %reduce-scatter.7.cloned.1.call-update) | async-done | bytes 524304 | tf_op jit(solution)/shard_map/reduce_scatter | solution.py:112
  414.1 2.9 fusion.39
  417.1 39.6 %all-reduce = (f32[2,512]{1,0:T(2,128)}, f32[2,512]{1,0:T(2,128)}, f32[2,512]{1,0:T(2,128)}) all-reduce(f32[2,512]{1,0:T(2,128)S(1)} %pad_maximum_fusion.3, f32[2,512]{1,0:T(2,128)S(1)} %pad_maximum_fusion.4, f32[2,512]{1,0:T(2,128)S(1)} %pad_maximum_fusion.5), channel_id=1, replica_groups=mesh['dp'=8,'mp'=4] {'dp','mp'}, use_global_device_ids=true, to_apply=%region_17.18 | all-reduce | flops 3072 | bytes 24576 | tf_op jit(solution)/shard_map/psum | solution.py:238
  (89 shorter events, 10.6 us)
Async XLA Ops:
  7.2 134.6 %copy-start = (bf16[512,512]{1,0:T(8,128)(2,1)S(1)}, bf16[512,512]{1,0:T(8,128)(2,1)}, u32[]{:S(2)}) copy-start(bf16[512,512]{1,0:T(8,128)(2,1)} %param.26) | copy-start | bytes 1572868
  7.2 32.3 %copy-start.18 = (bf16[3,512,128]{2,1,0:T(8,128)(2,1)S(1)}, bf16[3,512,128]{2,1,0:T(8,128)(2,1)}, u32[]{:S(2)}) copy-start(bf16[3,512,128]{2,1,0:T(8,128)(2,1)} %param.19) | copy-start | bytes 1179652
  7.2 27.7 %all-gather.5.cloned.1.call-start = ((), (), s32[]{:S(2)}) async-start(), calls=%async_computation.4 | async-start | bytes 2621440 | tf_op jit(solution)/shard_map/all_gather | solution.py:55
  7.9 84.2 %reduce-scatter.5.cloned.1.call-start = ((), (), s32[]{:S(2)}) async-start(), calls=%async_computation.5 | async-start | bytes 5242880 | tf_op jit(solution)/shard_map/reduce_scatter | solution.py:96
  34.9 4.5 copy-start.1
  41.1 1.5 copy-start.10
  41.3 2.0 copy-start.8
  41.3 2.0 copy-start.14
  42.7 2.0 copy-start.2
  43.3 1.4 copy-start.16
  44.7 2.8 copy-start.17
  44.8 47.4 %copy-start.9 = (bf16[8,64,512]{2,1,0:T(8,128)(2,1)S(1)}, bf16[8,64,512]{2,1,0:T(8,128)(2,1)}, u32[]{:S(2)}) copy-start(bf16[8,64,512]{2,1,0:T(8,128)(2,1)} %param.14) | copy-start | bytes 1572868
  47.5 70.2 %copy-start.13 = (bf16[512,512]{1,0:T(8,128)(2,1)S(1)}, bf16[512,512]{1,0:T(8,128)(2,1)}, u32[]{:S(2)}) copy-start(bf16[512,512]{1,0:T(8,128)(2,1)} %param.24) | copy-start | bytes 1572868
  47.5 70.2 %all-gather.7.cloned.1.call-start = ((), (), s32[]{:S(2)}) async-start(), calls=%async_computation.6 | async-start | bytes 2621440 | tf_op jit(solution)/shard_map/all_gather | solution.py:99
  94.9 46.9 %copy-start.19 = (f32[512]{0:T(512)S(1)}, f32[512]{0:T(512)}, u32[]{:S(2)}) copy-start(f32[512]{0:T(512)} %param.25) | copy-start | bytes 6148
  94.9 46.9 %all-gather.9.cloned.1.call-start = ((), (), s32[]{:S(2)}) async-start(), calls=%async_computation.8 | async-start | bytes 2621440 | tf_op jit(solution)/shard_map/all_gather | solution.py:118
  95.5 101.5 %reduce-scatter.9.cloned.1.call-start = ((), (), s32[]{:S(2)}) async-start(), calls=%async_computation.9 | async-start | bytes 5242880 | tf_op jit(solution)/shard_map/reduce_scatter | solution.py:130
  147.6 1.3 copy-start.4
  152.2 46.5 %copy-start.6 = (bf16[8,64,512]{2,1,0:T(8,128)(2,1)S(1)}, bf16[8,64,512]{2,1,0:T(8,128)(2,1)}, u32[]{:S(2)}) copy-start(bf16[8,64,512]{2,1,0:T(8,128)(2,1)} %param.27) | copy-start | bytes 1572868
  152.3 71.7 %all-gather.11.cloned.1.call-start = ((), (), s32[]{:S(2)}) async-start(), calls=%async_computation.10 | async-start | bytes 2621440 | tf_op jit(solution)/shard_map/all_gather | solution.py:134
  201.2 145.4 %all-reduce.5.cloned.1.call-start = ((), (), s32[]{:S(2)}) async-start(), calls=%async_computation.12 | async-start | bytes 3145728 | tf_op jit(solution)/shard_map/psum | solution.py:240
  201.2 4.5 copy-start.7
  226.3 0.8 copy-start.12
  230.9 11.7 %copy-start.11 = (bf16[1,8,256,128]{2,3,0,1:T(8,128)(2,1)S(1)}, bf16[1,8,256,128]{2,3,0,1:T(8,128)(2,1)}, u32[]{:S(2)}) copy-start(bf16[1,8,256,128]{2,3,0,1:T(8,128)(2,1)} %copy-done.10) | copy-start | bytes 1572868
  239.0 3.6 copy-start.5
  252.0 4.3 copy-start.15
  256.3 123.7 %reduce-scatter.11.cloned.1.call-start = ((), (), s32[]{:S(2)}) async-start(), calls=%async_computation.11 | async-start | bytes 2621440 | tf_op jit(solution)/shard_map/reduce_scatter | solution.py:181
  260.1 154.1 %reduce-scatter.7.cloned.1.call-start = ((), (), s32[]{:S(2)}) async-start(), calls=%async_computation.7 | async-start | bytes 2621440 | tf_op jit(solution)/shard_map/reduce_scatter | solution.py:112
  269.7 144.5 %copy-start.3 = (f32[8,64,512]{2,1,0:T(8,128)S(1)}, f32[8,64,512]{2,1,0:T(8,128)}, u32[]{:S(2)}) copy-start(f32[8,64,512]{2,1,0:T(8,128)} %reduce-scatter.9.cloned.1.call-done) | copy-start | bytes 3145732
Sparse Core Ops, SparseCore 0:
  9.6 25.2 all-gather.4
  47.6 44.4 reduce-scatter.4
  95.0 22.5 all-gather.6
  119.1 22.5 all-gather.8
  152.4 44.5 reduce-scatter.8
  201.3 22.5 all-gather.10
  256.4 90.1 all-reduce.4
  349.1 30.8 reduce-scatter.10
  382.7 31.3 reduce-scatter.6
where the time goes:
time: 464 us; the launch traced here: 463 us
  waiting for transfers between devices  278 us (60%)
  matrix products  64.8 us (14%)
  blocking collectives  61.4 us (13%)
  other arithmetic  31.5 us (7%)
  between operations  14.2 us (3%)
  local copies, waits for them, and re-layouts  12.9 us (3%)
    psum x1, waiting for transfers between devices, body(): lax.psum(weight_terms[0].astype(jnp.bfloat16), 'dp').astype(jnp.float32)  52 us
    reduce_scatter x1, waiting for transfers between devices, heads_layer(): lax.psum_scatter(attn_terms, 'mp', scatter_dimension=1, tiled=True)  44.6 us
    reduce_scatter x1, waiting for transfers between devices, heads_layer(): lax.psum_scatter(mid_terms, 'mp', scatter_dimension=1, tiled=True)  44.4 us
    psum x1, blocking collectives, body(): lax.psum((vector_terms[0], vector_terms[1], vector_terms[2]), ('dp', 'mp'))  39.6 us
    reduce_scatter x1, waiting for transfers between devices, heads_layer(): lax.psum_scatter(mlp_terms.astype(jnp.bfloat16), 'mp', scatter_dimension=...  32.2 us
    reduce_scatter x1, waiting for transfers between devices, heads_layer(): lax.psum_scatter(in_terms.astype(jnp.bfloat16), 'mp', scatter_dimension=1...  25.4 us
    all_gather x1, waiting for transfers between devices, heads_layer(): whole_x = lax.all_gather(tokens, 'mp', axis=1, tiled=True)  22.2 us
    all_gather x1, waiting for transfers between devices, heads_layer(): lax.all_gather((second_normalized * norm_scale_pair[1] + norm_offset_pair...  22.1 us
  transfers between devices with their start and end apart: 9, of which 9 were waited for; matrix products, arithmetic and copies ran while one was open for 10% of the time, Pallas kernels for 0%

commit v1 on v0

v1 whole, which is shorter than its diff:
```python
import jax
import jax.numpy as jnp
from jax import lax
from jax.sharding import PartitionSpec as P

HD = 64
F32 = jnp.float32
BF16 = jnp.bfloat16


def swap(v, axis, bit, size):
    return lax.ppermute(v, axis, [(i, i ^ bit) for i in range(size)])


def bits_of(size):
    return [1 << b for b in range(size.bit_length() - 1)]


def normalize(v):
    centre = v - jnp.mean(v, -1, keepdims=True)
    rstd = lax.rsqrt(jnp.mean(centre * centre, -1, keepdims=True) + 1e-05)
    return centre * rstd, rstd


def norm_back(g, normed, rstd, gain):
    e = g * gain
    return rstd * (
        e - jnp.mean(e, -1, keepdims=True) - normed * jnp.mean(e * normed, -1, keepdims=True)
    )


def gelu_fn(v):
    return jax.nn.gelu(v, approximate=True)


def make_body(n_dp, n_mp):
    def gather_mp(v):
        blocks = {0: v}
        for bit in reversed(bits_of(n_mp)):
            for k in list(blocks):
                blocks[k ^ bit] = swap(blocks[k], "mp", bit, n_mp)
        return [blocks[k] for k in range(n_mp)]

    def body(
        tokens,
        lengths,
        order_mask,
        norm_scale_pair,
        norm_offset_pair,
        w_qkv,
        qv_bias,
        order_bias,
        w_out,
        out_bias,
        w_up,
        up_bias,
        w_down,
        cotangent,
    ):
        rows, share, width = tokens.shape
        slots = order_mask.shape[1]
        own_rows = rows // n_mp
        me = lax.axis_index("mp")
        dpi = lax.axis_index("dp")
        factor = HD**-0.5

        def to_rows(v):
            parts = []
            for k in range(n_mp):
                part = lax.dynamic_slice_in_dim(v, (me ^ k) * own_rows, own_rows, 0)
                parts.append(part if k == 0 else swap(part, "mp", k, n_mp))
            return jnp.concatenate(parts, 1)

        def from_rows(v):
            parts = []
            for k in range(n_mp):
                part = v[:, k * share : (k + 1) * share]
                parts.append(part if k == 0 else swap(part, "mp", k, n_mp))
            stacked = jnp.stack(parts)
            natural = jnp.take(stacked, me ^ jnp.arange(n_mp), axis=0)
            return natural.reshape(rows, share, width)

        x_bf = to_rows(tokens)
        w_qkv_all = jnp.concatenate(gather_mp(w_qkv), 2)
        small = jnp.concatenate([qv_bias.reshape(-1), up_bias, order_bias])
        smalls = gather_mp(small)
        lane = qv_bias.shape[1]
        hid = up_bias.shape[0]
        qv_bias_all = jnp.concatenate([s[: 2 * lane].reshape(2, lane) for s in smalls], 1)
        up_bias_all = jnp.concatenate([s[2 * lane : 2 * lane + hid] for s in smalls])
        order_bias_all = jnp.concatenate([s[2 * lane + hid :] for s in smalls])
        w_out_all = jnp.concatenate(gather_mp(w_out), 0)
        dy_bf = to_rows(cotangent)
        w_up_all = jnp.concatenate(gather_mp(w_up), 1)
        w_down_all = jnp.concatenate(gather_mp(w_down), 0)

        slot_of = jnp.concatenate([(me ^ k) * share + jnp.arange(share) for k in range(n_mp)])
        own_len = lax.dynamic_slice_in_dim(lengths, me * own_rows, own_rows, 0)
        own_order = jnp.take(
            lax.dynamic_slice_in_dim(order_mask, me * own_rows, own_rows, 0), slot_of, axis=1
        )
        keep = slot_of[None, :] < own_len[:, None]
        keep_f = keep.astype(F32)
        heads = w_out_all.shape[0] // HD

        x = x_bf.astype(F32)
        n1, rstd1 = normalize(x)
        a1 = (n1 * norm_scale_pair[0] + norm_offset_pair[0]).astype(BF16)
        proj = jnp.einsum("rsd,tde->trse", a1, w_qkv_all, preferred_element_type=F32)
        split = (own_rows, slots, heads, HD)
        query = (proj[0] + qv_bias_all[0]).astype(BF16).reshape(split)
        keyed = proj[1].astype(BF16).reshape(split)
        value = (proj[2] + qv_bias_all[1]).astype(BF16).reshape(split)
        raw = jnp.einsum("rqhe,rkhe->rhqk", query, keyed, preferred_element_type=F32) * factor
        raw = raw + order_bias_all[None, :, None, None] * own_order.astype(F32)[:, None, None, :]
        scores = jnp.where(keep[:, None, None, :], raw, -1e30)
        expo = jnp.exp(scores - jnp.max(scores, -1, keepdims=True))
        probs = expo / jnp.sum(expo, -1, keepdims=True)
        probs_bf = probs.astype(BF16)
        attended = jnp.einsum("rhqk,rkhe->rqhe", probs_bf, value, preferred_element_type=F32)
        attended = (attended.reshape(own_rows, slots, heads * HD) * keep_f[:, :, None]).astype(BF16)
        x1 = x + jnp.dot(attended, w_out_all, preferred_element_type=F32) + out_bias[0]
        n2, rstd2 = normalize(x1)
        a2 = (n2 * norm_scale_pair[1] + norm_offset_pair[1]).astype(BF16)
        pre = jnp.dot(a2, w_up_all, preferred_element_type=F32) + up_bias_all
        gelu_out, gelu_pull = jax.vjp(gelu_fn, pre)
        hidden = gelu_out.astype(BF16)
        mixed = jnp.dot(hidden, w_down_all, preferred_element_type=F32)
        output = from_rows((x1 + mixed + out_bias[1]).astype(BF16))

        dy = dy_bf.astype(F32)
        g_down = jnp.einsum("rsf,rsd->fd", hidden, dy_bf, preferred_element_type=F32)
        d_hidden = jnp.dot(dy_bf, w_down_all.T, preferred_element_type=F32)
        d_pre = gelu_pull(d_hidden)[0].astype(BF16)
        g_up = jnp.einsum("rsf,rsd->fd", d_pre, a2, preferred_element_type=F32)
        g_up_bias = jnp.sum(d_pre.astype(F32), (0, 1))
        d_mid = jnp.dot(d_pre, w_up_all.T, preferred_element_type=F32)
        dx1 = dy + norm_back(d_mid, n2, rstd2, norm_scale_pair[1])
        d_att = dx1.astype(BF16)
        g_out = jnp.einsum("rse,rsd->ed", attended, d_att, preferred_element_type=F32)
        d_o = jnp.dot(d_att, w_out_all.T, preferred_element_type=F32).astype(BF16)
        d_o = (d_o * keep_f[:, :, None].astype(BF16)).reshape(split)
        d_value = jnp.einsum("rhqk,rqhe->rkhe", probs_bf, d_o, preferred_element_type=F32)
        d_probs = jnp.einsum("rqhe,rkhe->rhqk", d_o, value, preferred_element_type=F32)
        d_scores = probs * (d_probs - jnp.sum(probs * d_probs, -1, keepdims=True))
        d_scores = jnp.where(keep[:, None, None, :], d_scores, 0.0).astype(BF16)
        g_order = jnp.einsum(
            "rhqk,rk->h", d_scores, own_order.astype(BF16), preferred_element_type=F32
        )
        d_query = jnp.einsum("rhqk,rkhe->rqhe", d_scores, keyed, preferred_element_type=F32)
        d_key = jnp.einsum("rhqk,rqhe->rkhe", d_scores, query, preferred_element_type=F32)
        stacked = jnp.stack(
            [
                (d_query * factor).astype(BF16),
                (d_key * factor).astype(BF16),
                d_value.astype(BF16),
            ]
        ).reshape(3, own_rows, slots, heads * HD)
        g_qkv = jnp.einsum("trse,rsd->ted", stacked, a1, preferred_element_type=F32)
        g_q_bias = jnp.sum(stacked[0].astype(F32), (0, 1))
        g_v_bias = jnp.sum(stacked[2].astype(F32), (0, 1))
        d_in = jnp.einsum("trse,tde->rsd", stacked, w_qkv_all, preferred_element_type=F32)
        token_gradient = dx1 + norm_back(d_in, n1, rstd1, norm_scale_pair[0])
        token_gradient = from_rows(token_gradient.astype(BF16)).astype(F32)

        shared = jnp.stack(
            [
                jnp.sum(d_in * n1, (0, 1)),
                jnp.sum(d_mid * n2, (0, 1)),
                jnp.sum(d_in, (0, 1)),
                jnp.sum(d_mid, (0, 1)),
                jnp.sum(d_att.astype(F32), (0, 1)),
                jnp.sum(dy, (0, 1)),
            ]
        )

        mp_bits, dp_bits = bits_of(n_mp), bits_of(n_dp)
        dp_sub = jnp.zeros((1,), jnp.int32)
        for bit in reversed(dp_bits):
            dp_sub = jnp.concatenate([dp_sub, dp_sub + bit])
        mp_order = [0]
        for bit in reversed(mp_bits):
            mp_order = mp_order + [k + bit for k in mp_order]

        def reduce(parts):
            m = parts[0].shape[0]
            cut = [p.astype(BF16).reshape(n_dp, m // n_dp, -1) for p in parts]
            full = jnp.stack([jnp.take(cut[k], dpi ^ dp_sub, axis=0) for k in mp_order])
            steps = [("mp", bit, n_mp) for bit in mp_bits] + [("dp", bit, n_dp) for bit in dp_bits]
            v = full.reshape([2] * len(steps) + list(full.shape[2:]))
            for axis, bit, size in steps:
                v = (v[0].astype(F32) + swap(v[1], axis, bit, size).astype(F32)).astype(BF16)
            v = v[None]
            for bit in reversed(dp_bits):
                v = jnp.concatenate([v, swap(v, "dp", bit, n_dp)])
            place = jnp.argsort(dpi ^ dp_sub)
            return jnp.take(v, place, axis=0).reshape(m, -1).astype(F32)

        def blocks_of(v, axis):
            return jnp.split(v, n_mp, axis)

        r_down = reduce(blocks_of(g_down, 0))
        r_up = reduce(blocks_of(g_up, 0)).T
        r_att = reduce(
            [
                jnp.concatenate([q.reshape(-1, width), o])
                for q, o in zip(blocks_of(g_qkv, 1), blocks_of(g_out, 0))
            ]
        )
        r_qkv = r_att[: 3 * lane].reshape(3, lane, width).transpose(0, 2, 1)
        r_out = r_att[3 * lane :]

        per_head = order_bias.shape[0]
        owned = jnp.stack(
            [
                jnp.concatenate([a, b, c, d])
                for a, b, c, d in zip(
                    blocks_of(g_q_bias, 0),
                    blocks_of(g_v_bias, 0),
                    blocks_of(g_up_bias, 0),
                    blocks_of(g_order, 0),
                )
            ]
        )
        owned = jnp.stack([owned[k] for k in mp_order])
        flat = shared.reshape(-1)
        count = flat.shape[0]
        for bit in mp_bits:
            half = owned.shape[0] // 2
            got = swap(jnp.concatenate([flat, owned[half:].reshape(-1)]), "mp", bit, n_mp)
            flat = flat + got[:count]
            owned = owned[:half] + got[count:].reshape(half, -1)
        flat = jnp.concatenate([flat, owned[0]])
        for bit in dp_bits:
            flat = flat + swap(flat, "dp", bit, n_dp)
        shared = flat[:count].reshape(6, width)
        owned = flat[count:]
        return (
            output,
            token_gradient,
            shared[0:2],
            shared[2:4],
            r_qkv,
            owned[: 2 * lane].reshape(2, lane),
            owned[2 * lane + hid :],
            r_out,
            shared[4:6],
            r_up,
            owned[2 * lane : 2 * lane + hid],
            r_down,
        )

    return body


def solution(mesh):
    return jax.shard_map(
        make_body(mesh.shape["dp"], mesh.shape["mp"]),
        mesh=mesh,
        in_specs=(
            P("dp", "mp", None),
            P("dp"),
            P("dp", None),
            P(),
            P(),
            P(None, None, "mp"),
            P(None, "mp"),
            P("mp"),
            P("mp", None),
            P(),
            P(None, "mp"),
            P("mp"),
            P("mp", None),
            P("dp", "mp", None),
        ),
        out_specs=(
            P("dp", "mp", None),
            P("dp", "mp", None),
            P(),
            P(),
            P(None, None, "mp"),
            P(None, "mp"),
            P("mp"),
            P("mp", None),
            P(),
            P(None, "mp"),
            P("mp"),
            P("mp", None),
        ),
        check_vma=False,
    )
```

time: 464 us -> 315 us (0.68)
  waiting for transfers between devices: 278 us -> 76.9 us
  local copies, waits for them, and re-layouts: 12.9 us -> 78.4 us
  blocking collectives: 61.4 us -> 0 us
  starting transfers between devices: 0.77 us -> 50.1 us
  other arithmetic: 31.5 us -> 46.4 us
  between operations: 14.2 us -> 2.04 us
  matrix products: 64.8 us -> 59 us
    reduce_scatter x4 -> x0, waiting for transfers between devices: 147 us -> none  [the longest x1 44.6 us: heads_layer(): lax.psum_scatter(attn_terms, 'mp', scatter_dimension=1, tiled=True)]
    all_gather x4 -> x0, waiting for transfers between devices: 77.6 us -> none  [the longest x1 22.2 us: heads_layer(): whole_x = lax.all_gather(tokens, 'mp', axis=1, tiled=True)]
    ppermute x0 -> x56, waiting for transfers between devices: none -> 76.9 us  [swap(): return lax.ppermute(v, axis, [(i, i ^ bit) for i in range(size)])]
    psum x2 -> x0, blocking collectives: 61.4 us -> none  [the longest x1 39.6 us: body(): lax.psum((vector_terms[0], vector_terms[1], vector_terms[2]), ('dp', 'mp'))]
    psum x1 -> x0, waiting for transfers between devices: 52 us -> none  [body(): lax.psum(weight_terms[0].astype(jnp.bfloat16), 'dp').astype(jnp.float32)]
    ppermute x0 -> x56, starting transfers between devices: none -> 50.1 us  [swap(): return lax.ppermute(v, axis, [(i, i ^ bit) for i in range(size)])]
    gather x0 -> x18, local copies, waits for them, and re-layouts: none -> 28.4 us  [the longest x12 23.2 us: reduce(): full = jnp.stack([jnp.take(cut[k], dpi ^ dp_sub, axis=0) for k in mp_order])]
    split x0 -> x16, local copies, waits for them, and re-layouts: none -> 17.5 us  [blocks_of(): return jnp.split(v, n_mp, axis)]
  transfers between devices with their start and end apart: 9 -> 56, of which waited for: 9 -> 27; matrix products, arithmetic and copies ran while one was open for 10% -> 44% of each run, Pallas kernels for 0% -> 0%
where the time goes in v1:
time: 315 us; the launch traced here: 313 us
  local copies, waits for them, and re-layouts  78.4 us (25%)
  waiting for transfers between devices  76.9 us (24%)
  matrix products  59 us (19%)
  starting transfers between devices  50.1 us (16%)
  other arithmetic  46.4 us (15%)
    ppermute x56, waiting for transfers between devices, swap(): return lax.ppermute(v, axis, [(i, i ^ bit) for i in range(size)])  76.9 us
    ppermute x56, starting transfers between devices, swap(): return lax.ppermute(v, axis, [(i, i ^ bit) for i in range(size)])  50.1 us
    gather x12, local copies, waits for them, and re-layouts, reduce(): full = jnp.stack([jnp.take(cut[k], dpi ^ dp_sub, axis=0) for k in mp_order])  23.2 us
    split x16, local copies, waits for them, and re-layouts, blocks_of(): return jnp.split(v, n_mp, axis)  17.5 us
    dot_general x1, matrix products, body(): d_hidden = jnp.dot(dy_bf, w_down_all.T, preferred_element_type=F32)  8.35 us
    sub x1, matrix products, body(): d_scores = probs * (d_probs - jnp.sum(probs * d_probs, -1, keepdims=True))  7.05 us
    concatenate x4, other arithmetic, body(): jnp.concatenate([q.reshape(-1, width), o])  6.51 us
  transfers between devices with their start and end apart: 56, of which 27 were waited for; matrix products, arithmetic and copies ran while one was open for 44% of the time, Pallas kernels for 0%

profile of v1, /device:TPU:0, one launch (start us, length us, event | category | flops | bytes accessed | tf_op | source)
XLA Modules:
  0.0 312.9 jit_solution(16087260051134993224)
XLA Ops:
  1.4 3.0 collective-permute-start.7
  21.8 2.1 collective-permute-start.2
  31.8 2.0 collective-permute-done.10
  38.4 3.4 %fusion.107 = (f32[2,8,256]{2,1,0:T(8,128)S(1)}, f32[2,8,256,256]{2,3,1,0:T(8,128)}) fusion(f32[2,8,256]{2,1,0:T(8,128)S(1)} %broadcast_multiply_fusion, pred[2,256]{1,0:T(4,128)(4,1)S(1)} %get-tuple-element.43, bf16[2,256,8,64]{1,3,2,0:T(8,128)(2,1)S(1)} %bitcast.288, f32[2,256,8,64]{1,3,2,0:T(8,128)S(1)} %bitcast.269, f32[8,64]{1,0:T(8,128)S(1)} %add.315), kind=kOutput, calls=%fused_computation.307 | convolution fusion | flops 139985152 | bytes 5802496 | tf_op jit(solution)/shard_map/sub | solution.py:117
  41.9 3.1 %fusion.50 = f32[2,8,64,256]{3,2,1,0:T(8,128)S(1)} fusion(f32[2,8,256,256]{2,3,1,0:T(8,128)} %get-tuple-element.126, f32[2,8,256]{2,1,0:T(8,128)S(1)} %get-tuple-element.125, f32[2,256,8,64]{1,3,2,0:T(8,128)} %bitcast.304, f32[8,64]{1,0:T(8,128)S(1)} %add.304), kind=kOutput, calls=%fused_computation.113 | convolution fusion | flops 136839168 | bytes 6309888 | tf_op jit(solution)/shard_map/rhqk,rkhe->rqhe/dot_general | solution.py:120
  45.8 3.2 %collective-permute-done.13 = bf16[512,512]{1,0:T(8,128)(2,1)} collective-permute-done((bf16[512,512]{1,0:T(8,128)(2,1)}, bf16[512,512]{1,0:T(8,128)(2,1)}, u32[]{:S(2)}, u32[]{:S(2)}) %collective-permute-start.13) | collective-permute-done | bytes 524320 | tf_op jit(solution)/shard_map/ppermute | solution.py:12
  49.0 9.4 %collective-permute-done.16 = bf16[512,512]{1,0:T(8,128)(2,1)} collective-permute-done((bf16[512,512]{1,0:T(8,128)(2,1)}, bf16[512,512]{1,0:T(8,128)(2,1)}, u32[]{:S(2)}, u32[]{:S(2)}) %collective-permute-start.16) | collective-permute-done | bytes 524320 | tf_op jit(solution)/shard_map/ppermute | solution.py:12
  62.5 2.7 fusion.53
  65.8 3.2 %collective-permute-done.22 = bf16[2,64,512]{2,1,0:T(8,128)(2,1)S(1)} collective-permute-done((bf16[2,64,512]{2,1,0:T(8,128)(2,1)S(1)}, bf16[2,64,512]{2,1,0:T(8,128)(2,1)S(1)}, u32[]{:S(2)}, u32[]{:S(2)}) %collective-permute-start.22) | collective-permute-done | bytes 131104 | tf_op jit(solution)/shard_map/ppermute | solution.py:12
  69.0 8.4 %convert_reduce_fusion.1 = (f32[2048]{0:T(1024)}, bf16[2,256,2048]{2,1,0:T(8,128)(2,1)S(1)}) fusion(f32[2,256,2048]{2,1,0:T(8,128)S(1)} %fusion.53, f32[2048]{0:T(1024)S(1)} %copy-done.44, bf16[512,512]{1,0:T(8,128)(2,1)S(1)} %collective-permute-done.17, bf16[512,512]{1,0:T(8,128)(2,1)} %collective-permute-done.16, ...), kind=kOutput, calls=%fused_computation.32 | convolution fusion | flops 1108342784 | bytes 8929280 | tf_op jit(solution)/shard_map/dot_general | solution.py:133
  77.4 2.7 bitcast_convert_fusion.1
  80.1 3.5 %multiply_reduce_fusion.1 = (f32[512]{0:T(512)}, f32[2,256]{1,0:T(2,128)S(1)}, f32[2,256]{1,0:T(2,128)S(1)}, f32[512]{0:T(512)}, f32[2,256,512]{2,1,0:T(8,128)S(1)}) fusion(f32[2,256,512]{2,1,0:T(8,128)S(1)} %get-tuple-element.128, f32[2,256]{1,0:T(2,128)S(1)} %add_rsqrt_fusion, f32[2,256]{1,0:T(2,128)S(1)} %broadcast_multiply_fusion.5, ...), kind=kOutput, calls=%fused_computation.108 | convolution fusion | flops 1084487680 | bytes 6305792 | tf_op jit(solution)/shard_map/dot_general | solution.py:137
  88.5 4.4 %convert_reduce_fusion.4 = (f32[8,64]{1,0:T(8,128)}, bf16[2,8,64,256]{3,2,1,0:T(8,128)(2,1)}) fusion(bf16[2,256,8,64]{1,3,2,0:T(8,128)(2,1)S(1)} %bitcast.308, f32[2,8,256,256]{2,3,1,0:T(8,128)} %get-tuple-element.126, f32[2,8,256]{2,1,0:T(8,128)S(1)} %copy-done.81), kind=kOutput, calls=%fused_computation.105 | convolution fusion | flops 137100800 | bytes 5261312 | tf_op jit(solution)/shard_map/rhqk,rqhe->rkhe/dot_general | solution.py:143
  92.8 7.1 %convert_reduce_fusion = (bf16[2,8,256]{2,1,0:T(8,128)(2,1)}, bf16[2,8,256,256]{2,3,1,0:T(8,128)(2,1)S(1)}) fusion(bf16[2,256,8,64]{1,3,2,0:T(8,128)(2,1)} %bitcast.309, f32[2,8,256,256]{2,3,1,0:T(8,128)} %get-tuple-element.126, f32[2,8,256]{2,1,0:T(8,128)} %copy-done.80, pred[2,256]{1,0:T(4,128)(4,1)S(1)} %copy-done.56, f32[2,256,8,64]{1,3,2,0:T(8,128)} %bitcast.305, ...), kind=kOutput, calls=%fused_computation.31 | convolution fusion | flops 278921472 | bytes 7891456 | tf_op jit(solution)/shard_map/sub | solution.py:145
  99.9 3.0 fusion.27
  102.9 2.3 convert_reduce_fusion.5
  105.3 2.9 fusion.25
  111.5 2.2 bitcast_convert_fusion
  116.8 2.7 fusion.96
  121.8 2.4 gather_fusion.10
  124.2 2.6 gather_fusion.9
  126.9 2.4 gather_fusion.15
  129.3 2.4 gather_fusion.14
  131.7 2.0 copy.61
  133.7 2.0 copy.62
  143.9 2.0 copy.60
  145.9 2.6 bitcast_convert_fusion.2
  150.4 2.4 gather_fusion.3
  154.7 2.4 gather_fusion.6
  162.6 4.5 %fusion.43 = (f32[512]{0:T(512)}, f32[2,256]{1,0:T(2,128)S(1)}, f32[2,256]{1,0:T(2,128)S(1)}, f32[512]{0:T(512)}, f32[2,256,512]{2,1,0:T(8,128)}) fusion(f32[2,256]{1,0:T(2,128)} %copy-done.49, f32[2,256]{1,0:T(2,128)} %copy-done.39, bf16[2,64,512]{2,1,0:T(8,128)(2,1)S(1)} %collective-permute-done.2, bf16[2,64,512]{2,1,0:T(8,128)(2,1)} %copy-done.17, ...), kind=kOutput, calls=%fused_computation.90 | convolution fusion | flops 817625088 | bytes 4732928 | tf_op jit(solution)/shard_map/trse,tde->rsd/dot_general | solution.py:162
  174.3 2.5 gather_fusion.5
  178.7 2.5 gather_fusion.4
  182.1 5.0 %broadcast_select_fusion.5 = (bf16[8,64,512]{2,1,0:T(8,128)(2,1)}, bf16[8,64,512]{2,1,0:T(8,128)(2,1)}, bf16[8,64,512]{2,1,0:T(8,128)(2,1)}, bf16[8,64,512]{2,1,...) fusion(bf16[8,64,512]{2,1,0:T(8,128)(2,1)S(1)} %gather_fusion.1, ...), kind=kLoop, calls=%fused_computation.157 | loop fusion | flops 3145728 | bytes 12582920 | tf_op jit(solution)/shard_map/jit(_take)/select_n | solution.py:188
  195.4 2.3 pad_maximum_fusion.4
  201.5 2.6 collective-permute-start.31
  215.4 2.0 pad_maximum_fusion.10
  227.8 8.9 %collective-permute-done.49 = bf16[2,2,2,64,512]{4,3,2,1,0:T(8,128)(2,1)S(1)} collective-permute-done((bf16[2,2,2,64,512]{4,3,2,1,0:T(8,128)(2,1)S(1)}, bf16[2,2,2,64,512]{4,3,2,1,0:T(8,128)(2,1)S(1)}, u32[]{:S(2)}, u32[]{:S(2)}) %collective-permute-start.49) | collective-permute-done | bytes 524320 | tf_op jit(solution)/shard_map/ppermute | solution.py:12
  238.3 9.6 %collective-permute-done.41 = bf16[2,2,2,64,512]{4,3,2,1,0:T(8,128)(2,1)S(1)} collective-permute-done((bf16[2,2,2,64,512]{4,3,2,1,0:T(8,128)(2,1)S(1)}, bf16[2,2,2,64,512]{4,3,2,1,0:T(8,128)(2,1)S(1)}, u32[]{:S(2)}, u32[]{:S(2)}) %collective-permute-start.41) | collective-permute-done | bytes 524320 | tf_op jit(solution)/shard_map/ppermute | solution.py:12
  249.5 8.8 %collective-permute-done.33 = bf16[2,2,2,64,512]{4,3,2,1,0:T(8,128)(2,1)S(1)} collective-permute-done((bf16[2,2,2,64,512]{4,3,2,1,0:T(8,128)(2,1)S(1)}, bf16[2,2,2,64,512]{4,3,2,1,0:T(8,128)(2,1)S(1)}, u32[]{:S(2)}, u32[]{:S(2)}) %collective-permute-start.33) | collective-permute-done | bytes 524320 | tf_op jit(solution)/shard_map/ppermute | solution.py:12
  262.3 3.8 %collective-permute-done.34 = bf16[2,2,64,512]{3,2,1,0:T(8,128)(2,1)S(1)} collective-permute-done((bf16[2,2,64,512]{3,2,1,0:T(8,128)(2,1)S(1)}, bf16[2,2,64,512]{3,2,1,0:T(8,128)(2,1)S(1)}, u32[]{:S(2)}, u32[]{:S(2)}) %collective-permute-start.34) | collective-permute-done | bytes 262176 | tf_op jit(solution)/shard_map/ppermute | solution.py:12
  267.8 2.7 collective-permute-start.52
  271.6 2.9 collective-permute-start.36
  276.1 3.7 %collective-permute-done.44 = bf16[64,512]{1,0:T(8,128)(2,1)S(1)} collective-permute-done((bf16[64,512]{1,0:T(8,128)(2,1)S(1)}, bf16[64,512]{1,0:T(8,128)(2,1)S(1)}, u32[]{:S(2)}, u32[]{:S(2)}) %collective-permute-start.44) | collective-permute-done | bytes 65568 | tf_op jit(solution)/shard_map/ppermute | solution.py:12
  279.9 2.0 collective-permute-done.36
  288.3 3.1 collective-permute-done.54
  297.6 3.0 collective-permute-done.55
  301.4 3.1 %collective-permute-done.47 = bf16[4,64,512]{2,1,0:T(8,128)(2,1)S(1)} collective-permute-done((bf16[4,64,512]{2,1,0:T(8,128)(2,1)S(1)}, bf16[4,64,512]{2,1,0:T(8,128)(2,1)S(1)}, u32[]{:S(2)}, u32[]{:S(2)}) %collective-permute-start.47) | collective-permute-done | bytes 262176 | tf_op jit(solution)/shard_map/ppermute | solution.py:12
  305.4 2.0 collective-permute-done.39
  (440 shorter events, 141.2 us)
Async XLA Ops:
  1.4 20.4 %collective-permute-start.7 = (f32[770]{0:T(1024)S(1)}, f32[770]{0:T(1024)S(1)}, u32[]{:S(2)}, u32[]{:S(2)}) collective-permute-start(f32[770]{0:T(1024)S(1)} %pad_maximum_fusion.31), channel_id=1, source_target_pairs={{0,2},{1,3},{2,0},{3,1},{4,6},{5,7},{6,4},{7,5},{8,10},{9,11},{10,... | collective-permute-start | bytes 9248 | tf_op jit(solution)/shard_map/ppermute | solution.py:12
  4.4 19.5 %collective-permute-start.6 = (f32[770]{0:T(1024)S(1)}, f32[770]{0:T(1024)S(1)}, u32[]{:S(2)}, u32[]{:S(2)}) collective-permute-start(f32[770]{0:T(1024)S(1)} %pad_maximum_fusion.31), channel_id=1, source_target_pairs={{0,1},{1,0},{2,3},{3,2},{4,5},{5,4},{6,7},{7,6},{8,9},{9,8},{10,11... | collective-permute-start | bytes 9248 | tf_op jit(solution)/shard_map/ppermute | solution.py:12
  4.4 40.8 %collective-permute-start.9 = (bf16[128,512]{1,0:T(8,128)(2,1)}, bf16[128,512]{1,0:T(8,128)(2,1)}, u32[]{:S(2)}, u32[]{:S(2)}) collective-permute-start(bf16[128,512]{1,0:T(8,128)(2,1)} %param.26), channel_id=1, source_target_pairs={{0,1},{1,0},{2,3},{3,2},{4,5},{5,4},{6,7},{7,6},{8,9},{9,8},{10,11... | collective-permute-start | bytes 393224 | tf_op jit(solution)/shard_map/ppermute | solution.py:12
  6.0 24.9 %collective-permute-start.4 = (bf16[3,512,128]{1,2,0:T(8,128)(2,1)S(1)}, bf16[3,512,128]{1,2,0:T(8,128)(2,1)S(1)}, u32[]{:S(2)}, u32[]{:S(2)}) collective-permute-start(bf16[3,512,128]{1,2,0:T(8,128)(2,1)S(1)} %copy.49), channel_id=1, source_target_pairs={{0,2},{1,3},{2,0},{3,1},{4,6},{5,7},{6,4},{7,5},{8,10},{9,11},{10,... | collective-permute-start | bytes 1179656 | tf_op jit(solution)/shard_map/ppermute | solution.py:12
  7.3 20.8 %collective-permute-start = (bf16[2,64,512]{2,1,0:T(8,128)(2,1)S(1)}, bf16[2,64,512]{2,1,0:T(8,128)(2,1)S(1)}, u32[]{:S(2)}, u32[]{:S(2)}) collective-permute-start(bf16[2,64,512]{2,1,0:T(8,128)(2,1)S(1)} %get-tuple-element.78), channel_id=1, source_target_pairs={{0,1},{1,0},{2,3},{3,2},{4,5},{5,4},{6,7},{7,6},{8,9},{9,8},{10,11... | collective-permute-start | bytes 393224 | tf_op jit(solution)/shard_map/ppermute | solution.py:12
  21.8 8.2 %collective-permute-start.2 = (bf16[2,64,512]{2,1,0:T(8,128)(2,1)S(1)}, bf16[2,64,512]{2,1,0:T(8,128)(2,1)S(1)}, u32[]{:S(2)}, u32[]{:S(2)}) collective-permute-start(bf16[2,64,512]{2,1,0:T(8,128)(2,1)S(1)} %get-tuple-element.79), channel_id=1, source_target_pairs={{0,3},{1,2},{2,1},{3,0},{4,7},{5,6},{6,5},{7,4},{8,11},{9,10},{10,... | collective-permute-start | bytes 393224 | tf_op jit(solution)/shard_map/ppermute | solution.py:12
  25.0 5.7 %collective-permute-start.1 = (bf16[2,64,512]{2,1,0:T(8,128)(2,1)S(1)}, bf16[2,64,512]{2,1,0:T(8,128)(2,1)S(1)}, u32[]{:S(2)}, u32[]{:S(2)}) collective-permute-start(bf16[2,64,512]{2,1,0:T(8,128)(2,1)S(1)} %get-tuple-element.80), channel_id=1, source_target_pairs={{0,2},{1,3},{2,0},{3,1},{4,6},{5,7},{6,4},{7,5},{8,10},{9,11},{10,... | collective-permute-start | bytes 393224 | tf_op jit(solution)/shard_map/ppermute | solution.py:12
  28.1 5.7 %collective-permute-start.10 = (bf16[128,512]{1,0:T(8,128)(2,1)}, bf16[128,512]{1,0:T(8,128)(2,1)S(1)}, u32[]{:S(2)}, u32[]{:S(2)}) collective-permute-start(bf16[128,512]{1,0:T(8,128)(2,1)} %param.26), channel_id=1, source_target_pairs={{0,2},{1,3},{2,0},{3,1},{4,6},{5,7},{6,4},{7,5},{8,10},{9,11},{10,... | collective-permute-start | bytes 393224 | tf_op jit(solution)/shard_map/ppermute | solution.py:12
  30.7 29.5 %collective-permute-start.12 = (bf16[512,512]{1,0:T(8,128)(2,1)}, bf16[512,512]{1,0:T(8,128)(2,1)}, u32[]{:S(2)}, u32[]{:S(2)}) collective-permute-start(bf16[512,512]{1,0:T(8,128)(2,1)} %param.28), channel_id=1, source_target_pairs={{0,1},{1,0},{2,3},{3,2},{4,5},{5,4},{6,7},{7,6},{8,9},{9,8},{10,11... | collective-permute-start | bytes 1572872 | tf_op jit(solution)/shard_map/ppermute | solution.py:12
  33.8 15.2 %collective-permute-start.13 = (bf16[512,512]{1,0:T(8,128)(2,1)}, bf16[512,512]{1,0:T(8,128)(2,1)}, u32[]{:S(2)}, u32[]{:S(2)}) collective-permute-start(bf16[512,512]{1,0:T(8,128)(2,1)} %param.28), channel_id=1, source_target_pairs={{0,2},{1,3},{2,0},{3,1},{4,6},{5,7},{6,4},{7,5},{8,10},{9,11},{10,... | collective-permute-start | bytes 1572872 | tf_op jit(solution)/shard_map/ppermute | solution.py:12
  35.5 22.9 %collective-permute-start.16 = (bf16[512,512]{1,0:T(8,128)(2,1)}, bf16[512,512]{1,0:T(8,128)(2,1)}, u32[]{:S(2)}, u32[]{:S(2)}) collective-permute-start(bf16[512,512]{1,0:T(8,128)(2,1)} %param.30), channel_id=1, source_target_pairs={{0,2},{1,3},{2,0},{3,1},{4,6},{5,7},{6,4},{7,5},{8,10},{9,11},{10,... | collective-permute-start | bytes 1572872 | tf_op jit(solution)/shard_map/ppermute | solution.py:12
  35.9 9.9 %collective-permute-start.11 = (bf16[128,512]{1,0:T(8,128)(2,1)S(1)}, bf16[128,512]{1,0:T(8,128)(2,1)}, u32[]{:S(2)}, u32[]{:S(2)}) collective-permute-start(bf16[128,512]{1,0:T(8,128)(2,1)S(1)} %collective-permute-done.10), channel_id=1, source_target_pairs={{0,1},{1,0},{2,3},{3,2},{4,5},{5,4},{6,7},{7,6},{8,9},{9,8},{10,11... | collective-permute-start | bytes 393224 | tf_op jit(solution)/shard_map/ppermute | solution.py:12
  45.2 23.8 %collective-permute-start.15 = (bf16[512,512]{1,0:T(8,128)(2,1)}, bf16[512,512]{1,0:T(8,128)(2,1)S(1)}, u32[]{:S(2)}, u32[]{:S(2)}) collective-permute-start(bf16[512,512]{1,0:T(8,128)(2,1)} %param.30), channel_id=1, source_target_pairs={{0,1},{1,0},{2,3},{3,2},{4,5},{5,4},{6,7},{7,6},{8,9},{9,8},{10,11... | collective-permute-start | bytes 1572872 | tf_op jit(solution)/shard_map/ppermute | solution.py:12
  45.7 19.5 %collective-permute-start.21 = (bf16[2,64,512]{2,1,0:T(8,128)(2,1)S(1)}, bf16[2,64,512]{2,1,0:T(8,128)(2,1)S(1)}, u32[]{:S(2)}, u32[]{:S(2)}) collective-permute-start(bf16[2,64,512]{2,1,0:T(8,128)(2,1)S(1)} %copy-done.34), channel_id=1, source_target_pairs={{0,1},{1,0},{2,3},{3,2},{4,5},{5,4},{6,7},{7,6},{8,9},{9,8},{10,11... | collective-permute-start | bytes 393224 | tf_op jit(solution)/shard_map/ppermute | solution.py:12
  49.0 13.0 %collective-permute-start.14 = (bf16[512,512]{1,0:T(8,128)(2,1)}, bf16[512,512]{1,0:T(8,128)(2,1)S(1)}, u32[]{:S(2)}, u32[]{:S(2)}) collective-permute-start(bf16[512,512]{1,0:T(8,128)(2,1)} %collective-permute-done.13), channel_id=1, source_target_pairs={{0,1},{1,0},{2,3},{3,2},{4,5},{5,4},{6,7},{7,6},{8,9},{9,8},{10,11... | collective-permute-start | bytes 1572872 | tf_op jit(solution)/shard_map/ppermute | solution.py:12
  58.4 10.6 %collective-permute-start.17 = (bf16[512,512]{1,0:T(8,128)(2,1)}, bf16[512,512]{1,0:T(8,128)(2,1)S(1)}, u32[]{:S(2)}, u32[]{:S(2)}) collective-permute-start(bf16[512,512]{1,0:T(8,128)(2,1)} %collective-permute-done.16), channel_id=1, source_target_pairs={{0,1},{1,0},{2,3},{3,2},{4,5},{5,4},{6,7},{7,6},{8,9},{9,8},{10,11... | collective-permute-start | bytes 1572872 | tf_op jit(solution)/shard_map/ppermute | solution.py:12
  60.3 5.5 %collective-permute-start.23 = (bf16[2,64,512]{2,1,0:T(8,128)(2,1)S(1)}, bf16[2,64,512]{2,1,0:T(8,128)(2,1)S(1)}, u32[]{:S(2)}, u32[]{:S(2)}) collective-permute-start(bf16[2,64,512]{2,1,0:T(8,128)(2,1)S(1)} %copy-done.33), channel_id=1, source_target_pairs={{0,3},{1,2},{2,1},{3,0},{4,7},{5,6},{6,5},{7,4},{8,11},{9,10},{10,... | collective-permute-start | bytes 393224 | tf_op jit(solution)/shard_map/ppermute | solution.py:12
  62.0 7.0 %collective-permute-start.22 = (bf16[2,64,512]{2,1,0:T(8,128)(2,1)S(1)}, bf16[2,64,512]{2,1,0:T(8,128)(2,1)S(1)}, u32[]{:S(2)}, u32[]{:S(2)}) collective-permute-start(bf16[2,64,512]{2,1,0:T(8,128)(2,1)S(1)} %copy-done.32), channel_id=1, source_target_pairs={{0,2},{1,3},{2,0},{3,1},{4,6},{5,7},{6,4},{7,5},{8,10},{9,11},{10,... | collective-permute-start | bytes 393224 | tf_op jit(solution)/shard_map/ppermute | solution.py:12
  109.1 97.1 %collective-permute-start.20 = (bf16[2,64,512]{2,1,0:T(8,128)(2,1)}, bf16[2,64,512]{2,1,0:T(8,128)(2,1)}, u32[]{:S(2)}, u32[]{:S(2)}) collective-permute-start(bf16[2,64,512]{2,1,0:T(8,128)(2,1)} %get-tuple-element.74), channel_id=1, source_target_pairs={{0,3},{1,2},{2,1},{3,0},{4,7},{5,6},{6,5},{7,4},{8,11},{9,10},{10,... | collective-permute-start | bytes 393224 | tf_op jit(solution)/shard_map/ppermute | solution.py:12
  109.7 97.9 %collective-permute-start.19 = (bf16[2,64,512]{2,1,0:T(8,128)(2,1)}, bf16[2,64,512]{2,1,0:T(8,128)(2,1)}, u32[]{:S(2)}, u32[]{:S(2)}) collective-permute-start(bf16[2,64,512]{2,1,0:T(8,128)(2,1)} %get-tuple-element.75), channel_id=1, source_target_pairs={{0,2},{1,3},{2,0},{3,1},{4,6},{5,7},{6,4},{7,5},{8,10},{9,11},{10,... | collective-permute-start | bytes 393224 | tf_op jit(solution)/shard_map/ppermute | solution.py:12
  110.6 100.9 %collective-permute-start.18 = (bf16[2,64,512]{2,1,0:T(8,128)(2,1)}, bf16[2,64,512]{2,1,0:T(8,128)(2,1)}, u32[]{:S(2)}, u32[]{:S(2)}) collective-permute-start(bf16[2,64,512]{2,1,0:T(8,128)(2,1)} %get-tuple-element.76), channel_id=1, source_target_pairs={{0,1},{1,0},{2,3},{3,2},{4,5},{5,4},{6,7},{7,6},{8,9},{9,8},{10,11... | collective-permute-start | bytes 393224 | tf_op jit(solution)/shard_map/ppermute | solution.py:12
  172.2 16.3 %collective-permute-start.27 = (f32[4612]{0:T(1024)}, f32[4612]{0:T(1024)}, u32[]{:S(2)}, u32[]{:S(2)}) collective-permute-start(f32[4612]{0:T(1024)} %pad_maximum_fusion.26), channel_id=1, source_target_pairs={{0,1},{1,0},{2,3},{3,2},{4,5},{5,4},{6,7},{7,6},{8,9},{9,8},{10,11... | collective-permute-start | bytes 55352 | tf_op jit(solution)/shard_map/ppermute | solution.py:12
  197.6 22.5 %collective-permute-start.48 = (bf16[2,2,2,2,64,512]{5,4,3,2,1,0:T(8,128)(2,1)}, bf16[2,2,2,2,64,512]{5,4,3,2,1,0:T(8,128)(2,1)}, u32[]{:S(2)}, u32[]{:S(2)}) collective-permute-start(bf16[2,2,2,2,64,512]{5,4,3,2,1,0:T(8,128)(2,1)} %pad_maximum_fusion.4), channel_id=1, source_target_pairs={{0,1},{1,0},{2,3},{3,2},{4,5},{5,4},{6,7},{7,6},{8,9},{9,8},{10,11... | collective-permute-start | bytes 3145736 | tf_op jit(solution)/shard_map/ppermute | solution.py:12
  206.1 7.2 %collective-permute-start.26 = (bf16[2,64,512]{2,1,0:T(8,128)(2,1)}, bf16[2,64,512]{2,1,0:T(8,128)(2,1)S(1)}, u32[]{:S(2)}, u32[]{:S(2)}) collective-permute-start(bf16[2,64,512]{2,1,0:T(8,128)(2,1)} %get-tuple-element.66), channel_id=1, source_target_pairs={{0,3},{1,2},{2,1},{3,0},{4,7},{5,6},{6,5},{7,4},{8,11},{9,10},{10,... | collective-permute-start | bytes 393224 | tf_op jit(solution)/shard_map/ppermute | solution.py:12
  206.1 8.6 %collective-permute-start.25 = (bf16[2,64,512]{2,1,0:T(8,128)(2,1)S(1)}, bf16[2,64,512]{2,1,0:T(8,128)(2,1)S(1)}, u32[]{:S(2)}, u32[]{:S(2)}) collective-permute-start(bf16[2,64,512]{2,1,0:T(8,128)(2,1)S(1)} %get-tuple-element.67), channel_id=1, source_target_pairs={{0,2},{1,3},{2,0},{3,1},{4,6},{5,7},{6,4},{7,5},{8,10},{9,11},{10,... | collective-permute-start | bytes 393224 | tf_op jit(solution)/shard_map/ppermute | solution.py:12
  207.6 7.2 %collective-permute-start.24 = (bf16[2,64,512]{2,1,0:T(8,128)(2,1)S(1)}, bf16[2,64,512]{2,1,0:T(8,128)(2,1)S(1)}, u32[]{:S(2)}, u32[]{:S(2)}) collective-permute-start(bf16[2,64,512]{2,1,0:T(8,128)(2,1)S(1)} %get-tuple-element.68), channel_id=1, source_target_pairs={{0,1},{1,0},{2,3},{3,2},{4,5},{5,4},{6,7},{7,6},{8,9},{9,8},{10,11... | collective-permute-start | bytes 393224 | tf_op jit(solution)/shard_map/ppermute | solution.py:12
  211.5 10.9 %collective-permute-start.40 = (bf16[2,2,2,2,64,512]{5,4,3,2,1,0:T(8,128)(2,1)}, bf16[2,2,2,2,64,512]{5,4,3,2,1,0:T(8,128)(2,1)}, u32[]{:S(2)}, u32[]{:S(2)}) collective-permute-start(bf16[2,2,2,2,64,512]{5,4,3,2,1,0:T(8,128)(2,1)} %pad_maximum_fusion.3), channel_id=1, source_target_pairs={{0,1},{1,0},{2,3},{3,2},{4,5},{5,4},{6,7},{7,6},{8,9},{9,8},{10,11... | collective-permute-start | bytes 3145736 | tf_op jit(solution)/shard_map/ppermute | solution.py:12
  213.4 12.2 %collective-permute-start.32 = (bf16[2,2,2,2,64,512]{5,4,3,2,1,0:T(8,128)(2,1)}, bf16[2,2,2,2,64,512]{5,4,3,2,1,0:T(8,128)(2,1)}, u32[]{:S(2)}, u32[]{:S(2)}) collective-permute-start(bf16[2,2,2,2,64,512]{5,4,3,2,1,0:T(8,128)(2,1)} %pad_maximum_fusion.2), channel_id=1, source_target_pairs={{0,1},{1,0},{2,3},{3,2},{4,5},{5,4},{6,7},{7,6},{8,9},{9,8},{10,11... | collective-permute-start | bytes 3145736 | tf_op jit(solution)/shard_map/ppermute | solution.py:12
  221.8 14.8 %collective-permute-start.49 = (bf16[2,2,2,64,512]{4,3,2,1,0:T(8,128)(2,1)S(1)}, bf16[2,2,2,64,512]{4,3,2,1,0:T(8,128)(2,1)S(1)}, u32[]{:S(2)}, u32[]{:S(2)}) collective-permute-start(bf16[2,2,2,64,512]{4,3,2,1,0:T(8,128)(2,1)S(1)} %slice_bitcast_fusion), channel_id=1, source_target_pairs={{0,2},{1,3},{2,0},{3,1},{4,6},{5,7},{6,4},{7,5},{8,10},{9,11},{10,... | collective-permute-start | bytes 1572872 | tf_op jit(solution)/shard_map/ppermute | solution.py:12
  224.0 23.9 %collective-permute-start.41 = (bf16[2,2,2,64,512]{4,3,2,1,0:T(8,128)(2,1)S(1)}, bf16[2,2,2,64,512]{4,3,2,1,0:T(8,128)(2,1)S(1)}, u32[]{:S(2)}, u32[]{:S(2)}) collective-permute-start(bf16[2,2,2,64,512]{4,3,2,1,0:T(8,128)(2,1)S(1)} %slice_bitcast_fusion.2), channel_id=1, source_target_pairs={{0,2},{1,3},{2,0},{3,1},{4,6},{5,7},{6,4},{7,5},{8,10},{9,11},{10,... | collective-permute-start | bytes 1572872 | tf_op jit(solution)/shard_map/ppermute | solution.py:12
  227.2 31.1 %collective-permute-start.33 = (bf16[2,2,2,64,512]{4,3,2,1,0:T(8,128)(2,1)S(1)}, bf16[2,2,2,64,512]{4,3,2,1,0:T(8,128)(2,1)S(1)}, u32[]{:S(2)}, u32[]{:S(2)}) collective-permute-start(bf16[2,2,2,64,512]{4,3,2,1,0:T(8,128)(2,1)S(1)} %slice_bitcast_fusion.4), channel_id=1, source_target_pairs={{0,2},{1,3},{2,0},{3,1},{4,6},{5,7},{6,4},{7,5},{8,10},{9,11},{10,... | collective-permute-start | bytes 1572872 | tf_op jit(solution)/shard_map/ppermute | solution.py:12
  236.8 23.1 %collective-permute-start.50 = (bf16[2,2,64,512]{3,2,1,0:T(8,128)(2,1)S(1)}, bf16[2,2,64,512]{3,2,1,0:T(8,128)(2,1)S(1)}, u32[]{:S(2)}, u32[]{:S(2)}) collective-permute-start(bf16[2,2,64,512]{3,2,1,0:T(8,128)(2,1)S(1)} %slice_bitcast_fusion.6), channel_id=1, source_target_pairs={{0,4},{4,0},{8,12},{12,8},{16,20},{20,16},{24,28},{28,24},{1,5},{5... | collective-permute-start | bytes 786440 | tf_op jit(solution)/shard_map/ppermute | solution.py:12
  248.1 13.6 %collective-permute-start.42 = (bf16[2,2,64,512]{3,2,1,0:T(8,128)(2,1)S(1)}, bf16[2,2,64,512]{3,2,1,0:T(8,128)(2,1)S(1)}, u32[]{:S(2)}, u32[]{:S(2)}) collective-permute-start(bf16[2,2,64,512]{3,2,1,0:T(8,128)(2,1)S(1)} %slice_bitcast_fusion.8), channel_id=1, source_target_pairs={{0,4},{4,0},{8,12},{12,8},{16,20},{20,16},{24,28},{28,24},{1,5},{5... | collective-permute-start | bytes 786440 | tf_op jit(solution)/shard_map/ppermute | solution.py:12
  258.5 7.6 %collective-permute-start.34 = (bf16[2,2,64,512]{3,2,1,0:T(8,128)(2,1)S(1)}, bf16[2,2,64,512]{3,2,1,0:T(8,128)(2,1)S(1)}, u32[]{:S(2)}, u32[]{:S(2)}) collective-permute-start(bf16[2,2,64,512]{3,2,1,0:T(8,128)(2,1)S(1)} %slice_bitcast_fusion.10), channel_id=1, source_target_pairs={{0,4},{4,0},{8,12},{12,8},{16,20},{20,16},{24,28},{28,24},{1,5},{5... | collective-permute-start | bytes 786440 | tf_op jit(solution)/shard_map/ppermute | solution.py:12
  260.0 7.7 %collective-permute-start.51 = (bf16[2,64,512]{2,1,0:T(8,128)(2,1)S(1)}, bf16[2,64,512]{2,1,0:T(8,128)(2,1)S(1)}, u32[]{:S(2)}, u32[]{:S(2)}) collective-permute-start(bf16[2,64,512]{2,1,0:T(8,128)(2,1)S(1)} %slice_bitcast_fusion.12), channel_id=1, source_target_pairs={{0,8},{4,12},{8,0},{12,4},{16,24},{20,28},{24,16},{28,20},{1,9},{5... | collective-permute-start | bytes 393224 | tf_op jit(solution)/shard_map/ppermute | solution.py:12
  261.7 8.8 %collective-permute-start.43 = (bf16[2,64,512]{2,1,0:T(8,128)(2,1)S(1)}, bf16[2,64,512]{2,1,0:T(8,128)(2,1)S(1)}, u32[]{:S(2)}, u32[]{:S(2)}) collective-permute-start(bf16[2,64,512]{2,1,0:T(8,128)(2,1)S(1)} %slice_bitcast_fusion.14), channel_id=1, source_target_pairs={{0,8},{4,12},{8,0},{12,4},{16,24},{20,28},{24,16},{28,20},{1,9},{5... | collective-permute-start | bytes 393224 | tf_op jit(solution)/shard_map/ppermute | solution.py:12
  267.8 7.1 %collective-permute-start.52 = (bf16[64,512]{1,0:T(8,128)(2,1)S(1)}, bf16[64,512]{1,0:T(8,128)(2,1)S(1)}, u32[]{:S(2)}, u32[]{:S(2)}) collective-permute-start(bf16[64,512]{1,0:T(8,128)(2,1)S(1)} %slice_bitcast_fusion.20), channel_id=1, source_target_pairs={{0,16},{4,20},{8,24},{12,28},{16,0},{20,4},{24,8},{28,12},{1,17},{... | collective-permute-start | bytes 196616 | tf_op jit(solution)/shard_map/ppermute | solution.py:12
  270.6 9.3 %collective-permute-start.44 = (bf16[64,512]{1,0:T(8,128)(2,1)S(1)}, bf16[64,512]{1,0:T(8,128)(2,1)S(1)}, u32[]{:S(2)}, u32[]{:S(2)}) collective-permute-start(bf16[64,512]{1,0:T(8,128)(2,1)S(1)} %slice_bitcast_fusion.22), channel_id=1, source_target_pairs={{0,16},{4,20},{8,24},{12,28},{16,0},{20,4},{24,8},{28,12},{1,17},{... | collective-permute-start | bytes 196616 | tf_op jit(solution)/shard_map/ppermute | solution.py:12
  271.6 10.3 %collective-permute-start.36 = (bf16[64,512]{1,0:T(8,128)(2,1)S(1)}, bf16[64,512]{1,0:T(8,128)(2,1)S(1)}, u32[]{:S(2)}, u32[]{:S(2)}) collective-permute-start(bf16[64,512]{1,0:T(8,128)(2,1)S(1)} %slice_bitcast_fusion.24), channel_id=1, source_target_pairs={{0,16},{4,20},{8,24},{12,28},{16,0},{20,4},{24,8},{28,12},{1,17},{... | collective-permute-start | bytes 196616 | tf_op jit(solution)/shard_map/ppermute | solution.py:12
  274.9 9.9 %collective-permute-start.53 = (bf16[1,64,512]{2,1,0:T(8,128)(2,1)S(1)}, bf16[1,64,512]{2,1,0:T(8,128)(2,1)S(1)}, u32[]{:S(2)}, u32[]{:S(2)}) collective-permute-start(bf16[1,64,512]{2,1,0:T(8,128)(2,1)S(1)} %fusion.74), channel_id=1, source_target_pairs={{0,16},{4,20},{8,24},{12,28},{16,0},{20,4},{24,8},{28,12},{1,17},{... | collective-permute-start | bytes 196616 | tf_op jit(solution)/shard_map/ppermute | solution.py:12
  279.9 6.1 %collective-permute-start.45 = (bf16[1,64,512]{2,1,0:T(8,128)(2,1)S(1)}, bf16[1,64,512]{2,1,0:T(8,128)(2,1)S(1)}, u32[]{:S(2)}, u32[]{:S(2)}) collective-permute-start(bf16[1,64,512]{2,1,0:T(8,128)(2,1)S(1)} %fusion.73), channel_id=1, source_target_pairs={{0,16},{4,20},{8,24},{12,28},{16,0},{20,4},{24,8},{28,12},{1,17},{... | collective-permute-start | bytes 196616 | tf_op jit(solution)/shard_map/ppermute | solution.py:12
  282.0 5.8 %collective-permute-start.37 = (bf16[1,64,512]{2,1,0:T(8,128)(2,1)S(1)}, bf16[1,64,512]{2,1,0:T(8,128)(2,1)S(1)}, u32[]{:S(2)}, u32[]{:S(2)}) collective-permute-start(bf16[1,64,512]{2,1,0:T(8,128)(2,1)S(1)} %fusion.72), channel_id=1, source_target_pairs={{0,16},{4,20},{8,24},{12,28},{16,0},{20,4},{24,8},{28,12},{1,17},{... | collective-permute-start | bytes 196616 | tf_op jit(solution)/shard_map/ppermute | solution.py:12
  284.8 6.5 %collective-permute-start.54 = (bf16[2,64,512]{2,1,0:T(8,128)(2,1)S(1)}, bf16[2,64,512]{2,1,0:T(8,128)(2,1)S(1)}, u32[]{:S(2)}, u32[]{:S(2)}) collective-permute-start(bf16[2,64,512]{2,1,0:T(8,128)(2,1)S(1)} %pad_maximum_fusion.25), channel_id=1, source_target_pairs={{0,8},{4,12},{8,0},{12,4},{16,24},{20,28},{24,16},{28,20},{1,9},{5... | collective-permute-start | bytes 393224 | tf_op jit(solution)/shard_map/ppermute | solution.py:12
  286.0 7.6 %collective-permute-start.46 = (bf16[2,64,512]{2,1,0:T(8,128)(2,1)S(1)}, bf16[2,64,512]{2,1,0:T(8,128)(2,1)S(1)}, u32[]{:S(2)}, u32[]{:S(2)}) collective-permute-start(bf16[2,64,512]{2,1,0:T(8,128)(2,1)S(1)} %pad_maximum_fusion.24), channel_id=1, source_target_pairs={{0,8},{4,12},{8,0},{12,4},{16,24},{20,28},{24,16},{28,20},{1,9},{5... | collective-permute-start | bytes 393224 | tf_op jit(solution)/shard_map/ppermute | solution.py:12
  287.8 7.3 %collective-permute-start.38 = (bf16[2,64,512]{2,1,0:T(8,128)(2,1)S(1)}, bf16[2,64,512]{2,1,0:T(8,128)(2,1)S(1)}, u32[]{:S(2)}, u32[]{:S(2)}) collective-permute-start(bf16[2,64,512]{2,1,0:T(8,128)(2,1)S(1)} %pad_maximum_fusion.23), channel_id=1, source_target_pairs={{0,8},{4,12},{8,0},{12,4},{16,24},{20,28},{24,16},{28,20},{1,9},{5... | collective-permute-start | bytes 393224 | tf_op jit(solution)/shard_map/ppermute | solution.py:12
  291.4 9.3 %collective-permute-start.55 = (bf16[4,64,512]{2,1,0:T(8,128)(2,1)S(1)}, bf16[4,64,512]{2,1,0:T(8,128)(2,1)S(1)}, u32[]{:S(2)}, u32[]{:S(2)}) collective-permute-start(bf16[4,64,512]{2,1,0:T(8,128)(2,1)S(1)} %pad_maximum_fusion.22), channel_id=1, source_target_pairs={{0,4},{4,0},{8,12},{12,8},{16,20},{20,16},{24,28},{28,24},{1,5},{5... | collective-permute-start | bytes 786440 | tf_op jit(solution)/shard_map/ppermute | solution.py:12
  293.6 10.9 %collective-permute-start.47 = (bf16[4,64,512]{2,1,0:T(8,128)(2,1)S(1)}, bf16[4,64,512]{2,1,0:T(8,128)(2,1)S(1)}, u32[]{:S(2)}, u32[]{:S(2)}) collective-permute-start(bf16[4,64,512]{2,1,0:T(8,128)(2,1)S(1)} %pad_maximum_fusion.21), channel_id=1, source_target_pairs={{0,4},{4,0},{8,12},{12,8},{16,20},{20,16},{24,28},{28,24},{1,5},{5... | collective-permute-start | bytes 786440 | tf_op jit(solution)/shard_map/ppermute | solution.py:12
  295.1 12.2 %collective-permute-start.39 = (bf16[4,64,512]{2,1,0:T(8,128)(2,1)S(1)}, bf16[4,64,512]{2,1,0:T(8,128)(2,1)S(1)}, u32[]{:S(2)}, u32[]{:S(2)}) collective-permute-start(bf16[4,64,512]{2,1,0:T(8,128)(2,1)S(1)} %pad_maximum_fusion.20), channel_id=1, source_target_pairs={{0,4},{4,0},{8,12},{12,8},{16,20},{20,16},{24,28},{28,24},{1,5},{5... | collective-permute-start | bytes 786440 | tf_op jit(solution)/shard_map/ppermute | solution.py:12
  (90 other events, 1107.3 us)

commit v2 on v1

v2 whole, which is shorter than its diff:
```python
import jax
import jax.numpy as jnp
from jax import lax
from jax.experimental import pallas as pl
from jax.experimental.pallas import tpu as pltpu
from jax.sharding import PartitionSpec as P

HD = 64
PAIR = 2 * HD
LANES = 128
F32 = jnp.float32
BF16 = jnp.bfloat16
VMEM_LIMIT = 48 * 2**20
GELU_C = 0.7978845608028654
GELU_A = 0.044715
VEC = 8


def swap(v, axis, bit, size):
    return lax.ppermute(v, axis, [(i, i ^ bit) for i in range(size)])


def shape(dims, kind):
    return jax.ShapeDtypeStruct(tuple(dims), kind)


def run(name, fn, ins, outs, scratch=(), flops=0, smem=()):
    n_in, n_out = len(ins), len(outs)

    def kernel(*refs):
        fn(refs[:n_in], refs[n_in : n_in + n_out], refs[n_in + n_out :])

    moved = sum(v.size * v.dtype.itemsize for v in list(ins) + list(outs))
    return pl.pallas_call(
        kernel,
        out_shape=tuple(outs),
        in_specs=[
            pl.BlockSpec(memory_space=pltpu.SMEM if i in smem else pltpu.VMEM)
            for i in range(n_in)
        ],
        out_specs=tuple(pl.BlockSpec(memory_space=pltpu.VMEM) for _ in outs),
        scratch_shapes=list(scratch),
        compiler_params=pltpu.CompilerParams(vmem_limit_bytes=VMEM_LIMIT),
        cost_estimate=pl.CostEstimate(flops=int(flops), bytes_accessed=int(moved), transcendentals=0),
        name=name,
    )(*ins)


def dot(a, b):
    return jnp.dot(a, b, preferred_element_type=F32)


def dot_nt(a, b):
    return lax.dot_general(a, b, (((1,), (1,)), ((), ())), preferred_element_type=F32)


def dot_tn(a, b):
    return lax.dot_general(a, b, (((0,), (0,)), ((), ())), preferred_element_type=F32)


def normalize(v):
    centre = v - jnp.mean(v, -1, keepdims=True)
    rstd = lax.rsqrt(jnp.mean(centre * centre, -1, keepdims=True) + 1e-05)
    return centre * rstd, rstd


def norm_back(g, normed, rstd, gain):
    e = g * gain
    return rstd * (
        e - jnp.mean(e, -1, keepdims=True) - normed * jnp.mean(e * normed, -1, keepdims=True)
    )


def rows_of(start, size):
    return pl.ds(pl.multiple_of(start * size, size), size)


def place(dst, lanes, pieces, x_bit):
    if len(pieces) == 1:
        dst[:, lanes] = pieces[0][...]
        return
    half = dst.shape[0] // 2
    a, b = pieces[0][...], pieces[1][...]
    dst[:half, lanes] = jnp.where(x_bit == 0, a, b)
    dst[half:, lanes] = jnp.where(x_bit == 0, b, a)


def place_rows(dst, start, size, pieces, x_bit):
    if len(pieces) == 1:
        dst[start : start + size] = pieces[0][...]
        return
    half = size // 2
    a, b = pieces[0][...], pieces[1][...]
    dst[start : start + half] = jnp.where(x_bit == 0, a, b)
    dst[start + half : start + size] = jnp.where(x_bit == 0, b, a)


def take(refs, counts):
    out, at = [], 0
    for c in counts:
        out.append(refs[at : at + c])
        at += c
    assert at == len(refs)
    return out


def make_body(n_dp, n_mp):
    n_z = n_dp // 2
    groups = [[0, 1], list(range(2, n_mp))]

    def body(
        tokens,
        lengths,
        order_mask,
        norm_scale_pair,
        norm_offset_pair,
        w_qkv,
        qv_bias,
        order_bias,
        w_out,
        out_bias,
        w_up,
        up_bias,
        w_down,
        cotangent,
    ):
        rows, share, width = tokens.shape
        slots = order_mask.shape[1]
        own = rows // n_mp
        count = own * slots
        lane = qv_bias.shape[1]
        per = order_bias.shape[0]
        hid = up_bias.shape[0]
        hid_rows = hid // LANES
        piece = shape((own, share, width), BF16)
        sub = width // n_dp
        factor = HD**-0.5

        def mp_swap(v, bit):
            return swap(v, "mp", bit, n_mp)

        def dp_swap(v, bit):
            return swap(v, "dp", bit, n_dp)

        def gather_mp(v, first):
            halves = {0: [first]}
            for k in range(2, n_mp, 2):
                over_y = mp_swap(first, k)
                halves[k] = [over_y, dp_swap(over_y, 1)]
            blocks = {0: [v], 1: [mp_swap(v, 1)]}
            for k in range(2, n_mp, 2):
                blocks[k] = halves[k]
                blocks[k + 1] = [mp_swap(h, 1) for h in halves[k]]
            return [blocks[k] for k in range(n_mp)]

        def cut_tokens(ins, outs, _):
            me = lax.axis_index("mp")
            for k in range(n_mp):
                outs[k][...] = ins[0][pl.ds((me ^ k) * own, own)]

        token_parts = run("cut_tokens", cut_tokens, [tokens], [piece] * n_mp)
        token_parts = [
            v if k == 0 else mp_swap(v, k) for k, v in enumerate(token_parts)
        ]

        def first_halves(ins, outs, _):
            x_bit = lax.axis_index("dp") & 1
            for src, dst in zip(ins, outs):
                dst[...] = src[rows_of(x_bit, dst.shape[0])]

        flat_qkv = w_qkv.reshape(-1, lane)
        flats = [flat_qkv, w_out, w_up, w_down]
        firsts = run(
            "first_halves",
            first_halves,
            flats,
            [shape((v.shape[0] // 2, v.shape[1]), BF16) for v in flats],
        )
        small = jnp.concatenate(
            [
                jnp.pad(qv_bias, ((0, 0), (0, LANES - lane))),
                up_bias.reshape(hid_rows, LANES),
                jnp.pad(order_bias, (0, LANES - per))[None],
                jnp.zeros((VEC - 3 - hid_rows % VEC, LANES), F32),
            ]
        )
        smalls = [small] + [mp_swap(small, k) for k in range(1, n_mp)]
        cot_parts = run("cut_cotangent", cut_tokens, [cotangent], [piece] * n_mp)
        b_qkv = gather_mp(flat_qkv, firsts[0])
        b_out = gather_mp(w_out, firsts[1])
        cot_parts = [v if k == 0 else mp_swap(v, k) for k, v in enumerate(cot_parts)]
        b_up = gather_mp(w_up, firsts[2])
        b_down = gather_mp(w_down, firsts[3])

        def flat(blocks, group):
            return [p for k in group for p in blocks[k]], [len(blocks[k]) for k in group]

        def place_group(dst, pieces, counts, size, x_bit):
            for j, ps in enumerate(take(pieces, counts)):
                place(dst, slice(j * size, (j + 1) * size), ps, x_bit)

        def order_row(om_ref, me, r):
            v = om_ref[pl.ds(me * own + r, 1), :].astype(F32)
            v = jnp.broadcast_to(v, (8, slots))
            at = lax.broadcasted_iota(jnp.int32, (8, slots), 1)
            step = share
            while step < slots:
                turned = jnp.where(
                    (at & step) == 0, pltpu.roll(v, slots - step, 1), pltpu.roll(v, step, 1)
                )
                v = jnp.where((me * share) & step, turned, v)
                step *= 2
            return v[:1]

        def keep_row(me, length):
            at = lax.broadcasted_iota(jnp.int32, (1, slots), 1)
            return (at ^ (me * share)) < length

        def keep_column(me, length):
            at = lax.broadcasted_iota(jnp.int32, (slots, 1), 0)
            return ((at ^ (me * share)) < length).astype(F32)

        def head_mask(pair_value, h):
            at = lax.broadcasted_iota(jnp.int32, pair_value.shape, 1)
            return jnp.where((at >= HD) == (h % 2 == 1), pair_value, jnp.zeros_like(pair_value))

        def assemble(dst, parts):
            for r in range(own):
                for k in range(n_mp):
                    dst[r * slots + k * share : r * slots + (k + 1) * share] = parts[k][r]

        def attend(group, first):
            wide = lane * len(group)
            heads = wide // HD
            pieces, counts = flat(b_qkv, group)

            def fn(ins, outs, scratch):
                me, x_bit = lax.axis_index("mp"), lax.axis_index("dp") & 1
                weights = scratch[0]
                if first:
                    head, tail = ins[: n_mp + 4], ins[n_mp + 4 :]
                    lens, om, gains, shifts = head[n_mp:]
                    x_ref, a1_ref, qkv_ref, p_ref, att_ref = outs
                    assemble(x_ref, head[:n_mp])
                    normed, _ = normalize(x_ref[...].astype(F32))
                    a1_ref[...] = (normed * gains[0:1] + shifts[0:1]).astype(BF16)
                else:
                    lens, om, a1_ref = ins[:3]
                    tail = ins[3:]
                    qkv_ref, p_ref, att_ref = outs
                place_group(weights, tail[: len(pieces)], counts, lane, x_bit)
                biases = tail[len(pieces) :]
                a1 = a1_ref[...]
                for t in range(3):
                    y = dot(a1, weights[t * width : (t + 1) * width])
                    if t != 1:
                        y = y + jnp.concatenate(
                            [b[t // 2 : t // 2 + 1, :lane] for b in biases], 1
                        )
                    qkv_ref[t] = y.astype(BF16)
                for r in range(own):
                    length = lens[me * own + r]
                    order = order_row(om, me, r)
                    kept = keep_row(me, length)
                    column = keep_column(me, length)
                    here = slice(r * slots, (r + 1) * slots)
                    for pair in range(heads // 2):
                        cols = slice(pair * PAIR, (pair + 1) * PAIR)
                        q = qkv_ref[0, here, cols] * jnp.asarray(factor, BF16)
                        key = qkv_ref[1, here, cols]
                        val = qkv_ref[2, here, cols]
                        acc = None
                        for h in (2 * pair, 2 * pair + 1):
                            b = biases[h // per]
                            ob = b[2 + hid_rows : 3 + hid_rows, h % per : h % per + 1]
                            row = jnp.where(kept, ob * order, -1e30)
                            s = dot_nt(head_mask(q, h), key) + row
                            e = jnp.exp(s - jnp.max(s, -1, keepdims=True))
                            p = (e * (1.0 / jnp.sum(e, -1, keepdims=True))).astype(BF16)
                            p_ref[r * heads + h] = p
                            term = dot(p, head_mask(val, h))
                            acc = term if acc is None else acc + term
                        att_ref[here, cols] = (acc * column).astype(BF16)

            ins = (
                token_parts + [lengths, order_mask, norm_scale_pair, norm_offset_pair]
                if first
                else [lengths, order_mask, a1]
            )
            lead = [shape((count, width), BF16)] * 2 if first else []
            return run(
                "attend",
                fn,
                ins + pieces + [smalls[k] for k in group],
                lead
                + [
                    shape((3, count, wide), BF16),
                    shape((own * heads, slots, slots), BF16),
                    shape((count, wide), BF16),
                ],
                [pltpu.VMEM((3 * width, wide), BF16)],
                flops=2 * count * width * 3 * wide + 4 * count * slots * wide * 4,
                smem=(n_mp if first else 0,),
            )

        x, a1, qkv0, p0, att0 = attend(groups[0], True)
        qkv1, p1, att1 = attend(groups[1], False)

        def scatter(dst, src, block, dpi):
            for xi in range(2):
                for zi in range(n_z):
                    here = rows_of(dpi ^ (xi + 2 * zi), sub)
                    dst[block, xi, zi] = src[here, :]

        def mlp_block(k, j, a2, a2t, dy, dyt, wu, wd, bias, mixed, d_mid, gs, outs, dpi):
            up = jnp.concatenate([bias[2 + i : 3 + i, :] for i in range(hid_rows)], 1)
            pre = dot(a2[...], wu[...]) + up
            square = pre * pre
            t = jnp.tanh(pre * (GELU_C + (GELU_C * GELU_A) * square))
            half = 0.5 + 0.5 * t
            hidden = (pre * half).astype(BF16)
            slope = half + (pre * (1.0 - t * t)) * (
                0.5 * GELU_C + (1.5 * GELU_C * GELU_A) * square
            )
            d_hidden = dot_nt(dy[...], wd[...])
            d_pre = (slope * d_hidden).astype(BF16)
            mixed[...] += dot(hidden, wd[...])
            d_mid[...] += dot_nt(d_pre, wu[...])
            down_ref, up_ref = outs[k % 2], outs[2 + k % 2]
            g_down, g_up = gs.at[2 * j], gs.at[2 * j + 1]
            g_down[...] = dot(dyt[...], hidden).astype(BF16)
            scatter(down_ref, g_down, j // 2, dpi)
            g_up[...] = dot(a2t[...], d_pre).astype(BF16)
            scatter(up_ref, g_up, j // 2, dpi)
            outs[4][j] = jnp.sum(d_pre.astype(F32), 0, keepdims=True)

        def grad_shapes(n_blocks, m, c):
            half = n_blocks // 2
            return [shape((half, 2, n_z, m, c), BF16)] * 2

        full = shape((count, width), F32)
        full_bf = shape((count, width), BF16)
        turned = shape((width, count), BF16)
        g0, g1 = groups
        out_pieces, out_counts = flat(b_out, range(n_mp))

        def mlp_outs(n_blocks):
            return (
                grad_shapes(n_blocks, sub, hid)
                + grad_shapes(n_blocks, sub, hid)
                + [shape((n_blocks, 1, hid), F32)]
            )

        up0, up0_counts = flat(b_up, g0)
        down0, down0_counts = flat(b_down, g0)

        def mlp_first(ins, outs, scratch):
            x_bit, dpi = lax.axis_index("dp") & 1, lax.axis_index("dp")
            sizes = [6, len(out_pieces), n_mp, len(up0), len(down0), len(g0)]
            lead, wo_p, dy_p, wu_p, wd_p, biases = take(ins, sizes)
            x_ref, att0_ref, att1_ref, gains, shifts, ob = lead
            x1, a2, a2t, dy, dyt, mixed, d_mid = outs[:7]
            wo, gs = scratch
            for j, ps in enumerate(take(wo_p, out_counts)):
                place_rows(wo, j * lane, lane, ps, x_bit)
            cut = lane * len(g0)
            v = x_ref[...].astype(F32) + (
                dot(att0_ref[...], wo[:cut]) + dot(att1_ref[...], wo[cut:]) + ob[0:1]
            )
            x1[...] = v
            normed, _ = normalize(v)
            act = (normed * gains[1:2] + shifts[1:2]).astype(BF16)
            a2[...] = act
            a2t[...] = act.T
            assemble(dy, dy_p)
            dyt[...] = dy[...].T
            mixed[...] = jnp.zeros_like(mixed)
            d_mid[...] = jnp.zeros_like(d_mid)
            for j, k in enumerate(g0):
                mlp_block(
                    k, j, a2, a2t, dy, dyt, wu_p[j], wd_p[j], biases[j], mixed, d_mid, gs, outs[7:], dpi
                )

        block_flops = 12 * count * width * hid
        x1, a2, a2t, dy, dyt, mixed, d_mid, kd0, sd0, ku0, su0, gub0 = run(
            "mlp_first",
            mlp_first,
            [x, att0, att1, norm_scale_pair, norm_offset_pair, out_bias]
            + out_pieces
            + cot_parts
            + up0
            + down0
            + [smalls[k] for k in g0],
            [full, full_bf, turned, full_bf, turned, full, full] + mlp_outs(len(g0)),
            [pltpu.VMEM((width, width), BF16), pltpu.VMEM((2 * len(g0), width, hid), BF16)],
            flops=block_flops * len(g0) + 2 * count * width * width,
        )

        up1, up1_counts = flat(b_up, g1)
        down1, down1_counts = flat(b_down, g1)

        def mlp_second(ins, outs, scratch):
            x_bit, dpi = lax.axis_index("dp") & 1, lax.axis_index("dp")
            lead, wu_p, wd_p, biases = take(ins, [9, len(up1), len(down1), len(g1)])
            x1, a2, a2t, dy, dyt, mixed_in, d_mid_in, gains, ob = lead
            out_parts, (dx1, d_att, vec) = outs[:n_mp], outs[n_mp : n_mp + 3]
            mixed, d_mid, wus, wds, gs = scratch
            mixed[...] = mixed_in[...]
            d_mid[...] = d_mid_in[...]
            wu_p, wd_p = take(wu_p, up1_counts), take(wd_p, down1_counts)
            for j, k in enumerate(g1):
                wu, wd = wus.at[j], wds.at[j]
                place(wu, slice(0, hid), wu_p[j], x_bit)
                place(wd, slice(0, width), wd_p[j], x_bit)
                mlp_block(
                    k, j, a2, a2t, dy, dyt, wu, wd, biases[j], mixed, d_mid, gs, outs[n_mp + 3 :], dpi
                )
            v = x1[...]
            final = (v + (mixed[...] + ob[1:2])).astype(BF16)
            for r in range(own):
                for k in range(n_mp):
                    at = r * slots + k * share
                    out_parts[k][r] = final[at : at + share]
            normed, rstd = normalize(v)
            g = d_mid[...]
            dyf = dy[...].astype(F32)
            d = dyf + norm_back(g, normed, rstd, gains[1:2])
            dx1[...] = d
            low = d.astype(BF16)
            d_att[...] = low
            vec[0:1] = jnp.sum(g * normed, 0, keepdims=True)
            vec[1:2] = jnp.sum(g, 0, keepdims=True)
            vec[2:3] = jnp.sum(low.astype(F32), 0, keepdims=True)
            vec[3:4] = jnp.sum(dyf, 0, keepdims=True)

        second = run(
            "mlp_second",
            mlp_second,
            [x1, a2, a2t, dy, dyt, mixed, d_mid, norm_scale_pair, out_bias]
            + up1
            + down1
            + [smalls[k] for k in g1],
            [piece] * n_mp + [full, full_bf, shape((4, width), F32)] + mlp_outs(len(g1)),
            [
                pltpu.VMEM((count, width), F32),
                pltpu.VMEM((count, width), F32),
                pltpu.VMEM((len(g1), width, hid), BF16),
                pltpu.VMEM((len(g1), hid, width), BF16),
                pltpu.VMEM((2 * len(g1), width, hid), BF16),
            ],
            flops=block_flops * len(g1),
        )
        out_parts, (dx1, d_att, vec, kd1, sd1, ku1, su1, gub1) = second[:n_mp], second[n_mp:]

        vec_rows = n_dp * VEC
        qkv_pieces, qkv_counts = flat(b_qkv, range(n_mp))
        chunk = 4 * sub + 2 * VEC

        def attend_back(ins, outs, scratch):
            me, dpi = lax.axis_index("mp"), lax.axis_index("dp")
            x_bit = dpi & 1
            sizes = [3, 4, 2, 2, 2, 3, len(qkv_pieces), len(out_pieces)]
            (lens, om, gains), (x_ref, a1_ref, dx1, d_att), qkvs, ps, atts, (vec, gub_a, gub_b), wq_p, wo_p = take(ins, sizes)
            parts = outs[:n_mp]
            grads = outs[n_mp:]
            wqs, wos, dqkvs, gqs = scratch[:2], scratch[2:4], scratch[4:6], scratch[6:8]
            d_in, vec_f, shared = scratch[8:]
            wq_p, wo_p = take(wq_p, qkv_counts), take(wo_p, out_counts)
            a1t = a1_ref[...].T
            d_att_v = d_att[...]
            d_att_t = d_att_v.T
            d_in[...] = jnp.zeros_like(d_in)
            order_sums = {}
            for gi, group in enumerate(groups):
                wide = lane * len(group)
                heads = wide // HD
                qkv_ref, p_ref, att_ref = qkvs[gi], ps[gi], atts[gi]
                wq, wo, dqkv, gq = wqs[gi], wos[gi], dqkvs[gi], gqs[gi]
                for j, k in enumerate(group):
                    place(wq, slice(j * lane, (j + 1) * lane), wq_p[k], x_bit)
                    place_rows(wo, j * lane, lane, wo_p[k], x_bit)
                d_o = dot_nt(d_att_v, wo[:wide]).astype(BF16)
                for r in range(own):
                    length = lens[me * own + r]
                    order = order_row(om, me, r)
                    kept = keep_row(me, length)
                    column = keep_column(me, length).astype(BF16)
                    here = slice(r * slots, (r + 1) * slots)
                    for pair in range(heads // 2):
                        cols = slice(pair * PAIR, (pair + 1) * PAIR)
                        q = qkv_ref[0, here, cols] * jnp.asarray(factor, BF16)
                        key = qkv_ref[1, here, cols] * jnp.asarray(factor, BF16)
                        val = qkv_ref[2, here, cols]
                        do = d_o[here, cols] * column
                        dq = dk = dv = 0.0
                        for h in (2 * pair, 2 * pair + 1):
                            p_low = p_ref[r * heads + h]
                            p = p_low.astype(F32)
                            do_h = head_mask(do, h)
                            d_p = dot_nt(do_h, val)
                            inner = jnp.sum(p * d_p, -1, keepdims=True)
                            d_s = jnp.where(kept, p * (d_p - inner), 0.0).astype(BF16)
                            sums = dot(jnp.ones((8, slots), BF16), d_s)[:1] * order
                            name = (group[h // per], h % per)
                            old = order_sums.get(name)
                            order_sums[name] = sums if old is None else old + sums
                            dq = dq + dot(d_s, head_mask(key, h))
                            dk = dk + dot_tn(d_s, head_mask(q, h))
                            dv = dv + dot_tn(p_low, do_h)
                        dqkv[0, here, cols] = dq.astype(BF16)
                        dqkv[1, here, cols] = dk.astype(BF16)
                        dqkv[2, here, cols] = dv.astype(BF16)
                total = None
                for t in range(3):
                    g = dqkv[t, :, :wide]
                    gq[t, :, :wide] = dot(a1t, g).astype(BF16)
                    term = dot_nt(g, wq[t * width : (t + 1) * width, :wide])
                    total = term if total is None else total + term
                d_in[...] += total
                gq[3, :, :wide] = dot(d_att_t, att_ref[...]).astype(BF16)
                for j, k in enumerate(group):
                    dst = grads[2 * gi + k % 2]
                    cols = slice(j * lane, (j + 1) * lane)
                    for xi in range(2):
                        for zi in range(n_z):
                            at = rows_of(dpi ^ (xi + 2 * zi), sub)
                            for t in range(4):
                                dst[j // 2, xi, zi, t * sub : (t + 1) * sub] = gq[t, at, cols]
                    rows_q = jnp.sum(dqkv[0, :, cols].astype(F32), 0, keepdims=True)
                    rows_v = jnp.sum(dqkv[2, :, cols].astype(F32), 0, keepdims=True)
                    vec_f[k] = jnp.zeros((vec_rows, lane), F32)
                    at = 6 * width // lane
                    vec_f[k, at : at + 1] = rows_q
                    vec_f[k, at + 1 : at + 2] = rows_v
                    gub = (gub_a, gub_b)[gi][j]
                    for i in range(hid // lane):
                        vec_f[k, at + 2 + i : at + 3 + i] = gub[:, i * lane : (i + 1) * lane]
                    lanes = lax.broadcasted_iota(jnp.int32, (1, lane), 1)
                    row = jnp.zeros((1, lane), F32)
                    for i in range(per):
                        row = row + jnp.where(
                            lanes == i, jnp.sum(order_sums[(k, i)], -1, keepdims=True), 0.0
                        )
                    vec_f[k, at + 2 + hid // lane : at + 3 + hid // lane] = row
            normed, rstd = normalize(x_ref[...].astype(F32))
            g = d_in[...]
            final = (dx1[...] + norm_back(g, normed, rstd, gains[0:1])).astype(BF16)
            for r in range(own):
                for k in range(n_mp):
                    at = r * slots + k * share
                    parts[k][r] = final[at : at + share]
            shared[0:1] = jnp.sum(g * normed, 0, keepdims=True)
            shared[1:2] = vec[0:1]
            shared[2:3] = jnp.sum(g, 0, keepdims=True)
            shared[3:4] = vec[1:2]
            shared[4:5] = vec[2:3]
            shared[5:6] = vec[3:4]
            per_row = width // lane
            for gi, group in enumerate(groups):
                for j, k in enumerate(group):
                    for i in range(6):
                        for c in range(per_row):
                            at = i * per_row + c
                            vec_f[k, at : at + 1] = shared[i : i + 1, c * lane : (c + 1) * lane]
                    dst = grads[2 * gi + k % 2]
                    for xi in range(2):
                        for zi in range(n_z):
                            v = vec_f[k, rows_of(dpi ^ (xi + 2 * zi), VEC)]
                            dst[j // 2, xi, zi, 4 * sub :] = two_parts(v)

        def two_parts(v):
            high = v.astype(BF16)
            low = (v - high.astype(F32)).astype(BF16)
            return jnp.concatenate([high.astype(F32), low.astype(F32)], 0).astype(BF16)

        back = run(
            "attend_back",
            attend_back,
            [lengths, order_mask, norm_scale_pair]
            + [x, a1, dx1, d_att]
            + [qkv0, qkv1, p0, p1, att0, att1]
            + [vec, gub0, gub1]
            + qkv_pieces
            + out_pieces,
            [piece] * n_mp + grad_shapes(len(g0), chunk, lane) + grad_shapes(len(g1), chunk, lane),
            [
                *[pltpu.VMEM((3 * width, lane * len(g)), BF16) for g in groups],
                *[pltpu.VMEM((lane * len(g), width), BF16) for g in groups],
                *[pltpu.VMEM((3, count, lane * len(g)), BF16) for g in groups],
                *[pltpu.VMEM((4, width, lane * len(g)), BF16) for g in groups],
                pltpu.VMEM((count, width), F32),
                pltpu.VMEM((n_mp, vec_rows, lane), F32),
                pltpu.VMEM((8, width), F32),
            ],
            flops=2 * count * width * width * 8 + 24 * count * slots * width,
            smem=(0,),
        )
        grad_parts, (ka0, sa0, ka1, sa1) = back[:n_mp], back[n_mp:]

        def add_all(values, vectors):
            total = values[0].astype(F32)
            for v in values[1:]:
                total = total + v.astype(F32)
            if not vectors:
                return total.astype(BF16)
            m = total.shape[-2]
            head = total[..., : m - 2 * VEC, :]
            v = total[..., m - 2 * VEC : m - VEC, :] + total[..., m - VEC :, :]
            high = v.astype(BF16).astype(F32)
            return jnp.concatenate([head, high, v - high], -2).astype(BF16)

        def reduce(keep0, send0, keep1, send1, vectors):
            m, c = keep0.shape[-2:]

            def split_x(ins, outs, _):
                for n in range(ins[0].shape[0]):
                    for xi in range(2):
                        for zi in range(n_z):
                            outs[xi][n, zi] = add_all(
                                [ins[0][n, xi, zi], ins[1][n, xi, zi]], vectors
                            )

            def core_step(keep, send):
                got = mp_swap(send, 1)
                part = shape((keep.shape[0], n_z, m, c), BF16)
                kept, sent = run("add_core", split_x, [keep, got], [part, part])
                return kept, dp_swap(sent, 1)

            kept1, got1 = core_step(keep1, send1)

            def for_y(ins, outs, _):
                for n, o in enumerate(outs):
                    for zi in range(n_z):
                        o[zi] = add_all([ins[0][n, zi], ins[1][n, zi]], vectors)

            n_y = keep1.shape[0]
            over_y = run("add_x", for_y, [kept1, got1], [shape((n_z, m, c), BF16)] * n_y)
            over_y = [mp_swap(v, 2 * (n + 1)) for n, v in enumerate(over_y)]
            kept0, got0 = core_step(keep0, send0)

            def for_z(ins, outs, _):
                for zi, o in enumerate(outs):
                    o[...] = add_all(
                        [ins[0][0, zi], ins[1][0, zi]] + [v[zi] for v in ins[2:]], vectors
                    )

            over_z = run("add_y", for_z, [kept0, got0] + over_y, [shape((m, c), BF16)] * n_z)
            got = [dp_swap(v, 2 * zi) for zi, v in enumerate(over_z) if zi]

            def last(ins, outs, _):
                outs[0][...] = add_all([v[...] for v in ins], vectors)

            (done,) = run("add_z", last, [over_z[0]] + got, [shape((m, c), BF16)])
            same_x = [done] + [dp_swap(done, 2 * zi) for zi in range(1, n_z)]
            other_x = [dp_swap(v, 1) for v in same_x]
            return same_x + other_x

        def places(dpi):
            return [dpi ^ (xi + 2 * zi) for xi in range(2) for zi in range(n_z)]

        def turn(ins, outs, scratch):
            for at, v in zip(places(lax.axis_index("dp")), ins):
                scratch[0][rows_of(at, sub)] = v[...].astype(F32)
            outs[0][...] = scratch[0][...].T

        def straight(ins, outs, _):
            for at, v in zip(places(lax.axis_index("dp")), ins):
                outs[0][rows_of(at, sub)] = v[...].astype(F32)

        def unpack(ins, outs, scratch):
            r_qkv, r_out, small_out, shared = outs
            turned_out, vec_f = scratch
            for at, v in zip(places(lax.axis_index("dp")), ins):
                here = rows_of(at, sub)
                for t in range(3):
                    r_qkv[t, here] = v[t * sub : (t + 1) * sub].astype(F32)
                turned_out[here] = v[3 * sub : 4 * sub].astype(F32)
                pairs = v[4 * sub :].astype(F32)
                vec_f[rows_of(at, VEC)] = pairs[:VEC] + pairs[VEC:]
            r_out[...] = turned_out[...].T
            per_row = width // lane
            for i in range(6):
                shared[i : i + 1] = jnp.concatenate(
                    [vec_f[i * per_row + c : i * per_row + c + 1] for c in range(per_row)], 1
                )
            at = 6 * per_row
            small_out[...] = vec_f[at : at + small_out.shape[0]]

        (r_down,) = run(
            "finish_down",
            turn,
            reduce(kd0, sd0, kd1, sd1, False),
            [shape((hid, width), F32)],
            [pltpu.VMEM((width, hid), F32)],
        )
        (r_up,) = run(
            "finish_up", straight, reduce(ku0, su0, ku1, su1, False), [shape((width, hid), F32)]
        )
        r_qkv, r_out, small_out, shared = run(
            "finish_attention",
            unpack,
            reduce(ka0, sa0, ka1, sa1, True),
            [
                shape((3, width, lane), F32),
                shape((lane, width), F32),
                shape((3 + hid // lane, lane), F32),
                shape((6, width), F32),
            ],
            [pltpu.VMEM((width, lane), F32), pltpu.VMEM((vec_rows, lane), F32)],
        )

        def gather_rows(ins, outs, _):
            me = lax.axis_index("mp")
            for k in range(n_mp):
                outs[0][pl.ds((me ^ k) * own, own)] = ins[k][...].astype(outs[0].dtype)

        def send_back(parts, kind):
            parts = [v if k == 0 else mp_swap(v, k) for k, v in enumerate(parts)]
            return run("gather_rows", gather_rows, parts, [shape((rows, share, width), kind)])[0]

        output = send_back(out_parts, BF16)
        token_gradient = send_back(grad_parts, F32)
        return (
            output,
            token_gradient,
            shared[0:2],
            shared[2:4],
            r_qkv,
            small_out[:2],
            small_out[2 + hid // lane, :per],
            r_out,
            shared[4:6],
            r_up,
            small_out[2 : 2 + hid // lane].reshape(-1),
            r_down,
        )

    return body


def solution(mesh):
    return jax.shard_map(
        make_body(mesh.shape["dp"], mesh.shape["mp"]),
        mesh=mesh,
        in_specs=(
            P("dp", "mp", None),
            P("dp"),
            P("dp", None),
            P(),
            P(),
            P(None, None, "mp"),
            P(None, "mp"),
            P("mp"),
            P("mp", None),
            P(),
            P(None, "mp"),
            P("mp"),
            P("mp", None),
            P("dp", "mp", None),
        ),
        out_specs=(
            P("dp", "mp", None),
            P("dp", "mp", None),
            P(),
            P(),
            P(None, None, "mp"),
            P(None, "mp"),
            P("mp"),
            P("mp", None),
            P(),
            P(None, "mp"),
            P("mp"),
            P("mp", None),
        ),
        check_vma=False,
    )
```

time: 315 us -> 201 us (0.64)
  local copies, waits for them, and re-layouts: 78.4 us -> 14.6 us
  matrix products: 59 us -> 0 us
  other arithmetic: 46.4 us -> 0.07 us
  Pallas kernels: 0 us -> 41.4 us
  starting transfers between devices: 50.1 us -> 78.5 us
  waiting for transfers between devices: 76.9 us -> 65.1 us
    dot_general x17 -> x0, matrix products: 48.5 us -> none  [the longest x1 8.35 us: body(): d_hidden = jnp.dot(dy_bf, w_down_all.T, preferred_element_type=F32)]
    pallas_call x0 -> x28, Pallas kernels: none -> 41.4 us  [run(): pl.pallas_call(kernel, out_shape=tuple(outs), in_specs=[pl.BlockSpec(memo...]
    gather x18 -> x0, local copies, waits for them, and re-layouts: 28.4 us -> none  [the longest x12 23.2 us: reduce(): full = jnp.stack([jnp.take(cut[k], dpi ^ dp_sub, axis=0) for k in mp_order])]
    ppermute x56 -> x80, starting transfers between devices: 50.1 us -> 78.5 us  [swap(): return lax.ppermute(v, axis, [(i, i ^ bit) for i in range(size)])]
    split x16 -> x0, local copies, waits for them, and re-layouts: 17.5 us -> none  [blocks_of(): return jnp.split(v, n_mp, axis)]
    concatenate x26 -> x1, other arithmetic: 13.6 us -> 0.07 us  [body(): jnp.concatenate([jnp.pad(qv_bias, ((0, 0), (0, LANES - lane))), up_bias.r...]
    ppermute x56 -> x80, waiting for transfers between devices: 76.9 us -> 65.1 us  [swap(): return lax.ppermute(v, axis, [(i, i ^ bit) for i in range(size)])]
    sub x2 -> x0, matrix products: 10.5 us -> none  [the longest x1 7.05 us: body(): d_scores = probs * (d_probs - jnp.sum(probs * d_probs, -1, keepdims=True))]
  transfers between devices with their start and end apart: 56 -> 80, of which waited for: 27 -> 23; matrix products, arithmetic and copies ran while one was open for 44% -> 0% of each run, Pallas kernels for 0% -> 16%
where the time goes in v2:
time: 201 us
  starting transfers between devices  78.5 us (39%)
  waiting for transfers between devices  65.1 us (32%)
  Pallas kernels  41.4 us (21%)
  local copies, waits for them, and re-layouts  14.6 us (7%)
    ppermute x80, starting transfers between devices, swap(): return lax.ppermute(v, axis, [(i, i ^ bit) for i in range(size)])  78.5 us
    ppermute x80, waiting for transfers between devices, swap(): return lax.ppermute(v, axis, [(i, i ^ bit) for i in range(size)])  65.1 us
    pallas_call x28, Pallas kernels, run(): pl.pallas_call(kernel, out_shape=tuple(outs), in_specs=[pl.BlockSpec(memo...  41.4 us
    unnamed x58, local copies, waits for them, and re-layouts  12.3 us
  transfers between devices with their start and end apart: 80, of which 23 were waited for; matrix products, arithmetic and copies ran while one was open for 0% of the time, Pallas kernels for 16%

profile of v2, /device:TPU:0, one launch (start us, length us, event | category | flops | bytes accessed | tf_op | source)
XLA Modules:
  0.0 200.7 jit_solution(16149916653233769308)
XLA Ops:
  2.4 2.9 %collective-permute-start.1 = (bf16[2,64,512]{2,1,0:T(8,128)(2,1)S(1)}, bf16[2,64,512]{2,1,0:T(8,128)(2,1)S(1)}, u32[]{:S(2)}, u32[]{:S(2)}) collective-permute-start(bf16[2,64,512]{2,1,0:T(8,128)(2,1)S(1)} %get-tuple-element.94), channel_id=1, source_target_pairs={{0,2},{1,3},{2,0},{3,1},{4,6},{5,7},{6,4},{7,5},{8,10},{9,11},{10,... | collective-permute-start | bytes 393224 | tf_op jit(solution)/shard_map/ppermute | solution.py:20
  9.8 2.4 %collective-permute-done.10.refs_8_.refs_18_ = f32[8,128]{1,0:T(8,128)S(1)} collective-permute-done((f32[8,128]{1,0:T(8,128)S(1)}, f32[8,128]{1,0:T(8,128)S(1)}, u32[]{:S(2)}, u32[]{:S(2)}) %collective-permute-start.10) | collective-permute-done | bytes 4128 | tf_op jit(solution)/shard_map/ppermute | solution.py:20
  12.2 1.5 collective-permute-start.9
  13.7 2.1 %collective-permute-done.9.refs_7_.refs_17_ = f32[8,128]{1,0:T(8,128)S(1)} collective-permute-done((f32[8,128]{1,0:T(8,128)S(1)}, f32[8,128]{1,0:T(8,128)S(1)}, u32[]{:S(2)}, u32[]{:S(2)}) %collective-permute-start.9) | collective-permute-done | bytes 4128 | tf_op jit(solution)/shard_map/ppermute | solution.py:20
  20.8 1.7 collective-permute-done.2.refs_3_
  22.5 1.5 collective-permute-start.25
  25.8 2.3 %collective-permute-done.18.refs_15_ = bf16[2,64,512]{2,1,0:T(8,128)(2,1)S(1)} collective-permute-done((bf16[2,64,512]{2,1,0:T(8,128)(2,1)S(1)}, bf16[2,64,512]{2,1,0:T(8,128)(2,1)S(1)}, u32[]{:S(2)}, u32[]{:S(2)}) %collective-permute-start.18) | collective-permute-done | bytes 131104 | tf_op jit(solution)/shard_map/ppermute | solution.py:20
  28.4 1.5 collective-permute-start.13
  30.0 2.7 %collective-permute-done.13.refs_9_.refs_25_ = bf16[64,512]{1,0:T(8,128)(2,1)S(1)} collective-permute-done((bf16[64,512]{1,0:T(8,128)(2,1)S(1)}, bf16[64,512]{1,0:T(8,128)(2,1)S(1)}, u32[]{:S(2)}, u32[]{:S(2)}) %collective-permute-start.13) | collective-permute-done | bytes 65568 | tf_op jit(solution)/shard_map/ppermute | solution.py:20
  32.7 11.1 %collective-permute-done.5.refs_3_.refs_18_ = bf16[768,128]{1,0:T(8,128)(2,1)S(1)} collective-permute-done((bf16[768,128]{1,0:T(8,128)(2,1)S(1)}, bf16[768,128]{1,0:T(8,128)(2,1)S(1)}, u32[]{:S(2)}, u32[]{:S(2)}) %collective-permute-start.5) | collective-permute-done | bytes 196640 | tf_op jit(solution)/shard_map/ppermute | solution.py:20
  43.8 1.6 collective-permute-start.6
  45.6 5.6 %collective-permute-done.6.refs_4_.refs_19_ = bf16[768,128]{1,0:T(8,128)(2,1)S(1)} collective-permute-done((bf16[768,128]{1,0:T(8,128)(2,1)S(1)}, bf16[768,128]{1,0:T(8,128)(2,1)S(1)}, u32[]{:S(2)}, u32[]{:S(2)}) %collective-permute-start.6) | collective-permute-done | bytes 196640 | tf_op jit(solution)/shard_map/ppermute | solution.py:20
  51.1 1.5 collective-permute-start.22
  53.2 3.3 %attend.2 = (bf16[512,512]{1,0:T(8,128)(2,1)S(1)}, bf16[512,512]{1,0:T(8,128)(2,1)S(1)}, bf16[3,512,256]{2,1,0:T(8,128)(2,1)S(1)}, bf16[8,256,256]{2,1,0:T(8,128)(2,1)S(1)}, bf16[512,256]{1,0:T(8,128)(2,1)S(1)}) custom-call(bf16[2,64,512]{2,1,0:T(8,128)(2,1)S(1)} %get-tuple-element.92.refs_0_, bf16[2,64,512]{2,1,0:T(8,128)(2,1)S(1)} %collective-permute-done.refs_1_, ...), custom_call_target="tpu_custom_call" | custom-call | flops 939524096 | bytes 4481056 | tf_op jit(solution)/shard_map/attend/pallas_call | solution.py:34
  59.2 3.1 %attend.3 = (bf16[3,512,256]{2,1,0:T(8,128)(2,1)S(1)}, bf16[8,256,256]{2,1,0:T(8,128)(2,1)S(1)}, bf16[512,256]{1,0:T(8,128)(2,1)S(1)}) custom-call(s32[8]{0:T(128)S(1)} %copy-done.14, s32[8,256]{1,0:T(8,128)S(1)} %copy-done.10, bf16[512,512]{1,0:T(8,128)(2,1)S(1)} %get-tuple-element.98.refs_2_.refs_4_, ...), custom_call_target="tpu_custom_call" | custom-call | flops 939524096 | bytes 3424288 | tf_op jit(solution)/shard_map/attend/pallas_call | solution.py:34
  66.3 7.9 %mlp_first.1 = (f32[512,512]{1,0:T(8,128)}, bf16[512,512]{1,0:T(8,128)(2,1)S(1)}, bf16[512,512]{1,0:T(8,128)(2,1)S(1)}, bf16[512,512]{1,0:T(8,128)(2,1)S(1)}, bf...) custom-call(bf16[512,512]{1,0:T(8,128)(2,1)} %copy-done.19, ...), custom_call_target="tpu_custom_call" | custom-call | flops 3489660928 | bytes 11558912 | tf_op jit(solution)/shard_map/mlp_first/pallas_call | solution.py:34
  76.7 8.2 %mlp_second.1 = (bf16[2,64,512]{2,1,0:T(8,128)(2,1)S(1)}, bf16[2,64,512]{2,1,0:T(8,128)(2,1)S(1)}, bf16[2,64,512]{2,1,0:T(8,128)(2,1)S(1)}, bf16[2,64,512]{2,1,0...) custom-call(f32[512,512]{1,0:T(8,128)} %get-tuple-element.106.refs_0, ...), custom_call_target="tpu_custom_call" | custom-call | flops 3221225472 | bytes 11563008 | tf_op jit(solution)/shard_map/mlp_second/pallas_call | solution.py:34
  87.5 12.0 %attend_back.1 = (bf16[2,64,512]{2,1,0:T(8,128)(2,1)S(1)}, bf16[2,64,512]{2,1,0:T(8,128)(2,1)S(1)}, bf16[2,64,512]{2,1,0:T(8,128)(2,1)S(1)}, bf16[2,64,512]{2,1,...) custom-call(s32[8]{0:T(128)S(1)} %copy-done.14, ...), custom_call_target="tpu_custom_call" | custom-call | flops 3758096384 | bytes 11694112 | tf_op jit(solution)/shard_map/attend_back/pallas_call | solution.py:34
  101.8 4.2 %collective-permute-done.33.refs_2_ = bf16[2,64,512]{2,1,0:T(8,128)(2,1)S(1)} collective-permute-done((bf16[2,64,512]{2,1,0:T(8,128)(2,1)S(1)}, bf16[2,64,512]{2,1,0:T(8,128)(2,1)S(1)}, u32[]{:S(2)}, u32[]{:S(2)}) %collective-permute-start.33) | collective-permute-done | bytes 131104 | tf_op jit(solution)/shard_map/ppermute | solution.py:20
  106.6 1.6 collective-permute-start.53
  109.1 1.6 collective-permute-start.38
  110.8 5.1 %collective-permute-done.53.refs_1_ = bf16[1,4,64,512]{3,2,1,0:T(8,128)(2,1)S(1)} collective-permute-done((bf16[1,4,64,512]{3,2,1,0:T(8,128)(2,1)S(1)}, bf16[1,4,64,512]{3,2,1,0:T(8,128)(2,1)S(1)}, u32[]{:S(2)}, u32[]{:S(2)}) %collective-permute-start.53) | collective-permute-done | bytes 262176 | tf_op jit(solution)/shard_map/ppermute | solution.py:20
  115.9 1.5 collective-permute-start.51
  117.4 1.6 collective-permute-start.54
  119.1 2.4 %collective-permute-done.68.refs_1_ = bf16[1,4,64,512]{3,2,1,0:T(8,128)(2,1)S(1)} collective-permute-done((bf16[1,4,64,512]{3,2,1,0:T(8,128)(2,1)S(1)}, bf16[1,4,64,512]{3,2,1,0:T(8,128)(2,1)S(1)}, u32[]{:S(2)}, u32[]{:S(2)}) %collective-permute-start.68) | collective-permute-done | bytes 262176 | tf_op jit(solution)/shard_map/ppermute | solution.py:20
  121.5 1.5 collective-permute-start.66
  123.1 1.6 collective-permute-start.69
  124.7 2.7 %collective-permute-done.38.refs_1_ = bf16[1,4,272,128]{3,2,1,0:T(8,128)(2,1)S(1)} collective-permute-done((bf16[1,4,272,128]{3,2,1,0:T(8,128)(2,1)S(1)}, bf16[1,4,272,128]{3,2,1,0:T(8,128)(2,1)S(1)}, u32[]{:S(2)}, u32[]{:S(2)}) %collective-permute-start.38) | collective-permute-done | bytes 278560 | tf_op jit(solution)/shard_map/ppermute | solution.py:20
  127.4 1.5 collective-permute-start.36
  129.0 4.0 %collective-permute-done.51.refs_1_ = bf16[1,4,64,512]{3,2,1,0:T(8,128)(2,1)S(1)} collective-permute-done((bf16[1,4,64,512]{3,2,1,0:T(8,128)(2,1)S(1)}, bf16[1,4,64,512]{3,2,1,0:T(8,128)(2,1)S(1)}, u32[]{:S(2)}, u32[]{:S(2)}) %collective-permute-start.51) | collective-permute-done | bytes 262176 | tf_op jit(solution)/shard_map/ppermute | solution.py:20
  134.7 7.0 %collective-permute-done.34.refs_3_ = bf16[2,64,512]{2,1,0:T(8,128)(2,1)S(1)} collective-permute-done((bf16[2,64,512]{2,1,0:T(8,128)(2,1)S(1)}, bf16[2,64,512]{2,1,0:T(8,128)(2,1)S(1)}, u32[]{:S(2)}, u32[]{:S(2)}) %collective-permute-start.34) | collective-permute-done | bytes 131104 | tf_op jit(solution)/shard_map/ppermute | solution.py:20
  141.6 1.6 collective-permute-start.55
  143.2 2.6 %collective-permute-start.56 = (bf16[64,512]{1,0:T(8,128)(2,1)S(1)}, bf16[64,512]{1,0:T(8,128)(2,1)S(1)}, u32[]{:S(2)}, u32[]{:S(2)}) collective-permute-start(bf16[64,512]{1,0:T(8,128)(2,1)S(1)} %get-tuple-element.158), channel_id=1, source_target_pairs={{0,16},{4,20},{8,24},{12,28},{16,0},{20,4},{24,8},{28,12},{1,17},{... | collective-permute-start | bytes 196616 | tf_op jit(solution)/shard_map/ppermute | solution.py:20
  146.5 1.6 collective-permute-start.70
  148.0 2.5 %collective-permute-done.56.refs_2_ = bf16[64,512]{1,0:T(8,128)(2,1)S(1)} collective-permute-done((bf16[64,512]{1,0:T(8,128)(2,1)S(1)}, bf16[64,512]{1,0:T(8,128)(2,1)S(1)}, u32[]{:S(2)}, u32[]{:S(2)}) %collective-permute-start.56) | collective-permute-done | bytes 65568 | tf_op jit(solution)/shard_map/ppermute | solution.py:20
  152.3 2.1 %collective-permute-start.72 = (bf16[64,512]{1,0:T(8,128)(2,1)S(1)}, bf16[64,512]{1,0:T(8,128)(2,1)S(1)}, u32[]{:S(2)}, u32[]{:S(2)}) collective-permute-start(bf16[64,512]{1,0:T(8,128)(2,1)S(1)} %get-tuple-element.171), channel_id=1, source_target_pairs={{0,24},{4,28},{8,16},{12,20},{16,8},{20,12},{24,0},{28,4},{1,25},{... | collective-permute-start | bytes 196616 | tf_op jit(solution)/shard_map/ppermute | solution.py:20
  154.5 1.6 collective-permute-start.61
  156.0 1.7 collective-permute-start.60
  158.9 1.5 collective-permute-start.58
  160.5 2.1 %collective-permute-start.40 = (bf16[272,128]{1,0:T(8,128)(2,1)S(1)}, bf16[272,128]{1,0:T(8,128)(2,1)S(1)}, u32[]{:S(2)}, u32[]{:S(2)}) collective-permute-start(bf16[272,128]{1,0:T(8,128)(2,1)S(1)} %get-tuple-element.141), channel_id=1, source_target_pairs={{0,8},{4,12},{8,0},{12,4},{16,24},{20,28},{24,16},{28,20},{1,9},{5... | collective-permute-start | bytes 208904 | tf_op jit(solution)/shard_map/ppermute | solution.py:20
  162.7 2.3 %collective-permute-start.41 = (bf16[272,128]{1,0:T(8,128)(2,1)S(1)}, bf16[272,128]{1,0:T(8,128)(2,1)S(1)}, u32[]{:S(2)}, u32[]{:S(2)}) collective-permute-start(bf16[272,128]{1,0:T(8,128)(2,1)S(1)} %get-tuple-element.142), channel_id=1, source_target_pairs={{0,16},{4,20},{8,24},{12,28},{16,0},{20,4},{24,8},{28,12},{1,17},{... | collective-permute-start | bytes 208904 | tf_op jit(solution)/shard_map/ppermute | solution.py:20
  165.0 1.8 collective-permute-start.76
  166.8 2.5 %collective-permute-start.75 = (bf16[64,512]{1,0:T(8,128)(2,1)S(1)}, bf16[64,512]{1,0:T(8,128)(2,1)S(1)}, u32[]{:S(2)}, u32[]{:S(2)}) collective-permute-start(bf16[64,512]{1,0:T(8,128)(2,1)S(1)} %add_z.5.refs_0_), channel_id=1, source_target_pairs={{0,24},{4,28},{8,16},{12,20},{16,8},{20,12},{24,0},{28,4},{1,25},{... | collective-permute-start | bytes 196616 | tf_op jit(solution)/shard_map/ppermute | solution.py:20
  171.3 2.2 %collective-permute-done.75.refs_3_ = bf16[64,512]{1,0:T(8,128)(2,1)S(1)} collective-permute-done((bf16[64,512]{1,0:T(8,128)(2,1)S(1)}, bf16[64,512]{1,0:T(8,128)(2,1)S(1)}, u32[]{:S(2)}, u32[]{:S(2)}) %collective-permute-start.75) | collective-permute-done | bytes 65568 | tf_op jit(solution)/shard_map/ppermute | solution.py:20
  173.5 1.8 collective-permute-start.73
  178.3 2.0 collective-permute-start.45
  180.2 2.5 %collective-permute-start.43 = (bf16[272,128]{1,0:T(8,128)(2,1)S(1)}, bf16[272,128]{1,0:T(8,128)(2,1)S(1)}, u32[]{:S(2)}, u32[]{:S(2)}) collective-permute-start(bf16[272,128]{1,0:T(8,128)(2,1)S(1)} %add_z.3.refs_0_), channel_id=1, source_target_pairs={{0,8},{4,12},{8,0},{12,4},{16,24},{20,28},{24,16},{28,20},{1,9},{5... | collective-permute-start | bytes 208904 | tf_op jit(solution)/shard_map/ppermute | solution.py:20
  184.7 2.9 %collective-permute-done.79.refs_7_ = bf16[64,512]{1,0:T(8,128)(2,1)S(1)} collective-permute-done((bf16[64,512]{1,0:T(8,128)(2,1)S(1)}, bf16[64,512]{1,0:T(8,128)(2,1)S(1)}, u32[]{:S(2)}, u32[]{:S(2)}) %collective-permute-start.79) | collective-permute-done | bytes 65568 | tf_op jit(solution)/shard_map/ppermute | solution.py:20
  (205 shorter events, 55.6 us)
Async XLA Ops:
  0.7 18.1 %collective-permute-start.11 = (bf16[128,512]{1,0:T(8,128)(2,1)}, bf16[128,512]{1,0:T(8,128)(2,1)S(1)}, u32[]{:S(2)}, u32[]{:S(2)}) collective-permute-start(bf16[128,512]{1,0:T(8,128)(2,1)} %refs_22_.1), channel_id=1, source_target_pairs={{0,1},{1,0},{2,3},{3,2},{4,5},{5,4},{6,7},{7,6},{8,9},{9,8},{10,11... | collective-permute-start | bytes 393224 | tf_op jit(solution)/shard_map/ppermute | solution.py:20
  2.3 17.0 %collective-permute-start = (bf16[2,64,512]{2,1,0:T(8,128)(2,1)S(1)}, bf16[2,64,512]{2,1,0:T(8,128)(2,1)S(1)}, u32[]{:S(2)}, u32[]{:S(2)}) collective-permute-start(bf16[2,64,512]{2,1,0:T(8,128)(2,1)S(1)} %get-tuple-element.93), channel_id=1, source_target_pairs={{0,1},{1,0},{2,3},{3,2},{4,5},{5,4},{6,7},{7,6},{8,9},{9,8},{10,11... | collective-permute-start | bytes 393224 | tf_op jit(solution)/shard_map/ppermute | solution.py:20
  2.4 17.8 %collective-permute-start.1 = (bf16[2,64,512]{2,1,0:T(8,128)(2,1)S(1)}, bf16[2,64,512]{2,1,0:T(8,128)(2,1)S(1)}, u32[]{:S(2)}, u32[]{:S(2)}) collective-permute-start(bf16[2,64,512]{2,1,0:T(8,128)(2,1)S(1)} %get-tuple-element.94), channel_id=1, source_target_pairs={{0,2},{1,3},{2,0},{3,1},{4,6},{5,7},{6,4},{7,5},{8,10},{9,11},{10,... | collective-permute-start | bytes 393224 | tf_op jit(solution)/shard_map/ppermute | solution.py:20
  8.4 9.9 %collective-permute-start.12 = (bf16[64,512]{1,0:T(8,128)(2,1)S(1)}, bf16[64,512]{1,0:T(8,128)(2,1)S(1)}, u32[]{:S(2)}, u32[]{:S(2)}) collective-permute-start(bf16[64,512]{1,0:T(8,128)(2,1)S(1)} %get-tuple-element.101), channel_id=1, source_target_pairs={{0,2},{1,3},{2,0},{3,1},{4,6},{5,7},{6,4},{7,5},{8,10},{9,11},{10,... | collective-permute-start | bytes 196616 | tf_op jit(solution)/shard_map/ppermute | solution.py:20
  19.2 8.9 %collective-permute-start.18 = (bf16[2,64,512]{2,1,0:T(8,128)(2,1)S(1)}, bf16[2,64,512]{2,1,0:T(8,128)(2,1)S(1)}, u32[]{:S(2)}, u32[]{:S(2)}) collective-permute-start(bf16[2,64,512]{2,1,0:T(8,128)(2,1)S(1)} %get-tuple-element.105), channel_id=1, source_target_pairs={{0,3},{1,2},{2,1},{3,0},{4,7},{5,6},{6,5},{7,4},{8,11},{9,10},{10,... | collective-permute-start | bytes 393224 | tf_op jit(solution)/shard_map/ppermute | solution.py:20
  20.2 23.6 %collective-permute-start.21 = (bf16[256,512]{1,0:T(8,128)(2,1)S(1)}, bf16[256,512]{1,0:T(8,128)(2,1)S(1)}, u32[]{:S(2)}, u32[]{:S(2)}) collective-permute-start(bf16[256,512]{1,0:T(8,128)(2,1)S(1)} %get-tuple-element.113), channel_id=1, source_target_pairs={{0,2},{1,3},{2,0},{3,1},{4,6},{5,7},{6,4},{7,5},{8,10},{9,11},{10,... | collective-permute-start | bytes 786440 | tf_op jit(solution)/shard_map/ppermute | solution.py:20
  22.5 22.9 %collective-permute-start.25 = (bf16[256,512]{1,0:T(8,128)(2,1)S(1)}, bf16[256,512]{1,0:T(8,128)(2,1)S(1)}, u32[]{:S(2)}, u32[]{:S(2)}) collective-permute-start(bf16[256,512]{1,0:T(8,128)(2,1)S(1)} %get-tuple-element.114), channel_id=1, source_target_pairs={{0,2},{1,3},{2,0},{3,1},{4,6},{5,7},{6,4},{7,5},{8,10},{9,11},{10,... | collective-permute-start | bytes 786440 | tf_op jit(solution)/shard_map/ppermute | solution.py:20
  24.0 19.8 %collective-permute-start.5 = (bf16[768,128]{1,0:T(8,128)(2,1)S(1)}, bf16[768,128]{1,0:T(8,128)(2,1)S(1)}, u32[]{:S(2)}, u32[]{:S(2)}) collective-permute-start(bf16[768,128]{1,0:T(8,128)(2,1)S(1)} %get-tuple-element.99), channel_id=1, source_target_pairs={{0,2},{1,3},{2,0},{3,1},{4,6},{5,7},{6,4},{7,5},{8,10},{9,11},{10,... | collective-permute-start | bytes 589832 | tf_op jit(solution)/shard_map/ppermute | solution.py:20
  28.1 23.0 %collective-permute-start.3 = (bf16[1536,128]{1,0:T(8,128)(2,1)S(1)}, bf16[1536,128]{1,0:T(8,128)(2,1)S(1)}, u32[]{:S(2)}, u32[]{:S(2)}) collective-permute-start(bf16[1536,128]{1,0:T(8,128)(2,1)S(1)} %bitcast.10), channel_id=1, source_target_pairs={{0,1},{1,0},{2,3},{3,2},{4,5},{5,4},{6,7},{7,6},{8,9},{9,8},{10,11... | collective-permute-start | bytes 1179656 | tf_op jit(solution)/shard_map/ppermute | solution.py:20
  32.7 32.0 %collective-permute-start.19 = (bf16[512,512]{1,0:T(8,128)(2,1)S(1)}, bf16[512,512]{1,0:T(8,128)(2,1)S(1)}, u32[]{:S(2)}, u32[]{:S(2)}) collective-permute-start(bf16[512,512]{1,0:T(8,128)(2,1)S(1)} %copy-done.1), channel_id=1, source_target_pairs={{0,1},{1,0},{2,3},{3,2},{4,5},{5,4},{6,7},{7,6},{8,9},{9,8},{10,11... | collective-permute-start | bytes 1572872 | tf_op jit(solution)/shard_map/ppermute | solution.py:20
  43.8 21.7 %collective-permute-start.20 = (bf16[512,512]{1,0:T(8,128)(2,1)S(1)}, bf16[512,512]{1,0:T(8,128)(2,1)S(1)}, u32[]{:S(2)}, u32[]{:S(2)}) collective-permute-start(bf16[512,512]{1,0:T(8,128)(2,1)S(1)} %copy-done.3), channel_id=1, source_target_pairs={{0,1},{1,0},{2,3},{3,2},{4,5},{5,4},{6,7},{7,6},{8,9},{9,8},{10,11... | collective-permute-start | bytes 1572872 | tf_op jit(solution)/shard_map/ppermute | solution.py:20
  51.1 13.6 %collective-permute-start.22 = (bf16[256,512]{1,0:T(8,128)(2,1)S(1)}, bf16[256,512]{1,0:T(8,128)(2,1)S(1)}, u32[]{:S(2)}, u32[]{:S(2)}) collective-permute-start(bf16[256,512]{1,0:T(8,128)(2,1)S(1)} %collective-permute-done.21.refs_9_), channel_id=1, source_target_pairs={{0,4},{4,0},{8,12},{12,8},{16,20},{20,16},{24,28},{28,24},{1,5},{5... | collective-permute-start | bytes 786440 | tf_op jit(solution)/shard_map/ppermute | solution.py:20
  52.7 12.8 %collective-permute-start.26 = (bf16[256,512]{1,0:T(8,128)(2,1)S(1)}, bf16[256,512]{1,0:T(8,128)(2,1)S(1)}, u32[]{:S(2)}, u32[]{:S(2)}) collective-permute-start(bf16[256,512]{1,0:T(8,128)(2,1)S(1)} %collective-permute-done.25.refs_13_), channel_id=1, source_target_pairs={{0,4},{4,0},{8,12},{12,8},{16,20},{20,16},{24,28},{28,24},{1,5},{5... | collective-permute-start | bytes 786440 | tf_op jit(solution)/shard_map/ppermute | solution.py:20
  64.2 12.5 %collective-permute-start.23 = (bf16[256,512]{1,0:T(8,128)(2,1)S(1)}, bf16[256,512]{1,0:T(8,128)(2,1)S(1)}, u32[]{:S(2)}, u32[]{:S(2)}) collective-permute-start(bf16[256,512]{1,0:T(8,128)(2,1)S(1)} %collective-permute-done.21.refs_9_), channel_id=1, source_target_pairs={{0,1},{1,0},{2,3},{3,2},{4,5},{5,4},{6,7},{7,6},{8,9},{9,8},{10,11... | collective-permute-start | bytes 786440 | tf_op jit(solution)/shard_map/ppermute | solution.py:20
  64.7 12.0 %collective-permute-start.27 = (bf16[256,512]{1,0:T(8,128)(2,1)S(1)}, bf16[256,512]{1,0:T(8,128)(2,1)S(1)}, u32[]{:S(2)}, u32[]{:S(2)}) collective-permute-start(bf16[256,512]{1,0:T(8,128)(2,1)S(1)} %collective-permute-done.25.refs_13_), channel_id=1, source_target_pairs={{0,1},{1,0},{2,3},{3,2},{4,5},{5,4},{6,7},{7,6},{8,9},{9,8},{10,11... | collective-permute-start | bytes 786440 | tf_op jit(solution)/shard_map/ppermute | solution.py:20
  64.8 11.9 %collective-permute-start.24 = (bf16[256,512]{1,0:T(8,128)(2,1)S(1)}, bf16[256,512]{1,0:T(8,128)(2,1)S(1)}, u32[]{:S(2)}, u32[]{:S(2)}) collective-permute-start(bf16[256,512]{1,0:T(8,128)(2,1)S(1)} %collective-permute-done.22.refs_10_), channel_id=1, source_target_pairs={{0,1},{1,0},{2,3},{3,2},{4,5},{5,4},{6,7},{7,6},{8,9},{9,8},{10,11... | collective-permute-start | bytes 786440 | tf_op jit(solution)/shard_map/ppermute | solution.py:20
  65.5 11.2 %collective-permute-start.28 = (bf16[256,512]{1,0:T(8,128)(2,1)S(1)}, bf16[256,512]{1,0:T(8,128)(2,1)S(1)}, u32[]{:S(2)}, u32[]{:S(2)}) collective-permute-start(bf16[256,512]{1,0:T(8,128)(2,1)S(1)} %collective-permute-done.26.refs_14_), channel_id=1, source_target_pairs={{0,1},{1,0},{2,3},{3,2},{4,5},{5,4},{6,7},{7,6},{8,9},{9,8},{10,11... | collective-permute-start | bytes 786440 | tf_op jit(solution)/shard_map/ppermute | solution.py:20
  84.9 14.6 %collective-permute-start.29 = (bf16[2,64,512]{2,1,0:T(8,128)(2,1)S(1)}, bf16[2,64,512]{2,1,0:T(8,128)(2,1)S(1)}, u32[]{:S(2)}, u32[]{:S(2)}) collective-permute-start(bf16[2,64,512]{2,1,0:T(8,128)(2,1)S(1)} %get-tuple-element.116), channel_id=1, source_target_pairs={{0,1},{1,0},{2,3},{3,2},{4,5},{5,4},{6,7},{7,6},{8,9},{9,8},{10,11... | collective-permute-start | bytes 393224 | tf_op jit(solution)/shard_map/ppermute | solution.py:20
  85.4 14.6 %collective-permute-start.30 = (bf16[2,64,512]{2,1,0:T(8,128)(2,1)S(1)}, bf16[2,64,512]{2,1,0:T(8,128)(2,1)S(1)}, u32[]{:S(2)}, u32[]{:S(2)}) collective-permute-start(bf16[2,64,512]{2,1,0:T(8,128)(2,1)S(1)} %get-tuple-element.117), channel_id=1, source_target_pairs={{0,2},{1,3},{2,0},{3,1},{4,6},{5,7},{6,4},{7,5},{8,10},{9,11},{10,... | collective-permute-start | bytes 393224 | tf_op jit(solution)/shard_map/ppermute | solution.py:20
  86.9 13.2 %collective-permute-start.31 = (bf16[2,64,512]{2,1,0:T(8,128)(2,1)S(1)}, bf16[2,64,512]{2,1,0:T(8,128)(2,1)S(1)}, u32[]{:S(2)}, u32[]{:S(2)}) collective-permute-start(bf16[2,64,512]{2,1,0:T(8,128)(2,1)S(1)} %get-tuple-element.118), channel_id=1, source_target_pairs={{0,3},{1,2},{2,1},{3,0},{4,7},{5,6},{6,5},{7,4},{8,11},{9,10},{10,... | collective-permute-start | bytes 393224 | tf_op jit(solution)/shard_map/ppermute | solution.py:20
  86.9 19.1 %collective-permute-start.52 = (bf16[1,2,4,64,512]{4,3,2,1,0:T(8,128)(2,1)S(1)}, bf16[1,2,4,64,512]{4,3,2,1,0:T(8,128)(2,1)S(1)}, u32[]{:S(2)}, u32[]{:S(2)}) collective-permute-start(bf16[1,2,4,64,512]{4,3,2,1,0:T(8,128)(2,1)S(1)} %get-tuple-element.153), channel_id=1, source_target_pairs={{0,1},{1,0},{2,3},{3,2},{4,5},{5,4},{6,7},{7,6},{8,9},{9,8},{10,11... | collective-permute-start | bytes 1572872 | tf_op jit(solution)/shard_map/ppermute | solution.py:20
  87.5 19.1 %collective-permute-start.67 = (bf16[1,2,4,64,512]{4,3,2,1,0:T(8,128)(2,1)S(1)}, bf16[1,2,4,64,512]{4,3,2,1,0:T(8,128)(2,1)S(1)}, u32[]{:S(2)}, u32[]{:S(2)}) collective-permute-start(bf16[1,2,4,64,512]{4,3,2,1,0:T(8,128)(2,1)S(1)} %get-tuple-element.165), channel_id=1, source_target_pairs={{0,1},{1,0},{2,3},{3,2},{4,5},{5,4},{6,7},{7,6},{8,9},{9,8},{10,11... | collective-permute-start | bytes 1572872 | tf_op jit(solution)/shard_map/ppermute | solution.py:20
  100.0 8.3 %collective-permute-start.37 = (bf16[1,2,4,272,128]{4,3,2,1,0:T(8,128)(2,1)}, bf16[1,2,4,272,128]{4,3,2,1,0:T(8,128)(2,1)S(1)}, u32[]{:S(2)}, u32[]{:S(2)}) collective-permute-start(bf16[1,2,4,272,128]{4,3,2,1,0:T(8,128)(2,1)} %get-tuple-element.137), channel_id=1, source_target_pairs={{0,1},{1,0},{2,3},{3,2},{4,5},{5,4},{6,7},{7,6},{8,9},{9,8},{10,11... | collective-permute-start | bytes 1671176 | tf_op jit(solution)/shard_map/ppermute | solution.py:20
  105.9 11.5 %collective-permute-start.65 = (bf16[1,2,4,64,512]{4,3,2,1,0:T(8,128)(2,1)S(1)}, bf16[1,2,4,64,512]{4,3,2,1,0:T(8,128)(2,1)S(1)}, u32[]{:S(2)}, u32[]{:S(2)}) collective-permute-start(bf16[1,2,4,64,512]{4,3,2,1,0:T(8,128)(2,1)S(1)} %get-tuple-element.161), channel_id=1, source_target_pairs={{0,1},{1,0},{2,3},{3,2},{4,5},{5,4},{6,7},{7,6},{8,9},{9,8},{10,11... | collective-permute-start | bytes 1572872 | tf_op jit(solution)/shard_map/ppermute | solution.py:20
  106.0 17.1 %collective-permute-start.35 = (bf16[1,2,4,272,128]{4,3,2,1,0:T(8,128)(2,1)S(1)}, bf16[1,2,4,272,128]{4,3,2,1,0:T(8,128)(2,1)S(1)}, u32[]{:S(2)}, u32[]{:S(2)}) collective-permute-start(bf16[1,2,4,272,128]{4,3,2,1,0:T(8,128)(2,1)S(1)} %get-tuple-element.133), channel_id=1, source_target_pairs={{0,1},{1,0},{2,3},{3,2},{4,5},{5,4},{6,7},{7,6},{8,9},{9,8},{10,11... | collective-permute-start | bytes 1671176 | tf_op jit(solution)/shard_map/ppermute | solution.py:20
  106.6 9.2 %collective-permute-start.53 = (bf16[1,4,64,512]{3,2,1,0:T(8,128)(2,1)S(1)}, bf16[1,4,64,512]{3,2,1,0:T(8,128)(2,1)S(1)}, u32[]{:S(2)}, u32[]{:S(2)}) collective-permute-start(bf16[1,4,64,512]{3,2,1,0:T(8,128)(2,1)S(1)} %get-tuple-element.155), channel_id=1, source_target_pairs={{0,4},{4,0},{8,12},{12,8},{16,20},{20,16},{24,28},{28,24},{1,5},{5... | collective-permute-start | bytes 786440 | tf_op jit(solution)/shard_map/ppermute | solution.py:20
  108.3 13.1 %collective-permute-start.68 = (bf16[1,4,64,512]{3,2,1,0:T(8,128)(2,1)S(1)}, bf16[1,4,64,512]{3,2,1,0:T(8,128)(2,1)S(1)}, u32[]{:S(2)}, u32[]{:S(2)}) collective-permute-start(bf16[1,4,64,512]{3,2,1,0:T(8,128)(2,1)S(1)} %get-tuple-element.167), channel_id=1, source_target_pairs={{0,4},{4,0},{8,12},{12,8},{16,20},{20,16},{24,28},{28,24},{1,5},{5... | collective-permute-start | bytes 786440 | tf_op jit(solution)/shard_map/ppermute | solution.py:20
  109.1 18.4 %collective-permute-start.38 = (bf16[1,4,272,128]{3,2,1,0:T(8,128)(2,1)S(1)}, bf16[1,4,272,128]{3,2,1,0:T(8,128)(2,1)S(1)}, u32[]{:S(2)}, u32[]{:S(2)}) collective-permute-start(bf16[1,4,272,128]{3,2,1,0:T(8,128)(2,1)S(1)} %get-tuple-element.139), channel_id=1, source_target_pairs={{0,4},{4,0},{8,12},{12,8},{16,20},{20,16},{24,28},{28,24},{1,5},{5... | collective-permute-start | bytes 835592 | tf_op jit(solution)/shard_map/ppermute | solution.py:20
  115.9 17.2 %collective-permute-start.51 = (bf16[1,4,64,512]{3,2,1,0:T(8,128)(2,1)S(1)}, bf16[1,4,64,512]{3,2,1,0:T(8,128)(2,1)S(1)}, u32[]{:S(2)}, u32[]{:S(2)}) collective-permute-start(bf16[1,4,64,512]{3,2,1,0:T(8,128)(2,1)S(1)} %get-tuple-element.151), channel_id=1, source_target_pairs={{0,4},{4,0},{8,12},{12,8},{16,20},{20,16},{24,28},{28,24},{1,5},{5... | collective-permute-start | bytes 786440 | tf_op jit(solution)/shard_map/ppermute | solution.py:20
  117.4 17.1 %collective-permute-start.54 = (bf16[4,64,512]{2,1,0:T(8,128)(2,1)S(1)}, bf16[4,64,512]{2,1,0:T(8,128)(2,1)S(1)}, u32[]{:S(2)}, u32[]{:S(2)}) collective-permute-start(bf16[4,64,512]{2,1,0:T(8,128)(2,1)S(1)} %add_x.4), channel_id=1, source_target_pairs={{0,2},{1,3},{2,0},{3,1},{4,6},{5,7},{6,4},{7,5},{8,10},{9,11},{10,... | collective-permute-start | bytes 786440 | tf_op jit(solution)/shard_map/ppermute | solution.py:20
  121.5 21.8 %collective-permute-start.66 = (bf16[1,4,64,512]{3,2,1,0:T(8,128)(2,1)S(1)}, bf16[1,4,64,512]{3,2,1,0:T(8,128)(2,1)S(1)}, u32[]{:S(2)}, u32[]{:S(2)}) collective-permute-start(bf16[1,4,64,512]{3,2,1,0:T(8,128)(2,1)S(1)} %get-tuple-element.163), channel_id=1, source_target_pairs={{0,4},{4,0},{8,12},{12,8},{16,20},{20,16},{24,28},{28,24},{1,5},{5... | collective-permute-start | bytes 786440 | tf_op jit(solution)/shard_map/ppermute | solution.py:20
  123.1 22.8 %collective-permute-start.69 = (bf16[4,64,512]{2,1,0:T(8,128)(2,1)S(1)}, bf16[4,64,512]{2,1,0:T(8,128)(2,1)S(1)}, u32[]{:S(2)}, u32[]{:S(2)}) collective-permute-start(bf16[4,64,512]{2,1,0:T(8,128)(2,1)S(1)} %add_x.5), channel_id=1, source_target_pairs={{0,2},{1,3},{2,0},{3,1},{4,6},{5,7},{6,4},{7,5},{8,10},{9,11},{10,... | collective-permute-start | bytes 786440 | tf_op jit(solution)/shard_map/ppermute | solution.py:20
  127.4 27.0 %collective-permute-start.36 = (bf16[1,4,272,128]{3,2,1,0:T(8,128)(2,1)S(1)}, bf16[1,4,272,128]{3,2,1,0:T(8,128)(2,1)S(1)}, u32[]{:S(2)}, u32[]{:S(2)}) collective-permute-start(bf16[1,4,272,128]{3,2,1,0:T(8,128)(2,1)S(1)} %get-tuple-element.135), channel_id=1, source_target_pairs={{0,4},{4,0},{8,12},{12,8},{16,20},{20,16},{24,28},{28,24},{1,5},{5... | collective-permute-start | bytes 835592 | tf_op jit(solution)/shard_map/ppermute | solution.py:20
  133.1 23.0 %collective-permute-start.39 = (bf16[4,272,128]{2,1,0:T(8,128)(2,1)S(1)}, bf16[4,272,128]{2,1,0:T(8,128)(2,1)S(1)}, u32[]{:S(2)}, u32[]{:S(2)}) collective-permute-start(bf16[4,272,128]{2,1,0:T(8,128)(2,1)S(1)} %add_x.3), channel_id=1, source_target_pairs={{0,2},{1,3},{2,0},{3,1},{4,6},{5,7},{6,4},{7,5},{8,10},{9,11},{10,... | collective-permute-start | bytes 835592 | tf_op jit(solution)/shard_map/ppermute | solution.py:20
  146.5 11.3 %collective-permute-start.70 = (bf16[64,512]{1,0:T(8,128)(2,1)S(1)}, bf16[64,512]{1,0:T(8,128)(2,1)S(1)}, u32[]{:S(2)}, u32[]{:S(2)}) collective-permute-start(bf16[64,512]{1,0:T(8,128)(2,1)S(1)} %get-tuple-element.169), channel_id=1, source_target_pairs={{0,8},{4,12},{8,0},{12,4},{16,24},{20,28},{24,16},{28,20},{1,9},{5... | collective-permute-start | bytes 196616 | tf_op jit(solution)/shard_map/ppermute | solution.py:20
  150.5 8.4 %collective-permute-start.71 = (bf16[64,512]{1,0:T(8,128)(2,1)S(1)}, bf16[64,512]{1,0:T(8,128)(2,1)S(1)}, u32[]{:S(2)}, u32[]{:S(2)}) collective-permute-start(bf16[64,512]{1,0:T(8,128)(2,1)S(1)} %get-tuple-element.170), channel_id=1, source_target_pairs={{0,16},{4,20},{8,24},{12,28},{16,0},{20,4},{24,8},{28,12},{1,17},{... | collective-permute-start | bytes 196616 | tf_op jit(solution)/shard_map/ppermute | solution.py:20
  152.3 8.2 %collective-permute-start.72 = (bf16[64,512]{1,0:T(8,128)(2,1)S(1)}, bf16[64,512]{1,0:T(8,128)(2,1)S(1)}, u32[]{:S(2)}, u32[]{:S(2)}) collective-permute-start(bf16[64,512]{1,0:T(8,128)(2,1)S(1)} %get-tuple-element.171), channel_id=1, source_target_pairs={{0,24},{4,28},{8,16},{12,20},{16,8},{20,12},{24,0},{28,4},{1,25},{... | collective-permute-start | bytes 196616 | tf_op jit(solution)/shard_map/ppermute | solution.py:20
  154.5 8.3 %collective-permute-start.61 = (bf16[64,512]{1,0:T(8,128)(2,1)S(1)}, bf16[64,512]{1,0:T(8,128)(2,1)S(1)}, u32[]{:S(2)}, u32[]{:S(2)}) collective-permute-start(bf16[64,512]{1,0:T(8,128)(2,1)S(1)} %add_z.4.refs_0_), channel_id=1, source_target_pairs={{0,4},{4,0},{8,12},{12,8},{16,20},{20,16},{24,28},{28,24},{1,5},{5... | collective-permute-start | bytes 196616 | tf_op jit(solution)/shard_map/ppermute | solution.py:20
  156.0 9.0 %collective-permute-start.60 = (bf16[64,512]{1,0:T(8,128)(2,1)S(1)}, bf16[64,512]{1,0:T(8,128)(2,1)S(1)}, u32[]{:S(2)}, u32[]{:S(2)}) collective-permute-start(bf16[64,512]{1,0:T(8,128)(2,1)S(1)} %add_z.4.refs_0_), channel_id=1, source_target_pairs={{0,24},{4,28},{8,16},{12,20},{16,8},{20,12},{24,0},{28,4},{1,25},{... | collective-permute-start | bytes 196616 | tf_op jit(solution)/shard_map/ppermute | solution.py:20
  157.8 9.0 %collective-permute-start.59 = (bf16[64,512]{1,0:T(8,128)(2,1)S(1)}, bf16[64,512]{1,0:T(8,128)(2,1)S(1)}, u32[]{:S(2)}, u32[]{:S(2)}) collective-permute-start(bf16[64,512]{1,0:T(8,128)(2,1)S(1)} %add_z.4.refs_0_), channel_id=1, source_target_pairs={{0,16},{4,20},{8,24},{12,28},{16,0},{20,4},{24,8},{28,12},{1,17},{... | collective-permute-start | bytes 196616 | tf_op jit(solution)/shard_map/ppermute | solution.py:20
  158.9 10.4 %collective-permute-start.58 = (bf16[64,512]{1,0:T(8,128)(2,1)S(1)}, bf16[64,512]{1,0:T(8,128)(2,1)S(1)}, u32[]{:S(2)}, u32[]{:S(2)}) collective-permute-start(bf16[64,512]{1,0:T(8,128)(2,1)S(1)} %add_z.4.refs_0_), channel_id=1, source_target_pairs={{0,8},{4,12},{8,0},{12,4},{16,24},{20,28},{24,16},{28,20},{1,9},{5... | collective-permute-start | bytes 196616 | tf_op jit(solution)/shard_map/ppermute | solution.py:20
  160.5 14.8 %collective-permute-start.40 = (bf16[272,128]{1,0:T(8,128)(2,1)S(1)}, bf16[272,128]{1,0:T(8,128)(2,1)S(1)}, u32[]{:S(2)}, u32[]{:S(2)}) collective-permute-start(bf16[272,128]{1,0:T(8,128)(2,1)S(1)} %get-tuple-element.141), channel_id=1, source_target_pairs={{0,8},{4,12},{8,0},{12,4},{16,24},{20,28},{24,16},{28,20},{1,9},{5... | collective-permute-start | bytes 208904 | tf_op jit(solution)/shard_map/ppermute | solution.py:20
  162.7 13.4 %collective-permute-start.41 = (bf16[272,128]{1,0:T(8,128)(2,1)S(1)}, bf16[272,128]{1,0:T(8,128)(2,1)S(1)}, u32[]{:S(2)}, u32[]{:S(2)}) collective-permute-start(bf16[272,128]{1,0:T(8,128)(2,1)S(1)} %get-tuple-element.142), channel_id=1, source_target_pairs={{0,16},{4,20},{8,24},{12,28},{16,0},{20,4},{24,8},{28,12},{1,17},{... | collective-permute-start | bytes 208904 | tf_op jit(solution)/shard_map/ppermute | solution.py:20
  178.3 10.6 %collective-permute-start.45 = (bf16[272,128]{1,0:T(8,128)(2,1)S(1)}, bf16[272,128]{1,0:T(8,128)(2,1)S(1)}, u32[]{:S(2)}, u32[]{:S(2)}) collective-permute-start(bf16[272,128]{1,0:T(8,128)(2,1)S(1)} %add_z.3.refs_0_), channel_id=1, source_target_pairs={{0,24},{4,28},{8,16},{12,20},{16,8},{20,12},{24,0},{28,4},{1,25},{... | collective-permute-start | bytes 208904 | tf_op jit(solution)/shard_map/ppermute | solution.py:20
  180.2 9.5 %collective-permute-start.44 = (bf16[272,128]{1,0:T(8,128)(2,1)S(1)}, bf16[272,128]{1,0:T(8,128)(2,1)S(1)}, u32[]{:S(2)}, u32[]{:S(2)}) collective-permute-start(bf16[272,128]{1,0:T(8,128)(2,1)S(1)} %add_z.3.refs_0_), channel_id=1, source_target_pairs={{0,16},{4,20},{8,24},{12,28},{16,0},{20,4},{24,8},{28,12},{1,17},{... | collective-permute-start | bytes 208904 | tf_op jit(solution)/shard_map/ppermute | solution.py:20
  180.2 10.6 %collective-permute-start.43 = (bf16[272,128]{1,0:T(8,128)(2,1)S(1)}, bf16[272,128]{1,0:T(8,128)(2,1)S(1)}, u32[]{:S(2)}, u32[]{:S(2)}) collective-permute-start(bf16[272,128]{1,0:T(8,128)(2,1)S(1)} %add_z.3.refs_0_), channel_id=1, source_target_pairs={{0,8},{4,12},{8,0},{12,4},{16,24},{20,28},{24,16},{28,20},{1,9},{5... | collective-permute-start | bytes 208904 | tf_op jit(solution)/shard_map/ppermute | solution.py:20
  187.7 9.7 %collective-permute-start.46 = (bf16[272,128]{1,0:T(8,128)(2,1)S(1)}, bf16[272,128]{1,0:T(8,128)(2,1)S(1)}, u32[]{:S(2)}, u32[]{:S(2)}) collective-permute-start(bf16[272,128]{1,0:T(8,128)(2,1)S(1)} %add_z.3.refs_0_), channel_id=1, source_target_pairs={{0,4},{4,0},{8,12},{12,8},{16,20},{20,16},{24,28},{28,24},{1,5},{5... | collective-permute-start | bytes 208904 | tf_op jit(solution)/shard_map/ppermute | solution.py:20
  188.8 8.5 %collective-permute-start.49 = (bf16[272,128]{1,0:T(8,128)(2,1)S(1)}, bf16[272,128]{1,0:T(8,128)(2,1)S(1)}, u32[]{:S(2)}, u32[]{:S(2)}) collective-permute-start(bf16[272,128]{1,0:T(8,128)(2,1)S(1)} %collective-permute-done.45.refs_3_), channel_id=1, source_target_pairs={{0,4},{4,0},{8,12},{12,8},{16,20},{20,16},{24,28},{28,24},{1,5},{5... | collective-permute-start | bytes 208904 | tf_op jit(solution)/shard_map/ppermute | solution.py:20
  (61 other events, 450.9 us)

commit v3 on v2

v3 whole, which is shorter than its diff:
```python
import jax
import jax.numpy as jnp
from jax import lax
from jax.experimental import pallas as pl
from jax.experimental.pallas import tpu as pltpu
from jax.sharding import PartitionSpec as P

HD = 64
PAIR = 2 * HD
LANES = 128
F32 = jnp.float32
BF16 = jnp.bfloat16
VMEM_LIMIT = 28 * 2**20
GELU_C = 0.7978845608028654
GELU_A = 0.044715
VEC = 8


def swap(v, axis, bit, size):
    return lax.ppermute(v, axis, [(i, i ^ bit) for i in range(size)])


def bits_of(size):
    return [1 << b for b in range(size.bit_length() - 1)]


def shape(dims, kind):
    return jax.ShapeDtypeStruct(tuple(dims), kind)


def together(*lists):
    out = lax.optimization_barrier(tuple(tuple(v) for v in lists))
    return [list(v) for v in out]


def run(name, fn, ins, outs, scratch=(), smem=(), after=(), hbm=()):
    n_in, n_out, n_all = len(ins), len(outs), len(ins) + len(after)

    def kernel(*refs):
        fn(refs[:n_in], refs[n_all : n_all + n_out], refs[n_all + n_out :])

    return pl.pallas_call(
        kernel,
        out_shape=tuple(outs),
        in_specs=[
            pl.BlockSpec(
                memory_space=pltpu.SMEM if i in smem else pl.ANY if i in hbm else pltpu.VMEM
            )
            for i in range(n_in)
        ]
        + [pl.BlockSpec(memory_space=pl.ANY) for _ in after],
        out_specs=tuple(pl.BlockSpec(memory_space=pltpu.VMEM) for _ in outs),
        scratch_shapes=list(scratch),
        compiler_params=pltpu.CompilerParams(vmem_limit_bytes=VMEM_LIMIT),
        cost_estimate=pl.CostEstimate(flops=1, bytes_accessed=1, transcendentals=0),
        name=name,
    )(*ins, *after)


def dot(a, b):
    return jnp.dot(a, b, preferred_element_type=F32)


def dot_nt(a, b):
    return lax.dot_general(a, b, (((1,), (1,)), ((), ())), preferred_element_type=F32)


def dot_tn(a, b):
    return lax.dot_general(a, b, (((0,), (0,)), ((), ())), preferred_element_type=F32)


def normalize(v):
    centre = v - jnp.mean(v, -1, keepdims=True)
    rstd = lax.rsqrt(jnp.mean(centre * centre, -1, keepdims=True) + 1e-05)
    return centre * rstd, rstd


def norm_back(g, normed, rstd, gain):
    e = g * gain
    return rstd * (
        e - jnp.mean(e, -1, keepdims=True) - normed * jnp.mean(e * normed, -1, keepdims=True)
    )


def rows_of(start, size):
    return pl.ds(pl.multiple_of(start * size, size), size)


def whole(pieces, x_bit):
    if len(pieces) == 1:
        return pieces[0][...]
    a, b = pieces[0][...], pieces[1][...]
    first = x_bit == 0
    return jnp.concatenate([jnp.where(first, a, b), jnp.where(first, b, a)], 0)


def take(refs, counts):
    out, at = [], 0
    for c in counts:
        out.append(refs[at : at + c])
        at += c
    assert at == len(refs)
    return out


def three_parts(v):
    high = v.astype(BF16).astype(F32)
    rest = v - high
    middle = rest.astype(BF16).astype(F32)
    return jnp.concatenate([high, middle, rest - middle, jnp.zeros_like(v)], 0).astype(BF16)


def two_parts(v):
    high = v.astype(BF16).astype(F32)
    return jnp.concatenate([high, v - high], 0).astype(BF16)


def make_body(n_dp, n_mp):
    groups = [[0, 1], list(range(2, n_mp))]
    y_peers = list(range(2, n_mp, 2))
    def body(
        tokens,
        lengths,
        order_mask,
        norm_scale_pair,
        norm_offset_pair,
        w_qkv,
        qv_bias,
        order_bias,
        w_out,
        out_bias,
        w_up,
        up_bias,
        w_down,
        cotangent,
    ):
        rows, share, width = tokens.shape
        slots = order_mask.shape[1]
        own = rows // n_mp
        count = own * slots
        lane = qv_bias.shape[1]
        per = order_bias.shape[0]
        hid = up_bias.shape[0]
        hid_rows = hid // lane
        cols = width // lane
        piece = shape((own, share, width), BF16)
        sub = width // n_dp
        factor = HD**-0.5
        o_at, s_at = 3 * width, 4 * width
        bundle_rows = 4 * width + 4 * VEC

        def mp_swap(v, bit):
            return swap(v, "mp", bit, n_mp)

        def dp_swap(v, bit):
            return swap(v, "dp", bit, n_dp)

        def spread(parts):
            return [mp_swap(v, k + 1) for k, v in enumerate(parts)]

        def over_y(v):
            return [mp_swap(v, k) for k in y_peers]

        def spread_y(parts):
            return [mp_swap(v, k) for k, v in zip(y_peers, parts)]

        def cut_rows(ins, outs, scratch):
            me = lax.axis_index("mp")
            copies = [
                pltpu.make_async_copy(
                    v.at[pl.ds((me ^ k) * own, own)],
                    outs[i * n_mp + k],
                    scratch[0].at[i, k],
                )
                for i, v in enumerate(ins)
                for k in range(n_mp)
            ]
            for c in copies:
                c.start()
            for c in copies:
                c.wait()

        rows_cut = run(
            "cut_rows",
            cut_rows,
            [tokens, cotangent],
            [piece] * (2 * n_mp),
            [pltpu.SemaphoreType.DMA((2, n_mp))],
            hbm=(0, 1),
        )
        token_parts, cot_parts = list(rows_cut[:n_mp]), list(rows_cut[n_mp:])

        def pack(ins, outs, scratch):
            x_bit = lax.axis_index("dp") & 1
            bundle, half = outs
            copy = pltpu.make_async_copy(ins[0], bundle.at[pl.ds(0, o_at)], scratch[0])
            copy.start()
            for c in range(cols):
                bundle[o_at + c * lane : o_at + (c + 1) * lane] = ins[1][
                    :, c * lane : (c + 1) * lane
                ]
            small = jnp.concatenate(
                [
                    ins[2][...],
                    ins[3][...],
                    jnp.concatenate([ins[4][...], jnp.zeros((1, lane - per), F32)], 1),
                    jnp.zeros((VEC - 3 - hid_rows, lane), F32),
                ],
                0,
            )
            bundle[s_at:] = three_parts(small)
            copy.wait()
            half[...] = bundle[rows_of(x_bit, bundle_rows // 2)]

        bundle, bundle_half = run(
            "pack",
            pack,
            [
                w_qkv.reshape(-1, lane),
                w_out,
                qv_bias,
                up_bias.reshape(hid_rows, lane),
                order_bias.reshape(1, per),
            ],
            [shape((bundle_rows, lane), BF16), shape((bundle_rows // 2, lane), BF16)],
            [pltpu.SemaphoreType.DMA(())],
            hbm=(0,),
            after=[token_parts[0]],
        )
        def cut_halves(ins, outs, scratch):
            dpi = lax.axis_index("dp")
            copies = [
                pltpu.make_async_copy(
                    src.at[rows_of(bit, src.shape[0] // 2)],
                    outs[0].at[n] if joined else outs[n],
                    scratch[0].at[n],
                )
                for n, (src, bit) in enumerate(zip(ins, (dpi & 1, (dpi >> 1) & 1)))
            ]
            for c in copies:
                c.start()
            for c in copies:
                c.wait()

        joined = w_up.shape == w_down.shape
        half_shapes = [shape((v.shape[0] // 2, v.shape[1]), BF16) for v in (w_up, w_down)]
        half_parts = run(
            "cut_halves",
            cut_halves,
            [w_up, w_down],
            [shape((2,) + half_shapes[0].shape, BF16)] if joined else half_shapes,
            [pltpu.SemaphoreType.DMA((2,))],
            hbm=(0, 1),
            after=[bundle_half],
        )

        sends, (bundle, bundle_half) = together(token_parts[1:], [bundle, bundle_half])
        token_parts = token_parts[:1] + spread(sends)
        bundle_core, bundle_y = mp_swap(bundle, 1), over_y(bundle_half)

        bundle_y, halves, token_parts, near = together(
            bundle_y, half_parts, token_parts, [w_up, w_down]
        )
        bundle_x = [dp_swap(v, 1) for v in bundle_y]
        bundle_yc = [mp_swap(v, 1) for v in bundle_y]
        halves_y = [over_y(v) for v in halves]
        near_core = [mp_swap(v, 1) for v in near]

        def far(first, second, first_core, second_core):
            return [
                v
                for n in range(len(y_peers))
                for v in (first[n], second[n], first_core[n], second_core[n])
            ]

        def order_row(om_ref, me, r):
            v = om_ref[pl.ds(me * own + r, 1), :].astype(F32)
            v = jnp.broadcast_to(v, (8, slots))
            at = lax.broadcasted_iota(jnp.int32, (8, slots), 1)
            step = share
            while step < slots:
                turned = jnp.where(
                    (at & step) == 0, pltpu.roll(v, slots - step, 1), pltpu.roll(v, step, 1)
                )
                v = jnp.where((me * share) & step, turned, v)
                step *= 2
            return v[:1]

        def keep_row(me, length):
            at = lax.broadcasted_iota(jnp.int32, (1, slots), 1)
            return (at ^ (me * share)) < length

        def keep_column(me, length):
            at = lax.broadcasted_iota(jnp.int32, (slots, 1), 0)
            return ((at ^ (me * share)) < length).astype(F32)

        def head_mask(pair_value, h):
            at = lax.broadcasted_iota(jnp.int32, pair_value.shape, 1)
            return jnp.where((at >= HD) == (h % 2 == 1), pair_value, jnp.zeros_like(pair_value))

        def assemble(dst, parts):
            for r in range(own):
                for k in range(n_mp):
                    dst[r * slots + k * share : r * slots + (k + 1) * share] = parts[k][r]

        def cut_slots(dst, lead, value):
            for r in range(own):
                for k in range(n_mp):
                    at = r * slots + k * share
                    dst[k][lead + r] = value[at : at + share]

        def attend(group, first, pieces):
            wide = lane * len(group)
            heads = wide // HD
            counts = [len(pieces) // len(group)] * len(group)

            def fn(ins, outs, scratch):
                me, x_bit = lax.axis_index("mp"), lax.axis_index("dp") & 1
                qkv_ref, p_ref, att_ref, weights, wo, smalls = outs[-6:]
                if first:
                    lens, om, gains, shifts = ins[n_mp : n_mp + 4]
                    x_ref, a1_ref = outs[:2]
                    assemble(x_ref, ins[:n_mp])
                    normed, _ = normalize(x_ref[...].astype(F32))
                    a1_ref[...] = (normed * gains[0:1] + shifts[0:1]).astype(BF16)
                else:
                    lens, om, a1_ref = ins[:3]
                for j, ps in enumerate(take(ins[-len(pieces) :], counts)):
                    v = whole(ps, x_bit)
                    weights[:, j * lane : (j + 1) * lane] = v[:o_at]
                    for c in range(cols):
                        wo[j * lane : (j + 1) * lane, c * lane : (c + 1) * lane] = v[
                            o_at + c * lane : o_at + (c + 1) * lane
                        ]
                    parts = v[s_at:].astype(F32)
                    smalls[j] = parts[:VEC] + parts[VEC : 2 * VEC] + parts[2 * VEC : 3 * VEC]
                a1 = a1_ref[...]
                for t in range(3):
                    y = dot(a1, weights[t * width : (t + 1) * width])
                    if t != 1:
                        i = t // 2
                        y = y + jnp.concatenate(
                            [smalls[j, i : i + 1] for j in range(len(group))], 1
                        )
                    qkv_ref[t] = y.astype(BF16)
                for r in range(own):
                    length = lens[me * own + r]
                    order = order_row(om, me, r)
                    kept = keep_row(me, length)
                    column = keep_column(me, length)
                    here = slice(r * slots, (r + 1) * slots)
                    for pair in range(heads // 2):
                        at = slice(pair * PAIR, (pair + 1) * PAIR)
                        q = qkv_ref[0, here, at] * jnp.asarray(factor, BF16)
                        key = qkv_ref[1, here, at]
                        val = qkv_ref[2, here, at]
                        acc = None
                        for h in (2 * pair, 2 * pair + 1):
                            o = 2 + hid_rows
                            ob = smalls[h // per, o : o + 1, h % per : h % per + 1]
                            row = jnp.where(kept, ob * order, -1e30)
                            s = dot_nt(head_mask(q, h), key) + row
                            e = jnp.exp(s - jnp.max(s, -1, keepdims=True))
                            p = (e * (1.0 / jnp.sum(e, -1, keepdims=True))).astype(BF16)
                            p_ref[r * heads + h] = p
                            term = dot(p, head_mask(val, h))
                            acc = term if acc is None else acc + term
                        att_ref[here, at] = (acc * column).astype(BF16)

            ins = (
                token_parts + [lengths, order_mask, norm_scale_pair, norm_offset_pair]
                if first
                else [lengths, order_mask, a1]
            )
            lead = [shape((count, width), BF16)] * 2 if first else []
            return run(
                "attend",
                fn,
                ins + pieces,
                lead
                + [
                    shape((3, count, wide), BF16),
                    shape((own * heads, slots, slots), BF16),
                    shape((count, wide), BF16),
                    shape((3 * width, wide), BF16),
                    shape((wide, width), BF16),
                    shape((len(group), VEC, lane), F32),
                ],
                smem=(n_mp if first else 0,),
            )

        x, a1, qkv0, p0, att0, wq0, wo0, small0 = attend(groups[0], True, [bundle, bundle_core])

        bundle_x, (att0,) = together(bundle_x, [att0])
        bundle_xc = [mp_swap(v, 1) for v in bundle_x]
        qkv1, p1, att1, wq1, wo1, small1 = attend(
            groups[1], False, far(bundle_y, bundle_x, bundle_yc, bundle_xc)
        )

        def take_apart(ins, outs, _):
            for n, o in enumerate(outs):
                o[...] = ins[0][n]

        if joined:
            pairs = [run("take_apart", take_apart, [v], half_shapes, after=[att1]) for v in halves_y[0]]
            halves_y = list(zip(*pairs))
        up_y, down_y, (att1,), sends = together(*halves_y, [att1], cot_parts[1:])
        up_x, down_z = [dp_swap(v, 1) for v in up_y], [dp_swap(v, 2) for v in down_y]
        up_yc, down_yc = ([mp_swap(v, 1) for v in vs] for vs in (up_y, down_y))
        cot_parts = cot_parts[:1] + spread(sends)

        up_x, down_z, cot_parts = together(up_x, down_z, cot_parts)
        up_xc, down_zc = ([mp_swap(v, 1) for v in vs] for vs in (up_x, down_z))

        def scatter(dst, src, block, which, dpi):
            for p in range(n_dp):
                dst[block, which, p] = src[rows_of(dpi ^ p, sub), :]

        def mlp_block(
            j, a2, a2t, dy, dyt, wu, wd, bias, mixed, d_mid, gs, dst, block, bias_sums, dpi
        ):
            up = jnp.concatenate([bias[2 + i : 3 + i] for i in range(hid_rows)], 1)
            pre = dot(a2[...], wu) + up
            square = pre * pre
            t = jnp.tanh(pre * (GELU_C + (GELU_C * GELU_A) * square))
            half = 0.5 + 0.5 * t
            hidden = (pre * half).astype(BF16)
            slope = half + (pre * (1.0 - t * t)) * (
                0.5 * GELU_C + (1.5 * GELU_C * GELU_A) * square
            )
            d_hidden = dot_nt(dy[...], wd)
            d_pre = (slope * d_hidden).astype(BF16)
            mixed[...] += dot(hidden, wd)
            d_mid[...] += dot_nt(d_pre, wu)
            g_down, g_up = gs.at[2 * j], gs.at[2 * j + 1]
            g_down[...] = dot(dyt[...], hidden).astype(BF16)
            scatter(dst, g_down, block, 0, dpi)
            g_up[...] = dot(a2t[...], d_pre).astype(BF16)
            scatter(dst, g_up, block, 1, dpi)
            bias_sums[j] = jnp.sum(d_pre.astype(F32), 0, keepdims=True)

        def mlp_outs(n_blocks, n_arrays):
            both = shape((n_blocks // n_arrays, 2, n_dp, sub, hid), BF16)
            return [both] * n_arrays + [shape((n_blocks, 1, hid), F32)]

        full = shape((count, width), F32)
        full_bf = shape((count, width), BF16)
        turned = shape((width, count), BF16)
        g0, g1 = groups

        def mlp_first(ins, outs, scratch):
            dpi = lax.axis_index("dp")
            lead, dy_p, wu_p, wd_p = take(ins, [9, n_mp, len(g0), len(g0)])
            x_ref, att0_ref, att1_ref, wo0_ref, wo1_ref, smalls, gains, shifts, ob = lead
            x1, a2, a2t, dy, dyt, mixed, d_mid = outs[:7]
            v = x_ref[...].astype(F32) + (
                dot(att0_ref[...], wo0_ref[...]) + dot(att1_ref[...], wo1_ref[...]) + ob[0:1]
            )
            x1[...] = v
            normed, _ = normalize(v)
            act = (normed * gains[1:2] + shifts[1:2]).astype(BF16)
            a2[...] = act
            a2t[...] = act.T
            assemble(dy, dy_p)
            dyt[...] = dy[...].T
            mixed[...] = jnp.zeros_like(mixed)
            d_mid[...] = jnp.zeros_like(d_mid)
            for j, k in enumerate(g0):
                mlp_block(
                    j,
                    a2,
                    a2t,
                    dy,
                    dyt,
                    wu_p[j][...],
                    wd_p[j][...],
                    smalls[j],
                    mixed,
                    d_mid,
                    scratch[0],
                    outs[7 + k % 2],
                    0,
                    outs[9],
                    dpi,
                )

        x1, a2, a2t, dy, dyt, mixed, d_mid, keep0, send0, gub0 = run(
            "mlp_first",
            mlp_first,
            [x, att0, att1, wo0, wo1, small0, norm_scale_pair, norm_offset_pair, out_bias]
            + cot_parts
            + [near[0], near_core[0], near[1], near_core[1]],
            [full, full_bf, turned, full_bf, turned, full, full] + mlp_outs(len(g0), 2),
            [pltpu.VMEM((2 * len(g0), width, hid), BF16)],
        )

        got0 = mp_swap(send0, 1)

        up1 = far(up_y, up_x, up_yc, up_xc)
        down1 = far(down_y, down_z, down_yc, down_zc)

        def mlp_far(j, last):
            ks = g1[j::2]
            n_w = 2 * len(ks)

            def fn(ins, outs, scratch):
                dpi = lax.axis_index("dp")
                lead, wu_p, wd_p = take(ins, [10, n_w, n_w])
                x1, a2, a2t, dy, dyt, mixed_in, d_mid_in, smalls, gains, ob = lead
                mixed, d_mid, gs = scratch if last else (*outs[:2], scratch[0])
                mixed[...] = mixed_in[...]
                d_mid[...] = d_mid_in[...]
                grads, bias_sums = outs[-2:]
                for n, k in enumerate(ks):
                    mlp_block(
                        n,
                        a2,
                        a2t,
                        dy,
                        dyt,
                        whole(wu_p[2 * n : 2 * n + 2], dpi & 1),
                        whole(wd_p[2 * n : 2 * n + 2], (dpi >> 1) & 1),
                        smalls[2 * n + j],
                        mixed,
                        d_mid,
                        gs,
                        grads,
                        n,
                        bias_sums,
                        dpi,
                    )
                if not last:
                    return
                output, dx1, d_att, vec = outs[:4]
                v = x1[...]
                output[...] = (v + (mixed[...] + ob[1:2])).astype(BF16)
                normed, rstd = normalize(v)
                g = d_mid[...]
                dyf = dy[...].astype(F32)
                d = dyf + norm_back(g, normed, rstd, gains[1:2])
                dx1[...] = d
                low = d.astype(BF16)
                d_att[...] = low
                vec[0:1] = jnp.sum(g * normed, 0, keepdims=True)
                vec[1:2] = jnp.sum(g, 0, keepdims=True)
                vec[2:3] = jnp.sum(low.astype(F32), 0, keepdims=True)
                vec[3:4] = jnp.sum(dyf, 0, keepdims=True)

            sums = [pltpu.VMEM((count, width), F32)] * 2
            return run(
                "mlp_far",
                fn,
                [x1, a2, a2t, dy, dyt, mixed, d_mid, small1, norm_scale_pair, out_bias]
                + [v for n in range(len(ks)) for v in up1[4 * n + 2 * j : 4 * n + 2 * j + 2]]
                + [v for n in range(len(ks)) for v in down1[4 * n + 2 * j : 4 * n + 2 * j + 2]],
                ([full_bf, full, full_bf, shape((4, width), F32)] if last else [full, full])
                + mlp_outs(len(ks), 1),
                (sums if last else []) + [pltpu.VMEM((2 * len(ks), width, hid), BF16)],
            )

        mixed, d_mid, send1, gub1_odd = mlp_far(1, False)
        send1, mixed = together([send1, mixed])[0]
        got1 = mp_swap(send1, 1)
        out_rows, dx1, d_att, vec, keep1, gub1_even = mlp_far(0, True)

        def add_all(values, vectors=False):
            total = values[0].astype(F32)
            for v in values[1:]:
                total = total + v.astype(F32)
            if not vectors:
                return total.astype(BF16)
            m = total.shape[-2]
            head = total[: m - 2 * VEC]
            v = total[m - 2 * VEC : m - VEC] + total[m - VEC :]
            high = v.astype(BF16).astype(F32)
            return jnp.concatenate([head, high, v - high], 0).astype(BF16)

        n_y = len(y_peers)

        def split(places, bit):
            return [i for i, p in enumerate(places) if not p & bit], [
                i for i, p in enumerate(places) if p & bit
            ]

        def add_split(parts, places, bit, vectors=False):
            picks = split(places, bit)

            def fn(ins, outs, _):
                for dst, pick in zip(outs, picks):
                    for at, i in enumerate(pick):
                        dst[at] = add_all([v[i] for v in ins], vectors)

            half = shape((len(picks[0]),) + parts[0].shape[1:], BF16)
            kept, sent = run("add_split", fn, parts, [half, half])
            return kept, sent, [places[i] for i in picks[0]]

        def add_whole(parts, vectors=False):
            def fn(ins, outs, _):
                for i in range(outs[0].shape[0]):
                    outs[0][i] = add_all([v[i] for v in ins], vectors)

            return run("add_whole", fn, parts, [shape(parts[0].shape, BF16)])[0]

        every = list(range(n_dp))
        no_x, with_x = split(every, 1)
        last_bits = [b for b in bits_of(n_dp) if b > 2]

        def add_core_mlp(ins, outs, _):
            keep0, got0, keep1, got1 = ins
            kept, sent, mine = outs[:3]
            for n in range(1 + n_y):
                a, b, i = (keep0, got0, 0) if n == 0 else (keep1, got1, n - 1)
                for dst, pick in ((kept, no_x), (sent, with_x)):
                    for at, p in enumerate(pick):
                        dst[n, at] = add_all([a[i, 0, p], b[i, 0, p]])
                up = mine if n == 0 else outs[3 + n - 1]
                for p in every:
                    up[p] = add_all([a[i, 1, p], b[i, 1, p]])

        kept_d, sent_d, mine_u, *others_u = run(
            "add_core_mlp",
            add_core_mlp,
            [keep0, got0, keep1, got1],
            [shape((1 + n_y, n_dp // 2, sub, hid), BF16)] * 2
            + [shape((n_dp, sub, hid), BF16)] * (1 + n_y),
        )
        (sent_d, d_att), others_u = together([sent_d, d_att], others_u)
        got_d = dp_swap(sent_d, 1)
        got_u = spread_y(others_u)

        vec_rows = n_dp * VEC
        chunk = 4 * sub + 2 * VEC

        def attend_back(ins, outs, scratch):
            me, dpi = lax.axis_index("mp"), lax.axis_index("dp")
            (lens, om, gains), fulls, qkvs, ps, atts, wqs, wos, vecs = take(
                ins, [3, 5, 2, 2, 2, 2, 2, 4]
            )
            x_ref, a1_ref, dx1, d_att, out_ref = fulls
            vec, gub_near, gub_even, gub_odd = vecs
            parts = outs[:n_mp]
            grads = outs[n_mp:]
            dqkvs, gqs = scratch[:2], scratch[2:4]
            d_in, vec_f, shared = scratch[4:]
            a1t = a1_ref[...].T
            d_att_v = d_att[...]
            d_att_t = d_att_v.T
            d_in[...] = jnp.zeros_like(d_in)
            cut_slots(parts, 0, out_ref[...])
            order_sums = {}
            for gi, group in enumerate(groups):
                wide = lane * len(group)
                heads = wide // HD
                qkv_ref, p_ref, att_ref = qkvs[gi], ps[gi], atts[gi]
                wq, wo, dqkv, gq = wqs[gi], wos[gi], dqkvs[gi], gqs[gi]
                d_o = dot_nt(d_att_v, wo[...]).astype(BF16)
                for r in range(own):
                    length = lens[me * own + r]
                    order = order_row(om, me, r)
                    kept = keep_row(me, length)
                    column = keep_column(me, length).astype(BF16)
                    here = slice(r * slots, (r + 1) * slots)
                    for pair in range(heads // 2):
                        at = slice(pair * PAIR, (pair + 1) * PAIR)
                        q = qkv_ref[0, here, at] * jnp.asarray(factor, BF16)
                        key = qkv_ref[1, here, at] * jnp.asarray(factor, BF16)
                        val = qkv_ref[2, here, at]
                        do = d_o[here, at] * column
                        dq = dk = dv = 0.0
                        for h in (2 * pair, 2 * pair + 1):
                            p_low = p_ref[r * heads + h]
                            p = p_low.astype(F32)
                            do_h = head_mask(do, h)
                            d_p = dot_nt(do_h, val)
                            inner = jnp.sum(p * d_p, -1, keepdims=True)
                            d_s = jnp.where(kept, p * (d_p - inner), 0.0).astype(BF16)
                            sums = dot(jnp.ones((8, slots), BF16), d_s)[:1] * order
                            name = (group[h // per], h % per)
                            old = order_sums.get(name)
                            order_sums[name] = sums if old is None else old + sums
                            dq = dq + dot(d_s, head_mask(key, h))
                            dk = dk + dot_tn(d_s, head_mask(q, h))
                            dv = dv + dot_tn(p_low, do_h)
                        dqkv[0, here, at] = dq.astype(BF16)
                        dqkv[1, here, at] = dk.astype(BF16)
                        dqkv[2, here, at] = dv.astype(BF16)
                total = None
                for t in range(3):
                    g = dqkv[t]
                    gq[t] = dot(a1t, g).astype(BF16)
                    term = dot_nt(g, wq[t * width : (t + 1) * width])
                    total = term if total is None else total + term
                d_in[...] += total
                gq[3] = dot(d_att_t, att_ref[...]).astype(BF16)
                for j, k in enumerate(group):
                    dst = grads[2 * gi + k % 2]
                    at = slice(j * lane, (j + 1) * lane)
                    for p in range(n_dp):
                        here = rows_of(dpi ^ p, sub)
                        for t in range(4):
                            dst[j // 2, p, t * sub : (t + 1) * sub] = gq[t, here, at]
                    vec_f[k] = jnp.zeros((vec_rows, lane), F32)
                    base = 6 * cols
                    for n, t in enumerate((0, 2)):
                        vec_f[k, base + n : base + n + 1] = jnp.sum(
                            dqkv[t, :, at].astype(F32), 0, keepdims=True
                        )
                    gub = gub_near[j] if gi == 0 else (gub_even, gub_odd)[j % 2][j // 2]
                    for i in range(hid_rows):
                        vec_f[k, base + 2 + i : base + 3 + i] = gub[:, i * lane : (i + 1) * lane]
                    lanes = lax.broadcasted_iota(jnp.int32, (1, lane), 1)
                    row = jnp.zeros((1, lane), F32)
                    for i in range(per):
                        row = row + jnp.where(
                            lanes == i, jnp.sum(order_sums[(k, i)], -1, keepdims=True), 0.0
                        )
                    vec_f[k, base + 2 + hid_rows : base + 3 + hid_rows] = row
            normed, rstd = normalize(x_ref[...].astype(F32))
            g = d_in[...]
            cut_slots(
                parts, own, (dx1[...] + norm_back(g, normed, rstd, gains[0:1])).astype(BF16)
            )
            shared[0:1] = jnp.sum(g * normed, 0, keepdims=True)
            shared[1:2] = vec[0:1]
            shared[2:3] = jnp.sum(g, 0, keepdims=True)
            shared[3:4] = vec[1:2]
            shared[4:5] = vec[2:3]
            shared[5:6] = vec[3:4]
            for gi, group in enumerate(groups):
                for j, k in enumerate(group):
                    for i in range(6):
                        for c in range(cols):
                            at = i * cols + c
                            vec_f[k, at : at + 1] = shared[i : i + 1, c * lane : (c + 1) * lane]
                    dst = grads[2 * gi + k % 2]
                    for p in range(n_dp):
                        v = vec_f[k, rows_of(dpi ^ p, VEC)]
                        dst[j // 2, p, 4 * sub :] = two_parts(v)

        def grad_shapes(n_blocks):
            return [shape((n_blocks // 2, n_dp, chunk, lane), BF16)] * 2

        back = run(
            "attend_back",
            attend_back,
            [lengths, order_mask, norm_scale_pair]
            + [x, a1, dx1, d_att, out_rows]
            + [qkv0, qkv1, p0, p1, att0, att1, wq0, wq1, wo0, wo1]
            + [vec, gub0, gub1_even, gub1_odd],
            [shape((2 * own, share, width), BF16)] * n_mp + grad_shapes(len(g0)) + grad_shapes(len(g1)),
            [
                *[pltpu.VMEM((3, count, lane * len(g)), BF16) for g in groups],
                *[pltpu.VMEM((4, width, lane * len(g)), BF16) for g in groups],
                pltpu.VMEM((count, width), F32),
                pltpu.VMEM((n_mp, vec_rows, lane), F32),
                pltpu.VMEM((8, width), F32),
            ],
            smem=(0,),
        )
        row_parts, (ka0, sa0, ka1, sa1) = back[:n_mp], back[n_mp:]

        def add_x(ins, outs, _):
            for n in range(1 + n_y):
                for i in range(n_dp // 2):
                    outs[n][i] = add_all([ins[0][n, i], ins[1][n, i]])

        mine_d, *others_d = run(
            "add_x", add_x, [kept_d, got_d], [shape((n_dp // 2, sub, hid), BF16)] * (1 + n_y)
        )
        kept_u, sent_u, at_u = add_split([mine_u] + got_u, every, 2)
        others_d, (sent_u,), sends = together(others_d, [sent_u], [sa0, sa1])
        got_d = spread_y(others_d)
        got_u = dp_swap(sent_u, 2)
        ga0, ga1 = (mp_swap(v, 1) for v in sends)

        def add_core_att(ins, outs, _):
            keep0, got0, keep1, got1 = ins
            for n in range(1 + n_y):
                a, b, i = (keep0, got0, 0) if n == 0 else (keep1, got1, n - 1)
                for p in every:
                    outs[n][p] = add_all([a[i, p], b[i, p]], True)

        mine_a, *others_a = run(
            "add_core_att",
            add_core_att,
            [ka0, ga0, ka1, ga1],
            [shape((n_dp, chunk, lane), BF16)] * (1 + n_y),
        )
        kept_d, sent_d, at_d = add_split([mine_d] + got_d, no_x, 2)
        kept_u, sent_u, at_u = add_split([kept_u, got_u], at_u, 1)
        (sent_d, sent_u), others_a = together([sent_d, sent_u], others_a)
        got_d, got_u, got_a = dp_swap(sent_d, 2), dp_swap(sent_u, 1), spread_y(others_a)

        def join_split(parts_d, parts_u, places, bit):
            picks = split(places, bit)

            def fn(ins, outs, _):
                for n, mine in enumerate(take(ins, [len(parts_d), len(parts_u)])):
                    for dst, pick in zip(outs, picks):
                        for at, i in enumerate(pick):
                            dst[at, n] = add_all([v[i] for v in mine])

            half = shape((len(picks[0]), 2, sub, hid), BF16)
            kept, sent = run("join_split", fn, parts_d + parts_u, [half, half])
            return kept, sent, [places[i] for i in picks[0]]

        both, sent, at_both = join_split([kept_d, got_d], [kept_u, got_u], at_d, last_bits[0])
        got = dp_swap(sent, last_bits[0])
        for bit in last_bits[1:]:
            both, sent, at_both = add_split([both, got], at_both, bit)
            got = dp_swap(sent, bit)
        both = add_whole([both, got])
        kept_a, sent_a, at_a = add_split([mine_a] + got_a, every, 1, True)

        (both, sent_a), sends = together([both, sent_a], row_parts[1:])
        got = dp_swap(both, last_bits[-1])
        got_a = dp_swap(sent_a, 1)
        row_parts = list(row_parts[:1]) + spread(sends)
        for bit in reversed(last_bits):
            if bit != last_bits[-1]:
                got = dp_swap(both, bit)
            if bit != last_bits[0]:
                both, at_both = jnp.concatenate([both, got]), at_both + [p ^ bit for p in at_both]
        at_both = at_both + [p ^ last_bits[0] for p in at_both]

        def part(ins, outs, _):
            half = ins[0].shape[0]
            for n, o in enumerate(outs):
                for i in range(half):
                    o[i] = ins[0][i, n]
                    o[half + i] = ins[1][i, n]

        down, up = run("part", part, [both, got], [shape((len(at_both), sub, hid), BF16)] * 2)
        kept_a, sent_a, at_a = add_split([kept_a, got_a], at_a, 2, True)
        (down, up, sent_a), row_parts[2:3] = together([down, up, sent_a], row_parts[2:3])
        got_d, got_u, got_a = dp_swap(down, 2), dp_swap(up, 1), dp_swap(sent_a, 2)
        down, at_down = jnp.concatenate([down, got_d]), at_both + [p ^ 2 for p in at_both]
        up, at_up = jnp.concatenate([up, got_u]), at_both + [p ^ 1 for p in at_both]
        kept_a, sent_a, at_a = add_split([kept_a, got_a], at_a, last_bits[0], True)
        (down, up, sent_a), row_parts[3:4] = together([down, up, sent_a], row_parts[3:4])
        got_d, got_u, got_a = dp_swap(down, 1), dp_swap(up, 2), dp_swap(sent_a, last_bits[0])
        for bit in last_bits[1:]:
            kept_a, sent_a, at_a = add_split([kept_a, got_a], at_a, bit, True)
            got_a = dp_swap(sent_a, bit)
        att = add_whole([kept_a, got_a], True)
        for bit in [*reversed(last_bits), 2]:
            if bit == 2:
                (att, got_d, got_u), row_parts = together([att, got_d, got_u], row_parts)
            att = jnp.concatenate([att, dp_swap(att, bit)])
            at_a = at_a + [p ^ bit for p in at_a]
        got_a = dp_swap(att, 1)

        def finish_mlp(ins, outs, scratch):
            dpi = lax.axis_index("dp")
            for n, p in enumerate(at_down):
                for v, at in zip(ins[:2], (p, p ^ 1)):
                    scratch[0][rows_of(dpi ^ at, sub)] = v[n].astype(F32)
            for n, p in enumerate(at_up):
                for v, at in zip(ins[2:], (p, p ^ 2)):
                    outs[1][rows_of(dpi ^ at, sub)] = v[n].astype(F32)
            outs[0][...] = scratch[0][...].T

        r_down, r_up = run(
            "finish_mlp",
            finish_mlp,
            [down, got_d, up, got_u],
            [shape((hid, width), F32), shape((width, hid), F32)],
            [pltpu.VMEM((width, hid), F32)],
        )

        def finish_att(ins, outs, scratch):
            r_qkv, r_out, gain, shift, outb, qvb, upb, order = outs
            turned_out, vec_f = scratch
            dpi = lax.axis_index("dp")
            for src, n, p in [(0, n, p) for n, p in enumerate(at_a)] + [
                (1, n, p ^ 1) for n, p in enumerate(at_a)
            ]:
                v = ins[src][n]
                at = dpi ^ p
                here = rows_of(at, sub)
                for t in range(3):
                    r_qkv[t, here] = v[t * sub : (t + 1) * sub].astype(F32)
                turned_out[here] = v[3 * sub : 4 * sub].astype(F32)
                pairs = v[4 * sub :].astype(F32)
                vec_f[rows_of(at, VEC)] = pairs[:VEC] + pairs[VEC:]
            r_out[...] = turned_out[...].T
            for i in range(6):
                dst = (gain, shift, outb)[i // 2]
                dst[i % 2 : i % 2 + 1] = jnp.concatenate(
                    [vec_f[i * cols + c : i * cols + c + 1] for c in range(cols)], 1
                )
            base = 6 * cols
            qvb[...] = vec_f[base : base + 2]
            upb[...] = jnp.concatenate(
                [vec_f[base + 2 + i : base + 3 + i] for i in range(hid_rows)], 1
            )
            order[...] = vec_f[base + 2 + hid_rows : base + 3 + hid_rows, :per]

        pair_shape = shape((2, width), F32)
        def gather_rows(ins, outs, _):
            me = lax.axis_index("mp")
            for k in range(n_mp):
                here = pl.ds((me ^ k) * own, own)
                outs[0][here] = ins[k][:own]
                outs[1][here] = ins[k][own:].astype(F32)

        output, token_gradient = run(
            "gather_rows",
            gather_rows,
            row_parts,
            [shape((rows, share, width), BF16), shape((rows, share, width), F32)],
        )
        r_qkv, r_out, gain, shift, outb, qvb, upb, order = run(
            "finish_att",
            finish_att,
            [att, got_a],
            [
                shape((3, width, lane), F32),
                shape((lane, width), F32),
                pair_shape,
                pair_shape,
                pair_shape,
                shape((2, lane), F32),
                shape((1, hid), F32),
                shape((1, per), F32),
            ],
            [pltpu.VMEM((width, lane), F32), pltpu.VMEM((vec_rows, lane), F32)],
            after=[r_up, output],
        )

        return (
            output,
            token_gradient,
            gain,
            shift,
            r_qkv,
            qvb,
            order.reshape(per),
            r_out,
            outb,
            r_up,
            upb.reshape(hid),
            r_down,
        )

    return body


def solution(mesh):
    return jax.shard_map(
        make_body(mesh.shape["dp"], mesh.shape["mp"]),
        mesh=mesh,
        in_specs=(
            P("dp", "mp", None),
            P("dp"),
            P("dp", None),
            P(),
            P(),
            P(None, None, "mp"),
            P(None, "mp"),
            P("mp"),
            P("mp", None),
            P(),
            P(None, "mp"),
            P("mp"),
            P("mp", None),
            P("dp", "mp", None),
        ),
        out_specs=(
            P("dp", "mp", None),
            P("dp", "mp", None),
            P(),
            P(),
            P(None, None, "mp"),
            P(None, "mp"),
            P("mp"),
            P("mp", None),
            P(),
            P(None, "mp"),
            P("mp"),
            P("mp", None),
        ),
        check_vma=False,
    )
```

time: 201 us -> 148 us (0.74)
  starting transfers between devices: 78.5 us -> 46 us
  local copies, waits for them, and re-layouts: 14.6 us -> 3.38 us
  Pallas kernels: 41.4 us -> 33.4 us
    ppermute x80 -> x46, starting transfers between devices: 78.5 us -> 46 us  [swap(): return lax.ppermute(v, axis, [(i, i ^ bit) for i in range(size)])]
    unnamed x58 -> x33, local copies, waits for them, and re-layouts: 12.3 us -> 3.36 us
    pallas_call x28 -> x26, Pallas kernels: 41.4 us -> 33.4 us  [run(): pl.pallas_call(kernel, out_shape=tuple(outs), in_specs=[pl.BlockSpec(memo...]
    ppermute x80 -> x46, waiting for transfers between devices: 65.1 us -> 64 us  [swap(): return lax.ppermute(v, axis, [(i, i ^ bit) for i in range(size)])]
  transfers between devices with their start and end apart: 80 -> 46, of which waited for: 23 -> 22; matrix products, arithmetic and copies ran while one was open for 0% -> 0% of each run, Pallas kernels for 16% -> 20%
where the time goes in v3:
time: 148 us
  waiting for transfers between devices  64 us (43%)
  starting transfers between devices  46 us (31%)
  Pallas kernels  33.4 us (23%)
  local copies, waits for them, and re-layouts  3.38 us (2%)
    ppermute x46, waiting for transfers between devices, swap(): return lax.ppermute(v, axis, [(i, i ^ bit) for i in range(size)])  64 us
    ppermute x46, starting transfers between devices, swap(): return lax.ppermute(v, axis, [(i, i ^ bit) for i in range(size)])  46 us
    pallas_call x26, Pallas kernels, run(): pl.pallas_call(kernel, out_shape=tuple(outs), in_specs=[pl.BlockSpec(memo...  33.4 us
    unnamed x33, local copies, waits for them, and re-layouts  3.36 us
  transfers between devices with their start and end apart: 46, of which 22 were waited for; matrix products, arithmetic and copies ran while one was open for 0% of the time, Pallas kernels for 20%

profile of v3, /device:TPU:0, one launch (start us, length us, event | category | flops | bytes accessed | tf_op | source)
XLA Modules:
  0.0 148.0 jit_solution(1496169340887902793)
XLA Ops:
  2.8 1.4 cut_rows.1
  5.1 2.6 %collective-permute-start = (bf16[1040,128]{1,0:T(8,128)(2,1)S(1)}, bf16[1040,128]{1,0:T(8,128)(2,1)S(1)}, u32[]{:S(2)}, u32[]{:S(2)}) collective-permute-start(bf16[1040,128]{1,0:T(8,128)(2,1)S(1)} %get-tuple-element.167.refs_2_), channel_id=1, source_target_pairs={{0,2},{1,3},{2,0},{3,1},{4,6},{5,7},{6,4},{7,5},{8,10},{9,11},{10,... | collective-permute-start | bytes 798728 | tf_op jit(solution)/shard_map/ppermute | solution.py:20
  8.1 1.4 collective-permute-start.3
  9.6 8.1 %collective-permute-done.2.refs_2_ = bf16[2,64,512]{2,1,0:T(8,128)(2,1)S(1)} collective-permute-done((bf16[2,64,512]{2,1,0:T(8,128)(2,1)S(1)}, bf16[2,64,512]{2,1,0:T(8,128)(2,1)S(1)}, u32[]{:S(2)}, u32[]{:S(2)}) %collective-permute-start.2) | collective-permute-done | bytes 131104 | tf_op jit(solution)/shard_map/ppermute | solution.py:20
  17.8 2.3 %collective-permute-done.3.refs_3_ = bf16[2,64,512]{2,1,0:T(8,128)(2,1)S(1)} collective-permute-done((bf16[2,64,512]{2,1,0:T(8,128)(2,1)S(1)}, bf16[2,64,512]{2,1,0:T(8,128)(2,1)S(1)}, u32[]{:S(2)}, u32[]{:S(2)}) %collective-permute-start.3) | collective-permute-done | bytes 131104 | tf_op jit(solution)/shard_map/ppermute | solution.py:20
  20.0 1.5 %collective-permute-start.5 = (bf16[1040,128]{1,0:T(8,128)(2,1)S(1)}, bf16[1040,128]{1,0:T(8,128)(2,1)S(1)}, u32[]{:S(2)}, u32[]{:S(2)}) collective-permute-start(bf16[1040,128]{1,0:T(8,128)(2,1)S(1)} %collective-permute-done.refs_3_), channel_id=1, source_target_pairs={{0,4},{4,0},{8,12},{12,8},{16,20},{20,16},{24,28},{28,24},{1,5},{5... | collective-permute-start | bytes 798728 | tf_op jit(solution)/shard_map/ppermute | solution.py:20
  21.6 1.5 %collective-permute-start.6 = (bf16[2,256,512]{2,1,0:T(8,128)(2,1)S(1)}, bf16[2,256,512]{2,1,0:T(8,128)(2,1)S(1)}, u32[]{:S(2)}, u32[]{:S(2)}) collective-permute-start(bf16[2,256,512]{2,1,0:T(8,128)(2,1)S(1)} %cut_halves.1), channel_id=1, source_target_pairs={{0,2},{1,3},{2,0},{3,1},{4,6},{5,7},{6,4},{7,5},{8,10},{9,11},{10,... | collective-permute-start | bytes 1572872 | tf_op jit(solution)/shard_map/ppermute | solution.py:20
  23.1 3.4 %attend.2 = (bf16[512,512]{1,0:T(8,128)(2,1)S(1)}, bf16[512,512]{1,0:T(8,128)(2,1)S(1)}, bf16[3,512,256]{2,1,0:T(8,128)(2,1)S(1)}, bf16[8,256,256]{2,1,0:T(8,128...) custom-call(bf16[2,64,512]{2,1,0:T(8,128)(2,1)S(1)} %get-tuple-eleme, ...), custom_call_target="tpu_custom_call" | custom-call | flops 1 | bytes 1 | tf_op jit(solution)/shard_map/attend/pallas_call | solution.py:42
  26.5 2.0 %collective-permute-done.5.refs_4_ = bf16[1040,128]{1,0:T(8,128)(2,1)S(1)} collective-permute-done((bf16[1040,128]{1,0:T(8,128)(2,1)S(1)}, bf16[1040,128]{1,0:T(8,128)(2,1)S(1)}, u32[]{:S(2)}, u32[]{:S(2)}) %collective-permute-start.5) | collective-permute-done | bytes 266272 | tf_op jit(solution)/shard_map/ppermute | solution.py:20
  30.0 3.1 %attend.3 = (bf16[3,512,256]{2,1,0:T(8,128)(2,1)S(1)}, bf16[8,256,256]{2,1,0:T(8,128)(2,1)S(1)}, bf16[512,256]{1,0:T(8,128)(2,1)S(1)}, bf16[1536,256]{1,0:T(8,12...) custom-call(s32[8]{0:T(128)S(1)} %copy-done.12, s32[8,256]{1,0:T(8,128)S(1)} %copy-done.9, ...), custom_call_target="tpu_custom_call" | custom-call | flops 1 | bytes 1 | tf_op jit(solution)/shard_map/attend/pallas_call | solution.py:42
  33.1 2.3 %collective-permute-done.6.refs_0_ = bf16[2,256,512]{2,1,0:T(8,128)(2,1)S(1)} collective-permute-done((bf16[2,256,512]{2,1,0:T(8,128)(2,1)S(1)}, bf16[2,256,512]{2,1,0:T(8,128)(2,1)S(1)}, u32[]{:S(2)}, u32[]{:S(2)}) %collective-permute-start.6) | collective-permute-done | bytes 524320 | tf_op jit(solution)/shard_map/ppermute | solution.py:20
  36.0 1.5 %collective-permute-start.12 = (bf16[2,64,512]{2,1,0:T(8,128)(2,1)S(1)}, bf16[2,64,512]{2,1,0:T(8,128)(2,1)S(1)}, u32[]{:S(2)}, u32[]{:S(2)}) collective-permute-start(bf16[2,64,512]{2,1,0:T(8,128)(2,1)S(1)} %get-tuple-element.197), channel_id=1, source_target_pairs={{0,2},{1,3},{2,0},{3,1},{4,6},{5,7},{6,4},{7,5},{8,10},{9,11},{10,... | collective-permute-start | bytes 393224 | tf_op jit(solution)/shard_map/ppermute | solution.py:20
  38.1 1.6 %collective-permute-start.10 = (bf16[256,512]{1,0:T(8,128)(2,1)S(1)}, bf16[256,512]{1,0:T(8,128)(2,1)S(1)}, u32[]{:S(2)}, u32[]{:S(2)}) collective-permute-start(bf16[256,512]{1,0:T(8,128)(2,1)S(1)} %get-tuple-element.194.refs_12_), channel_id=1, source_target_pairs={{0,8},{4,12},{8,0},{12,4},{16,24},{20,28},{24,16},{28,20},{1,9},{5... | collective-permute-start | bytes 786440 | tf_op jit(solution)/shard_map/ppermute | solution.py:20
  39.7 1.8 %collective-permute-done.12.refs_11_ = bf16[2,64,512]{2,1,0:T(8,128)(2,1)S(1)} collective-permute-done((bf16[2,64,512]{2,1,0:T(8,128)(2,1)S(1)}, bf16[2,64,512]{2,1,0:T(8,128)(2,1)S(1)}, u32[]{:S(2)}, u32[]{:S(2)}) %collective-permute-start.12) | collective-permute-done | bytes 131104 | tf_op jit(solution)/shard_map/ppermute | solution.py:20
  41.9 5.4 %collective-permute-done.13.refs_12_ = bf16[2,64,512]{2,1,0:T(8,128)(2,1)S(1)} collective-permute-done((bf16[2,64,512]{2,1,0:T(8,128)(2,1)S(1)}, bf16[2,64,512]{2,1,0:T(8,128)(2,1)S(1)}, u32[]{:S(2)}, u32[]{:S(2)}) %collective-permute-start.13) | collective-permute-done | bytes 131104 | tf_op jit(solution)/shard_map/ppermute | solution.py:20
  48.4 5.0 %mlp_first.1 = (f32[512,512]{1,0:T(8,128)S(1)}, bf16[512,512]{1,0:T(8,128)(2,1)S(1)}, bf16[512,512]{1,0:T(8,128)(2,1)S(1)}, bf16[512,512]{1,0:T(8,128)(2,1)S(1)}...) custom-call(bf16[512,512]{1,0:T(8,128)(2,1)S(1)} %get-tuple-element., ...), custom_call_target="tpu_custom_call" | custom-call | flops 1 | bytes 1 | tf_op jit(solution)/shard_map/mlp_first/pallas_call | solution.py:42
  53.6 2.3 %mlp_far.2 = (f32[512,512]{1,0:T(8,128)S(1)}, f32[512,512]{1,0:T(8,128)S(1)}, bf16[1,2,8,64,512]{4,3,2,1,0:T(8,128)(2,1)S(1)}, f32[1,1,512]{2,1,0:T(1,128)S(1)}) custom-call(f32[512,512]{1,0:T(8,128)S(1)} %get-tuple-element.205.refs_0_, bf16[512,512]{1,0:T(8,128)(2,1)S(1)} %get-tuple-element.206.refs_1_, bf16[512,512]{1,0:T(8,128)(2,1)S(1)} %get-tuple-element.207.refs_2_, ...), custom_call_target="tpu_custom_call" | custom-call | flops 1 | bytes 1 | tf_op jit(solution)/shard_map/mlp_far/pallas_call | solution.py:42
  56.4 3.1 %mlp_far.3 = (bf16[512,512]{1,0:T(8,128)(2,1)S(1)}, f32[512,512]{1,0:T(8,128)S(1)}, bf16[512,512]{1,0:T(8,128)(2,1)S(1)}, f32[4,512]{1,0:T(4,128)S(1)}, bf16[1,2...) custom-call(f32[512,512]{1,0:T(8,128)S(1)} %get-tuple-element.205.refs_0_, ...), custom_call_target="tpu_custom_call" | custom-call | flops 1 | bytes 1 | tf_op jit(solution)/shard_map/mlp_far/pallas_call | solution.py:42
  60.1 1.4 collective-permute-start.23
  61.5 9.3 %attend_back.1 = (bf16[4,64,512]{2,1,0:T(8,128)(2,1)S(1)}, bf16[4,64,512]{2,1,0:T(8,128)(2,1)S(1)}, bf16[4,64,512]{2,1,0:T(8,128)(2,1)S(1)}, bf16[4,64,512]{2,1,...) custom-call(s32[8]{0:T(128)S(1)} %copy-done.12, ...), custom_call_target="tpu_custom_call" | custom-call | flops 1 | bytes 1 | tf_op jit(solution)/shard_map/attend_back/pallas_call | solution.py:42
  70.9 3.1 %collective-permute-done.22.refs_1_ = bf16[2,4,64,512]{3,2,1,0:T(8,128)(2,1)S(1)} collective-permute-done((bf16[2,4,64,512]{3,2,1,0:T(8,128)(2,1)S(1)}, bf16[2,4,64,512]{3,2,1,0:T(8,128)(2,1)S(1)}, u32[]{:S(2)}, u32[]{:S(2)}) %collective-permute-start.22) | collective-permute-done | bytes 524320 | tf_op jit(solution)/shard_map/ppermute | solution.py:20
  75.8 1.6 %collective-permute-start.27 = (bf16[4,64,512]{2,1,0:T(8,128)(2,1)S(1)}, bf16[4,64,512]{2,1,0:T(8,128)(2,1)S(1)}, u32[]{:S(2)}, u32[]{:S(2)}) collective-permute-start(bf16[4,64,512]{2,1,0:T(8,128)(2,1)S(1)} %get-tuple-element.256), channel_id=1, source_target_pairs={{0,8},{4,12},{8,0},{12,4},{16,24},{20,28},{24,16},{28,20},{1,9},{5... | collective-permute-start | bytes 786440 | tf_op jit(solution)/shard_map/ppermute | solution.py:20
  77.4 5.7 %collective-permute-done.26.refs_1_ = bf16[4,64,512]{2,1,0:T(8,128)(2,1)S(1)} collective-permute-done((bf16[4,64,512]{2,1,0:T(8,128)(2,1)S(1)}, bf16[4,64,512]{2,1,0:T(8,128)(2,1)S(1)}, u32[]{:S(2)}, u32[]{:S(2)}) %collective-permute-start.26) | collective-permute-done | bytes 262176 | tf_op jit(solution)/shard_map/ppermute | solution.py:20
  84.2 1.1 collective-permute-start.28
  85.3 1.7 %collective-permute-start.29 = (bf16[2,64,512]{2,1,0:T(8,128)(2,1)S(1)}, bf16[2,64,512]{2,1,0:T(8,128)(2,1)S(1)}, u32[]{:S(2)}, u32[]{:S(2)}) collective-permute-start(bf16[2,64,512]{2,1,0:T(8,128)(2,1)S(1)} %get-tuple-element.262), channel_id=1, source_target_pairs={{0,8},{4,12},{8,0},{12,4},{16,24},{20,28},{24,16},{28,20},{1,9},{5... | collective-permute-start | bytes 393224 | tf_op jit(solution)/shard_map/ppermute | solution.py:20
  86.9 1.5 %collective-permute-start.30 = (bf16[2,64,512]{2,1,0:T(8,128)(2,1)S(1)}, bf16[2,64,512]{2,1,0:T(8,128)(2,1)S(1)}, u32[]{:S(2)}, u32[]{:S(2)}) collective-permute-start(bf16[2,64,512]{2,1,0:T(8,128)(2,1)S(1)} %get-tuple-element.264), channel_id=1, source_target_pairs={{0,4},{4,0},{8,12},{12,8},{16,20},{20,16},{24,28},{28,24},{1,5},{5... | collective-permute-start | bytes 393224 | tf_op jit(solution)/shard_map/ppermute | solution.py:20
  88.4 1.8 %collective-permute-done.29.refs_1_ = bf16[2,64,512]{2,1,0:T(8,128)(2,1)S(1)} collective-permute-done((bf16[2,64,512]{2,1,0:T(8,128)(2,1)S(1)}, bf16[2,64,512]{2,1,0:T(8,128)(2,1)S(1)}, u32[]{:S(2)}, u32[]{:S(2)}) %collective-permute-start.29) | collective-permute-done | bytes 131104 | tf_op jit(solution)/shard_map/ppermute | solution.py:20
  90.2 1.7 %collective-permute-done.30.refs_3_ = bf16[2,64,512]{2,1,0:T(8,128)(2,1)S(1)} collective-permute-done((bf16[2,64,512]{2,1,0:T(8,128)(2,1)S(1)}, bf16[2,64,512]{2,1,0:T(8,128)(2,1)S(1)}, u32[]{:S(2)}, u32[]{:S(2)}) %collective-permute-start.30) | collective-permute-done | bytes 131104 | tf_op jit(solution)/shard_map/ppermute | solution.py:20
  92.0 2.7 %collective-permute-start.31 = (bf16[1,2,64,512]{3,2,1,0:T(8,128)(2,1)S(1)}, bf16[1,2,64,512]{3,2,1,0:T(8,128)(2,1)S(1)}, u32[]{:S(2)}, u32[]{:S(2)}) collective-permute-start(bf16[1,2,64,512]{3,2,1,0:T(8,128)(2,1)S(1)} %get-tuple-element.266), channel_id=1, source_target_pairs={{0,16},{4,20},{8,24},{12,28},{16,0},{20,4},{24,8},{28,12},{1,17},{... | collective-permute-start | bytes 393224 | tf_op jit(solution)/shard_map/ppermute | solution.py:20
  94.6 4.4 %collective-permute-done.31.refs_1_ = bf16[1,2,64,512]{3,2,1,0:T(8,128)(2,1)S(1)} collective-permute-done((bf16[1,2,64,512]{3,2,1,0:T(8,128)(2,1)S(1)}, bf16[1,2,64,512]{3,2,1,0:T(8,128)(2,1)S(1)}, u32[]{:S(2)}, u32[]{:S(2)}) %collective-permute-start.31) | collective-permute-done | bytes 131104 | tf_op jit(solution)/shard_map/ppermute | solution.py:20
  99.3 1.7 %collective-permute-start.32 = (bf16[4,272,128]{2,1,0:T(8,128)(2,1)S(1)}, bf16[4,272,128]{2,1,0:T(8,128)(2,1)S(1)}, u32[]{:S(2)}, u32[]{:S(2)}) collective-permute-start(bf16[4,272,128]{2,1,0:T(8,128)(2,1)S(1)} %get-tuple-element.271), channel_id=1, source_target_pairs={{0,4},{4,0},{8,12},{12,8},{16,20},{20,16},{24,28},{28,24},{1,5},{5... | collective-permute-start | bytes 835592 | tf_op jit(solution)/shard_map/ppermute | solution.py:20
  101.9 1.4 collective-permute-start.33
  103.3 5.6 %collective-permute-done.33.refs_1_ = bf16[1,2,64,512]{3,2,1,0:T(8,128)(2,1)S(1)} collective-permute-done((bf16[1,2,64,512]{3,2,1,0:T(8,128)(2,1)S(1)}, bf16[1,2,64,512]{3,2,1,0:T(8,128)(2,1)S(1)}, u32[]{:S(2)}, u32[]{:S(2)}) %collective-permute-start.33) | collective-permute-done | bytes 131104 | tf_op jit(solution)/shard_map/ppermute | solution.py:20
  110.6 1.9 %collective-permute-start.35 = (bf16[2,272,128]{2,1,0:T(8,128)(2,1)S(1)}, bf16[2,272,128]{2,1,0:T(8,128)(2,1)S(1)}, u32[]{:S(2)}, u32[]{:S(2)}) collective-permute-start(bf16[2,272,128]{2,1,0:T(8,128)(2,1)S(1)} %get-tuple-element.278), channel_id=1, source_target_pairs={{0,8},{4,12},{8,0},{12,4},{16,24},{20,28},{24,16},{28,20},{1,9},{5... | collective-permute-start | bytes 417800 | tf_op jit(solution)/shard_map/ppermute | solution.py:20
  112.6 2.1 %collective-permute-done.36 = bf16[2,64,512]{2,1,0:T(8,128)(2,1)S(1)} collective-permute-done((bf16[2,64,512]{2,1,0:T(8,128)(2,1)S(1)}, bf16[2,64,512]{2,1,0:T(8,128)(2,1)S(1)}, u32[]{:S(2)}, u32[]{:S(2)}) %collective-permute-start.36) | collective-permute-done | bytes 131104 | tf_op jit(solution)/shard_map/ppermute | solution.py:20
  115.5 1.6 %collective-permute-done.35.refs_1_ = bf16[2,272,128]{2,1,0:T(8,128)(2,1)S(1)} collective-permute-done((bf16[2,272,128]{2,1,0:T(8,128)(2,1)S(1)}, bf16[2,272,128]{2,1,0:T(8,128)(2,1)S(1)}, u32[]{:S(2)}, u32[]{:S(2)}) %collective-permute-start.35) | collective-permute-done | bytes 139296 | tf_op jit(solution)/shard_map/ppermute | solution.py:20
  118.0 1.9 %collective-permute-start.42 = (bf16[4,64,512]{2,1,0:T(8,128)(2,1)S(1)}, bf16[4,64,512]{2,1,0:T(8,128)(2,1)S(1)}, u32[]{:S(2)}, u32[]{:S(2)}) collective-permute-start(bf16[4,64,512]{2,1,0:T(8,128)(2,1)S(1)} %pad_maximum_fusion.1.refs_2_), channel_id=1, source_target_pairs={{0,8},{4,12},{8,0},{12,4},{16,24},{20,28},{24,16},{28,20},{1,9},{5... | collective-permute-start | bytes 786440 | tf_op jit(solution)/shard_map/ppermute | solution.py:20
  119.9 1.3 collective-permute-start.39
  121.2 5.5 %collective-permute-done.39.refs_1_ = bf16[1,272,128]{2,1,0:T(8,128)(2,1)S(1)} collective-permute-done((bf16[1,272,128]{2,1,0:T(8,128)(2,1)S(1)}, bf16[1,272,128]{2,1,0:T(8,128)(2,1)S(1)}, u32[]{:S(2)}, u32[]{:S(2)}) %collective-permute-start.39) | collective-permute-done | bytes 69664 | tf_op jit(solution)/shard_map/ppermute | solution.py:20
  126.7 3.4 %collective-permute-start.40 = (bf16[1,272,128]{2,1,0:T(8,128)(2,1)S(1)}, bf16[1,272,128]{2,1,0:T(8,128)(2,1)S(1)}, u32[]{:S(2)}, u32[]{:S(2)}) collective-permute-start(bf16[1,272,128]{2,1,0:T(8,128)(2,1)S(1)} %add_whole.3), channel_id=1, source_target_pairs={{0,16},{4,20},{8,24},{12,28},{16,0},{20,4},{24,8},{28,12},{1,17},{... | collective-permute-start | bytes 208904 | tf_op jit(solution)/shard_map/ppermute | solution.py:20
  130.2 2.9 %collective-permute-done.40 = bf16[1,272,128]{2,1,0:T(8,128)(2,1)S(1)} collective-permute-done((bf16[1,272,128]{2,1,0:T(8,128)(2,1)S(1)}, bf16[1,272,128]{2,1,0:T(8,128)(2,1)S(1)}, u32[]{:S(2)}, u32[]{:S(2)}) %collective-permute-start.40) | collective-permute-done | bytes 69664 | tf_op jit(solution)/shard_map/ppermute | solution.py:20
  133.1 3.1 %collective-permute-start.44 = (bf16[2,272,128]{2,1,0:T(8,128)(2,1)S(1)}, bf16[2,272,128]{2,1,0:T(8,128)(2,1)S(1)}, u32[]{:S(2)}, u32[]{:S(2)}) collective-permute-start(bf16[2,272,128]{2,1,0:T(8,128)(2,1)S(1)} %pad_maximum_fusion.2), channel_id=1, source_target_pairs={{0,8},{4,12},{8,0},{12,4},{16,24},{20,28},{24,16},{28,20},{1,9},{5... | collective-permute-start | bytes 417800 | tf_op jit(solution)/shard_map/ppermute | solution.py:20
  136.2 3.0 %collective-permute-done.44 = bf16[2,272,128]{2,1,0:T(8,128)(2,1)S(1)} collective-permute-done((bf16[2,272,128]{2,1,0:T(8,128)(2,1)S(1)}, bf16[2,272,128]{2,1,0:T(8,128)(2,1)S(1)}, u32[]{:S(2)}, u32[]{:S(2)}) %collective-permute-start.44) | collective-permute-done | bytes 139296 | tf_op jit(solution)/shard_map/ppermute | solution.py:20
  139.2 1.7 %collective-permute-start.45 = (bf16[4,272,128]{2,1,0:T(8,128)(2,1)S(1)}, bf16[4,272,128]{2,1,0:T(8,128)(2,1)S(1)}, u32[]{:S(2)}, u32[]{:S(2)}) collective-permute-start(bf16[4,272,128]{2,1,0:T(8,128)(2,1)S(1)} %constant_dynamic-update-slice_fusion.refs_0_), channel_id=1, source_target_pairs={{0,4},{4,0},{8,12},{12,8},{16,20},{20,16},{24,28},{28,24},{1,5},{5... | collective-permute-start | bytes 835592 | tf_op jit(solution)/shard_map/ppermute | solution.py:20
  141.0 1.7 %finish_mlp.1 = (f32[512,512]{1,0:T(8,128)}, f32[512,512]{1,0:T(8,128)}) custom-call(bf16[4,64,512]{2,1,0:T(8,128)(2,1)S(1)} %pad_maximum_fusion.refs_0_, bf16[4,64,512]{2,1,0:T(8,128)(2,1)S(1)} %collective-permute-done.41.refs_1_, bf16[4,64,512]{2,1,0:T(8,128)(2,1)S(1)} %pad_maximum_fusion.1.refs_2_, bf16[4,64,512]{2,1,0:T(8,128)(2,1)S(1)} %collective-permute-done.42.refs_3_), custom_call_target="tpu_custom_call" | custom-call | flops 1 | bytes 1 | tf_op jit(solution)/shard_map/finish_mlp/pallas_call | solution.py:42
  142.7 1.2 gather_rows.1
  143.9 1.9 %collective-permute-done.45.refs_1_ = bf16[4,272,128]{2,1,0:T(8,128)(2,1)S(1)} collective-permute-done((bf16[4,272,128]{2,1,0:T(8,128)(2,1)S(1)}, bf16[4,272,128]{2,1,0:T(8,128)(2,1)S(1)}, u32[]{:S(2)}, u32[]{:S(2)}) %collective-permute-start.45) | collective-permute-done | bytes 278560 | tf_op jit(solution)/shard_map/ppermute | solution.py:20
  146.9 1.1 finish_att.1
  (107 shorter events, 17.6 us)
Async XLA Ops:
  4.5 18.6 %copy-start.8 = (f32[2,512]{1,0:T(2,128)S(1)}, f32[2,512]{1,0:T(2,128)}, u32[]{:S(2)}) copy-start(f32[2,512]{1,0:T(2,128)} %refs_2_.3) | copy-start | bytes 12292
  4.6 18.6 %copy-start.9 = (s32[8,256]{1,0:T(8,128)S(1)}, s32[8,256]{1,0:T(8,128)}, u32[]{:S(2)}) copy-start(s32[8,256]{1,0:T(8,128)} %refs_1_.9) | copy-start | bytes 24580
  4.6 18.5 %collective-permute-start.4 = (bf16[2080,128]{1,0:T(8,128)(2,1)S(1)}, bf16[2080,128]{1,0:T(8,128)(2,1)S(1)}, u32[]{:S(2)}, u32[]{:S(2)}) collective-permute-start(bf16[2080,128]{1,0:T(8,128)(2,1)S(1)} %get-tuple-element.175.refs_8_), channel_id=1, source_target_pairs={{0,1},{1,0},{2,3},{3,2},{4,5},{5,4},{6,7},{7,6},{8,9},{9,8},{10,11... | collective-permute-start | bytes 1597448 | tf_op jit(solution)/shard_map/ppermute | solution.py:20
  5.1 14.9 %collective-permute-start = (bf16[1040,128]{1,0:T(8,128)(2,1)S(1)}, bf16[1040,128]{1,0:T(8,128)(2,1)S(1)}, u32[]{:S(2)}, u32[]{:S(2)}) collective-permute-start(bf16[1040,128]{1,0:T(8,128)(2,1)S(1)} %get-tuple-element.167.refs_2_), channel_id=1, source_target_pairs={{0,2},{1,3},{2,0},{3,1},{4,6},{5,7},{6,4},{7,5},{8,10},{9,11},{10,... | collective-permute-start | bytes 798728 | tf_op jit(solution)/shard_map/ppermute | solution.py:20
  7.7 1.9 %collective-permute-start.1 = (bf16[2,64,512]{2,1,0:T(8,128)(2,1)S(1)}, bf16[2,64,512]{2,1,0:T(8,128)(2,1)S(1)}, u32[]{:S(2)}, u32[]{:S(2)}) collective-permute-start(bf16[2,64,512]{2,1,0:T(8,128)(2,1)S(1)} %get-tuple-element.168), channel_id=1, source_target_pairs={{0,1},{1,0},{2,3},{3,2},{4,5},{5,4},{6,7},{7,6},{8,9},{9,8},{10,11... | collective-permute-start | bytes 393224 | tf_op jit(solution)/shard_map/ppermute | solution.py:20
  7.9 9.9 %collective-permute-start.2 = (bf16[2,64,512]{2,1,0:T(8,128)(2,1)S(1)}, bf16[2,64,512]{2,1,0:T(8,128)(2,1)S(1)}, u32[]{:S(2)}, u32[]{:S(2)}) collective-permute-start(bf16[2,64,512]{2,1,0:T(8,128)(2,1)S(1)} %get-tuple-element.169), channel_id=1, source_target_pairs={{0,2},{1,3},{2,0},{3,1},{4,6},{5,7},{6,4},{7,5},{8,10},{9,11},{10,... | collective-permute-start | bytes 393224 | tf_op jit(solution)/shard_map/ppermute | solution.py:20
  8.1 11.9 %collective-permute-start.3 = (bf16[2,64,512]{2,1,0:T(8,128)(2,1)S(1)}, bf16[2,64,512]{2,1,0:T(8,128)(2,1)S(1)}, u32[]{:S(2)}, u32[]{:S(2)}) collective-permute-start(bf16[2,64,512]{2,1,0:T(8,128)(2,1)S(1)} %get-tuple-element.170), channel_id=1, source_target_pairs={{0,3},{1,2},{2,1},{3,0},{4,7},{5,6},{6,5},{7,4},{8,11},{9,10},{10,... | collective-permute-start | bytes 393224 | tf_op jit(solution)/shard_map/ppermute | solution.py:20
  20.0 8.4 %collective-permute-start.5 = (bf16[1040,128]{1,0:T(8,128)(2,1)S(1)}, bf16[1040,128]{1,0:T(8,128)(2,1)S(1)}, u32[]{:S(2)}, u32[]{:S(2)}) collective-permute-start(bf16[1040,128]{1,0:T(8,128)(2,1)S(1)} %collective-permute-done.refs_3_), channel_id=1, source_target_pairs={{0,4},{4,0},{8,12},{12,8},{16,20},{20,16},{24,28},{28,24},{1,5},{5... | collective-permute-start | bytes 798728 | tf_op jit(solution)/shard_map/ppermute | solution.py:20
  21.6 13.8 %collective-permute-start.6 = (bf16[2,256,512]{2,1,0:T(8,128)(2,1)S(1)}, bf16[2,256,512]{2,1,0:T(8,128)(2,1)S(1)}, u32[]{:S(2)}, u32[]{:S(2)}) collective-permute-start(bf16[2,256,512]{2,1,0:T(8,128)(2,1)S(1)} %cut_halves.1), channel_id=1, source_target_pairs={{0,2},{1,3},{2,0},{3,1},{4,6},{5,7},{6,4},{7,5},{8,10},{9,11},{10,... | collective-permute-start | bytes 1572872 | tf_op jit(solution)/shard_map/ppermute | solution.py:20
  23.1 5.9 %collective-permute-start.7 = (bf16[1040,128]{1,0:T(8,128)(2,1)S(1)}, bf16[1040,128]{1,0:T(8,128)(2,1)S(1)}, u32[]{:S(2)}, u32[]{:S(2)}) collective-permute-start(bf16[1040,128]{1,0:T(8,128)(2,1)S(1)} %collective-permute-done.refs_3_), channel_id=1, source_target_pairs={{0,1},{1,0},{2,3},{3,2},{4,5},{5,4},{6,7},{7,6},{8,9},{9,8},{10,11... | collective-permute-start | bytes 798728 | tf_op jit(solution)/shard_map/ppermute | solution.py:20
  28.5 1.5 %collective-permute-start.8 = (bf16[1040,128]{1,0:T(8,128)(2,1)S(1)}, bf16[1040,128]{1,0:T(8,128)(2,1)S(1)}, u32[]{:S(2)}, u32[]{:S(2)}) collective-permute-start(bf16[1040,128]{1,0:T(8,128)(2,1)S(1)} %collective-permute-done.5.refs_4_), channel_id=1, source_target_pairs={{0,1},{1,0},{2,3},{3,2},{4,5},{5,4},{6,7},{7,6},{8,9},{9,8},{10,11... | collective-permute-start | bytes 798728 | tf_op jit(solution)/shard_map/ppermute | solution.py:20
  28.5 19.4 %collective-permute-start.14 = (bf16[512,512]{1,0:T(8,128)(2,1)S(1)}, bf16[512,512]{1,0:T(8,128)(2,1)S(1)}, u32[]{:S(2)}, u32[]{:S(2)}) collective-permute-start(bf16[512,512]{1,0:T(8,128)(2,1)S(1)} %copy-done), channel_id=1, source_target_pairs={{0,1},{1,0},{2,3},{3,2},{4,5},{5,4},{6,7},{7,6},{8,9},{9,8},{10,11... | collective-permute-start | bytes 1572872 | tf_op jit(solution)/shard_map/ppermute | solution.py:20
  35.5 2.6 %collective-permute-start.11 = (bf16[2,64,512]{2,1,0:T(8,128)(2,1)S(1)}, bf16[2,64,512]{2,1,0:T(8,128)(2,1)S(1)}, u32[]{:S(2)}, u32[]{:S(2)}) collective-permute-start(bf16[2,64,512]{2,1,0:T(8,128)(2,1)S(1)} %get-tuple-element.196), channel_id=1, source_target_pairs={{0,1},{1,0},{2,3},{3,2},{4,5},{5,4},{6,7},{7,6},{8,9},{9,8},{10,11... | collective-permute-start | bytes 393224 | tf_op jit(solution)/shard_map/ppermute | solution.py:20
  35.5 12.7 %collective-permute-start.15 = (bf16[512,512]{1,0:T(8,128)(2,1)S(1)}, bf16[512,512]{1,0:T(8,128)(2,1)S(1)}, u32[]{:S(2)}, u32[]{:S(2)}) collective-permute-start(bf16[512,512]{1,0:T(8,128)(2,1)S(1)} %copy-done.1), channel_id=1, source_target_pairs={{0,1},{1,0},{2,3},{3,2},{4,5},{5,4},{6,7},{7,6},{8,9},{9,8},{10,11... | collective-permute-start | bytes 1572872 | tf_op jit(solution)/shard_map/ppermute | solution.py:20
  36.0 5.5 %collective-permute-start.12 = (bf16[2,64,512]{2,1,0:T(8,128)(2,1)S(1)}, bf16[2,64,512]{2,1,0:T(8,128)(2,1)S(1)}, u32[]{:S(2)}, u32[]{:S(2)}) collective-permute-start(bf16[2,64,512]{2,1,0:T(8,128)(2,1)S(1)} %get-tuple-element.197), channel_id=1, source_target_pairs={{0,2},{1,3},{2,0},{3,1},{4,6},{5,7},{6,4},{7,5},{8,10},{9,11},{10,... | collective-permute-start | bytes 393224 | tf_op jit(solution)/shard_map/ppermute | solution.py:20
  37.5 9.8 %collective-permute-start.9 = (bf16[256,512]{1,0:T(8,128)(2,1)S(1)}, bf16[256,512]{1,0:T(8,128)(2,1)S(1)}, u32[]{:S(2)}, u32[]{:S(2)}) collective-permute-start(bf16[256,512]{1,0:T(8,128)(2,1)S(1)} %get-tuple-element.193.refs_10_), channel_id=1, source_target_pairs={{0,4},{4,0},{8,12},{12,8},{16,20},{20,16},{24,28},{28,24},{1,5},{5... | collective-permute-start | bytes 786440 | tf_op jit(solution)/shard_map/ppermute | solution.py:20
  38.1 9.7 %collective-permute-start.10 = (bf16[256,512]{1,0:T(8,128)(2,1)S(1)}, bf16[256,512]{1,0:T(8,128)(2,1)S(1)}, u32[]{:S(2)}, u32[]{:S(2)}) collective-permute-start(bf16[256,512]{1,0:T(8,128)(2,1)S(1)} %get-tuple-element.194.refs_12_), channel_id=1, source_target_pairs={{0,8},{4,12},{8,0},{12,4},{16,24},{20,28},{24,16},{28,20},{1,9},{5... | collective-permute-start | bytes 786440 | tf_op jit(solution)/shard_map/ppermute | solution.py:20
  41.5 5.7 %collective-permute-start.13 = (bf16[2,64,512]{2,1,0:T(8,128)(2,1)S(1)}, bf16[2,64,512]{2,1,0:T(8,128)(2,1)S(1)}, u32[]{:S(2)}, u32[]{:S(2)}) collective-permute-start(bf16[2,64,512]{2,1,0:T(8,128)(2,1)S(1)} %get-tuple-element.198), channel_id=1, source_target_pairs={{0,3},{1,2},{2,1},{3,0},{4,7},{5,6},{6,5},{7,4},{8,11},{9,10},{10,... | collective-permute-start | bytes 393224 | tf_op jit(solution)/shard_map/ppermute | solution.py:20
  47.2 6.4 %collective-permute-start.16 = (bf16[256,512]{1,0:T(8,128)(2,1)S(1)}, bf16[256,512]{1,0:T(8,128)(2,1)S(1)}, u32[]{:S(2)}, u32[]{:S(2)}) collective-permute-start(bf16[256,512]{1,0:T(8,128)(2,1)S(1)} %get-tuple-element.193.refs_10_), channel_id=1, source_target_pairs={{0,1},{1,0},{2,3},{3,2},{4,5},{5,4},{6,7},{7,6},{8,9},{9,8},{10,11... | collective-permute-start | bytes 786440 | tf_op jit(solution)/shard_map/ppermute | solution.py:20
  47.3 6.3 %collective-permute-start.18 = (bf16[256,512]{1,0:T(8,128)(2,1)S(1)}, bf16[256,512]{1,0:T(8,128)(2,1)S(1)}, u32[]{:S(2)}, u32[]{:S(2)}) collective-permute-start(bf16[256,512]{1,0:T(8,128)(2,1)S(1)} %get-tuple-element.194.refs_12_), channel_id=1, source_target_pairs={{0,1},{1,0},{2,3},{3,2},{4,5},{5,4},{6,7},{7,6},{8,9},{9,8},{10,11... | collective-permute-start | bytes 786440 | tf_op jit(solution)/shard_map/ppermute | solution.py:20
  47.7 5.9 %collective-permute-start.17 = (bf16[256,512]{1,0:T(8,128)(2,1)S(1)}, bf16[256,512]{1,0:T(8,128)(2,1)S(1)}, u32[]{:S(2)}, u32[]{:S(2)}) collective-permute-start(bf16[256,512]{1,0:T(8,128)(2,1)S(1)} %collective-permute-done.9.refs_11_), channel_id=1, source_target_pairs={{0,1},{1,0},{2,3},{3,2},{4,5},{5,4},{6,7},{7,6},{8,9},{9,8},{10,11... | collective-permute-start | bytes 786440 | tf_op jit(solution)/shard_map/ppermute | solution.py:20
  47.9 5.7 %collective-permute-start.19 = (bf16[256,512]{1,0:T(8,128)(2,1)S(1)}, bf16[256,512]{1,0:T(8,128)(2,1)S(1)}, u32[]{:S(2)}, u32[]{:S(2)}) collective-permute-start(bf16[256,512]{1,0:T(8,128)(2,1)S(1)} %collective-permute-done.10.refs_13_), channel_id=1, source_target_pairs={{0,1},{1,0},{2,3},{3,2},{4,5},{5,4},{6,7},{7,6},{8,9},{9,8},{10,11... | collective-permute-start | bytes 786440 | tf_op jit(solution)/shard_map/ppermute | solution.py:20
  53.4 6.0 %collective-permute-start.20 = (bf16[1,2,8,64,512]{4,3,2,1,0:T(8,128)(2,1)S(1)}, bf16[1,2,8,64,512]{4,3,2,1,0:T(8,128)(2,1)S(1)}, u32[]{:S(2)}, u32[]{:S(2)}) collective-permute-start(bf16[1,2,8,64,512]{4,3,2,1,0:T(8,128)(2,1)S(1)} %get-tuple-element.221), channel_id=1, source_target_pairs={{0,1},{1,0},{2,3},{3,2},{4,5},{5,4},{6,7},{7,6},{8,9},{9,8},{10,11... | collective-permute-start | bytes 3145736 | tf_op jit(solution)/shard_map/ppermute | solution.py:20
  55.9 3.5 %collective-permute-start.21 = (bf16[1,2,8,64,512]{4,3,2,1,0:T(8,128)(2,1)S(1)}, bf16[1,2,8,64,512]{4,3,2,1,0:T(8,128)(2,1)S(1)}, u32[]{:S(2)}, u32[]{:S(2)}) collective-permute-start(bf16[1,2,8,64,512]{4,3,2,1,0:T(8,128)(2,1)S(1)} %get-tuple-element.223), channel_id=1, source_target_pairs={{0,1},{1,0},{2,3},{3,2},{4,5},{5,4},{6,7},{7,6},{8,9},{9,8},{10,11... | collective-permute-start | bytes 3145736 | tf_op jit(solution)/shard_map/ppermute | solution.py:20
  59.9 14.0 %collective-permute-start.22 = (bf16[2,4,64,512]{3,2,1,0:T(8,128)(2,1)S(1)}, bf16[2,4,64,512]{3,2,1,0:T(8,128)(2,1)S(1)}, u32[]{:S(2)}, u32[]{:S(2)}) collective-permute-start(bf16[2,4,64,512]{3,2,1,0:T(8,128)(2,1)S(1)} %get-tuple-element.241), channel_id=1, source_target_pairs={{0,4},{4,0},{8,12},{12,8},{16,20},{20,16},{24,28},{28,24},{1,5},{5... | collective-permute-start | bytes 1572872 | tf_op jit(solution)/shard_map/ppermute | solution.py:20
  60.1 14.0 %collective-permute-start.23 = (bf16[8,64,512]{2,1,0:T(8,128)(2,1)S(1)}, bf16[8,64,512]{2,1,0:T(8,128)(2,1)S(1)}, u32[]{:S(2)}, u32[]{:S(2)}) collective-permute-start(bf16[8,64,512]{2,1,0:T(8,128)(2,1)S(1)} %get-tuple-element.244), channel_id=1, source_target_pairs={{0,2},{1,3},{2,0},{3,1},{4,6},{5,7},{6,4},{7,5},{8,10},{9,11},{10,... | collective-permute-start | bytes 1572872 | tf_op jit(solution)/shard_map/ppermute | solution.py:20
  74.2 9.7 %collective-permute-start.24 = (bf16[1,8,272,128]{3,2,1,0:T(8,128)(2,1)S(1)}, bf16[1,8,272,128]{3,2,1,0:T(8,128)(2,1)S(1)}, u32[]{:S(2)}, u32[]{:S(2)}) collective-permute-start(bf16[1,8,272,128]{3,2,1,0:T(8,128)(2,1)S(1)} %get-tuple-element.248), channel_id=1, source_target_pairs={{0,1},{1,0},{2,3},{3,2},{4,5},{5,4},{6,7},{7,6},{8,9},{9,8},{10,11... | collective-permute-start | bytes 1671176 | tf_op jit(solution)/shard_map/ppermute | solution.py:20
  74.3 9.6 %collective-permute-start.25 = (bf16[1,8,272,128]{3,2,1,0:T(8,128)(2,1)S(1)}, bf16[1,8,272,128]{3,2,1,0:T(8,128)(2,1)S(1)}, u32[]{:S(2)}, u32[]{:S(2)}) collective-permute-start(bf16[1,8,272,128]{3,2,1,0:T(8,128)(2,1)S(1)} %get-tuple-element.250), channel_id=1, source_target_pairs={{0,1},{1,0},{2,3},{3,2},{4,5},{5,4},{6,7},{7,6},{8,9},{9,8},{10,11... | collective-permute-start | bytes 1671176 | tf_op jit(solution)/shard_map/ppermute | solution.py:20
  74.8 8.3 %collective-permute-start.26 = (bf16[4,64,512]{2,1,0:T(8,128)(2,1)S(1)}, bf16[4,64,512]{2,1,0:T(8,128)(2,1)S(1)}, u32[]{:S(2)}, u32[]{:S(2)}) collective-permute-start(bf16[4,64,512]{2,1,0:T(8,128)(2,1)S(1)} %get-tuple-element.253), channel_id=1, source_target_pairs={{0,2},{1,3},{2,0},{3,1},{4,6},{5,7},{6,4},{7,5},{8,10},{9,11},{10,... | collective-permute-start | bytes 786440 | tf_op jit(solution)/shard_map/ppermute | solution.py:20
  75.8 8.0 %collective-permute-start.27 = (bf16[4,64,512]{2,1,0:T(8,128)(2,1)S(1)}, bf16[4,64,512]{2,1,0:T(8,128)(2,1)S(1)}, u32[]{:S(2)}, u32[]{:S(2)}) collective-permute-start(bf16[4,64,512]{2,1,0:T(8,128)(2,1)S(1)} %get-tuple-element.256), channel_id=1, source_target_pairs={{0,8},{4,12},{8,0},{12,4},{16,24},{20,28},{24,16},{28,20},{1,9},{5... | collective-permute-start | bytes 786440 | tf_op jit(solution)/shard_map/ppermute | solution.py:20
  84.2 14.9 %collective-permute-start.28 = (bf16[8,272,128]{2,1,0:T(8,128)(2,1)S(1)}, bf16[8,272,128]{2,1,0:T(8,128)(2,1)S(1)}, u32[]{:S(2)}, u32[]{:S(2)}) collective-permute-start(bf16[8,272,128]{2,1,0:T(8,128)(2,1)S(1)} %get-tuple-element.259), channel_id=1, source_target_pairs={{0,2},{1,3},{2,0},{3,1},{4,6},{5,7},{6,4},{7,5},{8,10},{9,11},{10,... | collective-permute-start | bytes 1671176 | tf_op jit(solution)/shard_map/ppermute | solution.py:20
  85.3 5.0 %collective-permute-start.29 = (bf16[2,64,512]{2,1,0:T(8,128)(2,1)S(1)}, bf16[2,64,512]{2,1,0:T(8,128)(2,1)S(1)}, u32[]{:S(2)}, u32[]{:S(2)}) collective-permute-start(bf16[2,64,512]{2,1,0:T(8,128)(2,1)S(1)} %get-tuple-element.262), channel_id=1, source_target_pairs={{0,8},{4,12},{8,0},{12,4},{16,24},{20,28},{24,16},{28,20},{1,9},{5... | collective-permute-start | bytes 393224 | tf_op jit(solution)/shard_map/ppermute | solution.py:20
  86.9 5.0 %collective-permute-start.30 = (bf16[2,64,512]{2,1,0:T(8,128)(2,1)S(1)}, bf16[2,64,512]{2,1,0:T(8,128)(2,1)S(1)}, u32[]{:S(2)}, u32[]{:S(2)}) collective-permute-start(bf16[2,64,512]{2,1,0:T(8,128)(2,1)S(1)} %get-tuple-element.264), channel_id=1, source_target_pairs={{0,4},{4,0},{8,12},{12,8},{16,20},{20,16},{24,28},{28,24},{1,5},{5... | collective-permute-start | bytes 393224 | tf_op jit(solution)/shard_map/ppermute | solution.py:20
  92.0 7.1 %collective-permute-start.31 = (bf16[1,2,64,512]{3,2,1,0:T(8,128)(2,1)S(1)}, bf16[1,2,64,512]{3,2,1,0:T(8,128)(2,1)S(1)}, u32[]{:S(2)}, u32[]{:S(2)}) collective-permute-start(bf16[1,2,64,512]{3,2,1,0:T(8,128)(2,1)S(1)} %get-tuple-element.266), channel_id=1, source_target_pairs={{0,16},{4,20},{8,24},{12,28},{16,0},{20,4},{24,8},{28,12},{1,17},{... | collective-permute-start | bytes 393224 | tf_op jit(solution)/shard_map/ppermute | solution.py:20
  99.3 9.7 %collective-permute-start.32 = (bf16[4,272,128]{2,1,0:T(8,128)(2,1)S(1)}, bf16[4,272,128]{2,1,0:T(8,128)(2,1)S(1)}, u32[]{:S(2)}, u32[]{:S(2)}) collective-permute-start(bf16[4,272,128]{2,1,0:T(8,128)(2,1)S(1)} %get-tuple-element.271), channel_id=1, source_target_pairs={{0,4},{4,0},{8,12},{12,8},{16,20},{20,16},{24,28},{28,24},{1,5},{5... | collective-permute-start | bytes 835592 | tf_op jit(solution)/shard_map/ppermute | solution.py:20
  101.0 8.1 %collective-permute-start.34 = (bf16[4,64,512]{2,1,0:T(8,128)(2,1)S(1)}, bf16[4,64,512]{2,1,0:T(8,128)(2,1)S(1)}, u32[]{:S(2)}, u32[]{:S(2)}) collective-permute-start(bf16[4,64,512]{2,1,0:T(8,128)(2,1)S(1)} %get-tuple-element.277), channel_id=1, source_target_pairs={{0,2},{1,3},{2,0},{3,1},{4,6},{5,7},{6,4},{7,5},{8,10},{9,11},{10,... | collective-permute-start | bytes 786440 | tf_op jit(solution)/shard_map/ppermute | solution.py:20
  101.9 7.0 %collective-permute-start.33 = (bf16[1,2,64,512]{3,2,1,0:T(8,128)(2,1)S(1)}, bf16[1,2,64,512]{3,2,1,0:T(8,128)(2,1)S(1)}, u32[]{:S(2)}, u32[]{:S(2)}) collective-permute-start(bf16[1,2,64,512]{3,2,1,0:T(8,128)(2,1)S(1)} %add_whole.2.refs_0_), channel_id=1, source_target_pairs={{0,16},{4,20},{8,24},{12,28},{16,0},{20,4},{24,8},{28,12},{1,17},{... | collective-permute-start | bytes 393224 | tf_op jit(solution)/shard_map/ppermute | solution.py:20
  109.0 5.7 %collective-permute-start.36 = (bf16[2,64,512]{2,1,0:T(8,128)(2,1)S(1)}, bf16[2,64,512]{2,1,0:T(8,128)(2,1)S(1)}, u32[]{:S(2)}, u32[]{:S(2)}) collective-permute-start(bf16[2,64,512]{2,1,0:T(8,128)(2,1)S(1)} %get-tuple-element.280), channel_id=1, source_target_pairs={{0,8},{4,12},{8,0},{12,4},{16,24},{20,28},{24,16},{28,20},{1,9},{5... | collective-permute-start | bytes 393224 | tf_op jit(solution)/shard_map/ppermute | solution.py:20
  109.1 8.3 %collective-permute-start.38 = (bf16[4,64,512]{2,1,0:T(8,128)(2,1)S(1)}, bf16[4,64,512]{2,1,0:T(8,128)(2,1)S(1)}, u32[]{:S(2)}, u32[]{:S(2)}) collective-permute-start(bf16[4,64,512]{2,1,0:T(8,128)(2,1)S(1)} %get-tuple-element.283), channel_id=1, source_target_pairs={{0,3},{1,2},{2,1},{3,0},{4,7},{5,6},{6,5},{7,4},{8,11},{9,10},{10,... | collective-permute-start | bytes 786440 | tf_op jit(solution)/shard_map/ppermute | solution.py:20
  109.2 6.3 %collective-permute-start.37 = (bf16[2,64,512]{2,1,0:T(8,128)(2,1)S(1)}, bf16[2,64,512]{2,1,0:T(8,128)(2,1)S(1)}, u32[]{:S(2)}, u32[]{:S(2)}) collective-permute-start(bf16[2,64,512]{2,1,0:T(8,128)(2,1)S(1)} %get-tuple-element.281), channel_id=1, source_target_pairs={{0,4},{4,0},{8,12},{12,8},{16,20},{20,16},{24,28},{28,24},{1,5},{5... | collective-permute-start | bytes 393224 | tf_op jit(solution)/shard_map/ppermute | solution.py:20
  109.8 23.3 %collective-permute-start.43 = (bf16[4,64,512]{2,1,0:T(8,128)(2,1)S(1)}, bf16[4,64,512]{2,1,0:T(8,128)(2,1)S(1)}, u32[]{:S(2)}, u32[]{:S(2)}) collective-permute-start(bf16[4,64,512]{2,1,0:T(8,128)(2,1)S(1)} %get-tuple-element.288), channel_id=1, source_target_pairs={{0,1},{1,0},{2,3},{3,2},{4,5},{5,4},{6,7},{7,6},{8,9},{9,8},{10,11... | collective-permute-start | bytes 786440 | tf_op jit(solution)/shard_map/ppermute | solution.py:20
  110.6 6.4 %collective-permute-start.35 = (bf16[2,272,128]{2,1,0:T(8,128)(2,1)S(1)}, bf16[2,272,128]{2,1,0:T(8,128)(2,1)S(1)}, u32[]{:S(2)}, u32[]{:S(2)}) collective-permute-start(bf16[2,272,128]{2,1,0:T(8,128)(2,1)S(1)} %get-tuple-element.278), channel_id=1, source_target_pairs={{0,8},{4,12},{8,0},{12,4},{16,24},{20,28},{24,16},{28,20},{1,9},{5... | collective-permute-start | bytes 417800 | tf_op jit(solution)/shard_map/ppermute | solution.py:20
  117.4 15.7 %collective-permute-start.41 = (bf16[4,64,512]{2,1,0:T(8,128)(2,1)S(1)}, bf16[4,64,512]{2,1,0:T(8,128)(2,1)S(1)}, u32[]{:S(2)}, u32[]{:S(2)}) collective-permute-start(bf16[4,64,512]{2,1,0:T(8,128)(2,1)S(1)} %pad_maximum_fusion.refs_0_), channel_id=1, source_target_pairs={{0,4},{4,0},{8,12},{12,8},{16,20},{20,16},{24,28},{28,24},{1,5},{5... | collective-permute-start | bytes 786440 | tf_op jit(solution)/shard_map/ppermute | solution.py:20
  118.0 15.1 %collective-permute-start.42 = (bf16[4,64,512]{2,1,0:T(8,128)(2,1)S(1)}, bf16[4,64,512]{2,1,0:T(8,128)(2,1)S(1)}, u32[]{:S(2)}, u32[]{:S(2)}) collective-permute-start(bf16[4,64,512]{2,1,0:T(8,128)(2,1)S(1)} %pad_maximum_fusion.1.refs_2_), channel_id=1, source_target_pairs={{0,8},{4,12},{8,0},{12,4},{16,24},{20,28},{24,16},{28,20},{1,9},{5... | collective-permute-start | bytes 786440 | tf_op jit(solution)/shard_map/ppermute | solution.py:20
  119.9 6.8 %collective-permute-start.39 = (bf16[1,272,128]{2,1,0:T(8,128)(2,1)S(1)}, bf16[1,272,128]{2,1,0:T(8,128)(2,1)S(1)}, u32[]{:S(2)}, u32[]{:S(2)}) collective-permute-start(bf16[1,272,128]{2,1,0:T(8,128)(2,1)S(1)} %get-tuple-element.284), channel_id=1, source_target_pairs={{0,16},{4,20},{8,24},{12,28},{16,0},{20,4},{24,8},{28,12},{1,17},{... | collective-permute-start | bytes 208904 | tf_op jit(solution)/shard_map/ppermute | solution.py:20
  126.7 6.4 %collective-permute-start.40 = (bf16[1,272,128]{2,1,0:T(8,128)(2,1)S(1)}, bf16[1,272,128]{2,1,0:T(8,128)(2,1)S(1)}, u32[]{:S(2)}, u32[]{:S(2)}) collective-permute-start(bf16[1,272,128]{2,1,0:T(8,128)(2,1)S(1)} %add_whole.3), channel_id=1, source_target_pairs={{0,16},{4,20},{8,24},{12,28},{16,0},{20,4},{24,8},{28,12},{1,17},{... | collective-permute-start | bytes 208904 | tf_op jit(solution)/shard_map/ppermute | solution.py:20
  133.1 6.1 %collective-permute-start.44 = (bf16[2,272,128]{2,1,0:T(8,128)(2,1)S(1)}, bf16[2,272,128]{2,1,0:T(8,128)(2,1)S(1)}, u32[]{:S(2)}, u32[]{:S(2)}) collective-permute-start(bf16[2,272,128]{2,1,0:T(8,128)(2,1)S(1)} %pad_maximum_fusion.2), channel_id=1, source_target_pairs={{0,8},{4,12},{8,0},{12,4},{16,24},{20,28},{24,16},{28,20},{1,9},{5... | collective-permute-start | bytes 417800 | tf_op jit(solution)/shard_map/ppermute | solution.py:20
  139.2 6.6 %collective-permute-start.45 = (bf16[4,272,128]{2,1,0:T(8,128)(2,1)S(1)}, bf16[4,272,128]{2,1,0:T(8,128)(2,1)S(1)}, u32[]{:S(2)}, u32[]{:S(2)}) collective-permute-start(bf16[4,272,128]{2,1,0:T(8,128)(2,1)S(1)} %constant_dynamic-update-slice_fusion.refs_0_), channel_id=1, source_target_pairs={{0,4},{4,0},{8,12},{12,8},{16,20},{20,16},{24,28},{28,24},{1,5},{5... | collective-permute-start | bytes 835592 | tf_op jit(solution)/shard_map/ppermute | solution.py:20
  (14 other events, 63.8 us)

commit v4 on v3

--- a/solution.py
+++ b/solution.py
@@ -11,6 +11,7 @@
 F32 = jnp.float32
 BF16 = jnp.bfloat16
 VMEM_LIMIT = 28 * 2**20
+VMEM_MOST = 60 * 2**20
 GELU_C = 0.7978845608028654
 GELU_A = 0.044715
 VEC = 8
@@ -33,7 +34,7 @@
     return [list(v) for v in out]
 
 
-def run(name, fn, ins, outs, scratch=(), smem=(), after=(), hbm=()):
+def run(name, fn, ins, outs, scratch=(), smem=(), after=(), hbm=(), limit=VMEM_LIMIT):
     n_in, n_out, n_all = len(ins), len(outs), len(ins) + len(after)
 
     def kernel(*refs):
@@ -51,7 +52,7 @@
         + [pl.BlockSpec(memory_space=pl.ANY) for _ in after],
         out_specs=tuple(pl.BlockSpec(memory_space=pltpu.VMEM) for _ in outs),
         scratch_shapes=list(scratch),
-        compiler_params=pltpu.CompilerParams(vmem_limit_bytes=VMEM_LIMIT),
+        compiler_params=pltpu.CompilerParams(vmem_limit_bytes=limit),
         cost_estimate=pl.CostEstimate(flops=1, bytes_accessed=1, transcendentals=0),
         name=name,
     )(*ins, *after)
@@ -155,8 +156,13 @@
         def dp_swap(v, bit):
             return swap(v, "dp", bit, n_dp)
 
-        def spread(parts):
-            return [mp_swap(v, k + 1) for k, v in enumerate(parts)]
+        def send_rows(core, pairs):
+            return [mp_swap(core, 1)] + spread_y(pairs)
+
+        def pass_rows(pairs):
+            half = pairs[0].shape[0] // 2
+            passed = [mp_swap(v[half:], 1) for v in pairs]
+            return [p for pair in zip(pairs, passed) for p in pair]
 
         def over_y(v):
             return [mp_swap(v, k) for k in y_peers]
@@ -164,107 +170,99 @@
         def spread_y(parts):
             return [mp_swap(v, k) for k, v in zip(y_peers, parts)]
 
-        def cut_rows(ins, outs, scratch):
+        row_shapes = [piece] * 2 + [shape((2 * own, share, width), BF16)] * len(y_peers)
+
+        def cut_copies(src, outs, sems):
             me = lax.axis_index("mp")
-            copies = [
-                pltpu.make_async_copy(
-                    v.at[pl.ds((me ^ k) * own, own)],
-                    outs[i * n_mp + k],
-                    scratch[0].at[i, k],
-                )
-                for i, v in enumerate(ins)
-                for k in range(n_mp)
-            ]
+            copies = []
+            for k in range(n_mp):
+                dst = outs[k] if k < 2 else outs[k // 2 + 1].at[pl.ds((k % 2) * own, own)]
+                here = src.at[pl.ds((me ^ k) * own, own)]
+                copies.append(pltpu.make_async_copy(here, dst, sems.at[k]))
             for c in copies:
                 c.start()
-            for c in copies:
-                c.wait()
-
-        rows_cut = run(
-            "cut_rows",
-            cut_rows,
-            [tokens, cotangent],
-            [piece] * (2 * n_mp),
-            [pltpu.SemaphoreType.DMA((2, n_mp))],
-            hbm=(0, 1),
-        )
-        token_parts, cot_parts = list(rows_cut[:n_mp]), list(rows_cut[n_mp:])
-
-        def pack(ins, outs, scratch):
+            return copies
+
+        def begin(ins, outs, scratch):
             x_bit = lax.axis_index("dp") & 1
-            bundle, half = outs
-            copy = pltpu.make_async_copy(ins[0], bundle.at[pl.ds(0, o_at)], scratch[0])
-            copy.start()
+            bundle, half = outs[-2:]
+            copies = cut_copies(ins[0], outs, scratch[0])
+            copies.append(
+                pltpu.make_async_copy(ins[1], bundle.at[pl.ds(0, o_at)], scratch[1])
+            )
+            copies[-1].start()
             for c in range(cols):
-                bundle[o_at + c * lane : o_at + (c + 1) * lane] = ins[1][
+                bundle[o_at + c * lane : o_at + (c + 1) * lane] = ins[2][
                     :, c * lane : (c + 1) * lane
                 ]
             small = jnp.concatenate(
                 [
-                    ins[2][...],
                     ins[3][...],
-                    jnp.concatenate([ins[4][...], jnp.zeros((1, lane - per), F32)], 1),
+                    ins[4][...],
+                    jnp.concatenate([ins[5][...], jnp.zeros((1, lane - per), F32)], 1),
                     jnp.zeros((VEC - 3 - hid_rows, lane), F32),
                 ],
                 0,
             )
             bundle[s_at:] = three_parts(small)
-            copy.wait()
+            for c in copies:
+                c.wait()
             half[...] = bundle[rows_of(x_bit, bundle_rows // 2)]
 
-        bundle, bundle_half = run(
-            "pack",
-            pack,
+        *token_parts, bundle, bundle_half = run(
+            "begin",
+            begin,
             [
+                tokens,
                 w_qkv.reshape(-1, lane),
                 w_out,
                 qv_bias,
                 up_bias.reshape(hid_rows, lane),
                 order_bias.reshape(1, per),
             ],
-            [shape((bundle_rows, lane), BF16), shape((bundle_rows // 2, lane), BF16)],
-            [pltpu.SemaphoreType.DMA(())],
-            hbm=(0,),
-            after=[token_parts[0]],
-        )
-        def cut_halves(ins, outs, scratch):
+            row_shapes
+            + [shape((bundle_rows, lane), BF16), shape((bundle_rows // 2, lane), BF16)],
+            [pltpu.SemaphoreType.DMA((n_mp,)), pltpu.SemaphoreType.DMA(())],
+            hbm=(0, 1),
+            limit=VMEM_MOST,
+        )
+
+        def cut_rest(ins, outs, scratch):
             dpi = lax.axis_index("dp")
-            copies = [
-                pltpu.make_async_copy(
-                    src.at[rows_of(bit, src.shape[0] // 2)],
-                    outs[0].at[n] if joined else outs[n],
-                    scratch[0].at[n],
-                )
-                for n, (src, bit) in enumerate(zip(ins, (dpi & 1, (dpi >> 1) & 1)))
-            ]
-            for c in copies:
-                c.start()
+            copies = cut_copies(ins[0], outs, scratch[0])
+            halves = outs[len(row_shapes) :]
+            for n, (src, bit) in enumerate(zip(ins[1:], (dpi & 1, (dpi >> 1) & 1))):
+                here = src.at[rows_of(bit, src.shape[0] // 2)]
+                dst = halves[0].at[n] if joined else halves[n]
+                copies.append(pltpu.make_async_copy(here, dst, scratch[1].at[n]))
+                copies[-1].start()
             for c in copies:
                 c.wait()
 
         joined = w_up.shape == w_down.shape
         half_shapes = [shape((v.shape[0] // 2, v.shape[1]), BF16) for v in (w_up, w_down)]
-        half_parts = run(
-            "cut_halves",
-            cut_halves,
-            [w_up, w_down],
-            [shape((2,) + half_shapes[0].shape, BF16)] if joined else half_shapes,
-            [pltpu.SemaphoreType.DMA((2,))],
-            hbm=(0, 1),
+        rest = run(
+            "cut_rest",
+            cut_rest,
+            [cotangent, w_up, w_down],
+            row_shapes
+            + ([shape((2,) + half_shapes[0].shape, BF16)] if joined else half_shapes),
+            [pltpu.SemaphoreType.DMA((n_mp,)), pltpu.SemaphoreType.DMA((2,))],
+            hbm=(0, 1, 2),
             after=[bundle_half],
         )
+        cot_parts, half_parts = list(rest[: len(row_shapes)]), rest[len(row_shapes) :]
 
         sends, (bundle, bundle_half) = together(token_parts[1:], [bundle, bundle_half])
-        token_parts = token_parts[:1] + spread(sends)
+        token_parts = token_parts[:1] + send_rows(sends[0], sends[1:])
         bundle_core, bundle_y = mp_swap(bundle, 1), over_y(bundle_half)
 
-        bundle_y, halves, token_parts, near = together(
-            bundle_y, half_parts, token_parts, [w_up, w_down]
-        )
+        bundle_y, token_parts, cot_parts = together(bundle_y, token_parts, cot_parts)
+        halves_y = [over_y(v) for v in half_parts]
+        token_parts = token_parts[:2] + pass_rows(token_parts[2:])
+        bundle_y, token_parts = together(bundle_y, token_parts)
         bundle_x = [dp_swap(v, 1) for v in bundle_y]
         bundle_yc = [mp_swap(v, 1) for v in bundle_y]
-        halves_y = [over_y(v) for v in halves]
-        near_core = [mp_swap(v, 1) for v in near]
 
         def far(first, second, first_core, second_core):
             return [
@@ -307,7 +305,8 @@
             for r in range(own):
                 for k in range(n_mp):
                     at = r * slots + k * share
-                    dst[k][lead + r] = value[at : at + share]
+                    to, first = (dst[k], 0) if k < 2 else (dst[k // 2 + 1], (k % 2) * 2 * own)
+                    to[first + lead + r] = value[at : at + share]
 
         def attend(group, first, pieces):
             wide = lane * len(group)
@@ -391,8 +390,9 @@
 
         x, a1, qkv0, p0, att0, wq0, wo0, small0 = attend(groups[0], True, [bundle, bundle_core])
 
-        bundle_x, (att0,) = together(bundle_x, [att0])
+        bundle_x, (att0,), near = together(bundle_x, [att0], [w_up, w_down])
         bundle_xc = [mp_swap(v, 1) for v in bundle_x]
+        near_core = [mp_swap(v, 1) for v in near]
         qkv1, p1, att1, wq1, wo1, small1 = attend(
             groups[1], False, far(bundle_y, bundle_x, bundle_yc, bundle_xc)
         )
@@ -404,21 +404,18 @@
         if joined:
             pairs = [run("take_apart", take_apart, [v], half_shapes, after=[att1]) for v in halves_y[0]]
             halves_y = list(zip(*pairs))
-        up_y, down_y, (att1,), sends = together(*halves_y, [att1], cot_parts[1:])
+        up_y, down_y, (att1,), near_core, sends = together(
+            *halves_y, [att1], near_core, cot_parts[1:]
+        )
         up_x, down_z = [dp_swap(v, 1) for v in up_y], [dp_swap(v, 2) for v in down_y]
-        up_yc, down_yc = ([mp_swap(v, 1) for v in vs] for vs in (up_y, down_y))
-        cot_parts = cot_parts[:1] + spread(sends)
-
-        up_x, down_z, cot_parts = together(up_x, down_z, cot_parts)
-        up_xc, down_zc = ([mp_swap(v, 1) for v in vs] for vs in (up_x, down_z))
+        cot_parts = cot_parts[:1] + send_rows(sends[0], sends[1:])
+        cot_parts = cot_parts[:2] + pass_rows(cot_parts[2:])
 
         def scatter(dst, src, block, which, dpi):
             for p in range(n_dp):
                 dst[block, which, p] = src[rows_of(dpi ^ p, sub), :]
 
-        def mlp_block(
-            j, a2, a2t, dy, dyt, wu, wd, bias, mixed, d_mid, gs, dst, block, bias_sums, dpi
-        ):
+        def mlp_forward(a2, wu, wd, bias, mixed):
             up = jnp.concatenate([bias[2 + i : 3 + i] for i in range(hid_rows)], 1)
             pre = dot(a2[...], wu) + up
             square = pre * pre
@@ -428,16 +425,19 @@
             slope = half + (pre * (1.0 - t * t)) * (
                 0.5 * GELU_C + (1.5 * GELU_C * GELU_A) * square
             )
+            mixed[...] += dot(hidden, wd)
+            return hidden, slope
+
+        def mlp_backward(hidden, slope, a2t, dy, dyt, wu, wd, d_mid, gs, dst, block, bias_sum, dpi):
             d_hidden = dot_nt(dy[...], wd)
             d_pre = (slope * d_hidden).astype(BF16)
-            mixed[...] += dot(hidden, wd)
             d_mid[...] += dot_nt(d_pre, wu)
-            g_down, g_up = gs.at[2 * j], gs.at[2 * j + 1]
+            g_down, g_up = gs.at[0], gs.at[1]
             g_down[...] = dot(dyt[...], hidden).astype(BF16)
             scatter(dst, g_down, block, 0, dpi)
             g_up[...] = dot(a2t[...], d_pre).astype(BF16)
             scatter(dst, g_up, block, 1, dpi)
-            bias_sums[j] = jnp.sum(d_pre.astype(F32), 0, keepdims=True)
+            bias_sum[...] = jnp.sum(d_pre.astype(F32), 0, keepdims=True)
 
         def mlp_outs(n_blocks, n_arrays):
             both = shape((n_blocks // n_arrays, 2, n_dp, sub, hid), BF16)
@@ -448,11 +448,10 @@
         turned = shape((width, count), BF16)
         g0, g1 = groups
 
-        def mlp_first(ins, outs, scratch):
-            dpi = lax.axis_index("dp")
-            lead, dy_p, wu_p, wd_p = take(ins, [9, n_mp, len(g0), len(g0)])
+        def mlp_near_forward(ins, outs, _):
+            lead, wu_p, wd_p = take(ins, [9, len(g0), len(g0)])
             x_ref, att0_ref, att1_ref, wo0_ref, wo1_ref, smalls, gains, shifts, ob = lead
-            x1, a2, a2t, dy, dyt, mixed, d_mid = outs[:7]
+            x1, a2, a2t, mixed, hidden, slope = outs
             v = x_ref[...].astype(F32) + (
                 dot(att0_ref[...], wo0_ref[...]) + dot(att1_ref[...], wo1_ref[...]) + ob[0:1]
             )
@@ -461,39 +460,60 @@
             act = (normed * gains[1:2] + shifts[1:2]).astype(BF16)
             a2[...] = act
             a2t[...] = act.T
+            mixed[...] = jnp.zeros_like(mixed)
+            for j in range(len(g0)):
+                hidden[j], slope[j] = mlp_forward(
+                    a2, wu_p[j][...], wd_p[j][...], smalls.at[j], mixed
+                )
+
+        near_up, near_down = [near[0], near_core[0]], [near[1], near_core[1]]
+        x1, a2, a2t, mixed, hidden, slope = run(
+            "mlp_near_forward",
+            mlp_near_forward,
+            [x, att0, att1, wo0, wo1, small0, norm_scale_pair, norm_offset_pair, out_bias]
+            + near_up
+            + near_down,
+            [full, full_bf, turned, full]
+            + [shape((len(g0), count, hid), BF16), shape((len(g0), count, hid), F32)],
+        )
+
+        def mlp_near_backward(ins, outs, scratch):
+            dpi = lax.axis_index("dp")
+            (hidden, slope, a2t), dy_p, wu_p, wd_p = take(ins, [3, n_mp, len(g0), len(g0)])
+            dy, dyt, d_mid = outs[:3]
             assemble(dy, dy_p)
             dyt[...] = dy[...].T
-            mixed[...] = jnp.zeros_like(mixed)
             d_mid[...] = jnp.zeros_like(d_mid)
             for j, k in enumerate(g0):
-                mlp_block(
-                    j,
-                    a2,
+                mlp_backward(
+                    hidden[j],
+                    slope[j],
                     a2t,
                     dy,
                     dyt,
                     wu_p[j][...],
                     wd_p[j][...],
-                    smalls[j],
-                    mixed,
                     d_mid,
-                    scratch[0],
-                    outs[7 + k % 2],
+                    scratch[j],
+                    outs[3 + k % 2],
                     0,
-                    outs[9],
+                    outs[5].at[j],
                     dpi,
                 )
 
-        x1, a2, a2t, dy, dyt, mixed, d_mid, keep0, send0, gub0 = run(
-            "mlp_first",
-            mlp_first,
-            [x, att0, att1, wo0, wo1, small0, norm_scale_pair, norm_offset_pair, out_bias]
-            + cot_parts
-            + [near[0], near_core[0], near[1], near_core[1]],
-            [full, full_bf, turned, full_bf, turned, full, full] + mlp_outs(len(g0), 2),
-            [pltpu.VMEM((2 * len(g0), width, hid), BF16)],
-        )
-
+        dy, dyt, d_mid, keep0, send0, gub0 = run(
+            "mlp_near_backward",
+            mlp_near_backward,
+            [hidden, slope, a2t] + cot_parts + near_up + near_down,
+            [full_bf, turned, full] + mlp_outs(len(g0), 2),
+            [pltpu.VMEM((2, width, hid), BF16)] * len(g0),
+        )
+
+        far_parts = together(up_y, up_x, down_y, down_z, [mixed])
+        up_y, up_x, down_y, down_z, (mixed,) = far_parts
+        up_yc, up_xc, down_yc, down_zc = (
+            [mp_swap(v, 1) for v in vs] for vs in (up_y, up_x, down_y, down_z)
+        )
         got0 = mp_swap(send0, 1)
 
         up1 = far(up_y, up_x, up_yc, up_xc)
@@ -507,26 +527,27 @@
                 dpi = lax.axis_index("dp")
                 lead, wu_p, wd_p = take(ins, [10, n_w, n_w])
                 x1, a2, a2t, dy, dyt, mixed_in, d_mid_in, smalls, gains, ob = lead
-                mixed, d_mid, gs = scratch if last else (*outs[:2], scratch[0])
+                (mixed, d_mid), gs = (scratch[:2], scratch[2:]) if last else (outs[:2], scratch)
                 mixed[...] = mixed_in[...]
                 d_mid[...] = d_mid_in[...]
                 grads, bias_sums = outs[-2:]
-                for n, k in enumerate(ks):
-                    mlp_block(
-                        n,
-                        a2,
+                for n in range(len(ks)):
+                    wu = whole(wu_p[2 * n : 2 * n + 2], dpi & 1)
+                    wd = whole(wd_p[2 * n : 2 * n + 2], (dpi >> 1) & 1)
+                    hidden, slope = mlp_forward(a2, wu, wd, smalls.at[2 * n + j], mixed)
+                    mlp_backward(
+                        hidden,
+                        slope,
                         a2t,
                         dy,
                         dyt,
-                        whole(wu_p[2 * n : 2 * n + 2], dpi & 1),
-                        whole(wd_p[2 * n : 2 * n + 2], (dpi >> 1) & 1),
-                        smalls[2 * n + j],
-                        mixed,
+                        wu,
+                        wd,
                         d_mid,
-                        gs,
+                        gs[n],
                         grads,
                         n,
-                        bias_sums,
+                        bias_sums.at[n],
                         dpi,
                     )
                 if not last:
@@ -555,7 +576,7 @@
                 + [v for n in range(len(ks)) for v in down1[4 * n + 2 * j : 4 * n + 2 * j + 2]],
                 ([full_bf, full, full_bf, shape((4, width), F32)] if last else [full, full])
                 + mlp_outs(len(ks), 1),
-                (sums if last else []) + [pltpu.VMEM((2 * len(ks), width, hid), BF16)],
+                (sums if last else []) + [pltpu.VMEM((2, width, hid), BF16)] * len(ks),
             )
 
         mixed, d_mid, send1, gub1_odd = mlp_far(1, False)
@@ -582,17 +603,29 @@
                 i for i, p in enumerate(places) if p & bit
             ]
 
-        def add_split(parts, places, bit, vectors=False):
+        def add_split(parts, places, bit, vectors=False, after=(), two=False, halves=()):
             picks = split(places, bit)
+            n_parts, n_half = len(parts), len(places) // 2
 
             def fn(ins, outs, _):
-                for dst, pick in zip(outs, picks):
+                for pick, dsts in zip(picks, (outs[:1], outs[1:])):
                     for at, i in enumerate(pick):
-                        dst[at] = add_all([v[i] for v in ins], vectors)
-
-            half = shape((len(picks[0]),) + parts[0].shape[1:], BF16)
-            kept, sent = run("add_split", fn, parts, [half, half])
-            return kept, sent, [places[i] for i in picks[0]]
+                        values = [v[i] for v in ins[:n_parts]]
+                        if halves:
+                            values.append(ins[n_parts + i // n_half][i % n_half])
+                        size = dsts[0].shape[0]
+                        dsts[at // size][at % size] = add_all(values, vectors)
+
+            n, rest = len(picks[0]), parts[0].shape[1:]
+            sizes = [n] + ([n // 2] * 2 if two else [n])
+            kept, *sent = run(
+                "add_split",
+                fn,
+                list(parts) + list(halves),
+                [shape((k,) + rest, BF16) for k in sizes],
+                after=after,
+            )
+            return kept, sent if two else sent[0], [places[i] for i in picks[0]]
 
         def add_whole(parts, vectors=False):
             def fn(ins, outs, _):
@@ -600,6 +633,13 @@
                     outs[0][i] = add_all([v[i] for v in ins], vectors)
 
             return run("add_whole", fn, parts, [shape(parts[0].shape, BF16)])[0]
+
+        def meet(mine, got, places, bit, vectors):
+            def fn(ins, outs, _):
+                for i, p in enumerate(places):
+                    outs[0][i] = add_all([ins[0][i], ins[1][places.index(p ^ bit)]], vectors)
+
+            return run("meet", fn, [mine, got], [shape(mine.shape, BF16)])[0]
 
         every = list(range(n_dp))
         no_x, with_x = split(every, 1)
@@ -638,8 +678,7 @@
             )
             x_ref, a1_ref, dx1, d_att, out_ref = fulls
             vec, gub_near, gub_even, gub_odd = vecs
-            parts = outs[:n_mp]
-            grads = outs[n_mp:]
+            parts, grads = outs[:-4], outs[-4:]
             dqkvs, gqs = scratch[:2], scratch[2:4]
             d_in, vec_f, shared = scratch[4:]
             a1t = a1_ref[...].T
@@ -747,7 +786,9 @@
             + [x, a1, dx1, d_att, out_rows]
             + [qkv0, qkv1, p0, p1, att0, att1, wq0, wq1, wo0, wo1]
             + [vec, gub0, gub1_even, gub1_odd],
-            [shape((2 * own, share, width), BF16)] * n_mp + grad_shapes(len(g0)) + grad_shapes(len(g1)),
+            [shape((2 * s.shape[0],) + s.shape[1:], BF16) for s in row_shapes]
+            + grad_shapes(len(g0))
+            + grad_shapes(len(g1)),
             [
                 *[pltpu.VMEM((3, count, lane * len(g)), BF16) for g in groups],
                 *[pltpu.VMEM((4, width, lane * len(g)), BF16) for g in groups],
@@ -757,7 +798,7 @@
             ],
             smem=(0,),
         )
-        row_parts, (ka0, sa0, ka1, sa1) = back[:n_mp], back[n_mp:]
+        row_parts, (ka0, sa0, ka1, sa1) = back[:-4], back[-4:]
 
         def add_x(ins, outs, _):
             for n in range(1 + n_y):
@@ -791,61 +832,60 @@
         (sent_d, sent_u), others_a = together([sent_d, sent_u], others_a)
         got_d, got_u, got_a = dp_swap(sent_d, 2), dp_swap(sent_u, 1), spread_y(others_a)
 
-        def join_split(parts_d, parts_u, places, bit):
-            picks = split(places, bit)
-
-            def fn(ins, outs, _):
-                for n, mine in enumerate(take(ins, [len(parts_d), len(parts_u)])):
-                    for dst, pick in zip(outs, picks):
-                        for at, i in enumerate(pick):
-                            dst[at, n] = add_all([v[i] for v in mine])
-
-            half = shape((len(picks[0]), 2, sub, hid), BF16)
-            kept, sent = run("join_split", fn, parts_d + parts_u, [half, half])
-            return kept, sent, [places[i] for i in picks[0]]
-
-        both, sent, at_both = join_split([kept_d, got_d], [kept_u, got_u], at_d, last_bits[0])
-        got = dp_swap(sent, last_bits[0])
-        for bit in last_bits[1:]:
-            both, sent, at_both = add_split([both, got], at_both, bit)
-            got = dp_swap(sent, bit)
-        both = add_whole([both, got])
-        kept_a, sent_a, at_a = add_split([mine_a] + got_a, every, 1, True)
-
-        (both, sent_a), sends = together([both, sent_a], row_parts[1:])
+        def join(ins, outs, _):
+            for n, mine in enumerate((ins[:2], ins[2:])):
+                for i in range(outs[0].shape[0]):
+                    outs[0][i, n] = add_all([v[i] for v in mine])
+
+        (both,) = run(
+            "join",
+            join,
+            [kept_d, got_d, kept_u, got_u],
+            [shape((len(at_d), 2, sub, hid), BF16)],
+        )
+        at_both = at_d
+        for bit in last_bits[:-1]:
+            kept, sent, at_both = add_split([both], at_both, bit)
+            both = add_whole([kept, dp_swap(sent, bit)])
         got = dp_swap(both, last_bits[-1])
-        got_a = dp_swap(sent_a, 1)
-        row_parts = list(row_parts[:1]) + spread(sends)
-        for bit in reversed(last_bits):
-            if bit != last_bits[-1]:
-                got = dp_swap(both, bit)
-            if bit != last_bits[0]:
-                both, at_both = jnp.concatenate([both, got]), at_both + [p ^ bit for p in at_both]
-        at_both = at_both + [p ^ last_bits[0] for p in at_both]
+        kept_a, sent_a, at_a = add_split([mine_a] + got_a, every, 1, True, two=True)
+        got_a = [dp_swap(v, 1) for v in sent_a]
+        both = meet(both, got, at_both, last_bits[-1], False)
+        for bit in reversed(last_bits[:-1]):
+            both, at_both = jnp.concatenate([both, dp_swap(both, bit)]), at_both + [
+                p ^ bit for p in at_both
+            ]
 
         def part(ins, outs, _):
-            half = ins[0].shape[0]
             for n, o in enumerate(outs):
-                for i in range(half):
+                for i in range(len(at_both)):
                     o[i] = ins[0][i, n]
-                    o[half + i] = ins[1][i, n]
-
-        down, up = run("part", part, [both, got], [shape((len(at_both), sub, hid), BF16)] * 2)
-        kept_a, sent_a, at_a = add_split([kept_a, got_a], at_a, 2, True)
-        (down, up, sent_a), row_parts[2:3] = together([down, up, sent_a], row_parts[2:3])
+
+        down, up = run("part", part, [both], [shape((len(at_both), sub, hid), BF16)] * 2)
+        kept_a, sent_a, at_a = add_split([kept_a], at_a, 2, True, [down], halves=got_a)
+
+        row_parts = list(row_parts)
+        row_parts[1:] = send_rows(row_parts[1], row_parts[2:])
+        down, up, sent_a = together([down, up, sent_a])[0]
         got_d, got_u, got_a = dp_swap(down, 2), dp_swap(up, 1), dp_swap(sent_a, 2)
         down, at_down = jnp.concatenate([down, got_d]), at_both + [p ^ 2 for p in at_both]
         up, at_up = jnp.concatenate([up, got_u]), at_both + [p ^ 1 for p in at_both]
-        kept_a, sent_a, at_a = add_split([kept_a, got_a], at_a, last_bits[0], True)
-        (down, up, sent_a), row_parts[3:4] = together([down, up, sent_a], row_parts[3:4])
+        if len(last_bits) > 1:
+            kept_a, sent_a, at_a = add_split([kept_a, got_a], at_a, last_bits[0], True)
+        else:
+            kept_a = sent_a = add_whole([kept_a, got_a], True)
         got_d, got_u, got_a = dp_swap(down, 1), dp_swap(up, 2), dp_swap(sent_a, last_bits[0])
         for bit in last_bits[1:]:
-            kept_a, sent_a, at_a = add_split([kept_a, got_a], at_a, bit, True)
+            if bit != last_bits[-1]:
+                kept_a, sent_a, at_a = add_split([kept_a, got_a], at_a, bit, True)
+            else:
+                kept_a = sent_a = add_whole([kept_a, got_a], True)
             got_a = dp_swap(sent_a, bit)
-        att = add_whole([kept_a, got_a], True)
-        for bit in [*reversed(last_bits), 2]:
+        att = meet(kept_a, got_a, at_a, last_bits[-1], True)
+        for bit in [*reversed(last_bits[:-1]), 2]:
             if bit == 2:
                 (att, got_d, got_u), row_parts = together([att, got_d, got_u], row_parts)
+                row_parts = row_parts[:2] + pass_rows(row_parts[2:])
             att = jnp.concatenate([att, dp_swap(att, bit)])
             at_a = at_a + [p ^ bit for p in at_a]
         got_a = dp_swap(att, 1)
@@ -859,12 +899,14 @@
                 for v, at in zip(ins[2:], (p, p ^ 2)):
                     outs[1][rows_of(dpi ^ at, sub)] = v[n].astype(F32)
             outs[0][...] = scratch[0][...].T
-
-        r_down, r_up = run(
+            outs[2][...] = jnp.zeros((8, LANES), F32)
+
+        mark = shape((8, LANES), F32)
+        r_down, r_up, mlp_mark = run(
             "finish_mlp",
             finish_mlp,
             [down, got_d, up, got_u],
-            [shape((hid, width), F32), shape((width, hid), F32)],
+            [shape((hid, width), F32), shape((width, hid), F32), mark],
             [pltpu.VMEM((width, hid), F32)],
         )
 
@@ -902,13 +944,14 @@
             for k in range(n_mp):
                 here = pl.ds((me ^ k) * own, own)
                 outs[0][here] = ins[k][:own]
-                outs[1][here] = ins[k][own:].astype(F32)
-
-        output, token_gradient = run(
+                outs[1][here] = ins[k][own : 2 * own].astype(F32)
+            outs[2][...] = jnp.zeros((8, LANES), F32)
+
+        output, token_gradient, rows_mark = run(
             "gather_rows",
             gather_rows,
             row_parts,
-            [shape((rows, share, width), BF16), shape((rows, share, width), F32)],
+            [shape((rows, share, width), BF16), shape((rows, share, width), F32), mark],
         )
         r_qkv, r_out, gain, shift, outb, qvb, upb, order = run(
             "finish_att",
@@ -925,7 +968,7 @@
                 shape((1, per), F32),
             ],
             [pltpu.VMEM((width, lane), F32), pltpu.VMEM((vec_rows, lane), F32)],
-            after=[r_up, output],
+            after=[mlp_mark, rows_mark],
         )
 
         return (

time: 148 us -> 135 us (0.912)
  waiting for transfers between devices: 64 us -> 50.2 us
  starting transfers between devices: 46 us -> 42.8 us
  Pallas kernels: 33.4 us -> 36 us
    ppermute x46 -> x45, waiting for transfers between devices: 64 us -> 50.2 us  [swap(): return lax.ppermute(v, axis, [(i, i ^ bit) for i in range(size)])]
    ppermute x46 -> x45, starting transfers between devices: 46 us -> 42.8 us  [swap(): return lax.ppermute(v, axis, [(i, i ^ bit) for i in range(size)])]
    pallas_call x26, Pallas kernels: 33.4 us -> 36 us  [run(): pl.pallas_call(kernel, out_shape=tuple(outs), in_specs=[pl.BlockSpec(memo...]
    unnamed x33 -> x29, local copies, waits for them, and re-layouts: 3.36 us -> 4.15 us
  transfers between devices with their start and end apart: 46 -> 45, of which waited for: 22 -> 23; matrix products, arithmetic and copies ran while one was open for 0% -> 0% of each run, Pallas kernels for 20% -> 23%
where the time goes in v4:
time: 135 us; the launch traced here: 134 us
  waiting for transfers between devices  50.2 us (37%)
  starting transfers between devices  42.8 us (32%)
  Pallas kernels  36 us (27%)
  local copies, waits for them, and re-layouts  4.22 us (3%)
    ppermute x45, waiting for transfers between devices, swap(): return lax.ppermute(v, axis, [(i, i ^ bit) for i in range(size)])  50.2 us
    ppermute x45, starting transfers between devices, swap(): return lax.ppermute(v, axis, [(i, i ^ bit) for i in range(size)])  42.8 us
    pallas_call x26, Pallas kernels, run(): pl.pallas_call(kernel, out_shape=tuple(outs), in_specs=[pl.BlockSpec(memo...  36 us
    unnamed x29, local copies, waits for them, and re-layouts  4.15 us
  transfers between devices with their start and end apart: 45, of which 23 were waited for; matrix products, arithmetic and copies ran while one was open for 0% of the time, Pallas kernels for 23%

profile of v4, /device:TPU:0, one launch (start us, length us, event | category | flops | bytes accessed | tf_op | source)
XLA Modules:
  0.0 134.2 jit_solution(2192095087349507096)
XLA Ops:
  0.7 3.3 %begin.1 = (bf16[2,64,512]{2,1,0:T(8,128)(2,1)}, bf16[2,64,512]{2,1,0:T(8,128)(2,1)}, bf16[4,64,512]{2,1,0:T(8,128)(2,1)}, bf16[2080,128]{1,0:T(8,128)(2,1)}, bf16[1040,128]{1,0:T(8,128)(2,1)}) custom-call(bf16[8,64,512]{2,1,0:T(8,128)(2,1)} %refs_0_.4, bf16[1536,128]{1,0:T(8,128)(2,1)} %bitcast.5, bf16[128,512]{1,0:T(8,128)(2,1)} %refs_2_.3, ...), custom_call_target="tpu_custom_call" | custom-call | flops 1 | bytes 1 | tf_op jit(solution)/shard_map/begin/pallas_call | solution.py:43
  4.1 3.0 %collective-permute-start = (bf16[1040,128]{1,0:T(8,128)(2,1)}, bf16[1040,128]{1,0:T(8,128)(2,1)S(1)}, u32[]{:S(2)}, u32[]{:S(2)}) collective-permute-start(bf16[1040,128]{1,0:T(8,128)(2,1)} %get-tuple-element.158.refs_3_), channel_id=1, source_target_pairs={{0,2},{1,3},{2,0},{3,1},{4,6},{5,7},{6,4},{7,5},{8,10},{9,11},{10,... | collective-permute-start | bytes 798728 | tf_op jit(solution)/shard_map/ppermute | solution.py:21
  7.7 1.0 copy-done
  12.5 6.8 %collective-permute-done.2.refs_2_ = bf16[4,64,512]{2,1,0:T(8,128)(2,1)S(1)} collective-permute-done((bf16[4,64,512]{2,1,0:T(8,128)(2,1)}, bf16[4,64,512]{2,1,0:T(8,128)(2,1)S(1)}, u32[]{:S(2)}, u32[]{:S(2)}) %collective-permute-start.2) | collective-permute-done | bytes 262176 | tf_op jit(solution)/shard_map/ppermute | solution.py:21
  19.4 1.3 collective-permute-done.3.refs_3_
  20.8 1.7 %collective-permute-start.5 = (bf16[1040,128]{1,0:T(8,128)(2,1)S(1)}, bf16[1040,128]{1,0:T(8,128)(2,1)S(1)}, u32[]{:S(2)}, u32[]{:S(2)}) collective-permute-start(bf16[1040,128]{1,0:T(8,128)(2,1)S(1)} %collective-permute-done.refs_3_), channel_id=1, source_target_pairs={{0,4},{4,0},{8,12},{12,8},{16,20},{20,16},{24,28},{28,24},{1,5},{5... | collective-permute-start | bytes 798728 | tf_op jit(solution)/shard_map/ppermute | solution.py:21
  22.5 1.5 %collective-permute-start.6 = (bf16[2,256,512]{2,1,0:T(8,128)(2,1)S(1)}, bf16[2,256,512]{2,1,0:T(8,128)(2,1)S(1)}, u32[]{:S(2)}, u32[]{:S(2)}) collective-permute-start(bf16[2,256,512]{2,1,0:T(8,128)(2,1)S(1)} %get-tuple-element.179), channel_id=1, source_target_pairs={{0,2},{1,3},{2,0},{3,1},{4,6},{5,7},{6,4},{7,5},{8,10},{9,11},{10,... | collective-permute-start | bytes 1572872 | tf_op jit(solution)/shard_map/ppermute | solution.py:21
  24.0 3.4 %attend.2 = (bf16[512,512]{1,0:T(8,128)(2,1)S(1)}, bf16[512,512]{1,0:T(8,128)(2,1)S(1)}, bf16[3,512,256]{2,1,0:T(8,128)(2,1)S(1)}, bf16[8,256,256]{2,1,0:T(8,128...) custom-call(bf16[2,64,512]{2,1,0:T(8,128)(2,1)S(1)} %copy-done.7, ...), custom_call_target="tpu_custom_call" | custom-call | flops 1 | bytes 1 | tf_op jit(solution)/shard_map/attend/pallas_call | solution.py:43
  27.4 1.8 %collective-permute-done.5.refs_4_ = bf16[1040,128]{1,0:T(8,128)(2,1)S(1)} collective-permute-done((bf16[1040,128]{1,0:T(8,128)(2,1)S(1)}, bf16[1040,128]{1,0:T(8,128)(2,1)S(1)}, u32[]{:S(2)}, u32[]{:S(2)}) %collective-permute-start.5) | collective-permute-done | bytes 266272 | tf_op jit(solution)/shard_map/ppermute | solution.py:21
  30.2 2.0 %collective-permute-done.7.refs_5_ = bf16[1040,128]{1,0:T(8,128)(2,1)S(1)} collective-permute-done((bf16[1040,128]{1,0:T(8,128)(2,1)S(1)}, bf16[1040,128]{1,0:T(8,128)(2,1)S(1)}, u32[]{:S(2)}, u32[]{:S(2)}) %collective-permute-start.7) | collective-permute-done | bytes 266272 | tf_op jit(solution)/shard_map/ppermute | solution.py:21
  32.6 3.1 %attend.3 = (bf16[3,512,256]{2,1,0:T(8,128)(2,1)S(1)}, bf16[8,256,256]{2,1,0:T(8,128)(2,1)S(1)}, bf16[512,256]{1,0:T(8,128)(2,1)S(1)}, bf16[1536,256]{1,0:T(8,12...) custom-call(s32[8]{0:T(128)S(1)} %copy-done.12, s32[8,256]{1,0:T(8,128)S(1)} %copy-done.9, ...), custom_call_target="tpu_custom_call" | custom-call | flops 1 | bytes 1 | tf_op jit(solution)/shard_map/attend/pallas_call | solution.py:43
  36.2 1.4 %collective-permute-start.14 = (bf16[256,512]{1,0:T(8,128)(2,1)S(1)}, bf16[256,512]{1,0:T(8,128)(2,1)S(1)}, u32[]{:S(2)}, u32[]{:S(2)}) collective-permute-start(bf16[256,512]{1,0:T(8,128)(2,1)S(1)} %get-tuple-element.210.refs_10_), channel_id=1, source_target_pairs={{0,4},{4,0},{8,12},{12,8},{16,20},{20,16},{24,28},{28,24},{1,5},{5... | collective-permute-start | bytes 786440 | tf_op jit(solution)/shard_map/ppermute | solution.py:21
  37.6 1.6 %collective-permute-start.15 = (bf16[256,512]{1,0:T(8,128)(2,1)S(1)}, bf16[256,512]{1,0:T(8,128)(2,1)S(1)}, u32[]{:S(2)}, u32[]{:S(2)}) collective-permute-start(bf16[256,512]{1,0:T(8,128)(2,1)S(1)} %get-tuple-element.212.refs_12_), channel_id=1, source_target_pairs={{0,8},{4,12},{8,0},{12,4},{16,24},{20,28},{24,16},{28,20},{1,9},{5... | collective-permute-start | bytes 786440 | tf_op jit(solution)/shard_map/ppermute | solution.py:21
  39.2 1.5 %collective-permute-start.12 = (bf16[4,64,512]{2,1,0:T(8,128)(2,1)S(1)}, bf16[4,64,512]{2,1,0:T(8,128)(2,1)S(1)}, u32[]{:S(2)}, u32[]{:S(2)}) collective-permute-start(bf16[4,64,512]{2,1,0:T(8,128)(2,1)S(1)} %get-tuple-element.201), channel_id=1, source_target_pairs={{0,2},{1,3},{2,0},{3,1},{4,6},{5,7},{6,4},{7,5},{8,10},{9,11},{10,... | collective-permute-start | bytes 786440 | tf_op jit(solution)/shard_map/ppermute | solution.py:21
  40.7 2.7 %mlp_near_forward.1 = (f32[512,512]{1,0:T(8,128)S(1)}, bf16[512,512]{1,0:T(8,128)(2,1)S(1)}, bf16[512,512]{1,0:T(8,128)(2,1)S(1)}, f32[512,512]{1,0:T(8,128)S(1)...) custom-call(bf16[512,512]{1,0:T(8,128)(2,1)S(1)} %get-tuple-element.174.refs_0_.refs_3_, ...), custom_call_target="tpu_custom_call" | custom-call | flops 1 | bytes 1 | tf_op jit(solution)/shard_map/mlp_near_forward/pallas_call | solution.py:43
  44.2 1.4 %collective-permute-done.15.refs_13_ = bf16[256,512]{1,0:T(8,128)(2,1)S(1)} collective-permute-done((bf16[256,512]{1,0:T(8,128)(2,1)S(1)}, bf16[256,512]{1,0:T(8,128)(2,1)S(1)}, u32[]{:S(2)}, u32[]{:S(2)}) %collective-permute-start.15) | collective-permute-done | bytes 262176 | tf_op jit(solution)/shard_map/ppermute | solution.py:21
  47.6 1.1 collective-permute-done.13.refs_6_
  48.7 2.5 %mlp_near_backward.1 = (bf16[512,512]{1,0:T(8,128)(2,1)S(1)}, bf16[512,512]{1,0:T(8,128)(2,1)S(1)}, f32[512,512]{1,0:T(8,128)S(1)}, bf16[1,2,8,64,512]{4,3,2,1,0...) custom-call(bf16[2,512,512]{2,1,0:T(8,128)(2,1)S(1)} %get-tuple-element.197.refs_0_, ...), custom_call_target="tpu_custom_call" | custom-call | flops 1 | bytes 1 | tf_op jit(solution)/shard_map/mlp_near_backward/pallas_call | solution.py:43
  51.5 2.1 %mlp_far.2 = (f32[512,512]{1,0:T(8,128)S(1)}, f32[512,512]{1,0:T(8,128)S(1)}, bf16[1,2,8,64,512]{4,3,2,1,0:T(8,128)(2,1)S(1)}, f32[1,1,512]{2,1,0:T(1,128)S(1)}) custom-call(f32[512,512]{1,0:T(8,128)S(1)} %get-tuple-element.194.refs_0_, bf16[512,512]{1,0:T(8,128)(2,1)S(1)} %get-tuple-element.195.refs_1_, bf16[512,512]{1,0:T(8,128)(2,1)S(1)} %get-tuple-element.196.refs_2_, ...), custom_call_target="tpu_custom_call" | custom-call | flops 1 | bytes 1 | tf_op jit(solution)/shard_map/mlp_far/pallas_call | solution.py:43
  54.0 3.1 %mlp_far.3 = (bf16[512,512]{1,0:T(8,128)(2,1)S(1)}, f32[512,512]{1,0:T(8,128)S(1)}, bf16[512,512]{1,0:T(8,128)(2,1)S(1)}, f32[4,512]{1,0:T(4,128)S(1)}, bf16[1,2...) custom-call(f32[512,512]{1,0:T(8,128)S(1)} %get-tuple-element.194.refs_0_, ...), custom_call_target="tpu_custom_call" | custom-call | flops 1 | bytes 1 | tf_op jit(solution)/shard_map/mlp_far/pallas_call | solution.py:43
  58.2 1.5 %collective-permute-start.23 = (bf16[8,64,512]{2,1,0:T(8,128)(2,1)S(1)}, bf16[8,64,512]{2,1,0:T(8,128)(2,1)S(1)}, u32[]{:S(2)}, u32[]{:S(2)}) collective-permute-start(bf16[8,64,512]{2,1,0:T(8,128)(2,1)S(1)} %get-tuple-element.243), channel_id=1, source_target_pairs={{0,2},{1,3},{2,0},{3,1},{4,6},{5,7},{6,4},{7,5},{8,10},{9,11},{10,... | collective-permute-start | bytes 1572872 | tf_op jit(solution)/shard_map/ppermute | solution.py:21
  59.7 9.3 %attend_back.1 = (bf16[4,64,512]{2,1,0:T(8,128)(2,1)S(1)}, bf16[4,64,512]{2,1,0:T(8,128)(2,1)S(1)}, bf16[8,64,512]{2,1,0:T(8,128)(2,1)S(1)}, bf16[1,8,272,128]{3...) custom-call(s32[8]{0:T(128)S(1)} %copy-done.12, ...), custom_call_target="tpu_custom_call" | custom-call | flops 1 | bytes 1 | tf_op jit(solution)/shard_map/attend_back/pallas_call | solution.py:43
  69.1 2.7 %collective-permute-done.22.refs_1_ = bf16[2,4,64,512]{3,2,1,0:T(8,128)(2,1)S(1)} collective-permute-done((bf16[2,4,64,512]{3,2,1,0:T(8,128)(2,1)S(1)}, bf16[2,4,64,512]{3,2,1,0:T(8,128)(2,1)S(1)}, u32[]{:S(2)}, u32[]{:S(2)}) %collective-permute-start.22) | collective-permute-done | bytes 524320 | tf_op jit(solution)/shard_map/ppermute | solution.py:21
  72.7 1.5 %collective-permute-start.26 = (bf16[4,64,512]{2,1,0:T(8,128)(2,1)S(1)}, bf16[4,64,512]{2,1,0:T(8,128)(2,1)S(1)}, u32[]{:S(2)}, u32[]{:S(2)}) collective-permute-start(bf16[4,64,512]{2,1,0:T(8,128)(2,1)S(1)} %get-tuple-element.252), channel_id=1, source_target_pairs={{0,2},{1,3},{2,0},{3,1},{4,6},{5,7},{6,4},{7,5},{8,10},{9,11},{10,... | collective-permute-start | bytes 786440 | tf_op jit(solution)/shard_map/ppermute | solution.py:21
  74.2 1.3 collective-permute-start.27
  75.5 5.5 %collective-permute-done.26.refs_1_ = bf16[4,64,512]{2,1,0:T(8,128)(2,1)S(1)} collective-permute-done((bf16[4,64,512]{2,1,0:T(8,128)(2,1)S(1)}, bf16[4,64,512]{2,1,0:T(8,128)(2,1)S(1)}, u32[]{:S(2)}, u32[]{:S(2)}) %collective-permute-start.26) | collective-permute-done | bytes 262176 | tf_op jit(solution)/shard_map/ppermute | solution.py:21
  81.1 1.2 collective-permute-done.27.refs_1_
  83.2 1.3 collective-permute-start.31
  84.5 1.5 %collective-permute-start.32 = (bf16[2,64,512]{2,1,0:T(8,128)(2,1)S(1)}, bf16[2,64,512]{2,1,0:T(8,128)(2,1)S(1)}, u32[]{:S(2)}, u32[]{:S(2)}) collective-permute-start(bf16[2,64,512]{2,1,0:T(8,128)(2,1)S(1)} %get-tuple-element.265), channel_id=1, source_target_pairs={{0,4},{4,0},{8,12},{12,8},{16,20},{20,16},{24,28},{28,24},{1,5},{5... | collective-permute-start | bytes 393224 | tf_op jit(solution)/shard_map/ppermute | solution.py:21
  86.0 2.2 %collective-permute-done.31.refs_1_ = bf16[2,64,512]{2,1,0:T(8,128)(2,1)S(1)} collective-permute-done((bf16[2,64,512]{2,1,0:T(8,128)(2,1)S(1)}, bf16[2,64,512]{2,1,0:T(8,128)(2,1)S(1)}, u32[]{:S(2)}, u32[]{:S(2)}) %collective-permute-start.31) | collective-permute-done | bytes 131104 | tf_op jit(solution)/shard_map/ppermute | solution.py:21
  88.1 1.3 collective-permute-done.32.refs_3_
  89.5 2.7 %collective-permute-start.33 = (bf16[2,2,64,512]{3,2,1,0:T(8,128)(2,1)S(1)}, bf16[2,2,64,512]{3,2,1,0:T(8,128)(2,1)S(1)}, u32[]{:S(2)}, u32[]{:S(2)}) collective-permute-start(bf16[2,2,64,512]{3,2,1,0:T(8,128)(2,1)S(1)} %join.1.refs_0_), channel_id=1, source_target_pairs={{0,16},{4,20},{8,24},{12,28},{16,0},{20,4},{24,8},{28,12},{1,17},{... | collective-permute-start | bytes 786440 | tf_op jit(solution)/shard_map/ppermute | solution.py:21
  92.2 3.9 %collective-permute-done.28.refs_1_ = bf16[8,272,128]{2,1,0:T(8,128)(2,1)S(1)} collective-permute-done((bf16[8,272,128]{2,1,0:T(8,128)(2,1)S(1)}, bf16[8,272,128]{2,1,0:T(8,128)(2,1)S(1)}, u32[]{:S(2)}, u32[]{:S(2)}) %collective-permute-start.28) | collective-permute-done | bytes 557088 | tf_op jit(solution)/shard_map/ppermute | solution.py:21
  96.2 1.6 %collective-permute-start.29 = (bf16[2,272,128]{2,1,0:T(8,128)(2,1)S(1)}, bf16[2,272,128]{2,1,0:T(8,128)(2,1)S(1)}, u32[]{:S(2)}, u32[]{:S(2)}) collective-permute-start(bf16[2,272,128]{2,1,0:T(8,128)(2,1)S(1)} %get-tuple-element.260), channel_id=1, source_target_pairs={{0,4},{4,0},{8,12},{12,8},{16,20},{20,16},{24,28},{28,24},{1,5},{5... | collective-permute-start | bytes 417800 | tf_op jit(solution)/shard_map/ppermute | solution.py:21
  98.3 3.7 %collective-permute-done.33.refs_1_ = bf16[2,2,64,512]{3,2,1,0:T(8,128)(2,1)S(1)} collective-permute-done((bf16[2,2,64,512]{3,2,1,0:T(8,128)(2,1)S(1)}, bf16[2,2,64,512]{3,2,1,0:T(8,128)(2,1)S(1)}, u32[]{:S(2)}, u32[]{:S(2)}) %collective-permute-start.33) | collective-permute-done | bytes 262176 | tf_op jit(solution)/shard_map/ppermute | solution.py:21
  102.1 1.4 %collective-permute-start.41 = (bf16[8,64,512]{2,1,0:T(8,128)(2,1)S(1)}, bf16[8,64,512]{2,1,0:T(8,128)(2,1)S(1)}, u32[]{:S(2)}, u32[]{:S(2)}) collective-permute-start(bf16[8,64,512]{2,1,0:T(8,128)(2,1)S(1)} %get-tuple-element.275), channel_id=1, source_target_pairs={{0,2},{1,3},{2,0},{3,1},{4,6},{5,7},{6,4},{7,5},{8,10},{9,11},{10,... | collective-permute-start | bytes 1572872 | tf_op jit(solution)/shard_map/ppermute | solution.py:21
  104.3 1.6 %collective-permute-start.38 = (bf16[2,64,512]{2,1,0:T(8,128)(2,1)S(1)}, bf16[2,64,512]{2,1,0:T(8,128)(2,1)S(1)}, u32[]{:S(2)}, u32[]{:S(2)}) collective-permute-start(bf16[2,64,512]{2,1,0:T(8,128)(2,1)S(1)} %get-tuple-element.272), channel_id=1, source_target_pairs={{0,4},{4,0},{8,12},{12,8},{16,20},{20,16},{24,28},{28,24},{1,5},{5... | collective-permute-start | bytes 393224 | tf_op jit(solution)/shard_map/ppermute | solution.py:21
  105.9 1.4 %collective-permute-start.34 = (bf16[2,272,128]{2,1,0:T(8,128)(2,1)S(1)}, bf16[2,272,128]{2,1,0:T(8,128)(2,1)S(1)}, u32[]{:S(2)}, u32[]{:S(2)}) collective-permute-start(bf16[2,272,128]{2,1,0:T(8,128)(2,1)S(1)} %get-tuple-element.270), channel_id=1, source_target_pairs={{0,8},{4,12},{8,0},{12,4},{16,24},{20,28},{24,16},{28,20},{1,9},{5... | collective-permute-start | bytes 417800 | tf_op jit(solution)/shard_map/ppermute | solution.py:21
  107.3 2.3 %collective-permute-done.36 = bf16[2,64,512]{2,1,0:T(8,128)(2,1)S(1)} collective-permute-done((bf16[2,64,512]{2,1,0:T(8,128)(2,1)S(1)}, bf16[2,64,512]{2,1,0:T(8,128)(2,1)S(1)}, u32[]{:S(2)}, u32[]{:S(2)}) %collective-permute-start.36) | collective-permute-done | bytes 131104 | tf_op jit(solution)/shard_map/ppermute | solution.py:21
  109.7 1.6 %collective-permute-start.37 = (bf16[4,64,512]{2,1,0:T(8,128)(2,1)S(1)}, bf16[4,64,512]{2,1,0:T(8,128)(2,1)S(1)}, u32[]{:S(2)}, u32[]{:S(2)}) collective-permute-start(bf16[4,64,512]{2,1,0:T(8,128)(2,1)S(1)} %constant_dynamic-update-slice_fusion.refs_0_), channel_id=1, source_target_pairs={{0,4},{4,0},{8,12},{12,8},{16,20},{20,16},{24,28},{28,24},{1,5},{5... | collective-permute-start | bytes 786440 | tf_op jit(solution)/shard_map/ppermute | solution.py:21
  112.1 2.9 %collective-permute-start.35 = (bf16[2,272,128]{2,1,0:T(8,128)(2,1)S(1)}, bf16[2,272,128]{2,1,0:T(8,128)(2,1)S(1)}, u32[]{:S(2)}, u32[]{:S(2)}) collective-permute-start(bf16[2,272,128]{2,1,0:T(8,128)(2,1)S(1)} %add_whole.1.refs_0_), channel_id=1, source_target_pairs={{0,16},{4,20},{8,24},{12,28},{16,0},{20,4},{24,8},{28,12},{1,17},{... | collective-permute-start | bytes 417800 | tf_op jit(solution)/shard_map/ppermute | solution.py:21
  115.0 4.2 %collective-permute-done.35.refs_1_ = bf16[2,272,128]{2,1,0:T(8,128)(2,1)S(1)} collective-permute-done((bf16[2,272,128]{2,1,0:T(8,128)(2,1)S(1)}, bf16[2,272,128]{2,1,0:T(8,128)(2,1)S(1)}, u32[]{:S(2)}, u32[]{:S(2)}) %collective-permute-start.35) | collective-permute-done | bytes 139296 | tf_op jit(solution)/shard_map/ppermute | solution.py:21
  119.7 3.7 %collective-permute-start.43 = (bf16[2,272,128]{2,1,0:T(8,128)(2,1)S(1)}, bf16[2,272,128]{2,1,0:T(8,128)(2,1)S(1)}, u32[]{:S(2)}, u32[]{:S(2)}) collective-permute-start(bf16[2,272,128]{2,1,0:T(8,128)(2,1)S(1)} %meet.3), channel_id=1, source_target_pairs={{0,8},{4,12},{8,0},{12,4},{16,24},{20,28},{24,16},{28,20},{1,9},{5... | collective-permute-start | bytes 417800 | tf_op jit(solution)/shard_map/ppermute | solution.py:21
  123.5 3.0 %collective-permute-done.43 = bf16[2,272,128]{2,1,0:T(8,128)(2,1)S(1)} collective-permute-done((bf16[2,272,128]{2,1,0:T(8,128)(2,1)S(1)}, bf16[2,272,128]{2,1,0:T(8,128)(2,1)S(1)}, u32[]{:S(2)}, u32[]{:S(2)}) %collective-permute-start.43) | collective-permute-done | bytes 139296 | tf_op jit(solution)/shard_map/ppermute | solution.py:21
  127.5 1.7 %finish_mlp.1 = (f32[512,512]{1,0:T(8,128)}, f32[512,512]{1,0:T(8,128)}, f32[8,128]{1,0:T(8,128)S(1)}) custom-call(bf16[4,64,512]{2,1,0:T(8,128)(2,1)S(1)} %constant_dynamic-update-slice_fusion.refs_0_, bf16[4,64,512]{2,1,0:T(8,128)(2,1)S(1)} %collective-permute-done.37.refs_1_, bf16[4,64,512]{2,1,0:T(8,128)(2,1)S(1)} %constant_dynamic-update-slice_fusion.2.refs_2_, ...), custom_call_target="tpu_custom_call" | custom-call | flops 1 | bytes 1 | tf_op jit(solution)/shard_map/finish_mlp/pallas_call | solution.py:43
  129.2 1.2 gather_rows.1
  130.4 2.7 %collective-permute-done.44.refs_1_ = bf16[4,272,128]{2,1,0:T(8,128)(2,1)S(1)} collective-permute-done((bf16[4,272,128]{2,1,0:T(8,128)(2,1)S(1)}, bf16[4,272,128]{2,1,0:T(8,128)(2,1)S(1)}, u32[]{:S(2)}, u32[]{:S(2)}) %collective-permute-start.44) | collective-permute-done | bytes 278560 | tf_op jit(solution)/shard_map/ppermute | solution.py:21
  133.1 1.1 finish_att.1
  (103 shorter events, 16.8 us)
Async XLA Ops:
  0.6 23.3 %copy-start.12 = (s32[8]{0:T(128)S(1)}, s32[8]{0:T(128)}, u32[]{:S(2)}) copy-start(s32[8]{0:T(128)} %refs_0_.7) | copy-start | bytes 100
  0.7 28.5 %copy-start.1 = (bf16[512,512]{1,0:T(8,128)(2,1)S(1)}, bf16[512,512]{1,0:T(8,128)(2,1)}, u32[]{:S(2)}) copy-start(bf16[512,512]{1,0:T(8,128)(2,1)} %refs_7_.4) | copy-start | bytes 1572868
  0.7 28.5 %copy-start.3 = (bf16[512,512]{1,0:T(8,128)(2,1)S(1)}, bf16[512,512]{1,0:T(8,128)(2,1)}, u32[]{:S(2)}) copy-start(bf16[512,512]{1,0:T(8,128)(2,1)} %refs_9_.3) | copy-start | bytes 1572868
  4.1 15.3 %collective-permute-start = (bf16[1040,128]{1,0:T(8,128)(2,1)}, bf16[1040,128]{1,0:T(8,128)(2,1)S(1)}, u32[]{:S(2)}, u32[]{:S(2)}) collective-permute-start(bf16[1040,128]{1,0:T(8,128)(2,1)} %get-tuple-element.158.refs_3_), channel_id=1, source_target_pairs={{0,2},{1,3},{2,0},{3,1},{4,6},{5,7},{6,4},{7,5},{8,10},{9,11},{10,... | collective-permute-start | bytes 798728 | tf_op jit(solution)/shard_map/ppermute | solution.py:21
  7.1 12.2 %collective-permute-start.2 = (bf16[4,64,512]{2,1,0:T(8,128)(2,1)}, bf16[4,64,512]{2,1,0:T(8,128)(2,1)S(1)}, u32[]{:S(2)}, u32[]{:S(2)}) collective-permute-start(bf16[4,64,512]{2,1,0:T(8,128)(2,1)} %get-tuple-element.161), channel_id=1, source_target_pairs={{0,2},{1,3},{2,0},{3,1},{4,6},{5,7},{6,4},{7,5},{8,10},{9,11},{10,... | collective-permute-start | bytes 786440 | tf_op jit(solution)/shard_map/ppermute | solution.py:21
  7.2 16.8 %collective-permute-start.4 = (bf16[2080,128]{1,0:T(8,128)(2,1)}, bf16[2080,128]{1,0:T(8,128)(2,1)S(1)}, u32[]{:S(2)}, u32[]{:S(2)}) collective-permute-start(bf16[2080,128]{1,0:T(8,128)(2,1)} %get-tuple-element.173.refs_8_), channel_id=1, source_target_pairs={{0,1},{1,0},{2,3},{3,2},{4,5},{5,4},{6,7},{7,6},{8,9},{9,8},{10,11... | collective-permute-start | bytes 1597448 | tf_op jit(solution)/shard_map/ppermute | solution.py:21
  7.2 5.4 %collective-permute-start.1 = (bf16[2,64,512]{2,1,0:T(8,128)(2,1)}, bf16[2,64,512]{2,1,0:T(8,128)(2,1)S(1)}, u32[]{:S(2)}, u32[]{:S(2)}) collective-permute-start(bf16[2,64,512]{2,1,0:T(8,128)(2,1)} %get-tuple-element.160), channel_id=1, source_target_pairs={{0,1},{1,0},{2,3},{3,2},{4,5},{5,4},{6,7},{7,6},{8,9},{9,8},{10,11... | collective-permute-start | bytes 393224 | tf_op jit(solution)/shard_map/ppermute | solution.py:21
  19.3 1.4 %collective-permute-start.3 = (bf16[2,64,512]{2,1,0:T(8,128)(2,1)S(1)}, bf16[2,64,512]{2,1,0:T(8,128)(2,1)S(1)}, u32[]{:S(2)}, u32[]{:S(2)}) collective-permute-start(bf16[2,64,512]{2,1,0:T(8,128)(2,1)S(1)} %slice.9), channel_id=1, source_target_pairs={{0,1},{1,0},{2,3},{3,2},{4,5},{5,4},{6,7},{7,6},{8,9},{9,8},{10,11... | collective-permute-start | bytes 393224 | tf_op jit(solution)/shard_map/ppermute | solution.py:21
  20.8 8.4 %collective-permute-start.5 = (bf16[1040,128]{1,0:T(8,128)(2,1)S(1)}, bf16[1040,128]{1,0:T(8,128)(2,1)S(1)}, u32[]{:S(2)}, u32[]{:S(2)}) collective-permute-start(bf16[1040,128]{1,0:T(8,128)(2,1)S(1)} %collective-permute-done.refs_3_), channel_id=1, source_target_pairs={{0,4},{4,0},{8,12},{12,8},{16,20},{20,16},{24,28},{28,24},{1,5},{5... | collective-permute-start | bytes 798728 | tf_op jit(solution)/shard_map/ppermute | solution.py:21
  22.5 13.7 %collective-permute-start.6 = (bf16[2,256,512]{2,1,0:T(8,128)(2,1)S(1)}, bf16[2,256,512]{2,1,0:T(8,128)(2,1)S(1)}, u32[]{:S(2)}, u32[]{:S(2)}) collective-permute-start(bf16[2,256,512]{2,1,0:T(8,128)(2,1)S(1)} %get-tuple-element.179), channel_id=1, source_target_pairs={{0,2},{1,3},{2,0},{3,1},{4,6},{5,7},{6,4},{7,5},{8,10},{9,11},{10,... | collective-permute-start | bytes 1572872 | tf_op jit(solution)/shard_map/ppermute | solution.py:21
  29.2 7.0 %collective-permute-start.9 = (bf16[512,512]{1,0:T(8,128)(2,1)S(1)}, bf16[512,512]{1,0:T(8,128)(2,1)S(1)}, u32[]{:S(2)}, u32[]{:S(2)}) collective-permute-start(bf16[512,512]{1,0:T(8,128)(2,1)S(1)} %copy-done.1), channel_id=1, source_target_pairs={{0,1},{1,0},{2,3},{3,2},{4,5},{5,4},{6,7},{7,6},{8,9},{9,8},{10,11... | collective-permute-start | bytes 1572872 | tf_op jit(solution)/shard_map/ppermute | solution.py:21
  29.2 7.0 %collective-permute-start.10 = (bf16[512,512]{1,0:T(8,128)(2,1)S(1)}, bf16[512,512]{1,0:T(8,128)(2,1)S(1)}, u32[]{:S(2)}, u32[]{:S(2)}) collective-permute-start(bf16[512,512]{1,0:T(8,128)(2,1)S(1)} %copy-done.3), channel_id=1, source_target_pairs={{0,1},{1,0},{2,3},{3,2},{4,5},{5,4},{6,7},{7,6},{8,9},{9,8},{10,11... | collective-permute-start | bytes 1572872 | tf_op jit(solution)/shard_map/ppermute | solution.py:21
  29.7 2.5 %collective-permute-start.7 = (bf16[1040,128]{1,0:T(8,128)(2,1)S(1)}, bf16[1040,128]{1,0:T(8,128)(2,1)S(1)}, u32[]{:S(2)}, u32[]{:S(2)}) collective-permute-start(bf16[1040,128]{1,0:T(8,128)(2,1)S(1)} %collective-permute-done.refs_3_), channel_id=1, source_target_pairs={{0,1},{1,0},{2,3},{3,2},{4,5},{5,4},{6,7},{7,6},{8,9},{9,8},{10,11... | collective-permute-start | bytes 798728 | tf_op jit(solution)/shard_map/ppermute | solution.py:21
  29.8 2.8 %collective-permute-start.8 = (bf16[1040,128]{1,0:T(8,128)(2,1)S(1)}, bf16[1040,128]{1,0:T(8,128)(2,1)S(1)}, u32[]{:S(2)}, u32[]{:S(2)}) collective-permute-start(bf16[1040,128]{1,0:T(8,128)(2,1)S(1)} %collective-permute-done.5.refs_4_), channel_id=1, source_target_pairs={{0,1},{1,0},{2,3},{3,2},{4,5},{5,4},{6,7},{7,6},{8,9},{9,8},{10,11... | collective-permute-start | bytes 798728 | tf_op jit(solution)/shard_map/ppermute | solution.py:21
  36.2 8.0 %collective-permute-start.14 = (bf16[256,512]{1,0:T(8,128)(2,1)S(1)}, bf16[256,512]{1,0:T(8,128)(2,1)S(1)}, u32[]{:S(2)}, u32[]{:S(2)}) collective-permute-start(bf16[256,512]{1,0:T(8,128)(2,1)S(1)} %get-tuple-element.210.refs_10_), channel_id=1, source_target_pairs={{0,4},{4,0},{8,12},{12,8},{16,20},{20,16},{24,28},{28,24},{1,5},{5... | collective-permute-start | bytes 786440 | tf_op jit(solution)/shard_map/ppermute | solution.py:21
  37.6 8.1 %collective-permute-start.15 = (bf16[256,512]{1,0:T(8,128)(2,1)S(1)}, bf16[256,512]{1,0:T(8,128)(2,1)S(1)}, u32[]{:S(2)}, u32[]{:S(2)}) collective-permute-start(bf16[256,512]{1,0:T(8,128)(2,1)S(1)} %get-tuple-element.212.refs_12_), channel_id=1, source_target_pairs={{0,8},{4,12},{8,0},{12,4},{16,24},{20,28},{24,16},{28,20},{1,9},{5... | collective-permute-start | bytes 786440 | tf_op jit(solution)/shard_map/ppermute | solution.py:21
  39.2 7.8 %collective-permute-start.12 = (bf16[4,64,512]{2,1,0:T(8,128)(2,1)S(1)}, bf16[4,64,512]{2,1,0:T(8,128)(2,1)S(1)}, u32[]{:S(2)}, u32[]{:S(2)}) collective-permute-start(bf16[4,64,512]{2,1,0:T(8,128)(2,1)S(1)} %get-tuple-element.201), channel_id=1, source_target_pairs={{0,2},{1,3},{2,0},{3,1},{4,6},{5,7},{6,4},{7,5},{8,10},{9,11},{10,... | collective-permute-start | bytes 786440 | tf_op jit(solution)/shard_map/ppermute | solution.py:21
  40.7 6.3 %collective-permute-start.11 = (bf16[2,64,512]{2,1,0:T(8,128)(2,1)S(1)}, bf16[2,64,512]{2,1,0:T(8,128)(2,1)S(1)}, u32[]{:S(2)}, u32[]{:S(2)}) collective-permute-start(bf16[2,64,512]{2,1,0:T(8,128)(2,1)S(1)} %get-tuple-element.200), channel_id=1, source_target_pairs={{0,1},{1,0},{2,3},{3,2},{4,5},{5,4},{6,7},{7,6},{8,9},{9,8},{10,11... | collective-permute-start | bytes 393224 | tf_op jit(solution)/shard_map/ppermute | solution.py:21
  45.7 5.8 %collective-permute-start.16 = (bf16[256,512]{1,0:T(8,128)(2,1)S(1)}, bf16[256,512]{1,0:T(8,128)(2,1)S(1)}, u32[]{:S(2)}, u32[]{:S(2)}) collective-permute-start(bf16[256,512]{1,0:T(8,128)(2,1)S(1)} %get-tuple-element.210.refs_10_), channel_id=1, source_target_pairs={{0,1},{1,0},{2,3},{3,2},{4,5},{5,4},{6,7},{7,6},{8,9},{9,8},{10,11... | collective-permute-start | bytes 786440 | tf_op jit(solution)/shard_map/ppermute | solution.py:21
  45.7 5.8 %collective-permute-start.17 = (bf16[256,512]{1,0:T(8,128)(2,1)S(1)}, bf16[256,512]{1,0:T(8,128)(2,1)S(1)}, u32[]{:S(2)}, u32[]{:S(2)}) collective-permute-start(bf16[256,512]{1,0:T(8,128)(2,1)S(1)} %collective-permute-done.14.refs_11_), channel_id=1, source_target_pairs={{0,1},{1,0},{2,3},{3,2},{4,5},{5,4},{6,7},{7,6},{8,9},{9,8},{10,11... | collective-permute-start | bytes 786440 | tf_op jit(solution)/shard_map/ppermute | solution.py:21
  46.2 5.3 %collective-permute-start.18 = (bf16[256,512]{1,0:T(8,128)(2,1)S(1)}, bf16[256,512]{1,0:T(8,128)(2,1)S(1)}, u32[]{:S(2)}, u32[]{:S(2)}) collective-permute-start(bf16[256,512]{1,0:T(8,128)(2,1)S(1)} %get-tuple-element.212.refs_12_), channel_id=1, source_target_pairs={{0,1},{1,0},{2,3},{3,2},{4,5},{5,4},{6,7},{7,6},{8,9},{9,8},{10,11... | collective-permute-start | bytes 786440 | tf_op jit(solution)/shard_map/ppermute | solution.py:21
  47.0 4.5 %collective-permute-start.19 = (bf16[256,512]{1,0:T(8,128)(2,1)S(1)}, bf16[256,512]{1,0:T(8,128)(2,1)S(1)}, u32[]{:S(2)}, u32[]{:S(2)}) collective-permute-start(bf16[256,512]{1,0:T(8,128)(2,1)S(1)} %collective-permute-done.15.refs_13_), channel_id=1, source_target_pairs={{0,1},{1,0},{2,3},{3,2},{4,5},{5,4},{6,7},{7,6},{8,9},{9,8},{10,11... | collective-permute-start | bytes 786440 | tf_op jit(solution)/shard_map/ppermute | solution.py:21
  47.0 1.7 %collective-permute-start.13 = (bf16[2,64,512]{2,1,0:T(8,128)(2,1)S(1)}, bf16[2,64,512]{2,1,0:T(8,128)(2,1)S(1)}, u32[]{:S(2)}, u32[]{:S(2)}) collective-permute-start(bf16[2,64,512]{2,1,0:T(8,128)(2,1)S(1)} %slice.12), channel_id=1, source_target_pairs={{0,1},{1,0},{2,3},{3,2},{4,5},{5,4},{6,7},{7,6},{8,9},{9,8},{10,11... | collective-permute-start | bytes 393224 | tf_op jit(solution)/shard_map/ppermute | solution.py:21
  51.2 5.9 %collective-permute-start.20 = (bf16[1,2,8,64,512]{4,3,2,1,0:T(8,128)(2,1)S(1)}, bf16[1,2,8,64,512]{4,3,2,1,0:T(8,128)(2,1)S(1)}, u32[]{:S(2)}, u32[]{:S(2)}) collective-permute-start(bf16[1,2,8,64,512]{4,3,2,1,0:T(8,128)(2,1)S(1)} %get-tuple-element.220), channel_id=1, source_target_pairs={{0,1},{1,0},{2,3},{3,2},{4,5},{5,4},{6,7},{7,6},{8,9},{9,8},{10,11... | collective-permute-start | bytes 3145736 | tf_op jit(solution)/shard_map/ppermute | solution.py:21
  53.7 3.5 %collective-permute-start.21 = (bf16[1,2,8,64,512]{4,3,2,1,0:T(8,128)(2,1)S(1)}, bf16[1,2,8,64,512]{4,3,2,1,0:T(8,128)(2,1)S(1)}, u32[]{:S(2)}, u32[]{:S(2)}) collective-permute-start(bf16[1,2,8,64,512]{4,3,2,1,0:T(8,128)(2,1)S(1)} %get-tuple-element.222), channel_id=1, source_target_pairs={{0,1},{1,0},{2,3},{3,2},{4,5},{5,4},{6,7},{7,6},{8,9},{9,8},{10,11... | collective-permute-start | bytes 3145736 | tf_op jit(solution)/shard_map/ppermute | solution.py:21
  57.6 14.1 %collective-permute-start.22 = (bf16[2,4,64,512]{3,2,1,0:T(8,128)(2,1)S(1)}, bf16[2,4,64,512]{3,2,1,0:T(8,128)(2,1)S(1)}, u32[]{:S(2)}, u32[]{:S(2)}) collective-permute-start(bf16[2,4,64,512]{3,2,1,0:T(8,128)(2,1)S(1)} %get-tuple-element.240), channel_id=1, source_target_pairs={{0,4},{4,0},{8,12},{12,8},{16,20},{20,16},{24,28},{28,24},{1,5},{5... | collective-permute-start | bytes 1572872 | tf_op jit(solution)/shard_map/ppermute | solution.py:21
  58.2 13.8 %collective-permute-start.23 = (bf16[8,64,512]{2,1,0:T(8,128)(2,1)S(1)}, bf16[8,64,512]{2,1,0:T(8,128)(2,1)S(1)}, u32[]{:S(2)}, u32[]{:S(2)}) collective-permute-start(bf16[8,64,512]{2,1,0:T(8,128)(2,1)S(1)} %get-tuple-element.243), channel_id=1, source_target_pairs={{0,2},{1,3},{2,0},{3,1},{4,6},{5,7},{6,4},{7,5},{8,10},{9,11},{10,... | collective-permute-start | bytes 1572872 | tf_op jit(solution)/shard_map/ppermute | solution.py:21
  72.1 10.2 %collective-permute-start.24 = (bf16[1,8,272,128]{3,2,1,0:T(8,128)(2,1)S(1)}, bf16[1,8,272,128]{3,2,1,0:T(8,128)(2,1)S(1)}, u32[]{:S(2)}, u32[]{:S(2)}) collective-permute-start(bf16[1,8,272,128]{3,2,1,0:T(8,128)(2,1)S(1)} %get-tuple-element.247), channel_id=1, source_target_pairs={{0,1},{1,0},{2,3},{3,2},{4,5},{5,4},{6,7},{7,6},{8,9},{9,8},{10,11... | collective-permute-start | bytes 1671176 | tf_op jit(solution)/shard_map/ppermute | solution.py:21
  72.2 10.1 %collective-permute-start.25 = (bf16[1,8,272,128]{3,2,1,0:T(8,128)(2,1)S(1)}, bf16[1,8,272,128]{3,2,1,0:T(8,128)(2,1)S(1)}, u32[]{:S(2)}, u32[]{:S(2)}) collective-permute-start(bf16[1,8,272,128]{3,2,1,0:T(8,128)(2,1)S(1)} %get-tuple-element.249), channel_id=1, source_target_pairs={{0,1},{1,0},{2,3},{3,2},{4,5},{5,4},{6,7},{7,6},{8,9},{9,8},{10,11... | collective-permute-start | bytes 1671176 | tf_op jit(solution)/shard_map/ppermute | solution.py:21
  72.7 8.3 %collective-permute-start.26 = (bf16[4,64,512]{2,1,0:T(8,128)(2,1)S(1)}, bf16[4,64,512]{2,1,0:T(8,128)(2,1)S(1)}, u32[]{:S(2)}, u32[]{:S(2)}) collective-permute-start(bf16[4,64,512]{2,1,0:T(8,128)(2,1)S(1)} %get-tuple-element.252), channel_id=1, source_target_pairs={{0,2},{1,3},{2,0},{3,1},{4,6},{5,7},{6,4},{7,5},{8,10},{9,11},{10,... | collective-permute-start | bytes 786440 | tf_op jit(solution)/shard_map/ppermute | solution.py:21
  74.2 8.0 %collective-permute-start.27 = (bf16[4,64,512]{2,1,0:T(8,128)(2,1)S(1)}, bf16[4,64,512]{2,1,0:T(8,128)(2,1)S(1)}, u32[]{:S(2)}, u32[]{:S(2)}) collective-permute-start(bf16[4,64,512]{2,1,0:T(8,128)(2,1)S(1)} %get-tuple-element.255), channel_id=1, source_target_pairs={{0,8},{4,12},{8,0},{12,4},{16,24},{20,28},{24,16},{28,20},{1,9},{5... | collective-permute-start | bytes 786440 | tf_op jit(solution)/shard_map/ppermute | solution.py:21
  82.6 13.5 %collective-permute-start.28 = (bf16[8,272,128]{2,1,0:T(8,128)(2,1)S(1)}, bf16[8,272,128]{2,1,0:T(8,128)(2,1)S(1)}, u32[]{:S(2)}, u32[]{:S(2)}) collective-permute-start(bf16[8,272,128]{2,1,0:T(8,128)(2,1)S(1)} %get-tuple-element.258), channel_id=1, source_target_pairs={{0,2},{1,3},{2,0},{3,1},{4,6},{5,7},{6,4},{7,5},{8,10},{9,11},{10,... | collective-permute-start | bytes 1671176 | tf_op jit(solution)/shard_map/ppermute | solution.py:21
  83.2 5.0 %collective-permute-start.31 = (bf16[2,64,512]{2,1,0:T(8,128)(2,1)S(1)}, bf16[2,64,512]{2,1,0:T(8,128)(2,1)S(1)}, u32[]{:S(2)}, u32[]{:S(2)}) collective-permute-start(bf16[2,64,512]{2,1,0:T(8,128)(2,1)S(1)} %get-tuple-element.263), channel_id=1, source_target_pairs={{0,8},{4,12},{8,0},{12,4},{16,24},{20,28},{24,16},{28,20},{1,9},{5... | collective-permute-start | bytes 393224 | tf_op jit(solution)/shard_map/ppermute | solution.py:21
  84.5 5.0 %collective-permute-start.32 = (bf16[2,64,512]{2,1,0:T(8,128)(2,1)S(1)}, bf16[2,64,512]{2,1,0:T(8,128)(2,1)S(1)}, u32[]{:S(2)}, u32[]{:S(2)}) collective-permute-start(bf16[2,64,512]{2,1,0:T(8,128)(2,1)S(1)} %get-tuple-element.265), channel_id=1, source_target_pairs={{0,4},{4,0},{8,12},{12,8},{16,20},{20,16},{24,28},{28,24},{1,5},{5... | collective-permute-start | bytes 393224 | tf_op jit(solution)/shard_map/ppermute | solution.py:21
  89.5 12.5 %collective-permute-start.33 = (bf16[2,2,64,512]{3,2,1,0:T(8,128)(2,1)S(1)}, bf16[2,2,64,512]{3,2,1,0:T(8,128)(2,1)S(1)}, u32[]{:S(2)}, u32[]{:S(2)}) collective-permute-start(bf16[2,2,64,512]{3,2,1,0:T(8,128)(2,1)S(1)} %join.1.refs_0_), channel_id=1, source_target_pairs={{0,16},{4,20},{8,24},{12,28},{16,0},{20,4},{24,8},{28,12},{1,17},{... | collective-permute-start | bytes 786440 | tf_op jit(solution)/shard_map/ppermute | solution.py:21
  96.2 7.2 %collective-permute-start.29 = (bf16[2,272,128]{2,1,0:T(8,128)(2,1)S(1)}, bf16[2,272,128]{2,1,0:T(8,128)(2,1)S(1)}, u32[]{:S(2)}, u32[]{:S(2)}) collective-permute-start(bf16[2,272,128]{2,1,0:T(8,128)(2,1)S(1)} %get-tuple-element.260), channel_id=1, source_target_pairs={{0,4},{4,0},{8,12},{12,8},{16,20},{20,16},{24,28},{28,24},{1,5},{5... | collective-permute-start | bytes 417800 | tf_op jit(solution)/shard_map/ppermute | solution.py:21
  97.8 5.7 %collective-permute-start.30 = (bf16[2,272,128]{2,1,0:T(8,128)(2,1)S(1)}, bf16[2,272,128]{2,1,0:T(8,128)(2,1)S(1)}, u32[]{:S(2)}, u32[]{:S(2)}) collective-permute-start(bf16[2,272,128]{2,1,0:T(8,128)(2,1)S(1)} %get-tuple-element.261), channel_id=1, source_target_pairs={{0,4},{4,0},{8,12},{12,8},{16,20},{20,16},{24,28},{28,24},{1,5},{5... | collective-permute-start | bytes 417800 | tf_op jit(solution)/shard_map/ppermute | solution.py:21
  98.3 20.9 %collective-permute-start.40 = (bf16[4,64,512]{2,1,0:T(8,128)(2,1)S(1)}, bf16[4,64,512]{2,1,0:T(8,128)(2,1)S(1)}, u32[]{:S(2)}, u32[]{:S(2)}) collective-permute-start(bf16[4,64,512]{2,1,0:T(8,128)(2,1)S(1)} %get-tuple-element.274), channel_id=1, source_target_pairs={{0,1},{1,0},{2,3},{3,2},{4,5},{5,4},{6,7},{7,6},{8,9},{9,8},{10,11... | collective-permute-start | bytes 786440 | tf_op jit(solution)/shard_map/ppermute | solution.py:21
  102.1 17.2 %collective-permute-start.41 = (bf16[8,64,512]{2,1,0:T(8,128)(2,1)S(1)}, bf16[8,64,512]{2,1,0:T(8,128)(2,1)S(1)}, u32[]{:S(2)}, u32[]{:S(2)}) collective-permute-start(bf16[8,64,512]{2,1,0:T(8,128)(2,1)S(1)} %get-tuple-element.275), channel_id=1, source_target_pairs={{0,2},{1,3},{2,0},{3,1},{4,6},{5,7},{6,4},{7,5},{8,10},{9,11},{10,... | collective-permute-start | bytes 1572872 | tf_op jit(solution)/shard_map/ppermute | solution.py:21
  103.6 6.1 %collective-permute-start.36 = (bf16[2,64,512]{2,1,0:T(8,128)(2,1)S(1)}, bf16[2,64,512]{2,1,0:T(8,128)(2,1)S(1)}, u32[]{:S(2)}, u32[]{:S(2)}) collective-permute-start(bf16[2,64,512]{2,1,0:T(8,128)(2,1)S(1)} %get-tuple-element.271.refs_3_), channel_id=1, source_target_pairs={{0,8},{4,12},{8,0},{12,4},{16,24},{20,28},{24,16},{28,20},{1,9},{5... | collective-permute-start | bytes 393224 | tf_op jit(solution)/shard_map/ppermute | solution.py:21
  104.3 6.9 %collective-permute-start.38 = (bf16[2,64,512]{2,1,0:T(8,128)(2,1)S(1)}, bf16[2,64,512]{2,1,0:T(8,128)(2,1)S(1)}, u32[]{:S(2)}, u32[]{:S(2)}) collective-permute-start(bf16[2,64,512]{2,1,0:T(8,128)(2,1)S(1)} %get-tuple-element.272), channel_id=1, source_target_pairs={{0,4},{4,0},{8,12},{12,8},{16,20},{20,16},{24,28},{28,24},{1,5},{5... | collective-permute-start | bytes 393224 | tf_op jit(solution)/shard_map/ppermute | solution.py:21
  105.9 6.1 %collective-permute-start.34 = (bf16[2,272,128]{2,1,0:T(8,128)(2,1)S(1)}, bf16[2,272,128]{2,1,0:T(8,128)(2,1)S(1)}, u32[]{:S(2)}, u32[]{:S(2)}) collective-permute-start(bf16[2,272,128]{2,1,0:T(8,128)(2,1)S(1)} %get-tuple-element.270), channel_id=1, source_target_pairs={{0,8},{4,12},{8,0},{12,4},{16,24},{20,28},{24,16},{28,20},{1,9},{5... | collective-permute-start | bytes 417800 | tf_op jit(solution)/shard_map/ppermute | solution.py:21
  109.7 9.6 %collective-permute-start.37 = (bf16[4,64,512]{2,1,0:T(8,128)(2,1)S(1)}, bf16[4,64,512]{2,1,0:T(8,128)(2,1)S(1)}, u32[]{:S(2)}, u32[]{:S(2)}) collective-permute-start(bf16[4,64,512]{2,1,0:T(8,128)(2,1)S(1)} %constant_dynamic-update-slice_fusion.refs_0_), channel_id=1, source_target_pairs={{0,4},{4,0},{8,12},{12,8},{16,20},{20,16},{24,28},{28,24},{1,5},{5... | collective-permute-start | bytes 786440 | tf_op jit(solution)/shard_map/ppermute | solution.py:21
  111.3 8.5 %collective-permute-start.39 = (bf16[4,64,512]{2,1,0:T(8,128)(2,1)S(1)}, bf16[4,64,512]{2,1,0:T(8,128)(2,1)S(1)}, u32[]{:S(2)}, u32[]{:S(2)}) collective-permute-start(bf16[4,64,512]{2,1,0:T(8,128)(2,1)S(1)} %constant_dynamic-update-slice_fusion.2.refs_2_), channel_id=1, source_target_pairs={{0,8},{4,12},{8,0},{12,4},{16,24},{20,28},{24,16},{28,20},{1,9},{5... | collective-permute-start | bytes 786440 | tf_op jit(solution)/shard_map/ppermute | solution.py:21
  112.1 7.1 %collective-permute-start.35 = (bf16[2,272,128]{2,1,0:T(8,128)(2,1)S(1)}, bf16[2,272,128]{2,1,0:T(8,128)(2,1)S(1)}, u32[]{:S(2)}, u32[]{:S(2)}) collective-permute-start(bf16[2,272,128]{2,1,0:T(8,128)(2,1)S(1)} %add_whole.1.refs_0_), channel_id=1, source_target_pairs={{0,16},{4,20},{8,24},{12,28},{16,0},{20,4},{24,8},{28,12},{1,17},{... | collective-permute-start | bytes 417800 | tf_op jit(solution)/shard_map/ppermute | solution.py:21
  119.7 6.7 %collective-permute-start.43 = (bf16[2,272,128]{2,1,0:T(8,128)(2,1)S(1)}, bf16[2,272,128]{2,1,0:T(8,128)(2,1)S(1)}, u32[]{:S(2)}, u32[]{:S(2)}) collective-permute-start(bf16[2,272,128]{2,1,0:T(8,128)(2,1)S(1)} %meet.3), channel_id=1, source_target_pairs={{0,8},{4,12},{8,0},{12,4},{16,24},{20,28},{24,16},{28,20},{1,9},{5... | collective-permute-start | bytes 417800 | tf_op jit(solution)/shard_map/ppermute | solution.py:21
  126.5 6.6 %collective-permute-start.44 = (bf16[4,272,128]{2,1,0:T(8,128)(2,1)S(1)}, bf16[4,272,128]{2,1,0:T(8,128)(2,1)S(1)}, u32[]{:S(2)}, u32[]{:S(2)}) collective-permute-start(bf16[4,272,128]{2,1,0:T(8,128)(2,1)S(1)} %constant_dynamic-update-slice_fusion.4.refs_0_), channel_id=1, source_target_pairs={{0,4},{4,0},{8,12},{12,8},{16,20},{20,16},{24,28},{28,24},{1,5},{5... | collective-permute-start | bytes 835592 | tf_op jit(solution)/shard_map/ppermute | solution.py:21
  127.4 1.8 %collective-permute-start.42 = (bf16[4,64,512]{2,1,0:T(8,128)(2,1)S(1)}, bf16[4,64,512]{2,1,0:T(8,128)(2,1)S(1)}, u32[]{:S(2)}, u32[]{:S(2)}) collective-permute-start(bf16[4,64,512]{2,1,0:T(8,128)(2,1)S(1)} %slice.11), channel_id=1, source_target_pairs={{0,1},{1,0},{2,3},{3,2},{4,5},{5,4},{6,7},{7,6},{8,9},{9,8},{10,11... | collective-permute-start | bytes 786440 | tf_op jit(solution)/shard_map/ppermute | solution.py:21
  (10 other events, 120.0 us)

commit v5 on v4

--- a/solution.py
+++ b/solution.py
@@ -257,12 +257,15 @@
         token_parts = token_parts[:1] + send_rows(sends[0], sends[1:])
         bundle_core, bundle_y = mp_swap(bundle, 1), over_y(bundle_half)
 
-        bundle_y, token_parts, cot_parts = together(bundle_y, token_parts, cot_parts)
+        near = [w_up, w_down]
+        near_core = [mp_swap(v, 1) for v in near]
+        bundle_y, (bundle_core,), token_parts[:2], half_parts, cot_parts, near_core = together(
+            bundle_y, [bundle_core], token_parts[:2], half_parts, cot_parts, near_core
+        )
         halves_y = [over_y(v) for v in half_parts]
-        token_parts = token_parts[:2] + pass_rows(token_parts[2:])
-        bundle_y, token_parts = together(bundle_y, token_parts)
         bundle_x = [dp_swap(v, 1) for v in bundle_y]
         bundle_yc = [mp_swap(v, 1) for v in bundle_y]
+        token_parts = token_parts[:2] + pass_rows(token_parts[2:])
 
         def far(first, second, first_core, second_core):
             return [
@@ -390,9 +393,9 @@
 
         x, a1, qkv0, p0, att0, wq0, wo0, small0 = attend(groups[0], True, [bundle, bundle_core])
 
-        bundle_x, (att0,), near = together(bundle_x, [att0], [w_up, w_down])
+        bundle_x, (att0,), sends = together(bundle_x, [att0], cot_parts[1:])
+        cot_parts = cot_parts[:1] + send_rows(sends[0], sends[1:])
         bundle_xc = [mp_swap(v, 1) for v in bundle_x]
-        near_core = [mp_swap(v, 1) for v in near]
         qkv1, p1, att1, wq1, wo1, small1 = attend(
             groups[1], False, far(bundle_y, bundle_x, bundle_yc, bundle_xc)
         )
@@ -404,12 +407,9 @@
         if joined:
             pairs = [run("take_apart", take_apart, [v], half_shapes, after=[att1]) for v in halves_y[0]]
             halves_y = list(zip(*pairs))
-        up_y, down_y, (att1,), near_core, sends = together(
-            *halves_y, [att1], near_core, cot_parts[1:]
-        )
+        up_y, down_y, (att1,), cot_parts[1:2] = together(*halves_y, [att1], cot_parts[1:2])
         up_x, down_z = [dp_swap(v, 1) for v in up_y], [dp_swap(v, 2) for v in down_y]
-        cot_parts = cot_parts[:1] + send_rows(sends[0], sends[1:])
-        cot_parts = cot_parts[:2] + pass_rows(cot_parts[2:])
+        up_yc, down_yc = ([mp_swap(v, 1) for v in vs] for vs in (up_y, down_y))
 
         def scatter(dst, src, block, which, dpi):
             for p in range(n_dp):
@@ -476,6 +476,9 @@
             [full, full_bf, turned, full]
             + [shape((len(g0), count, hid), BF16), shape((len(g0), count, hid), F32)],
         )
+
+        cot_parts[2:], (a2,) = together(cot_parts[2:], [a2])
+        cot_parts = cot_parts[:2] + pass_rows(cot_parts[2:])
 
         def mlp_near_backward(ins, outs, scratch):
             dpi = lax.axis_index("dp")
@@ -509,11 +512,8 @@
             [pltpu.VMEM((2, width, hid), BF16)] * len(g0),
         )
 
-        far_parts = together(up_y, up_x, down_y, down_z, [mixed])
-        up_y, up_x, down_y, down_z, (mixed,) = far_parts
-        up_yc, up_xc, down_yc, down_zc = (
-            [mp_swap(v, 1) for v in vs] for vs in (up_y, up_x, down_y, down_z)
-        )
+        up_yc, up_x, down_yc, down_z, (gub0,) = together(up_yc, up_x, down_yc, down_z, [gub0])
+        up_xc, down_zc = ([mp_swap(v, 1) for v in vs] for vs in (up_x, down_z))
         got0 = mp_swap(send0, 1)
 
         up1 = far(up_y, up_x, up_yc, up_xc)

time: 135 us -> 127 us (0.941)
  waiting for transfers between devices: 50.2 us -> 40.7 us
  starting transfers between devices: 42.8 us -> 45.2 us
    ppermute x45, waiting for transfers between devices: 50.2 us -> 40.7 us  [swap(): return lax.ppermute(v, axis, [(i, i ^ bit) for i in range(size)])]
    ppermute x45, starting transfers between devices: 42.8 us -> 45.2 us  [swap(): return lax.ppermute(v, axis, [(i, i ^ bit) for i in range(size)])]
  transfers between devices with their start and end apart: 45 -> 45, of which waited for: 23 -> 20; matrix products, arithmetic and copies ran while one was open for 0% -> 0% of each run, Pallas kernels for 23% -> 24%
where the time goes in v5:
time: 127 us
  starting transfers between devices  45.2 us (36%)
  waiting for transfers between devices  40.7 us (32%)
  Pallas kernels  35.9 us (28%)
  local copies, waits for them, and re-layouts  4.22 us (3%)
    ppermute x45, starting transfers between devices, swap(): return lax.ppermute(v, axis, [(i, i ^ bit) for i in range(size)])  45.2 us
    ppermute x45, waiting for transfers between devices, swap(): return lax.ppermute(v, axis, [(i, i ^ bit) for i in range(size)])  40.7 us
    pallas_call x26, Pallas kernels, run(): pl.pallas_call(kernel, out_shape=tuple(outs), in_specs=[pl.BlockSpec(memo...  35.9 us
    unnamed x29, local copies, waits for them, and re-layouts  4.15 us
  transfers between devices with their start and end apart: 45, of which 20 were waited for; matrix products, arithmetic and copies ran while one was open for 0% of the time, Pallas kernels for 24%

profile of v5, /device:TPU:0, one launch (start us, length us, event | category | flops | bytes accessed | tf_op | source)
XLA Modules:
  0.0 127.1 jit_solution(16589543911184633105)
XLA Ops:
  0.7 3.3 %begin.1 = (bf16[2,64,512]{2,1,0:T(8,128)(2,1)}, bf16[2,64,512]{2,1,0:T(8,128)(2,1)}, bf16[4,64,512]{2,1,0:T(8,128)(2,1)}, bf16[2080,128]{1,0:T(8,128)(2,1)}, bf16[1040,128]{1,0:T(8,128)(2,1)}) custom-call(bf16[8,64,512]{2,1,0:T(8,128)(2,1)} %refs_0_.4, bf16[1536,128]{1,0:T(8,128)(2,1)} %bitcast.5, bf16[128,512]{1,0:T(8,128)(2,1)} %refs_2_.3, ...), custom_call_target="tpu_custom_call" | custom-call | flops 1 | bytes 1 | tf_op jit(solution)/shard_map/begin/pallas_call | solution.py:43
  5.0 2.6 %collective-permute-start = (bf16[1040,128]{1,0:T(8,128)(2,1)}, bf16[1040,128]{1,0:T(8,128)(2,1)S(1)}, u32[]{:S(2)}, u32[]{:S(2)}) collective-permute-start(bf16[1040,128]{1,0:T(8,128)(2,1)} %get-tuple-element.155.refs_3_), channel_id=1, source_target_pairs={{0,2},{1,3},{2,0},{3,1},{4,6},{5,7},{6,4},{7,5},{8,10},{9,11},{10,... | collective-permute-start | bytes 798728 | tf_op jit(solution)/shard_map/ppermute | solution.py:21
  7.8 1.4 %collective-permute-done.2.refs_1_ = bf16[2,64,512]{2,1,0:T(8,128)(2,1)S(1)} collective-permute-done((bf16[2,64,512]{2,1,0:T(8,128)(2,1)}, bf16[2,64,512]{2,1,0:T(8,128)(2,1)S(1)}, u32[]{:S(2)}, u32[]{:S(2)}) %collective-permute-start.2) | collective-permute-done | bytes 131104 | tf_op jit(solution)/shard_map/ppermute | solution.py:21
  9.1 1.7 %collective-permute-start.5 = (bf16[4,64,512]{2,1,0:T(8,128)(2,1)}, bf16[4,64,512]{2,1,0:T(8,128)(2,1)S(1)}, u32[]{:S(2)}, u32[]{:S(2)}) collective-permute-start(bf16[4,64,512]{2,1,0:T(8,128)(2,1)} %get-tuple-element.165), channel_id=1, source_target_pairs={{0,2},{1,3},{2,0},{3,1},{4,6},{5,7},{6,4},{7,5},{8,10},{9,11},{10,... | collective-permute-start | bytes 786440 | tf_op jit(solution)/shard_map/ppermute | solution.py:21
  15.7 1.6 %collective-permute-start.7 = (bf16[1040,128]{1,0:T(8,128)(2,1)S(1)}, bf16[1040,128]{1,0:T(8,128)(2,1)S(1)}, u32[]{:S(2)}, u32[]{:S(2)}) collective-permute-start(bf16[1040,128]{1,0:T(8,128)(2,1)S(1)} %collective-permute-done.refs_3_), channel_id=1, source_target_pairs={{0,4},{4,0},{8,12},{12,8},{16,20},{20,16},{24,28},{28,24},{1,5},{5... | collective-permute-start | bytes 798728 | tf_op jit(solution)/shard_map/ppermute | solution.py:21
  17.3 1.3 %collective-permute-start.8 = (bf16[2,256,512]{2,1,0:T(8,128)(2,1)S(1)}, bf16[2,256,512]{2,1,0:T(8,128)(2,1)S(1)}, u32[]{:S(2)}, u32[]{:S(2)}) collective-permute-start(bf16[2,256,512]{2,1,0:T(8,128)(2,1)S(1)} %get-tuple-element.174), channel_id=1, source_target_pairs={{0,2},{1,3},{2,0},{3,1},{4,6},{5,7},{6,4},{7,5},{8,10},{9,11},{10,... | collective-permute-start | bytes 1572872 | tf_op jit(solution)/shard_map/ppermute | solution.py:21
  18.6 2.1 %collective-permute-done.5.refs_2_ = bf16[4,64,512]{2,1,0:T(8,128)(2,1)S(1)} collective-permute-done((bf16[4,64,512]{2,1,0:T(8,128)(2,1)}, bf16[4,64,512]{2,1,0:T(8,128)(2,1)S(1)}, u32[]{:S(2)}, u32[]{:S(2)}) %collective-permute-start.5) | collective-permute-done | bytes 262176 | tf_op jit(solution)/shard_map/ppermute | solution.py:21
  22.2 3.3 %attend.2 = (bf16[512,512]{1,0:T(8,128)(2,1)S(1)}, bf16[512,512]{1,0:T(8,128)(2,1)S(1)}, bf16[3,512,256]{2,1,0:T(8,128)(2,1)S(1)}, bf16[8,256,256]{2,1,0:T(8,128...) custom-call(bf16[2,64,512]{2,1,0:T(8,128)(2,1)S(1)} %copy-done.7, ...), custom_call_target="tpu_custom_call" | custom-call | flops 1 | bytes 1 | tf_op jit(solution)/shard_map/attend/pallas_call | solution.py:43
  25.8 2.0 %collective-permute-start.12 = (bf16[4,64,512]{2,1,0:T(8,128)(2,1)S(1)}, bf16[4,64,512]{2,1,0:T(8,128)(2,1)S(1)}, u32[]{:S(2)}, u32[]{:S(2)}) collective-permute-start(bf16[4,64,512]{2,1,0:T(8,128)(2,1)S(1)} %get-tuple-element.187), channel_id=1, source_target_pairs={{0,2},{1,3},{2,0},{3,1},{4,6},{5,7},{6,4},{7,5},{8,10},{9,11},{10,... | collective-permute-start | bytes 786440 | tf_op jit(solution)/shard_map/ppermute | solution.py:21
  27.8 3.1 %attend.3 = (bf16[3,512,256]{2,1,0:T(8,128)(2,1)S(1)}, bf16[8,256,256]{2,1,0:T(8,128)(2,1)S(1)}, bf16[512,256]{1,0:T(8,128)(2,1)S(1)}, bf16[1536,256]{1,0:T(8,12...) custom-call(s32[8]{0:T(128)S(1)} %copy-done.12, s32[8,256]{1,0:T(8,128)S(1)} %copy-done.9, ...), custom_call_target="tpu_custom_call" | custom-call | flops 1 | bytes 1 | tf_op jit(solution)/shard_map/attend/pallas_call | solution.py:43
  30.9 1.2 collective-permute-done.8.refs_0_
  32.3 1.8 %collective-permute-start.15 = (bf16[256,512]{1,0:T(8,128)(2,1)S(1)}, bf16[256,512]{1,0:T(8,128)(2,1)S(1)}, u32[]{:S(2)}, u32[]{:S(2)}) collective-permute-start(bf16[256,512]{1,0:T(8,128)(2,1)S(1)} %get-tuple-element.201.refs_10_), channel_id=1, source_target_pairs={{0,4},{4,0},{8,12},{12,8},{16,20},{20,16},{24,28},{28,24},{1,5},{5... | collective-permute-start | bytes 786440 | tf_op jit(solution)/shard_map/ppermute | solution.py:21
  34.2 1.6 %collective-permute-start.17 = (bf16[256,512]{1,0:T(8,128)(2,1)S(1)}, bf16[256,512]{1,0:T(8,128)(2,1)S(1)}, u32[]{:S(2)}, u32[]{:S(2)}) collective-permute-start(bf16[256,512]{1,0:T(8,128)(2,1)S(1)} %get-tuple-element.202.refs_12_), channel_id=1, source_target_pairs={{0,8},{4,12},{8,0},{12,4},{16,24},{20,28},{24,16},{28,20},{1,9},{5... | collective-permute-start | bytes 786440 | tf_op jit(solution)/shard_map/ppermute | solution.py:21
  35.8 2.7 %mlp_near_forward.1 = (f32[512,512]{1,0:T(8,128)S(1)}, bf16[512,512]{1,0:T(8,128)(2,1)S(1)}, bf16[512,512]{1,0:T(8,128)(2,1)S(1)}, f32[512,512]{1,0:T(8,128)S(1)...) custom-call(bf16[512,512]{1,0:T(8,128)(2,1)S(1)} %get-tuple-element.167.refs_0_.refs_3_, ...), custom_call_target="tpu_custom_call" | custom-call | flops 1 | bytes 1 | tf_op jit(solution)/shard_map/mlp_near_forward/pallas_call | solution.py:43
  38.6 1.3 %collective-permute-done.13.refs_6_ = bf16[2,64,512]{2,1,0:T(8,128)(2,1)S(1)} collective-permute-done((bf16[2,64,512]{2,1,0:T(8,128)(2,1)S(1)}, bf16[2,64,512]{2,1,0:T(8,128)(2,1)S(1)}, u32[]{:S(2)}, u32[]{:S(2)}) %collective-permute-start.13) | collective-permute-done | bytes 131104 | tf_op jit(solution)/shard_map/ppermute | solution.py:21
  39.9 2.5 %mlp_near_backward.1 = (bf16[512,512]{1,0:T(8,128)(2,1)S(1)}, bf16[512,512]{1,0:T(8,128)(2,1)S(1)}, f32[512,512]{1,0:T(8,128)S(1)}, bf16[1,2,8,64,512]{4,3,2,1,0...) custom-call(bf16[2,512,512]{2,1,0:T(8,128)(2,1)S(1)} %get-tuple-element.191.refs_0_, ...), custom_call_target="tpu_custom_call" | custom-call | flops 1 | bytes 1 | tf_op jit(solution)/shard_map/mlp_near_backward/pallas_call | solution.py:43
  44.6 2.1 %mlp_far.2 = (f32[512,512]{1,0:T(8,128)S(1)}, f32[512,512]{1,0:T(8,128)S(1)}, bf16[1,2,8,64,512]{4,3,2,1,0:T(8,128)(2,1)S(1)}, f32[1,1,512]{2,1,0:T(1,128)S(1)}) custom-call(f32[512,512]{1,0:T(8,128)S(1)} %get-tuple-element.186.refs_0_, bf16[512,512]{1,0:T(8,128)(2,1)S(1)} %get-tuple-element.189.refs_1_, bf16[512,512]{1,0:T(8,128)(2,1)S(1)} %get-tuple-element.190.refs_2_, ...), custom_call_target="tpu_custom_call" | custom-call | flops 1 | bytes 1 | tf_op jit(solution)/shard_map/mlp_far/pallas_call | solution.py:43
  47.0 3.1 %mlp_far.3 = (bf16[512,512]{1,0:T(8,128)(2,1)S(1)}, f32[512,512]{1,0:T(8,128)S(1)}, bf16[512,512]{1,0:T(8,128)(2,1)S(1)}, f32[4,512]{1,0:T(4,128)S(1)}, bf16[1,2...) custom-call(f32[512,512]{1,0:T(8,128)S(1)} %get-tuple-element.186.refs_0_, ...), custom_call_target="tpu_custom_call" | custom-call | flops 1 | bytes 1 | tf_op jit(solution)/shard_map/mlp_far/pallas_call | solution.py:43
  51.1 1.7 %collective-permute-start.23 = (bf16[8,64,512]{2,1,0:T(8,128)(2,1)S(1)}, bf16[8,64,512]{2,1,0:T(8,128)(2,1)S(1)}, u32[]{:S(2)}, u32[]{:S(2)}) collective-permute-start(bf16[8,64,512]{2,1,0:T(8,128)(2,1)S(1)} %get-tuple-element.237), channel_id=1, source_target_pairs={{0,2},{1,3},{2,0},{3,1},{4,6},{5,7},{6,4},{7,5},{8,10},{9,11},{10,... | collective-permute-start | bytes 1572872 | tf_op jit(solution)/shard_map/ppermute | solution.py:21
  52.8 9.3 %attend_back.1 = (bf16[4,64,512]{2,1,0:T(8,128)(2,1)S(1)}, bf16[4,64,512]{2,1,0:T(8,128)(2,1)S(1)}, bf16[8,64,512]{2,1,0:T(8,128)(2,1)S(1)}, bf16[1,8,272,128]{3...) custom-call(s32[8]{0:T(128)S(1)} %copy-done.12, ...), custom_call_target="tpu_custom_call" | custom-call | flops 1 | bytes 1 | tf_op jit(solution)/shard_map/attend_back/pallas_call | solution.py:43
  62.1 2.8 %collective-permute-done.22.refs_1_ = bf16[2,4,64,512]{3,2,1,0:T(8,128)(2,1)S(1)} collective-permute-done((bf16[2,4,64,512]{3,2,1,0:T(8,128)(2,1)S(1)}, bf16[2,4,64,512]{3,2,1,0:T(8,128)(2,1)S(1)}, u32[]{:S(2)}, u32[]{:S(2)}) %collective-permute-start.22) | collective-permute-done | bytes 524320 | tf_op jit(solution)/shard_map/ppermute | solution.py:21
  65.7 1.6 %collective-permute-start.26 = (bf16[4,64,512]{2,1,0:T(8,128)(2,1)S(1)}, bf16[4,64,512]{2,1,0:T(8,128)(2,1)S(1)}, u32[]{:S(2)}, u32[]{:S(2)}) collective-permute-start(bf16[4,64,512]{2,1,0:T(8,128)(2,1)S(1)} %get-tuple-element.246), channel_id=1, source_target_pairs={{0,2},{1,3},{2,0},{3,1},{4,6},{5,7},{6,4},{7,5},{8,10},{9,11},{10,... | collective-permute-start | bytes 786440 | tf_op jit(solution)/shard_map/ppermute | solution.py:21
  67.4 1.6 %collective-permute-start.27 = (bf16[4,64,512]{2,1,0:T(8,128)(2,1)S(1)}, bf16[4,64,512]{2,1,0:T(8,128)(2,1)S(1)}, u32[]{:S(2)}, u32[]{:S(2)}) collective-permute-start(bf16[4,64,512]{2,1,0:T(8,128)(2,1)S(1)} %get-tuple-element.249), channel_id=1, source_target_pairs={{0,8},{4,12},{8,0},{12,4},{16,24},{20,28},{24,16},{28,20},{1,9},{5... | collective-permute-start | bytes 786440 | tf_op jit(solution)/shard_map/ppermute | solution.py:21
  68.9 5.1 %collective-permute-done.26.refs_1_ = bf16[4,64,512]{2,1,0:T(8,128)(2,1)S(1)} collective-permute-done((bf16[4,64,512]{2,1,0:T(8,128)(2,1)S(1)}, bf16[4,64,512]{2,1,0:T(8,128)(2,1)S(1)}, u32[]{:S(2)}, u32[]{:S(2)}) %collective-permute-start.26) | collective-permute-done | bytes 262176 | tf_op jit(solution)/shard_map/ppermute | solution.py:21
  74.1 1.3 %collective-permute-done.27.refs_1_ = bf16[4,64,512]{2,1,0:T(8,128)(2,1)S(1)} collective-permute-done((bf16[4,64,512]{2,1,0:T(8,128)(2,1)S(1)}, bf16[4,64,512]{2,1,0:T(8,128)(2,1)S(1)}, u32[]{:S(2)}, u32[]{:S(2)}) %collective-permute-start.27) | collective-permute-done | bytes 262176 | tf_op jit(solution)/shard_map/ppermute | solution.py:21
  76.2 1.7 %collective-permute-start.31 = (bf16[2,64,512]{2,1,0:T(8,128)(2,1)S(1)}, bf16[2,64,512]{2,1,0:T(8,128)(2,1)S(1)}, u32[]{:S(2)}, u32[]{:S(2)}) collective-permute-start(bf16[2,64,512]{2,1,0:T(8,128)(2,1)S(1)} %get-tuple-element.257), channel_id=1, source_target_pairs={{0,8},{4,12},{8,0},{12,4},{16,24},{20,28},{24,16},{28,20},{1,9},{5... | collective-permute-start | bytes 393224 | tf_op jit(solution)/shard_map/ppermute | solution.py:21
  77.9 1.5 %collective-permute-start.32 = (bf16[2,64,512]{2,1,0:T(8,128)(2,1)S(1)}, bf16[2,64,512]{2,1,0:T(8,128)(2,1)S(1)}, u32[]{:S(2)}, u32[]{:S(2)}) collective-permute-start(bf16[2,64,512]{2,1,0:T(8,128)(2,1)S(1)} %get-tuple-element.259), channel_id=1, source_target_pairs={{0,4},{4,0},{8,12},{12,8},{16,20},{20,16},{24,28},{28,24},{1,5},{5... | collective-permute-start | bytes 393224 | tf_op jit(solution)/shard_map/ppermute | solution.py:21
  79.4 1.8 %collective-permute-done.31.refs_1_ = bf16[2,64,512]{2,1,0:T(8,128)(2,1)S(1)} collective-permute-done((bf16[2,64,512]{2,1,0:T(8,128)(2,1)S(1)}, bf16[2,64,512]{2,1,0:T(8,128)(2,1)S(1)}, u32[]{:S(2)}, u32[]{:S(2)}) %collective-permute-start.31) | collective-permute-done | bytes 131104 | tf_op jit(solution)/shard_map/ppermute | solution.py:21
  81.2 1.7 %collective-permute-done.32.refs_3_ = bf16[2,64,512]{2,1,0:T(8,128)(2,1)S(1)} collective-permute-done((bf16[2,64,512]{2,1,0:T(8,128)(2,1)S(1)}, bf16[2,64,512]{2,1,0:T(8,128)(2,1)S(1)}, u32[]{:S(2)}, u32[]{:S(2)}) %collective-permute-start.32) | collective-permute-done | bytes 131104 | tf_op jit(solution)/shard_map/ppermute | solution.py:21
  82.9 2.7 %collective-permute-start.33 = (bf16[2,2,64,512]{3,2,1,0:T(8,128)(2,1)S(1)}, bf16[2,2,64,512]{3,2,1,0:T(8,128)(2,1)S(1)}, u32[]{:S(2)}, u32[]{:S(2)}) collective-permute-start(bf16[2,2,64,512]{3,2,1,0:T(8,128)(2,1)S(1)} %join.1.refs_0_), channel_id=1, source_target_pairs={{0,16},{4,20},{8,24},{12,28},{16,0},{20,4},{24,8},{28,12},{1,17},{... | collective-permute-start | bytes 786440 | tf_op jit(solution)/shard_map/ppermute | solution.py:21
  85.6 3.7 %collective-permute-done.28.refs_1_ = bf16[8,272,128]{2,1,0:T(8,128)(2,1)S(1)} collective-permute-done((bf16[8,272,128]{2,1,0:T(8,128)(2,1)S(1)}, bf16[8,272,128]{2,1,0:T(8,128)(2,1)S(1)}, u32[]{:S(2)}, u32[]{:S(2)}) %collective-permute-start.28) | collective-permute-done | bytes 557088 | tf_op jit(solution)/shard_map/ppermute | solution.py:21
  89.4 1.6 %collective-permute-start.29 = (bf16[2,272,128]{2,1,0:T(8,128)(2,1)S(1)}, bf16[2,272,128]{2,1,0:T(8,128)(2,1)S(1)}, u32[]{:S(2)}, u32[]{:S(2)}) collective-permute-start(bf16[2,272,128]{2,1,0:T(8,128)(2,1)S(1)} %get-tuple-element.254), channel_id=1, source_target_pairs={{0,4},{4,0},{8,12},{12,8},{16,20},{20,16},{24,28},{28,24},{1,5},{5... | collective-permute-start | bytes 417800 | tf_op jit(solution)/shard_map/ppermute | solution.py:21
  91.5 3.5 %collective-permute-done.33.refs_1_ = bf16[2,2,64,512]{3,2,1,0:T(8,128)(2,1)S(1)} collective-permute-done((bf16[2,2,64,512]{3,2,1,0:T(8,128)(2,1)S(1)}, bf16[2,2,64,512]{3,2,1,0:T(8,128)(2,1)S(1)}, u32[]{:S(2)}, u32[]{:S(2)}) %collective-permute-start.33) | collective-permute-done | bytes 262176 | tf_op jit(solution)/shard_map/ppermute | solution.py:21
  95.1 1.7 %collective-permute-start.41 = (bf16[8,64,512]{2,1,0:T(8,128)(2,1)S(1)}, bf16[8,64,512]{2,1,0:T(8,128)(2,1)S(1)}, u32[]{:S(2)}, u32[]{:S(2)}) collective-permute-start(bf16[8,64,512]{2,1,0:T(8,128)(2,1)S(1)} %get-tuple-element.269), channel_id=1, source_target_pairs={{0,2},{1,3},{2,0},{3,1},{4,6},{5,7},{6,4},{7,5},{8,10},{9,11},{10,... | collective-permute-start | bytes 1572872 | tf_op jit(solution)/shard_map/ppermute | solution.py:21
  97.7 1.6 %collective-permute-start.38 = (bf16[2,64,512]{2,1,0:T(8,128)(2,1)S(1)}, bf16[2,64,512]{2,1,0:T(8,128)(2,1)S(1)}, u32[]{:S(2)}, u32[]{:S(2)}) collective-permute-start(bf16[2,64,512]{2,1,0:T(8,128)(2,1)S(1)} %get-tuple-element.266), channel_id=1, source_target_pairs={{0,4},{4,0},{8,12},{12,8},{16,20},{20,16},{24,28},{28,24},{1,5},{5... | collective-permute-start | bytes 393224 | tf_op jit(solution)/shard_map/ppermute | solution.py:21
  99.3 1.3 %collective-permute-start.34 = (bf16[2,272,128]{2,1,0:T(8,128)(2,1)S(1)}, bf16[2,272,128]{2,1,0:T(8,128)(2,1)S(1)}, u32[]{:S(2)}, u32[]{:S(2)}) collective-permute-start(bf16[2,272,128]{2,1,0:T(8,128)(2,1)S(1)} %get-tuple-element.264), channel_id=1, source_target_pairs={{0,8},{4,12},{8,0},{12,4},{16,24},{20,28},{24,16},{28,20},{1,9},{5... | collective-permute-start | bytes 417800 | tf_op jit(solution)/shard_map/ppermute | solution.py:21
  100.6 2.2 %collective-permute-done.36 = bf16[2,64,512]{2,1,0:T(8,128)(2,1)S(1)} collective-permute-done((bf16[2,64,512]{2,1,0:T(8,128)(2,1)S(1)}, bf16[2,64,512]{2,1,0:T(8,128)(2,1)S(1)}, u32[]{:S(2)}, u32[]{:S(2)}) %collective-permute-start.36) | collective-permute-done | bytes 131104 | tf_op jit(solution)/shard_map/ppermute | solution.py:21
  102.9 1.6 %collective-permute-start.37 = (bf16[4,64,512]{2,1,0:T(8,128)(2,1)S(1)}, bf16[4,64,512]{2,1,0:T(8,128)(2,1)S(1)}, u32[]{:S(2)}, u32[]{:S(2)}) collective-permute-start(bf16[4,64,512]{2,1,0:T(8,128)(2,1)S(1)} %constant_dynamic-update-slice_fusion.refs_0_), channel_id=1, source_target_pairs={{0,4},{4,0},{8,12},{12,8},{16,20},{20,16},{24,28},{28,24},{1,5},{5... | collective-permute-start | bytes 786440 | tf_op jit(solution)/shard_map/ppermute | solution.py:21
  105.3 3.3 %collective-permute-start.35 = (bf16[2,272,128]{2,1,0:T(8,128)(2,1)S(1)}, bf16[2,272,128]{2,1,0:T(8,128)(2,1)S(1)}, u32[]{:S(2)}, u32[]{:S(2)}) collective-permute-start(bf16[2,272,128]{2,1,0:T(8,128)(2,1)S(1)} %add_whole.1.refs_0_), channel_id=1, source_target_pairs={{0,16},{4,20},{8,24},{12,28},{16,0},{20,4},{24,8},{28,12},{1,17},{... | collective-permute-start | bytes 417800 | tf_op jit(solution)/shard_map/ppermute | solution.py:21
  108.6 3.7 %collective-permute-done.35.refs_1_ = bf16[2,272,128]{2,1,0:T(8,128)(2,1)S(1)} collective-permute-done((bf16[2,272,128]{2,1,0:T(8,128)(2,1)S(1)}, bf16[2,272,128]{2,1,0:T(8,128)(2,1)S(1)}, u32[]{:S(2)}, u32[]{:S(2)}) %collective-permute-start.35) | collective-permute-done | bytes 139296 | tf_op jit(solution)/shard_map/ppermute | solution.py:21
  112.4 1.1 collective-permute-done.39.refs_3_
  113.4 2.9 %collective-permute-start.43 = (bf16[2,272,128]{2,1,0:T(8,128)(2,1)S(1)}, bf16[2,272,128]{2,1,0:T(8,128)(2,1)S(1)}, u32[]{:S(2)}, u32[]{:S(2)}) collective-permute-start(bf16[2,272,128]{2,1,0:T(8,128)(2,1)S(1)} %meet.3), channel_id=1, source_target_pairs={{0,8},{4,12},{8,0},{12,4},{16,24},{20,28},{24,16},{28,20},{1,9},{5... | collective-permute-start | bytes 417800 | tf_op jit(solution)/shard_map/ppermute | solution.py:21
  116.4 3.0 %collective-permute-done.43 = bf16[2,272,128]{2,1,0:T(8,128)(2,1)S(1)} collective-permute-done((bf16[2,272,128]{2,1,0:T(8,128)(2,1)S(1)}, bf16[2,272,128]{2,1,0:T(8,128)(2,1)S(1)}, u32[]{:S(2)}, u32[]{:S(2)}) %collective-permute-start.43) | collective-permute-done | bytes 139296 | tf_op jit(solution)/shard_map/ppermute | solution.py:21
  119.4 1.2 collective-permute-start.44
  120.8 1.7 %finish_mlp.1 = (f32[512,512]{1,0:T(8,128)}, f32[512,512]{1,0:T(8,128)}, f32[8,128]{1,0:T(8,128)S(1)}) custom-call(bf16[4,64,512]{2,1,0:T(8,128)(2,1)S(1)} %constant_dynamic-update-slice_fusion.refs_0_, bf16[4,64,512]{2,1,0:T(8,128)(2,1)S(1)} %collective-permute-done.37.refs_1_, bf16[4,64,512]{2,1,0:T(8,128)(2,1)S(1)} %constant_dynamic-update-slice_fusion.2.refs_2_, ...), custom_call_target="tpu_custom_call" | custom-call | flops 1 | bytes 1 | tf_op jit(solution)/shard_map/finish_mlp/pallas_call | solution.py:43
  122.5 1.2 gather_rows.1
  123.8 2.3 %collective-permute-done.44.refs_1_ = bf16[4,272,128]{2,1,0:T(8,128)(2,1)S(1)} collective-permute-done((bf16[4,272,128]{2,1,0:T(8,128)(2,1)S(1)}, bf16[4,272,128]{2,1,0:T(8,128)(2,1)S(1)}, u32[]{:S(2)}, u32[]{:S(2)}) %collective-permute-start.44) | collective-permute-done | bytes 278560 | tf_op jit(solution)/shard_map/ppermute | solution.py:21
  126.1 1.1 finish_att.1
  (103 shorter events, 16.1 us)
Async XLA Ops:
  0.6 21.5 %copy-start.12 = (s32[8]{0:T(128)S(1)}, s32[8]{0:T(128)}, u32[]{:S(2)}) copy-start(s32[8]{0:T(128)} %refs_0_.7) | copy-start | bytes 100
  0.7 21.5 %copy-start.9 = (s32[8,256]{1,0:T(8,128)S(1)}, s32[8,256]{1,0:T(8,128)}, u32[]{:S(2)}) copy-start(s32[8,256]{1,0:T(8,128)} %refs_1_.5) | copy-start | bytes 24580
  0.7 21.5 %copy-start.8 = (f32[2,512]{1,0:T(2,128)S(1)}, f32[2,512]{1,0:T(2,128)}, u32[]{:S(2)}) copy-start(f32[2,512]{1,0:T(2,128)} %refs_2_.5) | copy-start | bytes 12292
  4.0 11.7 %collective-permute-start.1 = (bf16[2080,128]{1,0:T(8,128)(2,1)}, bf16[2080,128]{1,0:T(8,128)(2,1)S(1)}, u32[]{:S(2)}, u32[]{:S(2)}) collective-permute-start(bf16[2080,128]{1,0:T(8,128)(2,1)} %get-tuple-element.156.refs_8_), channel_id=1, source_target_pairs={{0,1},{1,0},{2,3},{3,2},{4,5},{5,4},{6,7},{7,6},{8,9},{9,8},{10,11... | collective-permute-start | bytes 1597448 | tf_op jit(solution)/shard_map/ppermute | solution.py:21
  4.5 11.2 %collective-permute-start.3 = (bf16[512,512]{1,0:T(8,128)(2,1)}, bf16[512,512]{1,0:T(8,128)(2,1)S(1)}, u32[]{:S(2)}, u32[]{:S(2)}) collective-permute-start(bf16[512,512]{1,0:T(8,128)(2,1)} %refs_7_.5), channel_id=1, source_target_pairs={{0,1},{1,0},{2,3},{3,2},{4,5},{5,4},{6,7},{7,6},{8,9},{9,8},{10,11... | collective-permute-start | bytes 1572872 | tf_op jit(solution)/shard_map/ppermute | solution.py:21
  4.6 11.1 %collective-permute-start.4 = (bf16[512,512]{1,0:T(8,128)(2,1)}, bf16[512,512]{1,0:T(8,128)(2,1)S(1)}, u32[]{:S(2)}, u32[]{:S(2)}) collective-permute-start(bf16[512,512]{1,0:T(8,128)(2,1)} %refs_9_.5), channel_id=1, source_target_pairs={{0,1},{1,0},{2,3},{3,2},{4,5},{5,4},{6,7},{7,6},{8,9},{9,8},{10,11... | collective-permute-start | bytes 1572872 | tf_op jit(solution)/shard_map/ppermute | solution.py:21
  5.0 10.7 %collective-permute-start = (bf16[1040,128]{1,0:T(8,128)(2,1)}, bf16[1040,128]{1,0:T(8,128)(2,1)S(1)}, u32[]{:S(2)}, u32[]{:S(2)}) collective-permute-start(bf16[1040,128]{1,0:T(8,128)(2,1)} %get-tuple-element.155.refs_3_), channel_id=1, source_target_pairs={{0,2},{1,3},{2,0},{3,1},{4,6},{5,7},{6,4},{7,5},{8,10},{9,11},{10,... | collective-permute-start | bytes 798728 | tf_op jit(solution)/shard_map/ppermute | solution.py:21
  7.6 1.6 %collective-permute-start.2 = (bf16[2,64,512]{2,1,0:T(8,128)(2,1)}, bf16[2,64,512]{2,1,0:T(8,128)(2,1)S(1)}, u32[]{:S(2)}, u32[]{:S(2)}) collective-permute-start(bf16[2,64,512]{2,1,0:T(8,128)(2,1)} %get-tuple-element.158), channel_id=1, source_target_pairs={{0,1},{1,0},{2,3},{3,2},{4,5},{5,4},{6,7},{7,6},{8,9},{9,8},{10,11... | collective-permute-start | bytes 393224 | tf_op jit(solution)/shard_map/ppermute | solution.py:21
  9.1 11.5 %collective-permute-start.5 = (bf16[4,64,512]{2,1,0:T(8,128)(2,1)}, bf16[4,64,512]{2,1,0:T(8,128)(2,1)S(1)}, u32[]{:S(2)}, u32[]{:S(2)}) collective-permute-start(bf16[4,64,512]{2,1,0:T(8,128)(2,1)} %get-tuple-element.165), channel_id=1, source_target_pairs={{0,2},{1,3},{2,0},{3,1},{4,6},{5,7},{6,4},{7,5},{8,10},{9,11},{10,... | collective-permute-start | bytes 786440 | tf_op jit(solution)/shard_map/ppermute | solution.py:21
  15.7 9.8 %collective-permute-start.7 = (bf16[1040,128]{1,0:T(8,128)(2,1)S(1)}, bf16[1040,128]{1,0:T(8,128)(2,1)S(1)}, u32[]{:S(2)}, u32[]{:S(2)}) collective-permute-start(bf16[1040,128]{1,0:T(8,128)(2,1)S(1)} %collective-permute-done.refs_3_), channel_id=1, source_target_pairs={{0,4},{4,0},{8,12},{12,8},{16,20},{20,16},{24,28},{28,24},{1,5},{5... | collective-permute-start | bytes 798728 | tf_op jit(solution)/shard_map/ppermute | solution.py:21
  17.3 14.9 %collective-permute-start.8 = (bf16[2,256,512]{2,1,0:T(8,128)(2,1)S(1)}, bf16[2,256,512]{2,1,0:T(8,128)(2,1)S(1)}, u32[]{:S(2)}, u32[]{:S(2)}) collective-permute-start(bf16[2,256,512]{2,1,0:T(8,128)(2,1)S(1)} %get-tuple-element.174), channel_id=1, source_target_pairs={{0,2},{1,3},{2,0},{3,1},{4,6},{5,7},{6,4},{7,5},{8,10},{9,11},{10,... | collective-permute-start | bytes 1572872 | tf_op jit(solution)/shard_map/ppermute | solution.py:21
  20.7 1.4 %collective-permute-start.6 = (bf16[2,64,512]{2,1,0:T(8,128)(2,1)S(1)}, bf16[2,64,512]{2,1,0:T(8,128)(2,1)S(1)}, u32[]{:S(2)}, u32[]{:S(2)}) collective-permute-start(bf16[2,64,512]{2,1,0:T(8,128)(2,1)S(1)} %slice.12), channel_id=1, source_target_pairs={{0,1},{1,0},{2,3},{3,2},{4,5},{5,4},{6,7},{7,6},{8,9},{9,8},{10,11... | collective-permute-start | bytes 393224 | tf_op jit(solution)/shard_map/ppermute | solution.py:21
  20.8 7.0 %collective-permute-start.9 = (bf16[1040,128]{1,0:T(8,128)(2,1)S(1)}, bf16[1040,128]{1,0:T(8,128)(2,1)S(1)}, u32[]{:S(2)}, u32[]{:S(2)}) collective-permute-start(bf16[1040,128]{1,0:T(8,128)(2,1)S(1)} %collective-permute-done.refs_3_), channel_id=1, source_target_pairs={{0,1},{1,0},{2,3},{3,2},{4,5},{5,4},{6,7},{7,6},{8,9},{9,8},{10,11... | collective-permute-start | bytes 798728 | tf_op jit(solution)/shard_map/ppermute | solution.py:21
  25.5 2.3 %collective-permute-start.10 = (bf16[1040,128]{1,0:T(8,128)(2,1)S(1)}, bf16[1040,128]{1,0:T(8,128)(2,1)S(1)}, u32[]{:S(2)}, u32[]{:S(2)}) collective-permute-start(bf16[1040,128]{1,0:T(8,128)(2,1)S(1)} %collective-permute-done.7.refs_4_), channel_id=1, source_target_pairs={{0,1},{1,0},{2,3},{3,2},{4,5},{5,4},{6,7},{7,6},{8,9},{9,8},{10,11... | collective-permute-start | bytes 798728 | tf_op jit(solution)/shard_map/ppermute | solution.py:21
  25.8 12.7 %collective-permute-start.12 = (bf16[4,64,512]{2,1,0:T(8,128)(2,1)S(1)}, bf16[4,64,512]{2,1,0:T(8,128)(2,1)S(1)}, u32[]{:S(2)}, u32[]{:S(2)}) collective-permute-start(bf16[4,64,512]{2,1,0:T(8,128)(2,1)S(1)} %get-tuple-element.187), channel_id=1, source_target_pairs={{0,2},{1,3},{2,0},{3,1},{4,6},{5,7},{6,4},{7,5},{8,10},{9,11},{10,... | collective-permute-start | bytes 786440 | tf_op jit(solution)/shard_map/ppermute | solution.py:21
  27.7 4.5 %collective-permute-start.11 = (bf16[2,64,512]{2,1,0:T(8,128)(2,1)S(1)}, bf16[2,64,512]{2,1,0:T(8,128)(2,1)S(1)}, u32[]{:S(2)}, u32[]{:S(2)}) collective-permute-start(bf16[2,64,512]{2,1,0:T(8,128)(2,1)S(1)} %get-tuple-element.179), channel_id=1, source_target_pairs={{0,1},{1,0},{2,3},{3,2},{4,5},{5,4},{6,7},{7,6},{8,9},{9,8},{10,11... | collective-permute-start | bytes 393224 | tf_op jit(solution)/shard_map/ppermute | solution.py:21
  32.2 10.2 %collective-permute-start.14 = (bf16[256,512]{1,0:T(8,128)(2,1)S(1)}, bf16[256,512]{1,0:T(8,128)(2,1)S(1)}, u32[]{:S(2)}, u32[]{:S(2)}) collective-permute-start(bf16[256,512]{1,0:T(8,128)(2,1)S(1)} %get-tuple-element.201.refs_10_), channel_id=1, source_target_pairs={{0,1},{1,0},{2,3},{3,2},{4,5},{5,4},{6,7},{7,6},{8,9},{9,8},{10,11... | collective-permute-start | bytes 786440 | tf_op jit(solution)/shard_map/ppermute | solution.py:21
  32.3 10.1 %collective-permute-start.15 = (bf16[256,512]{1,0:T(8,128)(2,1)S(1)}, bf16[256,512]{1,0:T(8,128)(2,1)S(1)}, u32[]{:S(2)}, u32[]{:S(2)}) collective-permute-start(bf16[256,512]{1,0:T(8,128)(2,1)S(1)} %get-tuple-element.201.refs_10_), channel_id=1, source_target_pairs={{0,4},{4,0},{8,12},{12,8},{16,20},{20,16},{24,28},{28,24},{1,5},{5... | collective-permute-start | bytes 786440 | tf_op jit(solution)/shard_map/ppermute | solution.py:21
  34.0 8.4 %collective-permute-start.16 = (bf16[256,512]{1,0:T(8,128)(2,1)S(1)}, bf16[256,512]{1,0:T(8,128)(2,1)S(1)}, u32[]{:S(2)}, u32[]{:S(2)}) collective-permute-start(bf16[256,512]{1,0:T(8,128)(2,1)S(1)} %get-tuple-element.202.refs_12_), channel_id=1, source_target_pairs={{0,1},{1,0},{2,3},{3,2},{4,5},{5,4},{6,7},{7,6},{8,9},{9,8},{10,11... | collective-permute-start | bytes 786440 | tf_op jit(solution)/shard_map/ppermute | solution.py:21
  34.2 8.6 %collective-permute-start.17 = (bf16[256,512]{1,0:T(8,128)(2,1)S(1)}, bf16[256,512]{1,0:T(8,128)(2,1)S(1)}, u32[]{:S(2)}, u32[]{:S(2)}) collective-permute-start(bf16[256,512]{1,0:T(8,128)(2,1)S(1)} %get-tuple-element.202.refs_12_), channel_id=1, source_target_pairs={{0,8},{4,12},{8,0},{12,4},{16,24},{20,28},{24,16},{28,20},{1,9},{5... | collective-permute-start | bytes 786440 | tf_op jit(solution)/shard_map/ppermute | solution.py:21
  38.5 1.4 %collective-permute-start.13 = (bf16[2,64,512]{2,1,0:T(8,128)(2,1)S(1)}, bf16[2,64,512]{2,1,0:T(8,128)(2,1)S(1)}, u32[]{:S(2)}, u32[]{:S(2)}) collective-permute-start(bf16[2,64,512]{2,1,0:T(8,128)(2,1)S(1)} %slice.10), channel_id=1, source_target_pairs={{0,1},{1,0},{2,3},{3,2},{4,5},{5,4},{6,7},{7,6},{8,9},{9,8},{10,11... | collective-permute-start | bytes 393224 | tf_op jit(solution)/shard_map/ppermute | solution.py:21
  42.7 1.5 %collective-permute-start.18 = (bf16[256,512]{1,0:T(8,128)(2,1)S(1)}, bf16[256,512]{1,0:T(8,128)(2,1)S(1)}, u32[]{:S(2)}, u32[]{:S(2)}) collective-permute-start(bf16[256,512]{1,0:T(8,128)(2,1)S(1)} %collective-permute-done.15.refs_11_), channel_id=1, source_target_pairs={{0,1},{1,0},{2,3},{3,2},{4,5},{5,4},{6,7},{7,6},{8,9},{9,8},{10,11... | collective-permute-start | bytes 786440 | tf_op jit(solution)/shard_map/ppermute | solution.py:21
  42.7 1.9 %collective-permute-start.19 = (bf16[256,512]{1,0:T(8,128)(2,1)S(1)}, bf16[256,512]{1,0:T(8,128)(2,1)S(1)}, u32[]{:S(2)}, u32[]{:S(2)}) collective-permute-start(bf16[256,512]{1,0:T(8,128)(2,1)S(1)} %collective-permute-done.17.refs_13_), channel_id=1, source_target_pairs={{0,1},{1,0},{2,3},{3,2},{4,5},{5,4},{6,7},{7,6},{8,9},{9,8},{10,11... | collective-permute-start | bytes 786440 | tf_op jit(solution)/shard_map/ppermute | solution.py:21
  43.2 6.9 %collective-permute-start.20 = (bf16[1,2,8,64,512]{4,3,2,1,0:T(8,128)(2,1)S(1)}, bf16[1,2,8,64,512]{4,3,2,1,0:T(8,128)(2,1)S(1)}, u32[]{:S(2)}, u32[]{:S(2)}) collective-permute-start(bf16[1,2,8,64,512]{4,3,2,1,0:T(8,128)(2,1)S(1)} %get-tuple-element.214), channel_id=1, source_target_pairs={{0,1},{1,0},{2,3},{3,2},{4,5},{5,4},{6,7},{7,6},{8,9},{9,8},{10,11... | collective-permute-start | bytes 3145736 | tf_op jit(solution)/shard_map/ppermute | solution.py:21
  46.8 3.4 %collective-permute-start.21 = (bf16[1,2,8,64,512]{4,3,2,1,0:T(8,128)(2,1)S(1)}, bf16[1,2,8,64,512]{4,3,2,1,0:T(8,128)(2,1)S(1)}, u32[]{:S(2)}, u32[]{:S(2)}) collective-permute-start(bf16[1,2,8,64,512]{4,3,2,1,0:T(8,128)(2,1)S(1)} %get-tuple-element.216), channel_id=1, source_target_pairs={{0,1},{1,0},{2,3},{3,2},{4,5},{5,4},{6,7},{7,6},{8,9},{9,8},{10,11... | collective-permute-start | bytes 3145736 | tf_op jit(solution)/shard_map/ppermute | solution.py:21
  50.6 14.3 %collective-permute-start.22 = (bf16[2,4,64,512]{3,2,1,0:T(8,128)(2,1)S(1)}, bf16[2,4,64,512]{3,2,1,0:T(8,128)(2,1)S(1)}, u32[]{:S(2)}, u32[]{:S(2)}) collective-permute-start(bf16[2,4,64,512]{3,2,1,0:T(8,128)(2,1)S(1)} %get-tuple-element.234), channel_id=1, source_target_pairs={{0,4},{4,0},{8,12},{12,8},{16,20},{20,16},{24,28},{28,24},{1,5},{5... | collective-permute-start | bytes 1572872 | tf_op jit(solution)/shard_map/ppermute | solution.py:21
  51.1 13.9 %collective-permute-start.23 = (bf16[8,64,512]{2,1,0:T(8,128)(2,1)S(1)}, bf16[8,64,512]{2,1,0:T(8,128)(2,1)S(1)}, u32[]{:S(2)}, u32[]{:S(2)}) collective-permute-start(bf16[8,64,512]{2,1,0:T(8,128)(2,1)S(1)} %get-tuple-element.237), channel_id=1, source_target_pairs={{0,2},{1,3},{2,0},{3,1},{4,6},{5,7},{6,4},{7,5},{8,10},{9,11},{10,... | collective-permute-start | bytes 1572872 | tf_op jit(solution)/shard_map/ppermute | solution.py:21
  65.2 10.3 %collective-permute-start.24 = (bf16[1,8,272,128]{3,2,1,0:T(8,128)(2,1)S(1)}, bf16[1,8,272,128]{3,2,1,0:T(8,128)(2,1)S(1)}, u32[]{:S(2)}, u32[]{:S(2)}) collective-permute-start(bf16[1,8,272,128]{3,2,1,0:T(8,128)(2,1)S(1)} %get-tuple-element.241), channel_id=1, source_target_pairs={{0,1},{1,0},{2,3},{3,2},{4,5},{5,4},{6,7},{7,6},{8,9},{9,8},{10,11... | collective-permute-start | bytes 1671176 | tf_op jit(solution)/shard_map/ppermute | solution.py:21
  65.2 10.2 %collective-permute-start.25 = (bf16[1,8,272,128]{3,2,1,0:T(8,128)(2,1)S(1)}, bf16[1,8,272,128]{3,2,1,0:T(8,128)(2,1)S(1)}, u32[]{:S(2)}, u32[]{:S(2)}) collective-permute-start(bf16[1,8,272,128]{3,2,1,0:T(8,128)(2,1)S(1)} %get-tuple-element.243), channel_id=1, source_target_pairs={{0,1},{1,0},{2,3},{3,2},{4,5},{5,4},{6,7},{7,6},{8,9},{9,8},{10,11... | collective-permute-start | bytes 1671176 | tf_op jit(solution)/shard_map/ppermute | solution.py:21
  65.7 8.3 %collective-permute-start.26 = (bf16[4,64,512]{2,1,0:T(8,128)(2,1)S(1)}, bf16[4,64,512]{2,1,0:T(8,128)(2,1)S(1)}, u32[]{:S(2)}, u32[]{:S(2)}) collective-permute-start(bf16[4,64,512]{2,1,0:T(8,128)(2,1)S(1)} %get-tuple-element.246), channel_id=1, source_target_pairs={{0,2},{1,3},{2,0},{3,1},{4,6},{5,7},{6,4},{7,5},{8,10},{9,11},{10,... | collective-permute-start | bytes 786440 | tf_op jit(solution)/shard_map/ppermute | solution.py:21
  67.4 8.0 %collective-permute-start.27 = (bf16[4,64,512]{2,1,0:T(8,128)(2,1)S(1)}, bf16[4,64,512]{2,1,0:T(8,128)(2,1)S(1)}, u32[]{:S(2)}, u32[]{:S(2)}) collective-permute-start(bf16[4,64,512]{2,1,0:T(8,128)(2,1)S(1)} %get-tuple-element.249), channel_id=1, source_target_pairs={{0,8},{4,12},{8,0},{12,4},{16,24},{20,28},{24,16},{28,20},{1,9},{5... | collective-permute-start | bytes 786440 | tf_op jit(solution)/shard_map/ppermute | solution.py:21
  75.7 13.5 %collective-permute-start.28 = (bf16[8,272,128]{2,1,0:T(8,128)(2,1)S(1)}, bf16[8,272,128]{2,1,0:T(8,128)(2,1)S(1)}, u32[]{:S(2)}, u32[]{:S(2)}) collective-permute-start(bf16[8,272,128]{2,1,0:T(8,128)(2,1)S(1)} %get-tuple-element.252), channel_id=1, source_target_pairs={{0,2},{1,3},{2,0},{3,1},{4,6},{5,7},{6,4},{7,5},{8,10},{9,11},{10,... | collective-permute-start | bytes 1671176 | tf_op jit(solution)/shard_map/ppermute | solution.py:21
  76.2 5.0 %collective-permute-start.31 = (bf16[2,64,512]{2,1,0:T(8,128)(2,1)S(1)}, bf16[2,64,512]{2,1,0:T(8,128)(2,1)S(1)}, u32[]{:S(2)}, u32[]{:S(2)}) collective-permute-start(bf16[2,64,512]{2,1,0:T(8,128)(2,1)S(1)} %get-tuple-element.257), channel_id=1, source_target_pairs={{0,8},{4,12},{8,0},{12,4},{16,24},{20,28},{24,16},{28,20},{1,9},{5... | collective-permute-start | bytes 393224 | tf_op jit(solution)/shard_map/ppermute | solution.py:21
  77.9 5.0 %collective-permute-start.32 = (bf16[2,64,512]{2,1,0:T(8,128)(2,1)S(1)}, bf16[2,64,512]{2,1,0:T(8,128)(2,1)S(1)}, u32[]{:S(2)}, u32[]{:S(2)}) collective-permute-start(bf16[2,64,512]{2,1,0:T(8,128)(2,1)S(1)} %get-tuple-element.259), channel_id=1, source_target_pairs={{0,4},{4,0},{8,12},{12,8},{16,20},{20,16},{24,28},{28,24},{1,5},{5... | collective-permute-start | bytes 393224 | tf_op jit(solution)/shard_map/ppermute | solution.py:21
  82.9 12.1 %collective-permute-start.33 = (bf16[2,2,64,512]{3,2,1,0:T(8,128)(2,1)S(1)}, bf16[2,2,64,512]{3,2,1,0:T(8,128)(2,1)S(1)}, u32[]{:S(2)}, u32[]{:S(2)}) collective-permute-start(bf16[2,2,64,512]{3,2,1,0:T(8,128)(2,1)S(1)} %join.1.refs_0_), channel_id=1, source_target_pairs={{0,16},{4,20},{8,24},{12,28},{16,0},{20,4},{24,8},{28,12},{1,17},{... | collective-permute-start | bytes 786440 | tf_op jit(solution)/shard_map/ppermute | solution.py:21
  89.4 7.4 %collective-permute-start.29 = (bf16[2,272,128]{2,1,0:T(8,128)(2,1)S(1)}, bf16[2,272,128]{2,1,0:T(8,128)(2,1)S(1)}, u32[]{:S(2)}, u32[]{:S(2)}) collective-permute-start(bf16[2,272,128]{2,1,0:T(8,128)(2,1)S(1)} %get-tuple-element.254), channel_id=1, source_target_pairs={{0,4},{4,0},{8,12},{12,8},{16,20},{20,16},{24,28},{28,24},{1,5},{5... | collective-permute-start | bytes 417800 | tf_op jit(solution)/shard_map/ppermute | solution.py:21
  91.0 5.8 %collective-permute-start.30 = (bf16[2,272,128]{2,1,0:T(8,128)(2,1)S(1)}, bf16[2,272,128]{2,1,0:T(8,128)(2,1)S(1)}, u32[]{:S(2)}, u32[]{:S(2)}) collective-permute-start(bf16[2,272,128]{2,1,0:T(8,128)(2,1)S(1)} %get-tuple-element.255), channel_id=1, source_target_pairs={{0,4},{4,0},{8,12},{12,8},{16,20},{20,16},{24,28},{28,24},{1,5},{5... | collective-permute-start | bytes 417800 | tf_op jit(solution)/shard_map/ppermute | solution.py:21
  91.5 20.9 %collective-permute-start.40 = (bf16[4,64,512]{2,1,0:T(8,128)(2,1)S(1)}, bf16[4,64,512]{2,1,0:T(8,128)(2,1)S(1)}, u32[]{:S(2)}, u32[]{:S(2)}) collective-permute-start(bf16[4,64,512]{2,1,0:T(8,128)(2,1)S(1)} %get-tuple-element.268), channel_id=1, source_target_pairs={{0,1},{1,0},{2,3},{3,2},{4,5},{5,4},{6,7},{7,6},{8,9},{9,8},{10,11... | collective-permute-start | bytes 786440 | tf_op jit(solution)/shard_map/ppermute | solution.py:21
  95.1 17.3 %collective-permute-start.41 = (bf16[8,64,512]{2,1,0:T(8,128)(2,1)S(1)}, bf16[8,64,512]{2,1,0:T(8,128)(2,1)S(1)}, u32[]{:S(2)}, u32[]{:S(2)}) collective-permute-start(bf16[8,64,512]{2,1,0:T(8,128)(2,1)S(1)} %get-tuple-element.269), channel_id=1, source_target_pairs={{0,2},{1,3},{2,0},{3,1},{4,6},{5,7},{6,4},{7,5},{8,10},{9,11},{10,... | collective-permute-start | bytes 1572872 | tf_op jit(solution)/shard_map/ppermute | solution.py:21
  96.9 6.0 %collective-permute-start.36 = (bf16[2,64,512]{2,1,0:T(8,128)(2,1)S(1)}, bf16[2,64,512]{2,1,0:T(8,128)(2,1)S(1)}, u32[]{:S(2)}, u32[]{:S(2)}) collective-permute-start(bf16[2,64,512]{2,1,0:T(8,128)(2,1)S(1)} %get-tuple-element.265.refs_3_), channel_id=1, source_target_pairs={{0,8},{4,12},{8,0},{12,4},{16,24},{20,28},{24,16},{28,20},{1,9},{5... | collective-permute-start | bytes 393224 | tf_op jit(solution)/shard_map/ppermute | solution.py:21
  97.7 6.7 %collective-permute-start.38 = (bf16[2,64,512]{2,1,0:T(8,128)(2,1)S(1)}, bf16[2,64,512]{2,1,0:T(8,128)(2,1)S(1)}, u32[]{:S(2)}, u32[]{:S(2)}) collective-permute-start(bf16[2,64,512]{2,1,0:T(8,128)(2,1)S(1)} %get-tuple-element.266), channel_id=1, source_target_pairs={{0,4},{4,0},{8,12},{12,8},{16,20},{20,16},{24,28},{28,24},{1,5},{5... | collective-permute-start | bytes 393224 | tf_op jit(solution)/shard_map/ppermute | solution.py:21
  99.3 5.9 %collective-permute-start.34 = (bf16[2,272,128]{2,1,0:T(8,128)(2,1)S(1)}, bf16[2,272,128]{2,1,0:T(8,128)(2,1)S(1)}, u32[]{:S(2)}, u32[]{:S(2)}) collective-permute-start(bf16[2,272,128]{2,1,0:T(8,128)(2,1)S(1)} %get-tuple-element.264), channel_id=1, source_target_pairs={{0,8},{4,12},{8,0},{12,4},{16,24},{20,28},{24,16},{28,20},{1,9},{5... | collective-permute-start | bytes 417800 | tf_op jit(solution)/shard_map/ppermute | solution.py:21
  102.9 9.5 %collective-permute-start.37 = (bf16[4,64,512]{2,1,0:T(8,128)(2,1)S(1)}, bf16[4,64,512]{2,1,0:T(8,128)(2,1)S(1)}, u32[]{:S(2)}, u32[]{:S(2)}) collective-permute-start(bf16[4,64,512]{2,1,0:T(8,128)(2,1)S(1)} %constant_dynamic-update-slice_fusion.refs_0_), channel_id=1, source_target_pairs={{0,4},{4,0},{8,12},{12,8},{16,20},{20,16},{24,28},{28,24},{1,5},{5... | collective-permute-start | bytes 786440 | tf_op jit(solution)/shard_map/ppermute | solution.py:21
  104.5 9.0 %collective-permute-start.39 = (bf16[4,64,512]{2,1,0:T(8,128)(2,1)S(1)}, bf16[4,64,512]{2,1,0:T(8,128)(2,1)S(1)}, u32[]{:S(2)}, u32[]{:S(2)}) collective-permute-start(bf16[4,64,512]{2,1,0:T(8,128)(2,1)S(1)} %constant_dynamic-update-slice_fusion.2.refs_2_), channel_id=1, source_target_pairs={{0,8},{4,12},{8,0},{12,4},{16,24},{20,28},{24,16},{28,20},{1,9},{5... | collective-permute-start | bytes 786440 | tf_op jit(solution)/shard_map/ppermute | solution.py:21
  105.3 7.0 %collective-permute-start.35 = (bf16[2,272,128]{2,1,0:T(8,128)(2,1)S(1)}, bf16[2,272,128]{2,1,0:T(8,128)(2,1)S(1)}, u32[]{:S(2)}, u32[]{:S(2)}) collective-permute-start(bf16[2,272,128]{2,1,0:T(8,128)(2,1)S(1)} %add_whole.1.refs_0_), channel_id=1, source_target_pairs={{0,16},{4,20},{8,24},{12,28},{16,0},{20,4},{24,8},{28,12},{1,17},{... | collective-permute-start | bytes 417800 | tf_op jit(solution)/shard_map/ppermute | solution.py:21
  113.4 6.0 %collective-permute-start.43 = (bf16[2,272,128]{2,1,0:T(8,128)(2,1)S(1)}, bf16[2,272,128]{2,1,0:T(8,128)(2,1)S(1)}, u32[]{:S(2)}, u32[]{:S(2)}) collective-permute-start(bf16[2,272,128]{2,1,0:T(8,128)(2,1)S(1)} %meet.3), channel_id=1, source_target_pairs={{0,8},{4,12},{8,0},{12,4},{16,24},{20,28},{24,16},{28,20},{1,9},{5... | collective-permute-start | bytes 417800 | tf_op jit(solution)/shard_map/ppermute | solution.py:21
  119.4 6.6 %collective-permute-start.44 = (bf16[4,272,128]{2,1,0:T(8,128)(2,1)S(1)}, bf16[4,272,128]{2,1,0:T(8,128)(2,1)S(1)}, u32[]{:S(2)}, u32[]{:S(2)}) collective-permute-start(bf16[4,272,128]{2,1,0:T(8,128)(2,1)S(1)} %constant_dynamic-update-slice_fusion.4.refs_0_), channel_id=1, source_target_pairs={{0,4},{4,0},{8,12},{12,8},{16,20},{20,16},{24,28},{28,24},{1,5},{5... | collective-permute-start | bytes 835592 | tf_op jit(solution)/shard_map/ppermute | solution.py:21
  120.7 1.8 %collective-permute-start.42 = (bf16[4,64,512]{2,1,0:T(8,128)(2,1)S(1)}, bf16[4,64,512]{2,1,0:T(8,128)(2,1)S(1)}, u32[]{:S(2)}, u32[]{:S(2)}) collective-permute-start(bf16[4,64,512]{2,1,0:T(8,128)(2,1)S(1)} %slice.11), channel_id=1, source_target_pairs={{0,1},{1,0},{2,3},{3,2},{4,5},{5,4},{6,7},{7,6},{8,9},{9,8},{10,11... | collective-permute-start | bytes 786440 | tf_op jit(solution)/shard_map/ppermute | solution.py:21
  (10 other events, 85.3 us)

commit v6 on v5

--- a/solution.py
+++ b/solution.py
@@ -627,6 +627,23 @@
             )
             return kept, sent if two else sent[0], [places[i] for i in picks[0]]
 
+        def add_parts(parts, picks, after=()):
+            counts = [len(p) for p in parts]
+
+            def fn(ins, outs, _):
+                for dst, pick in zip(outs, picks):
+                    for at, i in enumerate(pick):
+                        values = []
+                        for refs in take(ins, counts):
+                            n = refs[0].shape[0]
+                            values.append(refs[i // n][i % n])
+                        dst[at] = add_all(values, True)
+
+            flat_parts = [v for p in parts for v in p]
+            rest = flat_parts[0].shape[1:]
+            outs = [shape((len(p),) + rest, BF16) for p in picks]
+            return run("add_parts", fn, flat_parts, outs, after=after)
+
         def add_whole(parts, vectors=False):
             def fn(ins, outs, _):
                 for i in range(outs[0].shape[0]):
@@ -671,6 +688,13 @@
         vec_rows = n_dp * VEC
         chunk = 4 * sub + 2 * VEC
 
+        half_dp = n_dp // 2
+
+        def place_of(gi, k, p, grads):
+            if gi == 1 and k % 2:
+                return grads[3 + p // half_dp], p % half_dp
+            return grads[2 * gi + k % 2], p
+
         def attend_back(ins, outs, scratch):
             me, dpi = lax.axis_index("mp"), lax.axis_index("dp")
             (lens, om, gains), fulls, qkvs, ps, atts, wqs, wos, vecs = take(
@@ -678,7 +702,7 @@
             )
             x_ref, a1_ref, dx1, d_att, out_ref = fulls
             vec, gub_near, gub_even, gub_odd = vecs
-            parts, grads = outs[:-4], outs[-4:]
+            parts, grads = outs[:-5], outs[-5:]
             dqkvs, gqs = scratch[:2], scratch[2:4]
             d_in, vec_f, shared = scratch[4:]
             a1t = a1_ref[...].T
@@ -712,6 +736,7 @@
                             do_h = head_mask(do, h)
                             d_p = dot_nt(do_h, val)
                             inner = jnp.sum(p * d_p, -1, keepdims=True)
+                            inner = inner / jnp.sum(p, -1, keepdims=True)
                             d_s = jnp.where(kept, p * (d_p - inner), 0.0).astype(BF16)
                             sums = dot(jnp.ones((8, slots), BF16), d_s)[:1] * order
                             name = (group[h // per], h % per)
@@ -732,12 +757,12 @@
                 d_in[...] += total
                 gq[3] = dot(d_att_t, att_ref[...]).astype(BF16)
                 for j, k in enumerate(group):
-                    dst = grads[2 * gi + k % 2]
                     at = slice(j * lane, (j + 1) * lane)
                     for p in range(n_dp):
                         here = rows_of(dpi ^ p, sub)
+                        to, q = place_of(gi, k, p, grads)
                         for t in range(4):
-                            dst[j // 2, p, t * sub : (t + 1) * sub] = gq[t, here, at]
+                            to[j // 2, q, t * sub : (t + 1) * sub] = gq[t, here, at]
                     vec_f[k] = jnp.zeros((vec_rows, lane), F32)
                     base = 6 * cols
                     for n, t in enumerate((0, 2)):
@@ -771,13 +796,10 @@
                         for c in range(cols):
                             at = i * cols + c
                             vec_f[k, at : at + 1] = shared[i : i + 1, c * lane : (c + 1) * lane]
-                    dst = grads[2 * gi + k % 2]
                     for p in range(n_dp):
                         v = vec_f[k, rows_of(dpi ^ p, VEC)]
-                        dst[j // 2, p, 4 * sub :] = two_parts(v)
-
-        def grad_shapes(n_blocks):
-            return [shape((n_blocks // 2, n_dp, chunk, lane), BF16)] * 2
+                        to, q = place_of(gi, k, p, grads)
+                        to[j // 2, q, 4 * sub :] = two_parts(v)
 
         back = run(
             "attend_back",
@@ -787,8 +809,8 @@
             + [qkv0, qkv1, p0, p1, att0, att1, wq0, wq1, wo0, wo1]
             + [vec, gub0, gub1_even, gub1_odd],
             [shape((2 * s.shape[0],) + s.shape[1:], BF16) for s in row_shapes]
-            + grad_shapes(len(g0))
-            + grad_shapes(len(g1)),
+            + [shape((len(g) // 2, n_dp, chunk, lane), BF16) for g in (g0, g0, g1)]
+            + [shape((len(g1) // 2, half_dp, chunk, lane), BF16)] * 2,
             [
                 *[pltpu.VMEM((3, count, lane * len(g)), BF16) for g in groups],
                 *[pltpu.VMEM((4, width, lane * len(g)), BF16) for g in groups],
@@ -798,7 +820,22 @@
             ],
             smem=(0,),
         )
-        row_parts, (ka0, sa0, ka1, sa1) = back[:-4], back[-4:]
+        row_parts, (ka0, sa0, ka1, *sa1) = back[:-5], back[-5:]
+        ga0, ga1 = mp_swap(sa0, 1), [mp_swap(v, 1) for v in sa1]
+
+        def add_core_att(ins, outs, _):
+            for n in range(n_y):
+                for p in every:
+                    got = ins[1 + p // half_dp][n, p % half_dp]
+                    dst = outs[2 * n + p // half_dp]
+                    dst[p % half_dp] = add_all([ins[0][n, p], got], True)
+
+        others_a = run(
+            "add_core_att",
+            add_core_att,
+            [ka1] + ga1,
+            [shape((half_dp, chunk, lane), BF16)] * (2 * n_y),
+        )
 
         def add_x(ins, outs, _):
             for n in range(1 + n_y):
@@ -809,28 +846,15 @@
             "add_x", add_x, [kept_d, got_d], [shape((n_dp // 2, sub, hid), BF16)] * (1 + n_y)
         )
         kept_u, sent_u, at_u = add_split([mine_u] + got_u, every, 2)
-        others_d, (sent_u,), sends = together(others_d, [sent_u], [sa0, sa1])
+        others_d, (sent_u,), others_a = together(others_d, [sent_u], others_a)
         got_d = spread_y(others_d)
         got_u = dp_swap(sent_u, 2)
-        ga0, ga1 = (mp_swap(v, 1) for v in sends)
-
-        def add_core_att(ins, outs, _):
-            keep0, got0, keep1, got1 = ins
-            for n in range(1 + n_y):
-                a, b, i = (keep0, got0, 0) if n == 0 else (keep1, got1, n - 1)
-                for p in every:
-                    outs[n][p] = add_all([a[i, p], b[i, p]], True)
-
-        mine_a, *others_a = run(
-            "add_core_att",
-            add_core_att,
-            [ka0, ga0, ka1, ga1],
-            [shape((n_dp, chunk, lane), BF16)] * (1 + n_y),
-        )
+        got_a = [mp_swap(v, y_peers[n // 2]) for n, v in enumerate(others_a)]
+
         kept_d, sent_d, at_d = add_split([mine_d] + got_d, no_x, 2)
         kept_u, sent_u, at_u = add_split([kept_u, got_u], at_u, 1)
-        (sent_d, sent_u), others_a = together([sent_d, sent_u], others_a)
-        got_d, got_u, got_a = dp_swap(sent_d, 2), dp_swap(sent_u, 1), spread_y(others_a)
+        sent_d, sent_u = together([sent_d, sent_u])[0]
+        got_d, got_u = dp_swap(sent_d, 2), dp_swap(sent_u, 1)
 
         def join(ins, outs, _):
             for n, mine in enumerate((ins[:2], ins[2:])):
@@ -848,8 +872,19 @@
             kept, sent, at_both = add_split([both], at_both, bit)
             both = add_whole([kept, dp_swap(sent, bit)])
         got = dp_swap(both, last_bits[-1])
-        kept_a, sent_a, at_a = add_split([mine_a] + got_a, every, 1, True, two=True)
+        mine_a = [v.reshape(v.shape[1:]) for v in (ka0, ga0)]
+        at_a, with_x = split(every, 1)
+        kept_a, *sent_a = add_parts(
+            [[v] for v in mine_a] + [got_a[n : n + 2] for n in range(0, 2 * n_y, 2)],
+            [at_a, with_x[: len(with_x) // 2], with_x[len(with_x) // 2 :]],
+        )
         got_a = [dp_swap(v, 1) for v in sent_a]
+        keep, send = split(at_a, 2)
+        kept_a, *sent_a = add_parts(
+            [[kept_a], got_a], [keep, send[: len(send) // 2], send[len(send) // 2 :]]
+        )
+        got_a = [dp_swap(v, 2) for v in sent_a]
+        at_a = [at_a[i] for i in keep]
         both = meet(both, got, at_both, last_bits[-1], False)
         for bit in reversed(last_bits[:-1]):
             both, at_both = jnp.concatenate([both, dp_swap(both, bit)]), at_both + [
@@ -862,32 +897,26 @@
                     o[i] = ins[0][i, n]
 
         down, up = run("part", part, [both], [shape((len(at_both), sub, hid), BF16)] * 2)
-        kept_a, sent_a, at_a = add_split([kept_a], at_a, 2, True, [down], halves=got_a)
+
+        (sum_a,) = add_parts([[kept_a], got_a], [list(range(len(at_a)))], [down])
 
         row_parts = list(row_parts)
-        row_parts[1:] = send_rows(row_parts[1], row_parts[2:])
-        down, up, sent_a = together([down, up, sent_a])[0]
-        got_d, got_u, got_a = dp_swap(down, 2), dp_swap(up, 1), dp_swap(sent_a, 2)
+        row_parts[2:] = spread_y(row_parts[2:])
+        down, up = together([down, up])[0]
+        got_d, got_u = dp_swap(down, 2), dp_swap(up, 1)
+        for bit in last_bits[:-1]:
+            kept_a, sent_a, at_a = add_split([sum_a], at_a, bit, True)
+            sum_a = add_whole([kept_a, dp_swap(sent_a, bit)], True)
+        got_a = dp_swap(sum_a, last_bits[-1])
         down, at_down = jnp.concatenate([down, got_d]), at_both + [p ^ 2 for p in at_both]
         up, at_up = jnp.concatenate([up, got_u]), at_both + [p ^ 1 for p in at_both]
-        if len(last_bits) > 1:
-            kept_a, sent_a, at_a = add_split([kept_a, got_a], at_a, last_bits[0], True)
-        else:
-            kept_a = sent_a = add_whole([kept_a, got_a], True)
-        got_d, got_u, got_a = dp_swap(down, 1), dp_swap(up, 2), dp_swap(sent_a, last_bits[0])
-        for bit in last_bits[1:]:
-            if bit != last_bits[-1]:
-                kept_a, sent_a, at_a = add_split([kept_a, got_a], at_a, bit, True)
-            else:
-                kept_a = sent_a = add_whole([kept_a, got_a], True)
-            got_a = dp_swap(sent_a, bit)
-        att = meet(kept_a, got_a, at_a, last_bits[-1], True)
+        att = meet(sum_a, got_a, at_a, last_bits[-1], True)
+        got_d, got_u = dp_swap(down, 1), dp_swap(up, 2)
         for bit in [*reversed(last_bits[:-1]), 2]:
-            if bit == 2:
-                (att, got_d, got_u), row_parts = together([att, got_d, got_u], row_parts)
-                row_parts = row_parts[:2] + pass_rows(row_parts[2:])
             att = jnp.concatenate([att, dp_swap(att, bit)])
             at_a = at_a + [p ^ bit for p in at_a]
+        (att, got_d, got_u), row_parts = together([att, got_d, got_u], row_parts)
+        row_parts = [row_parts[0], mp_swap(row_parts[1], 1)] + pass_rows(row_parts[2:])
         got_a = dp_swap(att, 1)
 
         def finish_mlp(ins, outs, scratch):

time: 127 us -> 120 us (0.945)
  waiting for transfers between devices: 40.7 us -> 32.9 us
    ppermute x45 -> x48, waiting for transfers between devices: 40.7 us -> 32.9 us  [swap(): return lax.ppermute(v, axis, [(i, i ^ bit) for i in range(size)])]
    ppermute x45 -> x48, starting transfers between devices: 45.2 us -> 45.6 us  [swap(): return lax.ppermute(v, axis, [(i, i ^ bit) for i in range(size)])]
    unnamed x29 -> x28, local copies, waits for them, and re-layouts: 4.15 us -> 4.14 us
  transfers between devices with their start and end apart: 45 -> 48, of which waited for: 20 -> 21; matrix products, arithmetic and copies ran while one was open for 0% -> 0% of each run, Pallas kernels for 24% -> 26%
where the time goes in v6:
time: 120 us
  starting transfers between devices  45.6 us (38%)
  Pallas kernels  35.8 us (30%)
  waiting for transfers between devices  32.9 us (27%)
  local copies, waits for them, and re-layouts  4.19 us (3%)
    ppermute x48, starting transfers between devices, swap(): return lax.ppermute(v, axis, [(i, i ^ bit) for i in range(size)])  45.6 us
    pallas_call x26, Pallas kernels, run(): pl.pallas_call(kernel, out_shape=tuple(outs), in_specs=[pl.BlockSpec(memo...  35.8 us
    ppermute x48, waiting for transfers between devices, swap(): return lax.ppermute(v, axis, [(i, i ^ bit) for i in range(size)])  32.9 us
    unnamed x28, local copies, waits for them, and re-layouts  4.14 us
  transfers between devices with their start and end apart: 48, of which 21 were waited for; matrix products, arithmetic and copies ran while one was open for 0% of the time, Pallas kernels for 26%

profile of v6, /device:TPU:0, one launch (start us, length us, event | category | flops | bytes accessed | tf_op | source)
XLA Modules:
  0.0 119.6 jit_solution(6685996480416589223)
XLA Ops:
  0.7 3.3 %begin.1 = (bf16[2,64,512]{2,1,0:T(8,128)(2,1)}, bf16[2,64,512]{2,1,0:T(8,128)(2,1)}, bf16[4,64,512]{2,1,0:T(8,128)(2,1)}, bf16[2080,128]{1,0:T(8,128)(2,1)}, bf16[1040,128]{1,0:T(8,128)(2,1)}) custom-call(bf16[8,64,512]{2,1,0:T(8,128)(2,1)} %refs_0_.4, bf16[1536,128]{1,0:T(8,128)(2,1)} %bitcast.9, bf16[128,512]{1,0:T(8,128)(2,1)} %refs_2_.3, ...), custom_call_target="tpu_custom_call" | custom-call | flops 1 | bytes 1 | tf_op jit(solution)/shard_map/begin/pallas_call | solution.py:43
  5.0 2.6 %collective-permute-start = (bf16[1040,128]{1,0:T(8,128)(2,1)}, bf16[1040,128]{1,0:T(8,128)(2,1)S(1)}, u32[]{:S(2)}, u32[]{:S(2)}) collective-permute-start(bf16[1040,128]{1,0:T(8,128)(2,1)} %get-tuple-element.154.refs_3_), channel_id=1, source_target_pairs={{0,2},{1,3},{2,0},{3,1},{4,6},{5,7},{6,4},{7,5},{8,10},{9,11},{10,... | collective-permute-start | bytes 798728 | tf_op jit(solution)/shard_map/ppermute | solution.py:21
  7.8 1.4 %collective-permute-done.2.refs_1_ = bf16[2,64,512]{2,1,0:T(8,128)(2,1)S(1)} collective-permute-done((bf16[2,64,512]{2,1,0:T(8,128)(2,1)}, bf16[2,64,512]{2,1,0:T(8,128)(2,1)S(1)}, u32[]{:S(2)}, u32[]{:S(2)}) %collective-permute-start.2) | collective-permute-done | bytes 131104 | tf_op jit(solution)/shard_map/ppermute | solution.py:21
  9.1 1.7 %collective-permute-start.5 = (bf16[4,64,512]{2,1,0:T(8,128)(2,1)}, bf16[4,64,512]{2,1,0:T(8,128)(2,1)S(1)}, u32[]{:S(2)}, u32[]{:S(2)}) collective-permute-start(bf16[4,64,512]{2,1,0:T(8,128)(2,1)} %get-tuple-element.164), channel_id=1, source_target_pairs={{0,2},{1,3},{2,0},{3,1},{4,6},{5,7},{6,4},{7,5},{8,10},{9,11},{10,... | collective-permute-start | bytes 786440 | tf_op jit(solution)/shard_map/ppermute | solution.py:21
  10.8 1.0 copy-done
  11.9 1.0 copy-done.2
  12.9 1.0 copy-done.5
  15.7 1.6 %collective-permute-start.7 = (bf16[1040,128]{1,0:T(8,128)(2,1)S(1)}, bf16[1040,128]{1,0:T(8,128)(2,1)S(1)}, u32[]{:S(2)}, u32[]{:S(2)}) collective-permute-start(bf16[1040,128]{1,0:T(8,128)(2,1)S(1)} %collective-permute-done.refs_3_), channel_id=1, source_target_pairs={{0,4},{4,0},{8,12},{12,8},{16,20},{20,16},{24,28},{28,24},{1,5},{5... | collective-permute-start | bytes 798728 | tf_op jit(solution)/shard_map/ppermute | solution.py:21
  17.3 1.3 %collective-permute-start.8 = (bf16[2,256,512]{2,1,0:T(8,128)(2,1)S(1)}, bf16[2,256,512]{2,1,0:T(8,128)(2,1)S(1)}, u32[]{:S(2)}, u32[]{:S(2)}) collective-permute-start(bf16[2,256,512]{2,1,0:T(8,128)(2,1)S(1)} %get-tuple-element.173), channel_id=1, source_target_pairs={{0,2},{1,3},{2,0},{3,1},{4,6},{5,7},{6,4},{7,5},{8,10},{9,11},{10,... | collective-permute-start | bytes 1572872 | tf_op jit(solution)/shard_map/ppermute | solution.py:21
  18.6 2.1 %collective-permute-done.5.refs_2_ = bf16[4,64,512]{2,1,0:T(8,128)(2,1)S(1)} collective-permute-done((bf16[4,64,512]{2,1,0:T(8,128)(2,1)}, bf16[4,64,512]{2,1,0:T(8,128)(2,1)S(1)}, u32[]{:S(2)}, u32[]{:S(2)}) %collective-permute-start.5) | collective-permute-done | bytes 262176 | tf_op jit(solution)/shard_map/ppermute | solution.py:21
  22.2 3.3 %attend.2 = (bf16[512,512]{1,0:T(8,128)(2,1)S(1)}, bf16[512,512]{1,0:T(8,128)(2,1)S(1)}, bf16[3,512,256]{2,1,0:T(8,128)(2,1)S(1)}, bf16[8,256,256]{2,1,0:T(8,128...) custom-call(bf16[2,64,512]{2,1,0:T(8,128)(2,1)S(1)} %copy-done.7, ...), custom_call_target="tpu_custom_call" | custom-call | flops 1 | bytes 1 | tf_op jit(solution)/shard_map/attend/pallas_call | solution.py:43
  25.8 2.0 %collective-permute-start.12 = (bf16[4,64,512]{2,1,0:T(8,128)(2,1)S(1)}, bf16[4,64,512]{2,1,0:T(8,128)(2,1)S(1)}, u32[]{:S(2)}, u32[]{:S(2)}) collective-permute-start(bf16[4,64,512]{2,1,0:T(8,128)(2,1)S(1)} %get-tuple-element.186), channel_id=1, source_target_pairs={{0,2},{1,3},{2,0},{3,1},{4,6},{5,7},{6,4},{7,5},{8,10},{9,11},{10,... | collective-permute-start | bytes 786440 | tf_op jit(solution)/shard_map/ppermute | solution.py:21
  27.8 3.1 %attend.3 = (bf16[3,512,256]{2,1,0:T(8,128)(2,1)S(1)}, bf16[8,256,256]{2,1,0:T(8,128)(2,1)S(1)}, bf16[512,256]{1,0:T(8,128)(2,1)S(1)}, bf16[1536,256]{1,0:T(8,12...) custom-call(s32[8]{0:T(128)S(1)} %copy-done.12, s32[8,256]{1,0:T(8,128)S(1)} %copy-done.9, ...), custom_call_target="tpu_custom_call" | custom-call | flops 1 | bytes 1 | tf_op jit(solution)/shard_map/attend/pallas_call | solution.py:43
  30.9 1.2 %collective-permute-done.8.refs_0_ = bf16[2,256,512]{2,1,0:T(8,128)(2,1)S(1)} collective-permute-done((bf16[2,256,512]{2,1,0:T(8,128)(2,1)S(1)}, bf16[2,256,512]{2,1,0:T(8,128)(2,1)S(1)}, u32[]{:S(2)}, u32[]{:S(2)}) %collective-permute-start.8) | collective-permute-done | bytes 524320 | tf_op jit(solution)/shard_map/ppermute | solution.py:21
  32.3 1.8 %collective-permute-start.15 = (bf16[256,512]{1,0:T(8,128)(2,1)S(1)}, bf16[256,512]{1,0:T(8,128)(2,1)S(1)}, u32[]{:S(2)}, u32[]{:S(2)}) collective-permute-start(bf16[256,512]{1,0:T(8,128)(2,1)S(1)} %get-tuple-element.200.refs_10_), channel_id=1, source_target_pairs={{0,4},{4,0},{8,12},{12,8},{16,20},{20,16},{24,28},{28,24},{1,5},{5... | collective-permute-start | bytes 786440 | tf_op jit(solution)/shard_map/ppermute | solution.py:21
  34.2 1.6 %collective-permute-start.17 = (bf16[256,512]{1,0:T(8,128)(2,1)S(1)}, bf16[256,512]{1,0:T(8,128)(2,1)S(1)}, u32[]{:S(2)}, u32[]{:S(2)}) collective-permute-start(bf16[256,512]{1,0:T(8,128)(2,1)S(1)} %get-tuple-element.201.refs_12_), channel_id=1, source_target_pairs={{0,8},{4,12},{8,0},{12,4},{16,24},{20,28},{24,16},{28,20},{1,9},{5... | collective-permute-start | bytes 786440 | tf_op jit(solution)/shard_map/ppermute | solution.py:21
  35.8 2.7 %mlp_near_forward.1 = (f32[512,512]{1,0:T(8,128)S(1)}, bf16[512,512]{1,0:T(8,128)(2,1)S(1)}, bf16[512,512]{1,0:T(8,128)(2,1)S(1)}, f32[512,512]{1,0:T(8,128)S(1)...) custom-call(bf16[512,512]{1,0:T(8,128)(2,1)S(1)} %get-tuple-element.166.refs_0_.refs_3_, ...), custom_call_target="tpu_custom_call" | custom-call | flops 1 | bytes 1 | tf_op jit(solution)/shard_map/mlp_near_forward/pallas_call | solution.py:43
  38.6 1.3 %collective-permute-done.13.refs_6_ = bf16[2,64,512]{2,1,0:T(8,128)(2,1)S(1)} collective-permute-done((bf16[2,64,512]{2,1,0:T(8,128)(2,1)S(1)}, bf16[2,64,512]{2,1,0:T(8,128)(2,1)S(1)}, u32[]{:S(2)}, u32[]{:S(2)}) %collective-permute-start.13) | collective-permute-done | bytes 131104 | tf_op jit(solution)/shard_map/ppermute | solution.py:21
  39.9 2.5 %mlp_near_backward.1 = (bf16[512,512]{1,0:T(8,128)(2,1)S(1)}, bf16[512,512]{1,0:T(8,128)(2,1)S(1)}, f32[512,512]{1,0:T(8,128)S(1)}, bf16[1,2,8,64,512]{4,3,2,1,0...) custom-call(bf16[2,512,512]{2,1,0:T(8,128)(2,1)S(1)} %get-tuple-element.190.refs_0_, ...), custom_call_target="tpu_custom_call" | custom-call | flops 1 | bytes 1 | tf_op jit(solution)/shard_map/mlp_near_backward/pallas_call | solution.py:43
  44.6 2.1 %mlp_far.2 = (f32[512,512]{1,0:T(8,128)S(1)}, f32[512,512]{1,0:T(8,128)S(1)}, bf16[1,2,8,64,512]{4,3,2,1,0:T(8,128)(2,1)S(1)}, f32[1,1,512]{2,1,0:T(1,128)S(1)}) custom-call(f32[512,512]{1,0:T(8,128)S(1)} %get-tuple-element.185.refs_0_, bf16[512,512]{1,0:T(8,128)(2,1)S(1)} %get-tuple-element.188.refs_1_, bf16[512,512]{1,0:T(8,128)(2,1)S(1)} %get-tuple-element.189.refs_2_, ...), custom_call_target="tpu_custom_call" | custom-call | flops 1 | bytes 1 | tf_op jit(solution)/shard_map/mlp_far/pallas_call | solution.py:43
  47.0 3.1 %mlp_far.3 = (bf16[512,512]{1,0:T(8,128)(2,1)S(1)}, f32[512,512]{1,0:T(8,128)S(1)}, bf16[512,512]{1,0:T(8,128)(2,1)S(1)}, f32[4,512]{1,0:T(4,128)S(1)}, bf16[1,2...) custom-call(f32[512,512]{1,0:T(8,128)S(1)} %get-tuple-element.185.refs_0_, ...), custom_call_target="tpu_custom_call" | custom-call | flops 1 | bytes 1 | tf_op jit(solution)/shard_map/mlp_far/pallas_call | solution.py:43
  51.1 1.7 %collective-permute-start.24 = (bf16[8,64,512]{2,1,0:T(8,128)(2,1)S(1)}, bf16[8,64,512]{2,1,0:T(8,128)(2,1)S(1)}, u32[]{:S(2)}, u32[]{:S(2)}) collective-permute-start(bf16[8,64,512]{2,1,0:T(8,128)(2,1)S(1)} %get-tuple-element.237), channel_id=1, source_target_pairs={{0,2},{1,3},{2,0},{3,1},{4,6},{5,7},{6,4},{7,5},{8,10},{9,11},{10,... | collective-permute-start | bytes 1572872 | tf_op jit(solution)/shard_map/ppermute | solution.py:21
  52.8 9.3 %attend_back.1 = (bf16[4,64,512]{2,1,0:T(8,128)(2,1)S(1)}, bf16[4,64,512]{2,1,0:T(8,128)(2,1)S(1)}, bf16[8,64,512]{2,1,0:T(8,128)(2,1)S(1)}, bf16[1,8,272,128]{3...) custom-call(s32[8]{0:T(128)S(1)} %copy-done.12, ...), custom_call_target="tpu_custom_call" | custom-call | flops 1 | bytes 1 | tf_op jit(solution)/shard_map/attend_back/pallas_call | solution.py:43
  65.2 1.7 %collective-permute-start.33 = (bf16[4,64,512]{2,1,0:T(8,128)(2,1)S(1)}, bf16[4,64,512]{2,1,0:T(8,128)(2,1)S(1)}, u32[]{:S(2)}, u32[]{:S(2)}) collective-permute-start(bf16[4,64,512]{2,1,0:T(8,128)(2,1)S(1)} %get-tuple-element.253), channel_id=1, source_target_pairs={{0,2},{1,3},{2,0},{3,1},{4,6},{5,7},{6,4},{7,5},{8,10},{9,11},{10,... | collective-permute-start | bytes 786440 | tf_op jit(solution)/shard_map/ppermute | solution.py:21
  66.9 1.6 %collective-permute-start.34 = (bf16[4,64,512]{2,1,0:T(8,128)(2,1)S(1)}, bf16[4,64,512]{2,1,0:T(8,128)(2,1)S(1)}, u32[]{:S(2)}, u32[]{:S(2)}) collective-permute-start(bf16[4,64,512]{2,1,0:T(8,128)(2,1)S(1)} %get-tuple-element.257), channel_id=1, source_target_pairs={{0,8},{4,12},{8,0},{12,4},{16,24},{20,28},{24,16},{28,20},{1,9},{5... | collective-permute-start | bytes 786440 | tf_op jit(solution)/shard_map/ppermute | solution.py:21
  68.9 1.5 %collective-permute-start.28 = (bf16[4,272,128]{2,1,0:T(8,128)(2,1)S(1)}, bf16[4,272,128]{2,1,0:T(8,128)(2,1)S(1)}, u32[]{:S(2)}, u32[]{:S(2)}) collective-permute-start(bf16[4,272,128]{2,1,0:T(8,128)(2,1)S(1)} %get-tuple-element.245), channel_id=1, source_target_pairs={{0,2},{1,3},{2,0},{3,1},{4,6},{5,7},{6,4},{7,5},{8,10},{9,11},{10,... | collective-permute-start | bytes 835592 | tf_op jit(solution)/shard_map/ppermute | solution.py:21
  70.5 4.0 %collective-permute-done.33.refs_1_ = bf16[4,64,512]{2,1,0:T(8,128)(2,1)S(1)} collective-permute-done((bf16[4,64,512]{2,1,0:T(8,128)(2,1)S(1)}, bf16[4,64,512]{2,1,0:T(8,128)(2,1)S(1)}, u32[]{:S(2)}, u32[]{:S(2)}) %collective-permute-start.33) | collective-permute-done | bytes 262176 | tf_op jit(solution)/shard_map/ppermute | solution.py:21
  74.6 1.8 %collective-permute-start.35 = (bf16[2,64,512]{2,1,0:T(8,128)(2,1)S(1)}, bf16[2,64,512]{2,1,0:T(8,128)(2,1)S(1)}, u32[]{:S(2)}, u32[]{:S(2)}) collective-permute-start(bf16[2,64,512]{2,1,0:T(8,128)(2,1)S(1)} %get-tuple-element.259), channel_id=1, source_target_pairs={{0,8},{4,12},{8,0},{12,4},{16,24},{20,28},{24,16},{28,20},{1,9},{5... | collective-permute-start | bytes 393224 | tf_op jit(solution)/shard_map/ppermute | solution.py:21
  76.4 1.5 %collective-permute-start.36 = (bf16[2,64,512]{2,1,0:T(8,128)(2,1)S(1)}, bf16[2,64,512]{2,1,0:T(8,128)(2,1)S(1)}, u32[]{:S(2)}, u32[]{:S(2)}) collective-permute-start(bf16[2,64,512]{2,1,0:T(8,128)(2,1)S(1)} %get-tuple-element.261), channel_id=1, source_target_pairs={{0,4},{4,0},{8,12},{12,8},{16,20},{20,16},{24,28},{28,24},{1,5},{5... | collective-permute-start | bytes 393224 | tf_op jit(solution)/shard_map/ppermute | solution.py:21
  77.9 1.8 %collective-permute-done.35.refs_1_ = bf16[2,64,512]{2,1,0:T(8,128)(2,1)S(1)} collective-permute-done((bf16[2,64,512]{2,1,0:T(8,128)(2,1)S(1)}, bf16[2,64,512]{2,1,0:T(8,128)(2,1)S(1)}, u32[]{:S(2)}, u32[]{:S(2)}) %collective-permute-start.35) | collective-permute-done | bytes 131104 | tf_op jit(solution)/shard_map/ppermute | solution.py:21
  79.7 1.7 %collective-permute-done.36.refs_3_ = bf16[2,64,512]{2,1,0:T(8,128)(2,1)S(1)} collective-permute-done((bf16[2,64,512]{2,1,0:T(8,128)(2,1)S(1)}, bf16[2,64,512]{2,1,0:T(8,128)(2,1)S(1)}, u32[]{:S(2)}, u32[]{:S(2)}) %collective-permute-start.36) | collective-permute-done | bytes 131104 | tf_op jit(solution)/shard_map/ppermute | solution.py:21
  81.4 2.7 %collective-permute-start.37 = (bf16[2,2,64,512]{3,2,1,0:T(8,128)(2,1)S(1)}, bf16[2,2,64,512]{3,2,1,0:T(8,128)(2,1)S(1)}, u32[]{:S(2)}, u32[]{:S(2)}) collective-permute-start(bf16[2,2,64,512]{3,2,1,0:T(8,128)(2,1)S(1)} %join.1.refs_0_), channel_id=1, source_target_pairs={{0,16},{4,20},{8,24},{12,28},{16,0},{20,4},{24,8},{28,12},{1,17},{... | collective-permute-start | bytes 786440 | tf_op jit(solution)/shard_map/ppermute | solution.py:21
  85.2 1.5 %collective-permute-start.29 = (bf16[2,272,128]{2,1,0:T(8,128)(2,1)S(1)}, bf16[2,272,128]{2,1,0:T(8,128)(2,1)S(1)}, u32[]{:S(2)}, u32[]{:S(2)}) collective-permute-start(bf16[2,272,128]{2,1,0:T(8,128)(2,1)S(1)} %get-tuple-element.247), channel_id=1, source_target_pairs={{0,4},{4,0},{8,12},{12,8},{16,20},{20,16},{24,28},{28,24},{1,5},{5... | collective-permute-start | bytes 417800 | tf_op jit(solution)/shard_map/ppermute | solution.py:21
  87.2 1.5 %collective-permute-start.44 = (bf16[8,64,512]{2,1,0:T(8,128)(2,1)S(1)}, bf16[8,64,512]{2,1,0:T(8,128)(2,1)S(1)}, u32[]{:S(2)}, u32[]{:S(2)}) collective-permute-start(bf16[8,64,512]{2,1,0:T(8,128)(2,1)S(1)} %get-tuple-element.267), channel_id=1, source_target_pairs={{0,2},{1,3},{2,0},{3,1},{4,6},{5,7},{6,4},{7,5},{8,10},{9,11},{10,... | collective-permute-start | bytes 1572872 | tf_op jit(solution)/shard_map/ppermute | solution.py:21
  88.8 2.2 %collective-permute-done.29.refs_1_ = bf16[2,272,128]{2,1,0:T(8,128)(2,1)S(1)} collective-permute-done((bf16[2,272,128]{2,1,0:T(8,128)(2,1)S(1)}, bf16[2,272,128]{2,1,0:T(8,128)(2,1)S(1)}, u32[]{:S(2)}, u32[]{:S(2)}) %collective-permute-start.29) | collective-permute-done | bytes 139296 | tf_op jit(solution)/shard_map/ppermute | solution.py:21
  90.9 1.5 %collective-permute-done.30.refs_2_ = bf16[2,272,128]{2,1,0:T(8,128)(2,1)S(1)} collective-permute-done((bf16[2,272,128]{2,1,0:T(8,128)(2,1)S(1)}, bf16[2,272,128]{2,1,0:T(8,128)(2,1)S(1)}, u32[]{:S(2)}, u32[]{:S(2)}) %collective-permute-start.30) | collective-permute-done | bytes 139296 | tf_op jit(solution)/shard_map/ppermute | solution.py:21
  92.5 1.5 %collective-permute-start.31 = (bf16[1,272,128]{2,1,0:T(8,128)(2,1)S(1)}, bf16[1,272,128]{2,1,0:T(8,128)(2,1)S(1)}, u32[]{:S(2)}, u32[]{:S(2)}) collective-permute-start(bf16[1,272,128]{2,1,0:T(8,128)(2,1)S(1)} %get-tuple-element.250), channel_id=1, source_target_pairs={{0,8},{4,12},{8,0},{12,4},{16,24},{20,28},{24,16},{28,20},{1,9},{5... | collective-permute-start | bytes 208904 | tf_op jit(solution)/shard_map/ppermute | solution.py:21
  94.8 1.5 %collective-permute-start.40 = (bf16[2,64,512]{2,1,0:T(8,128)(2,1)S(1)}, bf16[2,64,512]{2,1,0:T(8,128)(2,1)S(1)}, u32[]{:S(2)}, u32[]{:S(2)}) collective-permute-start(bf16[2,64,512]{2,1,0:T(8,128)(2,1)S(1)} %get-tuple-element.262.refs_3_), channel_id=1, source_target_pairs={{0,8},{4,12},{8,0},{12,4},{16,24},{20,28},{24,16},{28,20},{1,9},{5... | collective-permute-start | bytes 393224 | tf_op jit(solution)/shard_map/ppermute | solution.py:21
  96.3 1.4 %collective-permute-start.42 = (bf16[2,64,512]{2,1,0:T(8,128)(2,1)S(1)}, bf16[2,64,512]{2,1,0:T(8,128)(2,1)S(1)}, u32[]{:S(2)}, u32[]{:S(2)}) collective-permute-start(bf16[2,64,512]{2,1,0:T(8,128)(2,1)S(1)} %get-tuple-element.264), channel_id=1, source_target_pairs={{0,4},{4,0},{8,12},{12,8},{16,20},{20,16},{24,28},{28,24},{1,5},{5... | collective-permute-start | bytes 393224 | tf_op jit(solution)/shard_map/ppermute | solution.py:21
  98.5 3.3 %collective-permute-start.38 = (bf16[2,272,128]{2,1,0:T(8,128)(2,1)S(1)}, bf16[2,272,128]{2,1,0:T(8,128)(2,1)S(1)}, u32[]{:S(2)}, u32[]{:S(2)}) collective-permute-start(bf16[2,272,128]{2,1,0:T(8,128)(2,1)S(1)} %add_parts.5.refs_0_), channel_id=1, source_target_pairs={{0,16},{4,20},{8,24},{12,28},{16,0},{20,4},{24,8},{28,12},{1,17},{... | collective-permute-start | bytes 417800 | tf_op jit(solution)/shard_map/ppermute | solution.py:21
  101.9 1.4 %collective-permute-start.41 = (bf16[4,64,512]{2,1,0:T(8,128)(2,1)S(1)}, bf16[4,64,512]{2,1,0:T(8,128)(2,1)S(1)}, u32[]{:S(2)}, u32[]{:S(2)}) collective-permute-start(bf16[4,64,512]{2,1,0:T(8,128)(2,1)S(1)} %constant_dynamic-update-slice_fusion.refs_0_), channel_id=1, source_target_pairs={{0,4},{4,0},{8,12},{12,8},{16,20},{20,16},{24,28},{28,24},{1,5},{5... | collective-permute-start | bytes 786440 | tf_op jit(solution)/shard_map/ppermute | solution.py:21
  103.9 2.5 %collective-permute-done.38.refs_1_ = bf16[2,272,128]{2,1,0:T(8,128)(2,1)S(1)} collective-permute-done((bf16[2,272,128]{2,1,0:T(8,128)(2,1)S(1)}, bf16[2,272,128]{2,1,0:T(8,128)(2,1)S(1)}, u32[]{:S(2)}, u32[]{:S(2)}) %collective-permute-start.38) | collective-permute-done | bytes 139296 | tf_op jit(solution)/shard_map/ppermute | solution.py:21
  106.7 5.1 %collective-permute-done.39 = bf16[2,272,128]{2,1,0:T(8,128)(2,1)S(1)} collective-permute-done((bf16[2,272,128]{2,1,0:T(8,128)(2,1)S(1)}, bf16[2,272,128]{2,1,0:T(8,128)(2,1)S(1)}, u32[]{:S(2)}, u32[]{:S(2)}) %collective-permute-start.39) | collective-permute-done | bytes 139296 | tf_op jit(solution)/shard_map/ppermute | solution.py:21
  111.9 1.1 collective-permute-start.47
  113.6 1.7 %finish_mlp.1 = (f32[512,512]{1,0:T(8,128)}, f32[512,512]{1,0:T(8,128)}, f32[8,128]{1,0:T(8,128)S(1)}) custom-call(bf16[4,64,512]{2,1,0:T(8,128)(2,1)S(1)} %constant_dynamic-update-slice_fusion.refs_0_, bf16[4,64,512]{2,1,0:T(8,128)(2,1)S(1)} %collective-permute-done.41.refs_1_, bf16[4,64,512]{2,1,0:T(8,128)(2,1)S(1)} %constant_dynamic-update-slice_fusion.2.refs_2_, ...), custom_call_target="tpu_custom_call" | custom-call | flops 1 | bytes 1 | tf_op jit(solution)/shard_map/finish_mlp/pallas_call | solution.py:43
  115.3 1.2 %gather_rows.1 = (bf16[8,64,512]{2,1,0:T(8,128)(2,1)}, f32[8,64,512]{2,1,0:T(8,128)}, f32[8,128]{1,0:T(8,128)S(1)}) custom-call(bf16[4,64,512]{2,1,0:T(8,128)(2,1)S(1)} %get-tuple-element.268.refs_0_, bf16[4,64,512]{2,1,0:T(8,128)(2,1)S(1)} %collective-permute-done.45.refs_1_, bf16[8,64,512]{2,1,0:T(8,128)(2,1)S(1)} %collective-permute-done.44.refs_2_, ...), custom_call_target="tpu_custom_call" | custom-call | flops 1 | bytes 1 | tf_op jit(solution)/shard_map/gather_rows/pallas_call | solution.py:43
  116.6 1.9 %collective-permute-done.47.refs_1_ = bf16[4,272,128]{2,1,0:T(8,128)(2,1)S(1)} collective-permute-done((bf16[4,272,128]{2,1,0:T(8,128)(2,1)S(1)}, bf16[4,272,128]{2,1,0:T(8,128)(2,1)S(1)}, u32[]{:S(2)}, u32[]{:S(2)}) %collective-permute-start.47) | collective-permute-done | bytes 278560 | tf_op jit(solution)/shard_map/ppermute | solution.py:21
  118.5 1.1 finish_att.1
  (108 shorter events, 17.1 us)
Async XLA Ops:
  4.0 11.7 %collective-permute-start.1 = (bf16[2080,128]{1,0:T(8,128)(2,1)}, bf16[2080,128]{1,0:T(8,128)(2,1)S(1)}, u32[]{:S(2)}, u32[]{:S(2)}) collective-permute-start(bf16[2080,128]{1,0:T(8,128)(2,1)} %get-tuple-element.155.refs_8_), channel_id=1, source_target_pairs={{0,1},{1,0},{2,3},{3,2},{4,5},{5,4},{6,7},{7,6},{8,9},{9,8},{10,11... | collective-permute-start | bytes 1597448 | tf_op jit(solution)/shard_map/ppermute | solution.py:21
  4.5 11.2 %collective-permute-start.3 = (bf16[512,512]{1,0:T(8,128)(2,1)}, bf16[512,512]{1,0:T(8,128)(2,1)S(1)}, u32[]{:S(2)}, u32[]{:S(2)}) collective-permute-start(bf16[512,512]{1,0:T(8,128)(2,1)} %refs_7_.5), channel_id=1, source_target_pairs={{0,1},{1,0},{2,3},{3,2},{4,5},{5,4},{6,7},{7,6},{8,9},{9,8},{10,11... | collective-permute-start | bytes 1572872 | tf_op jit(solution)/shard_map/ppermute | solution.py:21
  4.6 11.1 %collective-permute-start.4 = (bf16[512,512]{1,0:T(8,128)(2,1)}, bf16[512,512]{1,0:T(8,128)(2,1)S(1)}, u32[]{:S(2)}, u32[]{:S(2)}) collective-permute-start(bf16[512,512]{1,0:T(8,128)(2,1)} %refs_9_.5), channel_id=1, source_target_pairs={{0,1},{1,0},{2,3},{3,2},{4,5},{5,4},{6,7},{7,6},{8,9},{9,8},{10,11... | collective-permute-start | bytes 1572872 | tf_op jit(solution)/shard_map/ppermute | solution.py:21
  5.0 10.7 %collective-permute-start = (bf16[1040,128]{1,0:T(8,128)(2,1)}, bf16[1040,128]{1,0:T(8,128)(2,1)S(1)}, u32[]{:S(2)}, u32[]{:S(2)}) collective-permute-start(bf16[1040,128]{1,0:T(8,128)(2,1)} %get-tuple-element.154.refs_3_), channel_id=1, source_target_pairs={{0,2},{1,3},{2,0},{3,1},{4,6},{5,7},{6,4},{7,5},{8,10},{9,11},{10,... | collective-permute-start | bytes 798728 | tf_op jit(solution)/shard_map/ppermute | solution.py:21
  7.6 1.6 %collective-permute-start.2 = (bf16[2,64,512]{2,1,0:T(8,128)(2,1)}, bf16[2,64,512]{2,1,0:T(8,128)(2,1)S(1)}, u32[]{:S(2)}, u32[]{:S(2)}) collective-permute-start(bf16[2,64,512]{2,1,0:T(8,128)(2,1)} %get-tuple-element.157), channel_id=1, source_target_pairs={{0,1},{1,0},{2,3},{3,2},{4,5},{5,4},{6,7},{7,6},{8,9},{9,8},{10,11... | collective-permute-start | bytes 393224 | tf_op jit(solution)/shard_map/ppermute | solution.py:21
  9.1 11.5 %collective-permute-start.5 = (bf16[4,64,512]{2,1,0:T(8,128)(2,1)}, bf16[4,64,512]{2,1,0:T(8,128)(2,1)S(1)}, u32[]{:S(2)}, u32[]{:S(2)}) collective-permute-start(bf16[4,64,512]{2,1,0:T(8,128)(2,1)} %get-tuple-element.164), channel_id=1, source_target_pairs={{0,2},{1,3},{2,0},{3,1},{4,6},{5,7},{6,4},{7,5},{8,10},{9,11},{10,... | collective-permute-start | bytes 786440 | tf_op jit(solution)/shard_map/ppermute | solution.py:21
  15.7 9.8 %collective-permute-start.7 = (bf16[1040,128]{1,0:T(8,128)(2,1)S(1)}, bf16[1040,128]{1,0:T(8,128)(2,1)S(1)}, u32[]{:S(2)}, u32[]{:S(2)}) collective-permute-start(bf16[1040,128]{1,0:T(8,128)(2,1)S(1)} %collective-permute-done.refs_3_), channel_id=1, source_target_pairs={{0,4},{4,0},{8,12},{12,8},{16,20},{20,16},{24,28},{28,24},{1,5},{5... | collective-permute-start | bytes 798728 | tf_op jit(solution)/shard_map/ppermute | solution.py:21
  17.3 14.9 %collective-permute-start.8 = (bf16[2,256,512]{2,1,0:T(8,128)(2,1)S(1)}, bf16[2,256,512]{2,1,0:T(8,128)(2,1)S(1)}, u32[]{:S(2)}, u32[]{:S(2)}) collective-permute-start(bf16[2,256,512]{2,1,0:T(8,128)(2,1)S(1)} %get-tuple-element.173), channel_id=1, source_target_pairs={{0,2},{1,3},{2,0},{3,1},{4,6},{5,7},{6,4},{7,5},{8,10},{9,11},{10,... | collective-permute-start | bytes 1572872 | tf_op jit(solution)/shard_map/ppermute | solution.py:21
  20.7 1.4 %collective-permute-start.6 = (bf16[2,64,512]{2,1,0:T(8,128)(2,1)S(1)}, bf16[2,64,512]{2,1,0:T(8,128)(2,1)S(1)}, u32[]{:S(2)}, u32[]{:S(2)}) collective-permute-start(bf16[2,64,512]{2,1,0:T(8,128)(2,1)S(1)} %slice.12), channel_id=1, source_target_pairs={{0,1},{1,0},{2,3},{3,2},{4,5},{5,4},{6,7},{7,6},{8,9},{9,8},{10,11... | collective-permute-start | bytes 393224 | tf_op jit(solution)/shard_map/ppermute | solution.py:21
  20.8 7.0 %collective-permute-start.9 = (bf16[1040,128]{1,0:T(8,128)(2,1)S(1)}, bf16[1040,128]{1,0:T(8,128)(2,1)S(1)}, u32[]{:S(2)}, u32[]{:S(2)}) collective-permute-start(bf16[1040,128]{1,0:T(8,128)(2,1)S(1)} %collective-permute-done.refs_3_), channel_id=1, source_target_pairs={{0,1},{1,0},{2,3},{3,2},{4,5},{5,4},{6,7},{7,6},{8,9},{9,8},{10,11... | collective-permute-start | bytes 798728 | tf_op jit(solution)/shard_map/ppermute | solution.py:21
  25.5 2.3 %collective-permute-start.10 = (bf16[1040,128]{1,0:T(8,128)(2,1)S(1)}, bf16[1040,128]{1,0:T(8,128)(2,1)S(1)}, u32[]{:S(2)}, u32[]{:S(2)}) collective-permute-start(bf16[1040,128]{1,0:T(8,128)(2,1)S(1)} %collective-permute-done.7.refs_4_), channel_id=1, source_target_pairs={{0,1},{1,0},{2,3},{3,2},{4,5},{5,4},{6,7},{7,6},{8,9},{9,8},{10,11... | collective-permute-start | bytes 798728 | tf_op jit(solution)/shard_map/ppermute | solution.py:21
  25.8 12.7 %collective-permute-start.12 = (bf16[4,64,512]{2,1,0:T(8,128)(2,1)S(1)}, bf16[4,64,512]{2,1,0:T(8,128)(2,1)S(1)}, u32[]{:S(2)}, u32[]{:S(2)}) collective-permute-start(bf16[4,64,512]{2,1,0:T(8,128)(2,1)S(1)} %get-tuple-element.186), channel_id=1, source_target_pairs={{0,2},{1,3},{2,0},{3,1},{4,6},{5,7},{6,4},{7,5},{8,10},{9,11},{10,... | collective-permute-start | bytes 786440 | tf_op jit(solution)/shard_map/ppermute | solution.py:21
  27.7 4.5 %collective-permute-start.11 = (bf16[2,64,512]{2,1,0:T(8,128)(2,1)S(1)}, bf16[2,64,512]{2,1,0:T(8,128)(2,1)S(1)}, u32[]{:S(2)}, u32[]{:S(2)}) collective-permute-start(bf16[2,64,512]{2,1,0:T(8,128)(2,1)S(1)} %get-tuple-element.178), channel_id=1, source_target_pairs={{0,1},{1,0},{2,3},{3,2},{4,5},{5,4},{6,7},{7,6},{8,9},{9,8},{10,11... | collective-permute-start | bytes 393224 | tf_op jit(solution)/shard_map/ppermute | solution.py:21
  32.2 10.2 %collective-permute-start.14 = (bf16[256,512]{1,0:T(8,128)(2,1)S(1)}, bf16[256,512]{1,0:T(8,128)(2,1)S(1)}, u32[]{:S(2)}, u32[]{:S(2)}) collective-permute-start(bf16[256,512]{1,0:T(8,128)(2,1)S(1)} %get-tuple-element.200.refs_10_), channel_id=1, source_target_pairs={{0,1},{1,0},{2,3},{3,2},{4,5},{5,4},{6,7},{7,6},{8,9},{9,8},{10,11... | collective-permute-start | bytes 786440 | tf_op jit(solution)/shard_map/ppermute | solution.py:21
  32.3 10.1 %collective-permute-start.15 = (bf16[256,512]{1,0:T(8,128)(2,1)S(1)}, bf16[256,512]{1,0:T(8,128)(2,1)S(1)}, u32[]{:S(2)}, u32[]{:S(2)}) collective-permute-start(bf16[256,512]{1,0:T(8,128)(2,1)S(1)} %get-tuple-element.200.refs_10_), channel_id=1, source_target_pairs={{0,4},{4,0},{8,12},{12,8},{16,20},{20,16},{24,28},{28,24},{1,5},{5... | collective-permute-start | bytes 786440 | tf_op jit(solution)/shard_map/ppermute | solution.py:21
  34.0 8.4 %collective-permute-start.16 = (bf16[256,512]{1,0:T(8,128)(2,1)S(1)}, bf16[256,512]{1,0:T(8,128)(2,1)S(1)}, u32[]{:S(2)}, u32[]{:S(2)}) collective-permute-start(bf16[256,512]{1,0:T(8,128)(2,1)S(1)} %get-tuple-element.201.refs_12_), channel_id=1, source_target_pairs={{0,1},{1,0},{2,3},{3,2},{4,5},{5,4},{6,7},{7,6},{8,9},{9,8},{10,11... | collective-permute-start | bytes 786440 | tf_op jit(solution)/shard_map/ppermute | solution.py:21
  34.2 8.6 %collective-permute-start.17 = (bf16[256,512]{1,0:T(8,128)(2,1)S(1)}, bf16[256,512]{1,0:T(8,128)(2,1)S(1)}, u32[]{:S(2)}, u32[]{:S(2)}) collective-permute-start(bf16[256,512]{1,0:T(8,128)(2,1)S(1)} %get-tuple-element.201.refs_12_), channel_id=1, source_target_pairs={{0,8},{4,12},{8,0},{12,4},{16,24},{20,28},{24,16},{28,20},{1,9},{5... | collective-permute-start | bytes 786440 | tf_op jit(solution)/shard_map/ppermute | solution.py:21
  38.5 1.4 %collective-permute-start.13 = (bf16[2,64,512]{2,1,0:T(8,128)(2,1)S(1)}, bf16[2,64,512]{2,1,0:T(8,128)(2,1)S(1)}, u32[]{:S(2)}, u32[]{:S(2)}) collective-permute-start(bf16[2,64,512]{2,1,0:T(8,128)(2,1)S(1)} %slice.10), channel_id=1, source_target_pairs={{0,1},{1,0},{2,3},{3,2},{4,5},{5,4},{6,7},{7,6},{8,9},{9,8},{10,11... | collective-permute-start | bytes 393224 | tf_op jit(solution)/shard_map/ppermute | solution.py:21
  42.7 1.5 %collective-permute-start.18 = (bf16[256,512]{1,0:T(8,128)(2,1)S(1)}, bf16[256,512]{1,0:T(8,128)(2,1)S(1)}, u32[]{:S(2)}, u32[]{:S(2)}) collective-permute-start(bf16[256,512]{1,0:T(8,128)(2,1)S(1)} %collective-permute-done.15.refs_11_), channel_id=1, source_target_pairs={{0,1},{1,0},{2,3},{3,2},{4,5},{5,4},{6,7},{7,6},{8,9},{9,8},{10,11... | collective-permute-start | bytes 786440 | tf_op jit(solution)/shard_map/ppermute | solution.py:21
  42.7 1.9 %collective-permute-start.19 = (bf16[256,512]{1,0:T(8,128)(2,1)S(1)}, bf16[256,512]{1,0:T(8,128)(2,1)S(1)}, u32[]{:S(2)}, u32[]{:S(2)}) collective-permute-start(bf16[256,512]{1,0:T(8,128)(2,1)S(1)} %collective-permute-done.17.refs_13_), channel_id=1, source_target_pairs={{0,1},{1,0},{2,3},{3,2},{4,5},{5,4},{6,7},{7,6},{8,9},{9,8},{10,11... | collective-permute-start | bytes 786440 | tf_op jit(solution)/shard_map/ppermute | solution.py:21
  43.2 6.9 %collective-permute-start.20 = (bf16[1,2,8,64,512]{4,3,2,1,0:T(8,128)(2,1)S(1)}, bf16[1,2,8,64,512]{4,3,2,1,0:T(8,128)(2,1)S(1)}, u32[]{:S(2)}, u32[]{:S(2)}) collective-permute-start(bf16[1,2,8,64,512]{4,3,2,1,0:T(8,128)(2,1)S(1)} %get-tuple-element.213), channel_id=1, source_target_pairs={{0,1},{1,0},{2,3},{3,2},{4,5},{5,4},{6,7},{7,6},{8,9},{9,8},{10,11... | collective-permute-start | bytes 3145736 | tf_op jit(solution)/shard_map/ppermute | solution.py:21
  46.8 3.4 %collective-permute-start.21 = (bf16[1,2,8,64,512]{4,3,2,1,0:T(8,128)(2,1)S(1)}, bf16[1,2,8,64,512]{4,3,2,1,0:T(8,128)(2,1)S(1)}, u32[]{:S(2)}, u32[]{:S(2)}) collective-permute-start(bf16[1,2,8,64,512]{4,3,2,1,0:T(8,128)(2,1)S(1)} %get-tuple-element.215), channel_id=1, source_target_pairs={{0,1},{1,0},{2,3},{3,2},{4,5},{5,4},{6,7},{7,6},{8,9},{9,8},{10,11... | collective-permute-start | bytes 3145736 | tf_op jit(solution)/shard_map/ppermute | solution.py:21
  50.6 14.3 %collective-permute-start.23 = (bf16[2,4,64,512]{3,2,1,0:T(8,128)(2,1)S(1)}, bf16[2,4,64,512]{3,2,1,0:T(8,128)(2,1)S(1)}, u32[]{:S(2)}, u32[]{:S(2)}) collective-permute-start(bf16[2,4,64,512]{3,2,1,0:T(8,128)(2,1)S(1)} %get-tuple-element.234), channel_id=1, source_target_pairs={{0,4},{4,0},{8,12},{12,8},{16,20},{20,16},{24,28},{28,24},{1,5},{5... | collective-permute-start | bytes 1572872 | tf_op jit(solution)/shard_map/ppermute | solution.py:21
  51.1 13.9 %collective-permute-start.24 = (bf16[8,64,512]{2,1,0:T(8,128)(2,1)S(1)}, bf16[8,64,512]{2,1,0:T(8,128)(2,1)S(1)}, u32[]{:S(2)}, u32[]{:S(2)}) collective-permute-start(bf16[8,64,512]{2,1,0:T(8,128)(2,1)S(1)} %get-tuple-element.237), channel_id=1, source_target_pairs={{0,2},{1,3},{2,0},{3,1},{4,6},{5,7},{6,4},{7,5},{8,10},{9,11},{10,... | collective-permute-start | bytes 1572872 | tf_op jit(solution)/shard_map/ppermute | solution.py:21
  62.1 1.6 %collective-permute-start.25 = (bf16[1,4,272,128]{3,2,1,0:T(8,128)(2,1)S(1)}, bf16[1,4,272,128]{3,2,1,0:T(8,128)(2,1)S(1)}, u32[]{:S(2)}, u32[]{:S(2)}) collective-permute-start(bf16[1,4,272,128]{3,2,1,0:T(8,128)(2,1)S(1)} %get-tuple-element.240), channel_id=1, source_target_pairs={{0,1},{1,0},{2,3},{3,2},{4,5},{5,4},{6,7},{7,6},{8,9},{9,8},{10,11... | collective-permute-start | bytes 835592 | tf_op jit(solution)/shard_map/ppermute | solution.py:21
  62.2 1.9 %collective-permute-start.26 = (bf16[1,4,272,128]{3,2,1,0:T(8,128)(2,1)S(1)}, bf16[1,4,272,128]{3,2,1,0:T(8,128)(2,1)S(1)}, u32[]{:S(2)}, u32[]{:S(2)}) collective-permute-start(bf16[1,4,272,128]{3,2,1,0:T(8,128)(2,1)S(1)} %get-tuple-element.241), channel_id=1, source_target_pairs={{0,1},{1,0},{2,3},{3,2},{4,5},{5,4},{6,7},{7,6},{8,9},{9,8},{10,11... | collective-permute-start | bytes 835592 | tf_op jit(solution)/shard_map/ppermute | solution.py:21
  62.7 21.4 %collective-permute-start.22 = (bf16[1,8,272,128]{3,2,1,0:T(8,128)(2,1)S(1)}, bf16[1,8,272,128]{3,2,1,0:T(8,128)(2,1)S(1)}, u32[]{:S(2)}, u32[]{:S(2)}) collective-permute-start(bf16[1,8,272,128]{3,2,1,0:T(8,128)(2,1)S(1)} %get-tuple-element.232), channel_id=1, source_target_pairs={{0,1},{1,0},{2,3},{3,2},{4,5},{5,4},{6,7},{7,6},{8,9},{9,8},{10,11... | collective-permute-start | bytes 1671176 | tf_op jit(solution)/shard_map/ppermute | solution.py:21
  65.2 9.3 %collective-permute-start.33 = (bf16[4,64,512]{2,1,0:T(8,128)(2,1)S(1)}, bf16[4,64,512]{2,1,0:T(8,128)(2,1)S(1)}, u32[]{:S(2)}, u32[]{:S(2)}) collective-permute-start(bf16[4,64,512]{2,1,0:T(8,128)(2,1)S(1)} %get-tuple-element.253), channel_id=1, source_target_pairs={{0,2},{1,3},{2,0},{3,1},{4,6},{5,7},{6,4},{7,5},{8,10},{9,11},{10,... | collective-permute-start | bytes 786440 | tf_op jit(solution)/shard_map/ppermute | solution.py:21
  66.9 7.7 %collective-permute-start.34 = (bf16[4,64,512]{2,1,0:T(8,128)(2,1)S(1)}, bf16[4,64,512]{2,1,0:T(8,128)(2,1)S(1)}, u32[]{:S(2)}, u32[]{:S(2)}) collective-permute-start(bf16[4,64,512]{2,1,0:T(8,128)(2,1)S(1)} %get-tuple-element.257), channel_id=1, source_target_pairs={{0,8},{4,12},{8,0},{12,4},{16,24},{20,28},{24,16},{28,20},{1,9},{5... | collective-permute-start | bytes 786440 | tf_op jit(solution)/shard_map/ppermute | solution.py:21
  68.4 15.7 %collective-permute-start.27 = (bf16[4,272,128]{2,1,0:T(8,128)(2,1)S(1)}, bf16[4,272,128]{2,1,0:T(8,128)(2,1)S(1)}, u32[]{:S(2)}, u32[]{:S(2)}) collective-permute-start(bf16[4,272,128]{2,1,0:T(8,128)(2,1)S(1)} %get-tuple-element.244), channel_id=1, source_target_pairs={{0,2},{1,3},{2,0},{3,1},{4,6},{5,7},{6,4},{7,5},{8,10},{9,11},{10,... | collective-permute-start | bytes 835592 | tf_op jit(solution)/shard_map/ppermute | solution.py:21
  68.9 16.0 %collective-permute-start.28 = (bf16[4,272,128]{2,1,0:T(8,128)(2,1)S(1)}, bf16[4,272,128]{2,1,0:T(8,128)(2,1)S(1)}, u32[]{:S(2)}, u32[]{:S(2)}) collective-permute-start(bf16[4,272,128]{2,1,0:T(8,128)(2,1)S(1)} %get-tuple-element.245), channel_id=1, source_target_pairs={{0,2},{1,3},{2,0},{3,1},{4,6},{5,7},{6,4},{7,5},{8,10},{9,11},{10,... | collective-permute-start | bytes 835592 | tf_op jit(solution)/shard_map/ppermute | solution.py:21
  74.6 5.0 %collective-permute-start.35 = (bf16[2,64,512]{2,1,0:T(8,128)(2,1)S(1)}, bf16[2,64,512]{2,1,0:T(8,128)(2,1)S(1)}, u32[]{:S(2)}, u32[]{:S(2)}) collective-permute-start(bf16[2,64,512]{2,1,0:T(8,128)(2,1)S(1)} %get-tuple-element.259), channel_id=1, source_target_pairs={{0,8},{4,12},{8,0},{12,4},{16,24},{20,28},{24,16},{28,20},{1,9},{5... | collective-permute-start | bytes 393224 | tf_op jit(solution)/shard_map/ppermute | solution.py:21
  76.4 5.0 %collective-permute-start.36 = (bf16[2,64,512]{2,1,0:T(8,128)(2,1)S(1)}, bf16[2,64,512]{2,1,0:T(8,128)(2,1)S(1)}, u32[]{:S(2)}, u32[]{:S(2)}) collective-permute-start(bf16[2,64,512]{2,1,0:T(8,128)(2,1)S(1)} %get-tuple-element.261), channel_id=1, source_target_pairs={{0,4},{4,0},{8,12},{12,8},{16,20},{20,16},{24,28},{28,24},{1,5},{5... | collective-permute-start | bytes 393224 | tf_op jit(solution)/shard_map/ppermute | solution.py:21
  81.4 12.6 %collective-permute-start.37 = (bf16[2,2,64,512]{3,2,1,0:T(8,128)(2,1)S(1)}, bf16[2,2,64,512]{3,2,1,0:T(8,128)(2,1)S(1)}, u32[]{:S(2)}, u32[]{:S(2)}) collective-permute-start(bf16[2,2,64,512]{3,2,1,0:T(8,128)(2,1)S(1)} %join.1.refs_0_), channel_id=1, source_target_pairs={{0,16},{4,20},{8,24},{12,28},{16,0},{20,4},{24,8},{28,12},{1,17},{... | collective-permute-start | bytes 786440 | tf_op jit(solution)/shard_map/ppermute | solution.py:21
  85.2 5.8 %collective-permute-start.29 = (bf16[2,272,128]{2,1,0:T(8,128)(2,1)S(1)}, bf16[2,272,128]{2,1,0:T(8,128)(2,1)S(1)}, u32[]{:S(2)}, u32[]{:S(2)}) collective-permute-start(bf16[2,272,128]{2,1,0:T(8,128)(2,1)S(1)} %get-tuple-element.247), channel_id=1, source_target_pairs={{0,4},{4,0},{8,12},{12,8},{16,20},{20,16},{24,28},{28,24},{1,5},{5... | collective-permute-start | bytes 417800 | tf_op jit(solution)/shard_map/ppermute | solution.py:21
  86.6 5.8 %collective-permute-start.30 = (bf16[2,272,128]{2,1,0:T(8,128)(2,1)S(1)}, bf16[2,272,128]{2,1,0:T(8,128)(2,1)S(1)}, u32[]{:S(2)}, u32[]{:S(2)}) collective-permute-start(bf16[2,272,128]{2,1,0:T(8,128)(2,1)S(1)} %get-tuple-element.248), channel_id=1, source_target_pairs={{0,4},{4,0},{8,12},{12,8},{16,20},{20,16},{24,28},{28,24},{1,5},{5... | collective-permute-start | bytes 417800 | tf_op jit(solution)/shard_map/ppermute | solution.py:21
  87.2 24.6 %collective-permute-start.44 = (bf16[8,64,512]{2,1,0:T(8,128)(2,1)S(1)}, bf16[8,64,512]{2,1,0:T(8,128)(2,1)S(1)}, u32[]{:S(2)}, u32[]{:S(2)}) collective-permute-start(bf16[8,64,512]{2,1,0:T(8,128)(2,1)S(1)} %get-tuple-element.267), channel_id=1, source_target_pairs={{0,2},{1,3},{2,0},{3,1},{4,6},{5,7},{6,4},{7,5},{8,10},{9,11},{10,... | collective-permute-start | bytes 1572872 | tf_op jit(solution)/shard_map/ppermute | solution.py:21
  92.5 5.2 %collective-permute-start.31 = (bf16[1,272,128]{2,1,0:T(8,128)(2,1)S(1)}, bf16[1,272,128]{2,1,0:T(8,128)(2,1)S(1)}, u32[]{:S(2)}, u32[]{:S(2)}) collective-permute-start(bf16[1,272,128]{2,1,0:T(8,128)(2,1)S(1)} %get-tuple-element.250), channel_id=1, source_target_pairs={{0,8},{4,12},{8,0},{12,4},{16,24},{20,28},{24,16},{28,20},{1,9},{5... | collective-permute-start | bytes 208904 | tf_op jit(solution)/shard_map/ppermute | solution.py:21
  94.1 4.4 %collective-permute-start.32 = (bf16[1,272,128]{2,1,0:T(8,128)(2,1)S(1)}, bf16[1,272,128]{2,1,0:T(8,128)(2,1)S(1)}, u32[]{:S(2)}, u32[]{:S(2)}) collective-permute-start(bf16[1,272,128]{2,1,0:T(8,128)(2,1)S(1)} %get-tuple-element.251), channel_id=1, source_target_pairs={{0,8},{4,12},{8,0},{12,4},{16,24},{20,28},{24,16},{28,20},{1,9},{5... | collective-permute-start | bytes 208904 | tf_op jit(solution)/shard_map/ppermute | solution.py:21
  94.8 7.1 %collective-permute-start.40 = (bf16[2,64,512]{2,1,0:T(8,128)(2,1)S(1)}, bf16[2,64,512]{2,1,0:T(8,128)(2,1)S(1)}, u32[]{:S(2)}, u32[]{:S(2)}) collective-permute-start(bf16[2,64,512]{2,1,0:T(8,128)(2,1)S(1)} %get-tuple-element.262.refs_3_), channel_id=1, source_target_pairs={{0,8},{4,12},{8,0},{12,4},{16,24},{20,28},{24,16},{28,20},{1,9},{5... | collective-permute-start | bytes 393224 | tf_op jit(solution)/shard_map/ppermute | solution.py:21
  96.3 7.0 %collective-permute-start.42 = (bf16[2,64,512]{2,1,0:T(8,128)(2,1)S(1)}, bf16[2,64,512]{2,1,0:T(8,128)(2,1)S(1)}, u32[]{:S(2)}, u32[]{:S(2)}) collective-permute-start(bf16[2,64,512]{2,1,0:T(8,128)(2,1)S(1)} %get-tuple-element.264), channel_id=1, source_target_pairs={{0,4},{4,0},{8,12},{12,8},{16,20},{20,16},{24,28},{28,24},{1,5},{5... | collective-permute-start | bytes 393224 | tf_op jit(solution)/shard_map/ppermute | solution.py:21
  98.5 7.8 %collective-permute-start.38 = (bf16[2,272,128]{2,1,0:T(8,128)(2,1)S(1)}, bf16[2,272,128]{2,1,0:T(8,128)(2,1)S(1)}, u32[]{:S(2)}, u32[]{:S(2)}) collective-permute-start(bf16[2,272,128]{2,1,0:T(8,128)(2,1)S(1)} %add_parts.5.refs_0_), channel_id=1, source_target_pairs={{0,16},{4,20},{8,24},{12,28},{16,0},{20,4},{24,8},{28,12},{1,17},{... | collective-permute-start | bytes 417800 | tf_op jit(solution)/shard_map/ppermute | solution.py:21
  101.9 10.0 %collective-permute-start.41 = (bf16[4,64,512]{2,1,0:T(8,128)(2,1)S(1)}, bf16[4,64,512]{2,1,0:T(8,128)(2,1)S(1)}, u32[]{:S(2)}, u32[]{:S(2)}) collective-permute-start(bf16[4,64,512]{2,1,0:T(8,128)(2,1)S(1)} %constant_dynamic-update-slice_fusion.refs_0_), channel_id=1, source_target_pairs={{0,4},{4,0},{8,12},{12,8},{16,20},{20,16},{24,28},{28,24},{1,5},{5... | collective-permute-start | bytes 786440 | tf_op jit(solution)/shard_map/ppermute | solution.py:21
  103.3 8.6 %collective-permute-start.43 = (bf16[4,64,512]{2,1,0:T(8,128)(2,1)S(1)}, bf16[4,64,512]{2,1,0:T(8,128)(2,1)S(1)}, u32[]{:S(2)}, u32[]{:S(2)}) collective-permute-start(bf16[4,64,512]{2,1,0:T(8,128)(2,1)S(1)} %constant_dynamic-update-slice_fusion.2.refs_2_), channel_id=1, source_target_pairs={{0,8},{4,12},{8,0},{12,4},{16,24},{20,28},{24,16},{28,20},{1,9},{5... | collective-permute-start | bytes 786440 | tf_op jit(solution)/shard_map/ppermute | solution.py:21
  106.4 5.5 %collective-permute-start.39 = (bf16[2,272,128]{2,1,0:T(8,128)(2,1)S(1)}, bf16[2,272,128]{2,1,0:T(8,128)(2,1)S(1)}, u32[]{:S(2)}, u32[]{:S(2)}) collective-permute-start(bf16[2,272,128]{2,1,0:T(8,128)(2,1)S(1)} %meet.3), channel_id=1, source_target_pairs={{0,8},{4,12},{8,0},{12,4},{16,24},{20,28},{24,16},{28,20},{1,9},{5... | collective-permute-start | bytes 417800 | tf_op jit(solution)/shard_map/ppermute | solution.py:21
  111.9 6.6 %collective-permute-start.47 = (bf16[4,272,128]{2,1,0:T(8,128)(2,1)S(1)}, bf16[4,272,128]{2,1,0:T(8,128)(2,1)S(1)}, u32[]{:S(2)}, u32[]{:S(2)}) collective-permute-start(bf16[4,272,128]{2,1,0:T(8,128)(2,1)S(1)} %pad_maximum_fusion.refs_0_), channel_id=1, source_target_pairs={{0,4},{4,0},{8,12},{12,8},{16,20},{20,16},{24,28},{28,24},{1,5},{5... | collective-permute-start | bytes 835592 | tf_op jit(solution)/shard_map/ppermute | solution.py:21
  113.0 2.3 %collective-permute-start.45 = (bf16[4,64,512]{2,1,0:T(8,128)(2,1)S(1)}, bf16[4,64,512]{2,1,0:T(8,128)(2,1)S(1)}, u32[]{:S(2)}, u32[]{:S(2)}) collective-permute-start(bf16[4,64,512]{2,1,0:T(8,128)(2,1)S(1)} %get-tuple-element.269), channel_id=1, source_target_pairs={{0,1},{1,0},{2,3},{3,2},{4,5},{5,4},{6,7},{7,6},{8,9},{9,8},{10,11... | collective-permute-start | bytes 786440 | tf_op jit(solution)/shard_map/ppermute | solution.py:21
  113.0 2.3 %collective-permute-start.46 = (bf16[4,64,512]{2,1,0:T(8,128)(2,1)S(1)}, bf16[4,64,512]{2,1,0:T(8,128)(2,1)S(1)}, u32[]{:S(2)}, u32[]{:S(2)}) collective-permute-start(bf16[4,64,512]{2,1,0:T(8,128)(2,1)S(1)} %slice.11), channel_id=1, source_target_pairs={{0,1},{1,0},{2,3},{3,2},{4,5},{5,4},{6,7},{7,6},{8,9},{9,8},{10,11... | collective-permute-start | bytes 786440 | tf_op jit(solution)/shard_map/ppermute | solution.py:21
  (13 other events, 149.7 us)

commit v7 on v6

--- a/solution.py
+++ b/solution.py
@@ -87,12 +87,16 @@
     return pl.ds(pl.multiple_of(start * size, size), size)
 
 
-def whole(pieces, x_bit):
-    if len(pieces) == 1:
-        return pieces[0][...]
-    a, b = pieces[0][...], pieces[1][...]
-    first = x_bit == 0
+def in_order(a, b, bit):
+    first = bit == 0
     return jnp.concatenate([jnp.where(first, a, b), jnp.where(first, b, a)], 0)
+
+
+def whole(pieces, x_bit, z_bit=None):
+    values = [v[...] for v in pieces]
+    if len(values) == 4:
+        return in_order(in_order(*values[:2], x_bit), in_order(*values[2:], x_bit), z_bit)
+    return in_order(*values, x_bit) if len(values) == 2 else values[0]
 
 
 def take(refs, counts):
@@ -108,7 +112,8 @@
     high = v.astype(BF16).astype(F32)
     rest = v - high
     middle = rest.astype(BF16).astype(F32)
-    return jnp.concatenate([high, middle, rest - middle, jnp.zeros_like(v)], 0).astype(BF16)
+    zeros = jnp.zeros((5 * v.shape[0], v.shape[1]), F32)
+    return jnp.concatenate([high, middle, rest - middle, zeros], 0).astype(BF16)
 
 
 def two_parts(v):
@@ -148,7 +153,7 @@
         sub = width // n_dp
         factor = HD**-0.5
         o_at, s_at = 3 * width, 4 * width
-        bundle_rows = 4 * width + 4 * VEC
+        bundle_rows = 4 * width + 8 * VEC
 
         def mp_swap(v, bit):
             return swap(v, "mp", bit, n_mp)
@@ -184,8 +189,8 @@
             return copies
 
         def begin(ins, outs, scratch):
-            x_bit = lax.axis_index("dp") & 1
-            bundle, half = outs[-2:]
+            dpi = lax.axis_index("dp")
+            bundle, quarter = outs[-2:]
             copies = cut_copies(ins[0], outs, scratch[0])
             copies.append(
                 pltpu.make_async_copy(ins[1], bundle.at[pl.ds(0, o_at)], scratch[1])
@@ -207,9 +212,10 @@
             bundle[s_at:] = three_parts(small)
             for c in copies:
                 c.wait()
-            half[...] = bundle[rows_of(x_bit, bundle_rows // 2)]
-
-        *token_parts, bundle, bundle_half = run(
+            mine = 2 * ((dpi >> 1) & 1) + (dpi & 1)
+            quarter[...] = bundle[rows_of(mine, bundle_rows // 4)]
+
+        *token_parts, bundle, bundle_quarter = run(
             "begin",
             begin,
             [
@@ -221,7 +227,7 @@
                 order_bias.reshape(1, per),
             ],
             row_shapes
-            + [shape((bundle_rows, lane), BF16), shape((bundle_rows // 2, lane), BF16)],
+            + [shape((bundle_rows, lane), BF16), shape((bundle_rows // 4, lane), BF16)],
             [pltpu.SemaphoreType.DMA((n_mp,)), pltpu.SemaphoreType.DMA(())],
             hbm=(0, 1),
             limit=VMEM_MOST,
@@ -249,30 +255,28 @@
             + ([shape((2,) + half_shapes[0].shape, BF16)] if joined else half_shapes),
             [pltpu.SemaphoreType.DMA((n_mp,)), pltpu.SemaphoreType.DMA((2,))],
             hbm=(0, 1, 2),
-            after=[bundle_half],
+            after=[bundle_quarter],
+            limit=VMEM_MOST,
         )
         cot_parts, half_parts = list(rest[: len(row_shapes)]), rest[len(row_shapes) :]
 
-        sends, (bundle, bundle_half) = together(token_parts[1:], [bundle, bundle_half])
+        sends, (bundle, bundle_quarter) = together(token_parts[1:], [bundle, bundle_quarter])
         token_parts = token_parts[:1] + send_rows(sends[0], sends[1:])
-        bundle_core, bundle_y = mp_swap(bundle, 1), over_y(bundle_half)
+        bundle_core, bundle_y = mp_swap(bundle, 1), over_y(bundle_quarter)
 
         near = [w_up, w_down]
         near_core = [mp_swap(v, 1) for v in near]
-        bundle_y, (bundle_core,), token_parts[:2], half_parts, cot_parts, near_core = together(
-            bundle_y, [bundle_core], token_parts[:2], half_parts, cot_parts, near_core
+        bundle_y, (bundle_core,), token_parts[:2], near_core = together(
+            bundle_y, [bundle_core], token_parts[:2], near_core
         )
         halves_y = [over_y(v) for v in half_parts]
-        bundle_x = [dp_swap(v, 1) for v in bundle_y]
+        bundle_x, bundle_z = ([dp_swap(v, bit) for v in bundle_y] for bit in (1, 2))
+        bundle_xz = [dp_swap(v, 2) for v in bundle_x]
         bundle_yc = [mp_swap(v, 1) for v in bundle_y]
         token_parts = token_parts[:2] + pass_rows(token_parts[2:])
 
-        def far(first, second, first_core, second_core):
-            return [
-                v
-                for n in range(len(y_peers))
-                for v in (first[n], second[n], first_core[n], second_core[n])
-            ]
+        def far(even, odd):
+            return [v[n] for n in range(len(y_peers)) for vs in (even, odd) for v in vs]
 
         def order_row(om_ref, me, r):
             v = om_ref[pl.ds(me * own + r, 1), :].astype(F32)
@@ -317,7 +321,7 @@
             counts = [len(pieces) // len(group)] * len(group)
 
             def fn(ins, outs, scratch):
-                me, x_bit = lax.axis_index("mp"), lax.axis_index("dp") & 1
+                me, dpi = lax.axis_index("mp"), lax.axis_index("dp")
                 qkv_ref, p_ref, att_ref, weights, wo, smalls = outs[-6:]
                 if first:
                     lens, om, gains, shifts = ins[n_mp : n_mp + 4]
@@ -328,7 +332,7 @@
                 else:
                     lens, om, a1_ref = ins[:3]
                 for j, ps in enumerate(take(ins[-len(pieces) :], counts)):
-                    v = whole(ps, x_bit)
+                    v = whole(ps, dpi & 1, (dpi >> 1) & 1)
                     weights[:, j * lane : (j + 1) * lane] = v[:o_at]
                     for c in range(cols):
                         wo[j * lane : (j + 1) * lane, c * lane : (c + 1) * lane] = v[
@@ -393,11 +397,18 @@
 
         x, a1, qkv0, p0, att0, wq0, wo0, small0 = attend(groups[0], True, [bundle, bundle_core])
 
-        bundle_x, (att0,), sends = together(bundle_x, [att0], cot_parts[1:])
+        bundle_x, bundle_z, bundle_xz, (att0,), sends = together(
+            bundle_x, bundle_z, bundle_xz, [att0], cot_parts[1:]
+        )
         cot_parts = cot_parts[:1] + send_rows(sends[0], sends[1:])
-        bundle_xc = [mp_swap(v, 1) for v in bundle_x]
+        bundle_xc, bundle_zc, bundle_xzc = (
+            [mp_swap(v, 1) for v in vs] for vs in (bundle_x, bundle_z, bundle_xz)
+        )
         qkv1, p1, att1, wq1, wo1, small1 = attend(
-            groups[1], False, far(bundle_y, bundle_x, bundle_yc, bundle_xc)
+            groups[1], False, far(
+                (bundle_y, bundle_x, bundle_z, bundle_xz),
+                (bundle_yc, bundle_xc, bundle_zc, bundle_xzc),
+            )
         )
 
         def take_apart(ins, outs, _):
@@ -516,8 +527,8 @@
         up_xc, down_zc = ([mp_swap(v, 1) for v in vs] for vs in (up_x, down_z))
         got0 = mp_swap(send0, 1)
 
-        up1 = far(up_y, up_x, up_yc, up_xc)
-        down1 = far(down_y, down_z, down_yc, down_zc)
+        up1 = far((up_y, up_x), (up_yc, up_xc))
+        down1 = far((down_y, down_z), (down_yc, down_zc))
 
         def mlp_far(j, last):
             ks = g1[j::2]
@@ -525,7 +536,7 @@
 
             def fn(ins, outs, scratch):
                 dpi = lax.axis_index("dp")
-                lead, wu_p, wd_p = take(ins, [10, n_w, n_w])
+                lead, wu_p, wd_p, done = take(ins, [10, n_w, n_w, 2 if last else 0])
                 x1, a2, a2t, dy, dyt, mixed_in, d_mid_in, smalls, gains, ob = lead
                 (mixed, d_mid), gs = (scratch[:2], scratch[2:]) if last else (outs[:2], scratch)
                 mixed[...] = mixed_in[...]
@@ -534,7 +545,10 @@
                 for n in range(len(ks)):
                     wu = whole(wu_p[2 * n : 2 * n + 2], dpi & 1)
                     wd = whole(wd_p[2 * n : 2 * n + 2], (dpi >> 1) & 1)
-                    hidden, slope = mlp_forward(a2, wu, wd, smalls.at[2 * n + j], mixed)
+                    if last:
+                        hidden, slope = done[0][n], done[1][n]
+                    else:
+                        hidden, slope = mlp_forward(a2, wu, wd, smalls.at[2 * n + j], mixed)
                     mlp_backward(
                         hidden,
                         slope,
@@ -573,12 +587,33 @@
                 fn,
                 [x1, a2, a2t, dy, dyt, mixed, d_mid, small1, norm_scale_pair, out_bias]
                 + [v for n in range(len(ks)) for v in up1[4 * n + 2 * j : 4 * n + 2 * j + 2]]
-                + [v for n in range(len(ks)) for v in down1[4 * n + 2 * j : 4 * n + 2 * j + 2]],
+                + [v for n in range(len(ks)) for v in down1[4 * n + 2 * j : 4 * n + 2 * j + 2]]
+                + ([far_hidden, far_slope] if last else []),
                 ([full_bf, full, full_bf, shape((4, width), F32)] if last else [full, full])
                 + mlp_outs(len(ks), 1),
                 (sums if last else []) + [pltpu.VMEM((2, width, hid), BF16)] * len(ks),
             )
 
+        def mlp_even_forward(ins, outs, _):
+            dpi = lax.axis_index("dp")
+            n_w = 2 * len(y_peers)
+            (a2, mixed_in, smalls), wu_p, wd_p = take(ins, [3, n_w, n_w])
+            mixed, hidden, slope = outs
+            mixed[...] = mixed_in[...]
+            for n in range(len(y_peers)):
+                wu = whole(wu_p[2 * n : 2 * n + 2], dpi & 1)
+                wd = whole(wd_p[2 * n : 2 * n + 2], (dpi >> 1) & 1)
+                hidden[n], slope[n] = mlp_forward(a2, wu, wd, smalls.at[2 * n], mixed)
+
+        mixed, far_hidden, far_slope = run(
+            "mlp_even_forward",
+            mlp_even_forward,
+            [a2, mixed, small1]
+            + [v for pair in zip(up_y, up_x) for v in pair]
+            + [v for pair in zip(down_y, down_z) for v in pair],
+            [full]
+            + [shape((len(y_peers), count, hid), kind) for kind in (BF16, F32)],
+        )
         mixed, d_mid, send1, gub1_odd = mlp_far(1, False)
         send1, mixed = together([send1, mixed])[0]
         got1 = mp_swap(send1, 1)

time: 120 us -> 117 us (0.975)
  waiting for transfers between devices: 32.9 us -> 29.6 us
  local copies, waits for them, and re-layouts: 4.19 us -> 1.02 us
  Pallas kernels: 35.8 us -> 37.6 us
  starting transfers between devices: 45.6 us -> 47.1 us
    ppermute x48 -> x52, waiting for transfers between devices: 32.9 us -> 29.6 us  [swap(): return lax.ppermute(v, axis, [(i, i ^ bit) for i in range(size)])]
    unnamed x28 -> x22, local copies, waits for them, and re-layouts: 4.14 us -> 0.96 us
    pallas_call x26 -> x27, Pallas kernels: 35.8 us -> 37.6 us  [run(): pl.pallas_call(kernel, out_shape=tuple(outs), in_specs=[pl.BlockSpec(memo...]
    ppermute x48 -> x52, starting transfers between devices: 45.6 us -> 47.1 us  [swap(): return lax.ppermute(v, axis, [(i, i ^ bit) for i in range(size)])]
  transfers between devices with their start and end apart: 48 -> 52, of which waited for: 21 -> 22; matrix products, arithmetic and copies ran while one was open for 0% -> 0% of each run, Pallas kernels for 26% -> 28%
where the time goes in v7:
time: 117 us; the launch traced here: 116 us
  starting transfers between devices  47.1 us (40%)
  Pallas kernels  37.6 us (32%)
  waiting for transfers between devices  29.6 us (25%)
    ppermute x52, starting transfers between devices, swap(): return lax.ppermute(v, axis, [(i, i ^ bit) for i in range(size)])  47.1 us
    pallas_call x27, Pallas kernels, run(): pl.pallas_call(kernel, out_shape=tuple(outs), in_specs=[pl.BlockSpec(memo...  37.6 us
    ppermute x52, waiting for transfers between devices, swap(): return lax.ppermute(v, axis, [(i, i ^ bit) for i in range(size)])  29.6 us
  transfers between devices with their start and end apart: 52, of which 22 were waited for; matrix products, arithmetic and copies ran while one was open for 0% of the time, Pallas kernels for 28%

profile of v7, /device:TPU:0, one launch (start us, length us, event | category | flops | bytes accessed | tf_op | source)
XLA Modules:
  0.0 116.4 jit_solution(3633377888252104295)
XLA Ops:
  0.7 3.2 %begin.1 = (bf16[2,64,512]{2,1,0:T(8,128)(2,1)}, bf16[2,64,512]{2,1,0:T(8,128)(2,1)}, bf16[4,64,512]{2,1,0:T(8,128)(2,1)}, bf16[2112,128]{1,0:T(8,128)(2,1)}, bf16[528,128]{1,0:T(8,128)(2,1)}) custom-call(bf16[8,64,512]{2,1,0:T(8,128)(2,1)} %refs_0_.4, bf16[1536,128]{1,0:T(8,128)(2,1)} %bitcast.9, bf16[128,512]{1,0:T(8,128)(2,1)} %refs_2_.3, ...), custom_call_target="tpu_custom_call" | custom-call | flops 1 | bytes 1 | tf_op jit(solution)/shard_map/begin/pallas_call | solution.py:43
  5.0 2.9 %collective-permute-start = (bf16[528,128]{1,0:T(8,128)(2,1)}, bf16[528,128]{1,0:T(8,128)(2,1)S(1)}, u32[]{:S(2)}, u32[]{:S(2)}) collective-permute-start(bf16[528,128]{1,0:T(8,128)(2,1)} %get-tuple-element.155.refs_3_), channel_id=1, source_target_pairs={{0,2},{1,3},{2,0},{3,1},{4,6},{5,7},{6,4},{7,5},{8,10},{9,11},{10,... | collective-permute-start | bytes 405512 | tf_op jit(solution)/shard_map/ppermute | solution.py:21
  8.0 2.8 %collective-permute-start.5 = (bf16[4,64,512]{2,1,0:T(8,128)(2,1)}, bf16[4,64,512]{2,1,0:T(8,128)(2,1)S(1)}, u32[]{:S(2)}, u32[]{:S(2)}) collective-permute-start(bf16[4,64,512]{2,1,0:T(8,128)(2,1)} %get-tuple-element.161), channel_id=1, source_target_pairs={{0,2},{1,3},{2,0},{3,1},{4,6},{5,7},{6,4},{7,5},{8,10},{9,11},{10,... | collective-permute-start | bytes 786440 | tf_op jit(solution)/shard_map/ppermute | solution.py:21
  10.8 1.2 %collective-permute-done.refs_3_ = bf16[528,128]{1,0:T(8,128)(2,1)S(1)} collective-permute-done((bf16[528,128]{1,0:T(8,128)(2,1)}, bf16[528,128]{1,0:T(8,128)(2,1)S(1)}, u32[]{:S(2)}, u32[]{:S(2)}) %collective-permute-start) | collective-permute-done | bytes 135200 | tf_op jit(solution)/shard_map/ppermute | solution.py:21
  12.0 1.8 %collective-permute-start.7 = (bf16[528,128]{1,0:T(8,128)(2,1)S(1)}, bf16[528,128]{1,0:T(8,128)(2,1)S(1)}, u32[]{:S(2)}, u32[]{:S(2)}) collective-permute-start(bf16[528,128]{1,0:T(8,128)(2,1)S(1)} %collective-permute-done.refs_3_), channel_id=1, source_target_pairs={{0,4},{4,0},{8,12},{12,8},{16,20},{20,16},{24,28},{28,24},{1,5},{5... | collective-permute-start | bytes 405512 | tf_op jit(solution)/shard_map/ppermute | solution.py:21
  13.8 2.3 %cut_rest.1 = (bf16[2,64,512]{2,1,0:T(8,128)(2,1)}, bf16[2,64,512]{2,1,0:T(8,128)(2,1)}, bf16[4,64,512]{2,1,0:T(8,128)(2,1)}, bf16[2,256,512]{2,1,0:T(8,128)(2,1)}) custom-call(bf16[8,64,512]{2,1,0:T(8,128)(2,1)} %refs_0_.5, bf16[512,512]{1,0:T(8,128)(2,1)} %refs_7_.5, bf16[512,512]{1,0:T(8,128)(2,1)} %refs_9_.5, bf16[528,128]{1,0:T(8,128)(2,1)} %get-tuple-element.155.refs_3_), custom_call_target="tpu_custom_call" | custom-call | flops 1 | bytes 1 | tf_op jit(solution)/shard_map/cut_rest/pallas_call | solution.py:43
  16.1 1.6 %collective-permute-start.10 = (bf16[2,256,512]{2,1,0:T(8,128)(2,1)}, bf16[2,256,512]{2,1,0:T(8,128)(2,1)S(1)}, u32[]{:S(2)}, u32[]{:S(2)}) collective-permute-start(bf16[2,256,512]{2,1,0:T(8,128)(2,1)} %get-tuple-element.170), channel_id=1, source_target_pairs={{0,2},{1,3},{2,0},{3,1},{4,6},{5,7},{6,4},{7,5},{8,10},{9,11},{10,... | collective-permute-start | bytes 1572872 | tf_op jit(solution)/shard_map/ppermute | solution.py:21
  17.7 1.6 %collective-permute-start.8 = (bf16[528,128]{1,0:T(8,128)(2,1)S(1)}, bf16[528,128]{1,0:T(8,128)(2,1)S(1)}, u32[]{:S(2)}, u32[]{:S(2)}) collective-permute-start(bf16[528,128]{1,0:T(8,128)(2,1)S(1)} %collective-permute-done.refs_3_), channel_id=1, source_target_pairs={{0,8},{4,12},{8,0},{12,4},{16,24},{20,28},{24,16},{28,20},{1,9},{5... | collective-permute-start | bytes 405512 | tf_op jit(solution)/shard_map/ppermute | solution.py:21
  22.1 3.3 %attend.2 = (bf16[512,512]{1,0:T(8,128)(2,1)S(1)}, bf16[512,512]{1,0:T(8,128)(2,1)S(1)}, bf16[3,512,256]{2,1,0:T(8,128)(2,1)S(1)}, bf16[8,256,256]{2,1,0:T(8,128...) custom-call(bf16[2,64,512]{2,1,0:T(8,128)(2,1)S(1)} %copy-done.4, ...), custom_call_target="tpu_custom_call" | custom-call | flops 1 | bytes 1 | tf_op jit(solution)/shard_map/attend/pallas_call | solution.py:43
  27.4 3.1 %attend.3 = (bf16[3,512,256]{2,1,0:T(8,128)(2,1)S(1)}, bf16[8,256,256]{2,1,0:T(8,128)(2,1)S(1)}, bf16[512,256]{1,0:T(8,128)(2,1)S(1)}, bf16[1536,256]{1,0:T(8,12...) custom-call(s32[8]{0:T(128)S(1)} %copy-done.9, s32[8,256]{1,0:T(8,128)S(1)} %copy-done.6, ...), custom_call_target="tpu_custom_call" | custom-call | flops 1 | bytes 1 | tf_op jit(solution)/shard_map/attend/pallas_call | solution.py:43
  30.6 1.2 %collective-permute-start.19 = (bf16[256,512]{1,0:T(8,128)(2,1)S(1)}, bf16[256,512]{1,0:T(8,128)(2,1)S(1)}, u32[]{:S(2)}, u32[]{:S(2)}) collective-permute-start(bf16[256,512]{1,0:T(8,128)(2,1)S(1)} %get-tuple-element.198.refs_3_.refs_10_), channel_id=1, source_target_pairs={{0,4},{4,0},{8,12},{12,8},{16,20},{20,16},{24,28},{28,24},{1,5},{5... | collective-permute-start | bytes 786440 | tf_op jit(solution)/shard_map/ppermute | solution.py:21
  32.0 1.3 %collective-permute-start.21 = (bf16[256,512]{1,0:T(8,128)(2,1)S(1)}, bf16[256,512]{1,0:T(8,128)(2,1)S(1)}, u32[]{:S(2)}, u32[]{:S(2)}) collective-permute-start(bf16[256,512]{1,0:T(8,128)(2,1)S(1)} %get-tuple-element.199.refs_5_.refs_12_), channel_id=1, source_target_pairs={{0,8},{4,12},{8,0},{12,4},{16,24},{20,28},{24,16},{28,20},{1,9},{5... | collective-permute-start | bytes 786440 | tf_op jit(solution)/shard_map/ppermute | solution.py:21
  33.3 2.7 %mlp_near_forward.1 = (f32[512,512]{1,0:T(8,128)S(1)}, bf16[512,512]{1,0:T(8,128)(2,1)S(1)}, bf16[512,512]{1,0:T(8,128)(2,1)S(1)}, f32[512,512]{1,0:T(8,128)S(1)...) custom-call(bf16[512,512]{1,0:T(8,128)(2,1)S(1)} %get-tuple-element.163.refs_0_.refs_3_, ...), custom_call_target="tpu_custom_call" | custom-call | flops 1 | bytes 1 | tf_op jit(solution)/shard_map/mlp_near_forward/pallas_call | solution.py:43
  36.5 1.0 collective-permute-done.17.refs_6_
  37.5 2.5 %mlp_near_backward.1 = (bf16[512,512]{1,0:T(8,128)(2,1)S(1)}, bf16[512,512]{1,0:T(8,128)(2,1)S(1)}, f32[512,512]{1,0:T(8,128)S(1)}, bf16[1,2,8,64,512]{4,3,2,1,0...) custom-call(bf16[2,512,512]{2,1,0:T(8,128)(2,1)S(1)} %get-tuple-element.189.refs_0_, ...), custom_call_target="tpu_custom_call" | custom-call | flops 1 | bytes 1 | tf_op jit(solution)/shard_map/mlp_near_backward/pallas_call | solution.py:43
  41.0 1.1 mlp_even_forward.1
  42.4 2.4 %mlp_far.2 = (f32[512,512]{1,0:T(8,128)S(1)}, f32[512,512]{1,0:T(8,128)S(1)}, bf16[1,2,8,64,512]{4,3,2,1,0:T(8,128)(2,1)S(1)}, f32[1,1,512]{2,1,0:T(1,128)S(1)}) custom-call(f32[512,512]{1,0:T(8,128)S(1)} %get-tuple-element.184.refs_0_, bf16[512,512]{1,0:T(8,128)(2,1)S(1)} %get-tuple-element.187.refs_0_.refs_1_, ...), custom_call_target="tpu_custom_call" | custom-call | flops 1 | bytes 1 | tf_op jit(solution)/shard_map/mlp_far/pallas_call | solution.py:43
  45.2 2.1 %mlp_far.3 = (bf16[512,512]{1,0:T(8,128)(2,1)S(1)}, f32[512,512]{1,0:T(8,128)S(1)}, bf16[512,512]{1,0:T(8,128)(2,1)S(1)}, f32[4,512]{1,0:T(4,128)S(1)}, bf16[1,2...) custom-call(f32[512,512]{1,0:T(8,128)S(1)} %get-tuple-element.184.refs_0_, ...), custom_call_target="tpu_custom_call" | custom-call | flops 1 | bytes 1 | tf_op jit(solution)/shard_map/mlp_far/pallas_call | solution.py:43
  48.0 1.0 collective-permute-start.27
  49.0 1.0 collective-permute-start.28
  50.0 9.3 %attend_back.1 = (bf16[4,64,512]{2,1,0:T(8,128)(2,1)S(1)}, bf16[4,64,512]{2,1,0:T(8,128)(2,1)S(1)}, bf16[8,64,512]{2,1,0:T(8,128)(2,1)S(1)}, bf16[1,8,272,128]{3...) custom-call(s32[8]{0:T(128)S(1)} %copy-done.9, ...), custom_call_target="tpu_custom_call" | custom-call | flops 1 | bytes 1 | tf_op jit(solution)/shard_map/attend_back/pallas_call | solution.py:43
  60.2 1.0 collective-permute-done.29.refs_1_
  63.0 1.0 collective-permute-start.37
  64.0 1.6 %collective-permute-start.38 = (bf16[4,64,512]{2,1,0:T(8,128)(2,1)S(1)}, bf16[4,64,512]{2,1,0:T(8,128)(2,1)S(1)}, u32[]{:S(2)}, u32[]{:S(2)}) collective-permute-start(bf16[4,64,512]{2,1,0:T(8,128)(2,1)S(1)} %get-tuple-element.259), channel_id=1, source_target_pairs={{0,8},{4,12},{8,0},{12,4},{16,24},{20,28},{24,16},{28,20},{1,9},{5... | collective-permute-start | bytes 786440 | tf_op jit(solution)/shard_map/ppermute | solution.py:21
  65.5 1.1 collective-permute-start.31
  66.6 0.9 collective-permute-start.32
  67.6 4.7 %collective-permute-done.37.refs_1_ = bf16[4,64,512]{2,1,0:T(8,128)(2,1)S(1)} collective-permute-done((bf16[4,64,512]{2,1,0:T(8,128)(2,1)S(1)}, bf16[4,64,512]{2,1,0:T(8,128)(2,1)S(1)}, u32[]{:S(2)}, u32[]{:S(2)}) %collective-permute-start.37) | collective-permute-done | bytes 262176 | tf_op jit(solution)/shard_map/ppermute | solution.py:21
  72.4 1.7 %collective-permute-start.39 = (bf16[2,64,512]{2,1,0:T(8,128)(2,1)S(1)}, bf16[2,64,512]{2,1,0:T(8,128)(2,1)S(1)}, u32[]{:S(2)}, u32[]{:S(2)}) collective-permute-start(bf16[2,64,512]{2,1,0:T(8,128)(2,1)S(1)} %get-tuple-element.261), channel_id=1, source_target_pairs={{0,8},{4,12},{8,0},{12,4},{16,24},{20,28},{24,16},{28,20},{1,9},{5... | collective-permute-start | bytes 393224 | tf_op jit(solution)/shard_map/ppermute | solution.py:21
  74.9 2.6 %collective-permute-done.39.refs_1_ = bf16[2,64,512]{2,1,0:T(8,128)(2,1)S(1)} collective-permute-done((bf16[2,64,512]{2,1,0:T(8,128)(2,1)S(1)}, bf16[2,64,512]{2,1,0:T(8,128)(2,1)S(1)}, u32[]{:S(2)}, u32[]{:S(2)}) %collective-permute-start.39) | collective-permute-done | bytes 131104 | tf_op jit(solution)/shard_map/ppermute | solution.py:21
  77.5 1.6 %collective-permute-done.40.refs_3_ = bf16[2,64,512]{2,1,0:T(8,128)(2,1)S(1)} collective-permute-done((bf16[2,64,512]{2,1,0:T(8,128)(2,1)S(1)}, bf16[2,64,512]{2,1,0:T(8,128)(2,1)S(1)}, u32[]{:S(2)}, u32[]{:S(2)}) %collective-permute-start.40) | collective-permute-done | bytes 131104 | tf_op jit(solution)/shard_map/ppermute | solution.py:21
  79.1 2.6 %collective-permute-start.41 = (bf16[2,2,64,512]{3,2,1,0:T(8,128)(2,1)S(1)}, bf16[2,2,64,512]{3,2,1,0:T(8,128)(2,1)S(1)}, u32[]{:S(2)}, u32[]{:S(2)}) collective-permute-start(bf16[2,2,64,512]{3,2,1,0:T(8,128)(2,1)S(1)} %join.1.refs_0_), channel_id=1, source_target_pairs={{0,16},{4,20},{8,24},{12,28},{16,0},{20,4},{24,8},{28,12},{1,17},{... | collective-permute-start | bytes 786440 | tf_op jit(solution)/shard_map/ppermute | solution.py:21
  82.6 1.3 %collective-permute-start.33 = (bf16[2,272,128]{2,1,0:T(8,128)(2,1)S(1)}, bf16[2,272,128]{2,1,0:T(8,128)(2,1)S(1)}, u32[]{:S(2)}, u32[]{:S(2)}) collective-permute-start(bf16[2,272,128]{2,1,0:T(8,128)(2,1)S(1)} %get-tuple-element.249), channel_id=1, source_target_pairs={{0,4},{4,0},{8,12},{12,8},{16,20},{20,16},{24,28},{28,24},{1,5},{5... | collective-permute-start | bytes 417800 | tf_op jit(solution)/shard_map/ppermute | solution.py:21
  84.6 1.0 collective-permute-start.48
  85.7 2.3 %collective-permute-done.33.refs_1_ = bf16[2,272,128]{2,1,0:T(8,128)(2,1)S(1)} collective-permute-done((bf16[2,272,128]{2,1,0:T(8,128)(2,1)S(1)}, bf16[2,272,128]{2,1,0:T(8,128)(2,1)S(1)}, u32[]{:S(2)}, u32[]{:S(2)}) %collective-permute-start.33) | collective-permute-done | bytes 139296 | tf_op jit(solution)/shard_map/ppermute | solution.py:21
  87.9 1.5 %collective-permute-done.34.refs_2_ = bf16[2,272,128]{2,1,0:T(8,128)(2,1)S(1)} collective-permute-done((bf16[2,272,128]{2,1,0:T(8,128)(2,1)S(1)}, bf16[2,272,128]{2,1,0:T(8,128)(2,1)S(1)}, u32[]{:S(2)}, u32[]{:S(2)}) %collective-permute-start.34) | collective-permute-done | bytes 139296 | tf_op jit(solution)/shard_map/ppermute | solution.py:21
  89.5 1.7 %collective-permute-start.35 = (bf16[1,272,128]{2,1,0:T(8,128)(2,1)S(1)}, bf16[1,272,128]{2,1,0:T(8,128)(2,1)S(1)}, u32[]{:S(2)}, u32[]{:S(2)}) collective-permute-start(bf16[1,272,128]{2,1,0:T(8,128)(2,1)S(1)} %get-tuple-element.252), channel_id=1, source_target_pairs={{0,8},{4,12},{8,0},{12,4},{16,24},{20,28},{24,16},{28,20},{1,9},{5... | collective-permute-start | bytes 208904 | tf_op jit(solution)/shard_map/ppermute | solution.py:21
  91.7 1.7 %collective-permute-start.44 = (bf16[2,64,512]{2,1,0:T(8,128)(2,1)S(1)}, bf16[2,64,512]{2,1,0:T(8,128)(2,1)S(1)}, u32[]{:S(2)}, u32[]{:S(2)}) collective-permute-start(bf16[2,64,512]{2,1,0:T(8,128)(2,1)S(1)} %get-tuple-element.264.refs_3_), channel_id=1, source_target_pairs={{0,8},{4,12},{8,0},{12,4},{16,24},{20,28},{24,16},{28,20},{1,9},{5... | collective-permute-start | bytes 393224 | tf_op jit(solution)/shard_map/ppermute | solution.py:21
  93.4 1.6 %collective-permute-start.46 = (bf16[2,64,512]{2,1,0:T(8,128)(2,1)S(1)}, bf16[2,64,512]{2,1,0:T(8,128)(2,1)S(1)}, u32[]{:S(2)}, u32[]{:S(2)}) collective-permute-start(bf16[2,64,512]{2,1,0:T(8,128)(2,1)S(1)} %get-tuple-element.266), channel_id=1, source_target_pairs={{0,4},{4,0},{8,12},{12,8},{16,20},{20,16},{24,28},{28,24},{1,5},{5... | collective-permute-start | bytes 393224 | tf_op jit(solution)/shard_map/ppermute | solution.py:21
  95.1 1.0 collective-permute-done.36.refs_2_
  96.1 2.7 %collective-permute-start.42 = (bf16[2,272,128]{2,1,0:T(8,128)(2,1)S(1)}, bf16[2,272,128]{2,1,0:T(8,128)(2,1)S(1)}, u32[]{:S(2)}, u32[]{:S(2)}) collective-permute-start(bf16[2,272,128]{2,1,0:T(8,128)(2,1)S(1)} %add_parts.5.refs_0_), channel_id=1, source_target_pairs={{0,16},{4,20},{8,24},{12,28},{16,0},{20,4},{24,8},{28,12},{1,17},{... | collective-permute-start | bytes 417800 | tf_op jit(solution)/shard_map/ppermute | solution.py:21
  99.0 1.9 %collective-permute-start.45 = (bf16[4,64,512]{2,1,0:T(8,128)(2,1)S(1)}, bf16[4,64,512]{2,1,0:T(8,128)(2,1)S(1)}, u32[]{:S(2)}, u32[]{:S(2)}) collective-permute-start(bf16[4,64,512]{2,1,0:T(8,128)(2,1)S(1)} %constant_dynamic-update-slice_fusion.refs_0_), channel_id=1, source_target_pairs={{0,4},{4,0},{8,12},{12,8},{16,20},{20,16},{24,28},{28,24},{1,5},{5... | collective-permute-start | bytes 786440 | tf_op jit(solution)/shard_map/ppermute | solution.py:21
  101.0 2.6 %collective-permute-done.42.refs_1_ = bf16[2,272,128]{2,1,0:T(8,128)(2,1)S(1)} collective-permute-done((bf16[2,272,128]{2,1,0:T(8,128)(2,1)S(1)}, bf16[2,272,128]{2,1,0:T(8,128)(2,1)S(1)}, u32[]{:S(2)}, u32[]{:S(2)}) %collective-permute-start.42) | collective-permute-done | bytes 139296 | tf_op jit(solution)/shard_map/ppermute | solution.py:21
  103.9 4.8 %collective-permute-done.43 = bf16[2,272,128]{2,1,0:T(8,128)(2,1)S(1)} collective-permute-done((bf16[2,272,128]{2,1,0:T(8,128)(2,1)S(1)}, bf16[2,272,128]{2,1,0:T(8,128)(2,1)S(1)}, u32[]{:S(2)}, u32[]{:S(2)}) %collective-permute-start.43) | collective-permute-done | bytes 139296 | tf_op jit(solution)/shard_map/ppermute | solution.py:21
  108.8 1.8 %collective-permute-start.51 = (bf16[4,272,128]{2,1,0:T(8,128)(2,1)S(1)}, bf16[4,272,128]{2,1,0:T(8,128)(2,1)S(1)}, u32[]{:S(2)}, u32[]{:S(2)}) collective-permute-start(bf16[4,272,128]{2,1,0:T(8,128)(2,1)S(1)} %pad_maximum_fusion.refs_0_), channel_id=1, source_target_pairs={{0,4},{4,0},{8,12},{12,8},{16,20},{20,16},{24,28},{28,24},{1,5},{5... | collective-permute-start | bytes 835592 | tf_op jit(solution)/shard_map/ppermute | solution.py:21
  111.2 1.7 %finish_mlp.1 = (f32[512,512]{1,0:T(8,128)}, f32[512,512]{1,0:T(8,128)}, f32[8,128]{1,0:T(8,128)S(1)}) custom-call(bf16[4,64,512]{2,1,0:T(8,128)(2,1)S(1)} %constant_dynamic-update-slice_fusion.refs_0_, bf16[4,64,512]{2,1,0:T(8,128)(2,1)S(1)} %collective-permute-done.45.refs_1_, bf16[4,64,512]{2,1,0:T(8,128)(2,1)S(1)} %constant_dynamic-update-slice_fusion.2.refs_2_, ...), custom_call_target="tpu_custom_call" | custom-call | flops 1 | bytes 1 | tf_op jit(solution)/shard_map/finish_mlp/pallas_call | solution.py:43
  112.9 1.2 %gather_rows.1 = (bf16[8,64,512]{2,1,0:T(8,128)(2,1)}, f32[8,64,512]{2,1,0:T(8,128)}, f32[8,128]{1,0:T(8,128)S(1)}) custom-call(bf16[4,64,512]{2,1,0:T(8,128)(2,1)S(1)} %get-tuple-element.270.refs_0_, bf16[4,64,512]{2,1,0:T(8,128)(2,1)S(1)} %collective-permute-done.49.refs_1_, bf16[8,64,512]{2,1,0:T(8,128)(2,1)S(1)} %collective-permute-done.48.refs_2_, ...), custom_call_target="tpu_custom_call" | custom-call | flops 1 | bytes 1 | tf_op jit(solution)/shard_map/gather_rows/pallas_call | solution.py:43
  114.2 1.2 %collective-permute-done.51.refs_1_ = bf16[4,272,128]{2,1,0:T(8,128)(2,1)S(1)} collective-permute-done((bf16[4,272,128]{2,1,0:T(8,128)(2,1)S(1)}, bf16[4,272,128]{2,1,0:T(8,128)(2,1)S(1)}, u32[]{:S(2)}, u32[]{:S(2)}) %collective-permute-start.51) | collective-permute-done | bytes 278560 | tf_op jit(solution)/shard_map/ppermute | solution.py:21
  115.4 1.1 finish_att.1
  (111 shorter events, 16.2 us)
Async XLA Ops:
  3.9 8.1 %collective-permute-start.1 = (bf16[2112,128]{1,0:T(8,128)(2,1)}, bf16[2112,128]{1,0:T(8,128)(2,1)S(1)}, u32[]{:S(2)}, u32[]{:S(2)}) collective-permute-start(bf16[2112,128]{1,0:T(8,128)(2,1)} %get-tuple-element.156.refs_8_), channel_id=1, source_target_pairs={{0,1},{1,0},{2,3},{3,2},{4,5},{5,4},{6,7},{7,6},{8,9},{9,8},{10,11... | collective-permute-start | bytes 1622024 | tf_op jit(solution)/shard_map/ppermute | solution.py:21
  4.4 7.6 %collective-permute-start.3 = (bf16[512,512]{1,0:T(8,128)(2,1)}, bf16[512,512]{1,0:T(8,128)(2,1)S(1)}, u32[]{:S(2)}, u32[]{:S(2)}) collective-permute-start(bf16[512,512]{1,0:T(8,128)(2,1)} %refs_7_.5), channel_id=1, source_target_pairs={{0,1},{1,0},{2,3},{3,2},{4,5},{5,4},{6,7},{7,6},{8,9},{9,8},{10,11... | collective-permute-start | bytes 1572872 | tf_op jit(solution)/shard_map/ppermute | solution.py:21
  4.5 7.5 %collective-permute-start.4 = (bf16[512,512]{1,0:T(8,128)(2,1)}, bf16[512,512]{1,0:T(8,128)(2,1)S(1)}, u32[]{:S(2)}, u32[]{:S(2)}) collective-permute-start(bf16[512,512]{1,0:T(8,128)(2,1)} %refs_9_.5), channel_id=1, source_target_pairs={{0,1},{1,0},{2,3},{3,2},{4,5},{5,4},{6,7},{7,6},{8,9},{9,8},{10,11... | collective-permute-start | bytes 1572872 | tf_op jit(solution)/shard_map/ppermute | solution.py:21
  5.0 3.0 %collective-permute-start.2 = (bf16[2,64,512]{2,1,0:T(8,128)(2,1)}, bf16[2,64,512]{2,1,0:T(8,128)(2,1)S(1)}, u32[]{:S(2)}, u32[]{:S(2)}) collective-permute-start(bf16[2,64,512]{2,1,0:T(8,128)(2,1)} %get-tuple-element.158), channel_id=1, source_target_pairs={{0,1},{1,0},{2,3},{3,2},{4,5},{5,4},{6,7},{7,6},{8,9},{9,8},{10,11... | collective-permute-start | bytes 393224 | tf_op jit(solution)/shard_map/ppermute | solution.py:21
  5.0 7.0 %collective-permute-start = (bf16[528,128]{1,0:T(8,128)(2,1)}, bf16[528,128]{1,0:T(8,128)(2,1)S(1)}, u32[]{:S(2)}, u32[]{:S(2)}) collective-permute-start(bf16[528,128]{1,0:T(8,128)(2,1)} %get-tuple-element.155.refs_3_), channel_id=1, source_target_pairs={{0,2},{1,3},{2,0},{3,1},{4,6},{5,7},{6,4},{7,5},{8,10},{9,11},{10,... | collective-permute-start | bytes 405512 | tf_op jit(solution)/shard_map/ppermute | solution.py:21
  8.0 11.7 %collective-permute-start.5 = (bf16[4,64,512]{2,1,0:T(8,128)(2,1)}, bf16[4,64,512]{2,1,0:T(8,128)(2,1)S(1)}, u32[]{:S(2)}, u32[]{:S(2)}) collective-permute-start(bf16[4,64,512]{2,1,0:T(8,128)(2,1)} %get-tuple-element.161), channel_id=1, source_target_pairs={{0,2},{1,3},{2,0},{3,1},{4,6},{5,7},{6,4},{7,5},{8,10},{9,11},{10,... | collective-permute-start | bytes 786440 | tf_op jit(solution)/shard_map/ppermute | solution.py:21
  12.0 7.2 %collective-permute-start.7 = (bf16[528,128]{1,0:T(8,128)(2,1)S(1)}, bf16[528,128]{1,0:T(8,128)(2,1)S(1)}, u32[]{:S(2)}, u32[]{:S(2)}) collective-permute-start(bf16[528,128]{1,0:T(8,128)(2,1)S(1)} %collective-permute-done.refs_3_), channel_id=1, source_target_pairs={{0,4},{4,0},{8,12},{12,8},{16,20},{20,16},{24,28},{28,24},{1,5},{5... | collective-permute-start | bytes 405512 | tf_op jit(solution)/shard_map/ppermute | solution.py:21
  16.1 14.5 %collective-permute-start.10 = (bf16[2,256,512]{2,1,0:T(8,128)(2,1)}, bf16[2,256,512]{2,1,0:T(8,128)(2,1)S(1)}, u32[]{:S(2)}, u32[]{:S(2)}) collective-permute-start(bf16[2,256,512]{2,1,0:T(8,128)(2,1)} %get-tuple-element.170), channel_id=1, source_target_pairs={{0,2},{1,3},{2,0},{3,1},{4,6},{5,7},{6,4},{7,5},{8,10},{9,11},{10,... | collective-permute-start | bytes 1572872 | tf_op jit(solution)/shard_map/ppermute | solution.py:21
  17.7 7.8 %collective-permute-start.8 = (bf16[528,128]{1,0:T(8,128)(2,1)S(1)}, bf16[528,128]{1,0:T(8,128)(2,1)S(1)}, u32[]{:S(2)}, u32[]{:S(2)}) collective-permute-start(bf16[528,128]{1,0:T(8,128)(2,1)S(1)} %collective-permute-done.refs_3_), channel_id=1, source_target_pairs={{0,8},{4,12},{8,0},{12,4},{16,24},{20,28},{24,16},{28,20},{1,9},{5... | collective-permute-start | bytes 405512 | tf_op jit(solution)/shard_map/ppermute | solution.py:21
  19.3 6.2 %collective-permute-start.9 = (bf16[528,128]{1,0:T(8,128)(2,1)S(1)}, bf16[528,128]{1,0:T(8,128)(2,1)S(1)}, u32[]{:S(2)}, u32[]{:S(2)}) collective-permute-start(bf16[528,128]{1,0:T(8,128)(2,1)S(1)} %collective-permute-done.7.refs_4_), channel_id=1, source_target_pairs={{0,8},{4,12},{8,0},{12,4},{16,24},{20,28},{24,16},{28,20},{1,9},{5... | collective-permute-start | bytes 405512 | tf_op jit(solution)/shard_map/ppermute | solution.py:21
  19.8 6.4 %collective-permute-start.11 = (bf16[528,128]{1,0:T(8,128)(2,1)S(1)}, bf16[528,128]{1,0:T(8,128)(2,1)S(1)}, u32[]{:S(2)}, u32[]{:S(2)}) collective-permute-start(bf16[528,128]{1,0:T(8,128)(2,1)S(1)} %collective-permute-done.refs_3_), channel_id=1, source_target_pairs={{0,1},{1,0},{2,3},{3,2},{4,5},{5,4},{6,7},{7,6},{8,9},{9,8},{10,11... | collective-permute-start | bytes 405512 | tf_op jit(solution)/shard_map/ppermute | solution.py:21
  26.2 9.8 %collective-permute-start.16 = (bf16[4,64,512]{2,1,0:T(8,128)(2,1)}, bf16[4,64,512]{2,1,0:T(8,128)(2,1)S(1)}, u32[]{:S(2)}, u32[]{:S(2)}) collective-permute-start(bf16[4,64,512]{2,1,0:T(8,128)(2,1)} %get-tuple-element.185), channel_id=1, source_target_pairs={{0,2},{1,3},{2,0},{3,1},{4,6},{5,7},{6,4},{7,5},{8,10},{9,11},{10,... | collective-permute-start | bytes 786440 | tf_op jit(solution)/shard_map/ppermute | solution.py:21
  26.9 3.7 %collective-permute-start.15 = (bf16[2,64,512]{2,1,0:T(8,128)(2,1)}, bf16[2,64,512]{2,1,0:T(8,128)(2,1)S(1)}, u32[]{:S(2)}, u32[]{:S(2)}) collective-permute-start(bf16[2,64,512]{2,1,0:T(8,128)(2,1)} %get-tuple-element.177), channel_id=1, source_target_pairs={{0,1},{1,0},{2,3},{3,2},{4,5},{5,4},{6,7},{7,6},{8,9},{9,8},{10,11... | collective-permute-start | bytes 393224 | tf_op jit(solution)/shard_map/ppermute | solution.py:21
  30.6 9.4 %collective-permute-start.19 = (bf16[256,512]{1,0:T(8,128)(2,1)S(1)}, bf16[256,512]{1,0:T(8,128)(2,1)S(1)}, u32[]{:S(2)}, u32[]{:S(2)}) collective-permute-start(bf16[256,512]{1,0:T(8,128)(2,1)S(1)} %get-tuple-element.198.refs_3_.refs_10_), channel_id=1, source_target_pairs={{0,4},{4,0},{8,12},{12,8},{16,20},{20,16},{24,28},{28,24},{1,5},{5... | collective-permute-start | bytes 786440 | tf_op jit(solution)/shard_map/ppermute | solution.py:21
  31.8 8.3 %collective-permute-start.18 = (bf16[256,512]{1,0:T(8,128)(2,1)S(1)}, bf16[256,512]{1,0:T(8,128)(2,1)S(1)}, u32[]{:S(2)}, u32[]{:S(2)}) collective-permute-start(bf16[256,512]{1,0:T(8,128)(2,1)S(1)} %get-tuple-element.198.refs_3_.refs_10_), channel_id=1, source_target_pairs={{0,1},{1,0},{2,3},{3,2},{4,5},{5,4},{6,7},{7,6},{8,9},{9,8},{10,11... | collective-permute-start | bytes 786440 | tf_op jit(solution)/shard_map/ppermute | solution.py:21
  32.0 8.6 %collective-permute-start.21 = (bf16[256,512]{1,0:T(8,128)(2,1)S(1)}, bf16[256,512]{1,0:T(8,128)(2,1)S(1)}, u32[]{:S(2)}, u32[]{:S(2)}) collective-permute-start(bf16[256,512]{1,0:T(8,128)(2,1)S(1)} %get-tuple-element.199.refs_5_.refs_12_), channel_id=1, source_target_pairs={{0,8},{4,12},{8,0},{12,4},{16,24},{20,28},{24,16},{28,20},{1,9},{5... | collective-permute-start | bytes 786440 | tf_op jit(solution)/shard_map/ppermute | solution.py:21
  33.3 7.3 %collective-permute-start.20 = (bf16[256,512]{1,0:T(8,128)(2,1)S(1)}, bf16[256,512]{1,0:T(8,128)(2,1)S(1)}, u32[]{:S(2)}, u32[]{:S(2)}) collective-permute-start(bf16[256,512]{1,0:T(8,128)(2,1)S(1)} %get-tuple-element.199.refs_5_.refs_12_), channel_id=1, source_target_pairs={{0,1},{1,0},{2,3},{3,2},{4,5},{5,4},{6,7},{7,6},{8,9},{9,8},{10,11... | collective-permute-start | bytes 786440 | tf_op jit(solution)/shard_map/ppermute | solution.py:21
  36.0 1.5 %collective-permute-start.17 = (bf16[2,64,512]{2,1,0:T(8,128)(2,1)S(1)}, bf16[2,64,512]{2,1,0:T(8,128)(2,1)S(1)}, u32[]{:S(2)}, u32[]{:S(2)}) collective-permute-start(bf16[2,64,512]{2,1,0:T(8,128)(2,1)S(1)} %slice.10), channel_id=1, source_target_pairs={{0,1},{1,0},{2,3},{3,2},{4,5},{5,4},{6,7},{7,6},{8,9},{9,8},{10,11... | collective-permute-start | bytes 393224 | tf_op jit(solution)/shard_map/ppermute | solution.py:21
  40.5 1.7 %collective-permute-start.22 = (bf16[256,512]{1,0:T(8,128)(2,1)S(1)}, bf16[256,512]{1,0:T(8,128)(2,1)S(1)}, u32[]{:S(2)}, u32[]{:S(2)}) collective-permute-start(bf16[256,512]{1,0:T(8,128)(2,1)S(1)} %collective-permute-done.19.refs_4_.refs_11_), channel_id=1, source_target_pairs={{0,1},{1,0},{2,3},{3,2},{4,5},{5,4},{6,7},{7,6},{8,9},{9,8},{10,11... | collective-permute-start | bytes 786440 | tf_op jit(solution)/shard_map/ppermute | solution.py:21
  40.5 1.9 %collective-permute-start.23 = (bf16[256,512]{1,0:T(8,128)(2,1)S(1)}, bf16[256,512]{1,0:T(8,128)(2,1)S(1)}, u32[]{:S(2)}, u32[]{:S(2)}) collective-permute-start(bf16[256,512]{1,0:T(8,128)(2,1)S(1)} %collective-permute-done.21.refs_6_.refs_13_), channel_id=1, source_target_pairs={{0,1},{1,0},{2,3},{3,2},{4,5},{5,4},{6,7},{7,6},{8,9},{9,8},{10,11... | collective-permute-start | bytes 786440 | tf_op jit(solution)/shard_map/ppermute | solution.py:21
  41.0 6.2 %collective-permute-start.24 = (bf16[1,2,8,64,512]{4,3,2,1,0:T(8,128)(2,1)S(1)}, bf16[1,2,8,64,512]{4,3,2,1,0:T(8,128)(2,1)S(1)}, u32[]{:S(2)}, u32[]{:S(2)}) collective-permute-start(bf16[1,2,8,64,512]{4,3,2,1,0:T(8,128)(2,1)S(1)} %get-tuple-element.215), channel_id=1, source_target_pairs={{0,1},{1,0},{2,3},{3,2},{4,5},{5,4},{6,7},{7,6},{8,9},{9,8},{10,11... | collective-permute-start | bytes 3145736 | tf_op jit(solution)/shard_map/ppermute | solution.py:21
  44.8 2.7 %collective-permute-start.25 = (bf16[1,2,8,64,512]{4,3,2,1,0:T(8,128)(2,1)S(1)}, bf16[1,2,8,64,512]{4,3,2,1,0:T(8,128)(2,1)S(1)}, u32[]{:S(2)}, u32[]{:S(2)}) collective-permute-start(bf16[1,2,8,64,512]{4,3,2,1,0:T(8,128)(2,1)S(1)} %get-tuple-element.217), channel_id=1, source_target_pairs={{0,1},{1,0},{2,3},{3,2},{4,5},{5,4},{6,7},{7,6},{8,9},{9,8},{10,11... | collective-permute-start | bytes 3145736 | tf_op jit(solution)/shard_map/ppermute | solution.py:21
  48.0 14.2 %collective-permute-start.27 = (bf16[2,4,64,512]{3,2,1,0:T(8,128)(2,1)S(1)}, bf16[2,4,64,512]{3,2,1,0:T(8,128)(2,1)S(1)}, u32[]{:S(2)}, u32[]{:S(2)}) collective-permute-start(bf16[2,4,64,512]{3,2,1,0:T(8,128)(2,1)S(1)} %get-tuple-element.236), channel_id=1, source_target_pairs={{0,4},{4,0},{8,12},{12,8},{16,20},{20,16},{24,28},{28,24},{1,5},{5... | collective-permute-start | bytes 1572872 | tf_op jit(solution)/shard_map/ppermute | solution.py:21
  49.0 13.8 %collective-permute-start.28 = (bf16[8,64,512]{2,1,0:T(8,128)(2,1)S(1)}, bf16[8,64,512]{2,1,0:T(8,128)(2,1)S(1)}, u32[]{:S(2)}, u32[]{:S(2)}) collective-permute-start(bf16[8,64,512]{2,1,0:T(8,128)(2,1)S(1)} %get-tuple-element.239), channel_id=1, source_target_pairs={{0,2},{1,3},{2,0},{3,1},{4,6},{5,7},{6,4},{7,5},{8,10},{9,11},{10,... | collective-permute-start | bytes 1572872 | tf_op jit(solution)/shard_map/ppermute | solution.py:21
  59.3 1.8 %collective-permute-start.29 = (bf16[1,4,272,128]{3,2,1,0:T(8,128)(2,1)S(1)}, bf16[1,4,272,128]{3,2,1,0:T(8,128)(2,1)S(1)}, u32[]{:S(2)}, u32[]{:S(2)}) collective-permute-start(bf16[1,4,272,128]{3,2,1,0:T(8,128)(2,1)S(1)} %get-tuple-element.242), channel_id=1, source_target_pairs={{0,1},{1,0},{2,3},{3,2},{4,5},{5,4},{6,7},{7,6},{8,9},{9,8},{10,11... | collective-permute-start | bytes 835592 | tf_op jit(solution)/shard_map/ppermute | solution.py:21
  59.6 1.9 %collective-permute-start.30 = (bf16[1,4,272,128]{3,2,1,0:T(8,128)(2,1)S(1)}, bf16[1,4,272,128]{3,2,1,0:T(8,128)(2,1)S(1)}, u32[]{:S(2)}, u32[]{:S(2)}) collective-permute-start(bf16[1,4,272,128]{3,2,1,0:T(8,128)(2,1)S(1)} %get-tuple-element.243), channel_id=1, source_target_pairs={{0,1},{1,0},{2,3},{3,2},{4,5},{5,4},{6,7},{7,6},{8,9},{9,8},{10,11... | collective-permute-start | bytes 835592 | tf_op jit(solution)/shard_map/ppermute | solution.py:21
  60.1 21.7 %collective-permute-start.26 = (bf16[1,8,272,128]{3,2,1,0:T(8,128)(2,1)S(1)}, bf16[1,8,272,128]{3,2,1,0:T(8,128)(2,1)S(1)}, u32[]{:S(2)}, u32[]{:S(2)}) collective-permute-start(bf16[1,8,272,128]{3,2,1,0:T(8,128)(2,1)S(1)} %get-tuple-element.234), channel_id=1, source_target_pairs={{0,1},{1,0},{2,3},{3,2},{4,5},{5,4},{6,7},{7,6},{8,9},{9,8},{10,11... | collective-permute-start | bytes 1671176 | tf_op jit(solution)/shard_map/ppermute | solution.py:21
  63.0 9.3 %collective-permute-start.37 = (bf16[4,64,512]{2,1,0:T(8,128)(2,1)S(1)}, bf16[4,64,512]{2,1,0:T(8,128)(2,1)S(1)}, u32[]{:S(2)}, u32[]{:S(2)}) collective-permute-start(bf16[4,64,512]{2,1,0:T(8,128)(2,1)S(1)} %get-tuple-element.255), channel_id=1, source_target_pairs={{0,2},{1,3},{2,0},{3,1},{4,6},{5,7},{6,4},{7,5},{8,10},{9,11},{10,... | collective-permute-start | bytes 786440 | tf_op jit(solution)/shard_map/ppermute | solution.py:21
  64.0 8.4 %collective-permute-start.38 = (bf16[4,64,512]{2,1,0:T(8,128)(2,1)S(1)}, bf16[4,64,512]{2,1,0:T(8,128)(2,1)S(1)}, u32[]{:S(2)}, u32[]{:S(2)}) collective-permute-start(bf16[4,64,512]{2,1,0:T(8,128)(2,1)S(1)} %get-tuple-element.259), channel_id=1, source_target_pairs={{0,8},{4,12},{8,0},{12,4},{16,24},{20,28},{24,16},{28,20},{1,9},{5... | collective-permute-start | bytes 786440 | tf_op jit(solution)/shard_map/ppermute | solution.py:21
  65.5 16.2 %collective-permute-start.31 = (bf16[4,272,128]{2,1,0:T(8,128)(2,1)S(1)}, bf16[4,272,128]{2,1,0:T(8,128)(2,1)S(1)}, u32[]{:S(2)}, u32[]{:S(2)}) collective-permute-start(bf16[4,272,128]{2,1,0:T(8,128)(2,1)S(1)} %get-tuple-element.246), channel_id=1, source_target_pairs={{0,2},{1,3},{2,0},{3,1},{4,6},{5,7},{6,4},{7,5},{8,10},{9,11},{10,... | collective-permute-start | bytes 835592 | tf_op jit(solution)/shard_map/ppermute | solution.py:21
  66.6 15.7 %collective-permute-start.32 = (bf16[4,272,128]{2,1,0:T(8,128)(2,1)S(1)}, bf16[4,272,128]{2,1,0:T(8,128)(2,1)S(1)}, u32[]{:S(2)}, u32[]{:S(2)}) collective-permute-start(bf16[4,272,128]{2,1,0:T(8,128)(2,1)S(1)} %get-tuple-element.247), channel_id=1, source_target_pairs={{0,2},{1,3},{2,0},{3,1},{4,6},{5,7},{6,4},{7,5},{8,10},{9,11},{10,... | collective-permute-start | bytes 835592 | tf_op jit(solution)/shard_map/ppermute | solution.py:21
  72.4 5.0 %collective-permute-start.39 = (bf16[2,64,512]{2,1,0:T(8,128)(2,1)S(1)}, bf16[2,64,512]{2,1,0:T(8,128)(2,1)S(1)}, u32[]{:S(2)}, u32[]{:S(2)}) collective-permute-start(bf16[2,64,512]{2,1,0:T(8,128)(2,1)S(1)} %get-tuple-element.261), channel_id=1, source_target_pairs={{0,8},{4,12},{8,0},{12,4},{16,24},{20,28},{24,16},{28,20},{1,9},{5... | collective-permute-start | bytes 393224 | tf_op jit(solution)/shard_map/ppermute | solution.py:21
  74.1 5.0 %collective-permute-start.40 = (bf16[2,64,512]{2,1,0:T(8,128)(2,1)S(1)}, bf16[2,64,512]{2,1,0:T(8,128)(2,1)S(1)}, u32[]{:S(2)}, u32[]{:S(2)}) collective-permute-start(bf16[2,64,512]{2,1,0:T(8,128)(2,1)S(1)} %get-tuple-element.263), channel_id=1, source_target_pairs={{0,4},{4,0},{8,12},{12,8},{16,20},{20,16},{24,28},{28,24},{1,5},{5... | collective-permute-start | bytes 393224 | tf_op jit(solution)/shard_map/ppermute | solution.py:21
  79.1 12.1 %collective-permute-start.41 = (bf16[2,2,64,512]{3,2,1,0:T(8,128)(2,1)S(1)}, bf16[2,2,64,512]{3,2,1,0:T(8,128)(2,1)S(1)}, u32[]{:S(2)}, u32[]{:S(2)}) collective-permute-start(bf16[2,2,64,512]{3,2,1,0:T(8,128)(2,1)S(1)} %join.1.refs_0_), channel_id=1, source_target_pairs={{0,16},{4,20},{8,24},{12,28},{16,0},{20,4},{24,8},{28,12},{1,17},{... | collective-permute-start | bytes 786440 | tf_op jit(solution)/shard_map/ppermute | solution.py:21
  82.6 5.4 %collective-permute-start.33 = (bf16[2,272,128]{2,1,0:T(8,128)(2,1)S(1)}, bf16[2,272,128]{2,1,0:T(8,128)(2,1)S(1)}, u32[]{:S(2)}, u32[]{:S(2)}) collective-permute-start(bf16[2,272,128]{2,1,0:T(8,128)(2,1)S(1)} %get-tuple-element.249), channel_id=1, source_target_pairs={{0,4},{4,0},{8,12},{12,8},{16,20},{20,16},{24,28},{28,24},{1,5},{5... | collective-permute-start | bytes 417800 | tf_op jit(solution)/shard_map/ppermute | solution.py:21
  83.8 5.6 %collective-permute-start.34 = (bf16[2,272,128]{2,1,0:T(8,128)(2,1)S(1)}, bf16[2,272,128]{2,1,0:T(8,128)(2,1)S(1)}, u32[]{:S(2)}, u32[]{:S(2)}) collective-permute-start(bf16[2,272,128]{2,1,0:T(8,128)(2,1)S(1)} %get-tuple-element.250), channel_id=1, source_target_pairs={{0,4},{4,0},{8,12},{12,8},{16,20},{20,16},{24,28},{28,24},{1,5},{5... | collective-permute-start | bytes 417800 | tf_op jit(solution)/shard_map/ppermute | solution.py:21
  84.6 24.1 %collective-permute-start.48 = (bf16[8,64,512]{2,1,0:T(8,128)(2,1)S(1)}, bf16[8,64,512]{2,1,0:T(8,128)(2,1)S(1)}, u32[]{:S(2)}, u32[]{:S(2)}) collective-permute-start(bf16[8,64,512]{2,1,0:T(8,128)(2,1)S(1)} %get-tuple-element.269), channel_id=1, source_target_pairs={{0,2},{1,3},{2,0},{3,1},{4,6},{5,7},{6,4},{7,5},{8,10},{9,11},{10,... | collective-permute-start | bytes 1572872 | tf_op jit(solution)/shard_map/ppermute | solution.py:21
  89.5 5.6 %collective-permute-start.35 = (bf16[1,272,128]{2,1,0:T(8,128)(2,1)S(1)}, bf16[1,272,128]{2,1,0:T(8,128)(2,1)S(1)}, u32[]{:S(2)}, u32[]{:S(2)}) collective-permute-start(bf16[1,272,128]{2,1,0:T(8,128)(2,1)S(1)} %get-tuple-element.252), channel_id=1, source_target_pairs={{0,8},{4,12},{8,0},{12,4},{16,24},{20,28},{24,16},{28,20},{1,9},{5... | collective-permute-start | bytes 208904 | tf_op jit(solution)/shard_map/ppermute | solution.py:21
  91.2 4.8 %collective-permute-start.36 = (bf16[1,272,128]{2,1,0:T(8,128)(2,1)S(1)}, bf16[1,272,128]{2,1,0:T(8,128)(2,1)S(1)}, u32[]{:S(2)}, u32[]{:S(2)}) collective-permute-start(bf16[1,272,128]{2,1,0:T(8,128)(2,1)S(1)} %get-tuple-element.253), channel_id=1, source_target_pairs={{0,8},{4,12},{8,0},{12,4},{16,24},{20,28},{24,16},{28,20},{1,9},{5... | collective-permute-start | bytes 208904 | tf_op jit(solution)/shard_map/ppermute | solution.py:21
  91.7 7.3 %collective-permute-start.44 = (bf16[2,64,512]{2,1,0:T(8,128)(2,1)S(1)}, bf16[2,64,512]{2,1,0:T(8,128)(2,1)S(1)}, u32[]{:S(2)}, u32[]{:S(2)}) collective-permute-start(bf16[2,64,512]{2,1,0:T(8,128)(2,1)S(1)} %get-tuple-element.264.refs_3_), channel_id=1, source_target_pairs={{0,8},{4,12},{8,0},{12,4},{16,24},{20,28},{24,16},{28,20},{1,9},{5... | collective-permute-start | bytes 393224 | tf_op jit(solution)/shard_map/ppermute | solution.py:21
  93.4 5.4 %collective-permute-start.46 = (bf16[2,64,512]{2,1,0:T(8,128)(2,1)S(1)}, bf16[2,64,512]{2,1,0:T(8,128)(2,1)S(1)}, u32[]{:S(2)}, u32[]{:S(2)}) collective-permute-start(bf16[2,64,512]{2,1,0:T(8,128)(2,1)S(1)} %get-tuple-element.266), channel_id=1, source_target_pairs={{0,4},{4,0},{8,12},{12,8},{16,20},{20,16},{24,28},{28,24},{1,5},{5... | collective-permute-start | bytes 393224 | tf_op jit(solution)/shard_map/ppermute | solution.py:21
  96.1 7.4 %collective-permute-start.42 = (bf16[2,272,128]{2,1,0:T(8,128)(2,1)S(1)}, bf16[2,272,128]{2,1,0:T(8,128)(2,1)S(1)}, u32[]{:S(2)}, u32[]{:S(2)}) collective-permute-start(bf16[2,272,128]{2,1,0:T(8,128)(2,1)S(1)} %add_parts.5.refs_0_), channel_id=1, source_target_pairs={{0,16},{4,20},{8,24},{12,28},{16,0},{20,4},{24,8},{28,12},{1,17},{... | collective-permute-start | bytes 417800 | tf_op jit(solution)/shard_map/ppermute | solution.py:21
  98.9 9.9 %collective-permute-start.47 = (bf16[4,64,512]{2,1,0:T(8,128)(2,1)S(1)}, bf16[4,64,512]{2,1,0:T(8,128)(2,1)S(1)}, u32[]{:S(2)}, u32[]{:S(2)}) collective-permute-start(bf16[4,64,512]{2,1,0:T(8,128)(2,1)S(1)} %constant_dynamic-update-slice_fusion.2.refs_2_), channel_id=1, source_target_pairs={{0,8},{4,12},{8,0},{12,4},{16,24},{20,28},{24,16},{28,20},{1,9},{5... | collective-permute-start | bytes 786440 | tf_op jit(solution)/shard_map/ppermute | solution.py:21
  99.0 9.7 %collective-permute-start.45 = (bf16[4,64,512]{2,1,0:T(8,128)(2,1)S(1)}, bf16[4,64,512]{2,1,0:T(8,128)(2,1)S(1)}, u32[]{:S(2)}, u32[]{:S(2)}) collective-permute-start(bf16[4,64,512]{2,1,0:T(8,128)(2,1)S(1)} %constant_dynamic-update-slice_fusion.refs_0_), channel_id=1, source_target_pairs={{0,4},{4,0},{8,12},{12,8},{16,20},{20,16},{24,28},{28,24},{1,5},{5... | collective-permute-start | bytes 786440 | tf_op jit(solution)/shard_map/ppermute | solution.py:21
  103.6 5.1 %collective-permute-start.43 = (bf16[2,272,128]{2,1,0:T(8,128)(2,1)S(1)}, bf16[2,272,128]{2,1,0:T(8,128)(2,1)S(1)}, u32[]{:S(2)}, u32[]{:S(2)}) collective-permute-start(bf16[2,272,128]{2,1,0:T(8,128)(2,1)S(1)} %meet.3), channel_id=1, source_target_pairs={{0,8},{4,12},{8,0},{12,4},{16,24},{20,28},{24,16},{28,20},{1,9},{5... | collective-permute-start | bytes 417800 | tf_op jit(solution)/shard_map/ppermute | solution.py:21
  108.8 6.6 %collective-permute-start.51 = (bf16[4,272,128]{2,1,0:T(8,128)(2,1)S(1)}, bf16[4,272,128]{2,1,0:T(8,128)(2,1)S(1)}, u32[]{:S(2)}, u32[]{:S(2)}) collective-permute-start(bf16[4,272,128]{2,1,0:T(8,128)(2,1)S(1)} %pad_maximum_fusion.refs_0_), channel_id=1, source_target_pairs={{0,4},{4,0},{8,12},{12,8},{16,20},{20,16},{24,28},{28,24},{1,5},{5... | collective-permute-start | bytes 835592 | tf_op jit(solution)/shard_map/ppermute | solution.py:21
  110.6 2.3 %collective-permute-start.50 = (bf16[4,64,512]{2,1,0:T(8,128)(2,1)S(1)}, bf16[4,64,512]{2,1,0:T(8,128)(2,1)S(1)}, u32[]{:S(2)}, u32[]{:S(2)}) collective-permute-start(bf16[4,64,512]{2,1,0:T(8,128)(2,1)S(1)} %slice.11), channel_id=1, source_target_pairs={{0,1},{1,0},{2,3},{3,2},{4,5},{5,4},{6,7},{7,6},{8,9},{9,8},{10,11... | collective-permute-start | bytes 786440 | tf_op jit(solution)/shard_map/ppermute | solution.py:21
  110.7 2.2 %collective-permute-start.49 = (bf16[4,64,512]{2,1,0:T(8,128)(2,1)S(1)}, bf16[4,64,512]{2,1,0:T(8,128)(2,1)S(1)}, u32[]{:S(2)}, u32[]{:S(2)}) collective-permute-start(bf16[4,64,512]{2,1,0:T(8,128)(2,1)S(1)} %get-tuple-element.271), channel_id=1, source_target_pairs={{0,1},{1,0},{2,3},{3,2},{4,5},{5,4},{6,7},{7,6},{8,9},{9,8},{10,11... | collective-permute-start | bytes 786440 | tf_op jit(solution)/shard_map/ppermute | solution.py:21
  (14 other events, 153.6 us)

commit v8 on v7

--- a/solution.py
+++ b/solution.py
@@ -273,6 +273,34 @@
         bundle_x, bundle_z = ([dp_swap(v, bit) for v in bundle_y] for bit in (1, 2))
         bundle_xz = [dp_swap(v, 2) for v in bundle_x]
         bundle_yc = [mp_swap(v, 1) for v in bundle_y]
+        def unpacked(n):
+            return [
+                shape((3 * width, lane * n), BF16),
+                shape((lane * n, width), BF16),
+                shape((n, VEC, lane), F32),
+            ]
+
+        def unpack(pieces, outs, n):
+            dpi = lax.axis_index("dp")
+            weights, wo, smalls = outs
+            for j, ps in enumerate(take(pieces, [len(pieces) // n] * n)):
+                v = whole(ps, dpi & 1, (dpi >> 1) & 1)
+                weights[:, j * lane : (j + 1) * lane] = v[:o_at]
+                for c in range(cols):
+                    wo[j * lane : (j + 1) * lane, c * lane : (c + 1) * lane] = v[
+                        o_at + c * lane : o_at + (c + 1) * lane
+                    ]
+                parts = v[s_at:].astype(F32)
+                smalls[j] = parts[:VEC] + parts[VEC : 2 * VEC] + parts[2 * VEC : 3 * VEC]
+
+        near_unpacked = run(
+            "unpack",
+            lambda ins, outs, _: unpack(ins, outs, 2),
+            [bundle, bundle_core],
+            unpacked(2),
+        )
+
+        token_parts[2:], near_unpacked = together(token_parts[2:], near_unpacked)
         token_parts = token_parts[:2] + pass_rows(token_parts[2:])
 
         def far(even, odd):
@@ -315,14 +343,16 @@
                     to, first = (dst[k], 0) if k < 2 else (dst[k // 2 + 1], (k % 2) * 2 * own)
                     to[first + lead + r] = value[at : at + share]
 
-        def attend(group, first, pieces):
+        def attend(group, first, pieces, ready=()):
             wide = lane * len(group)
             heads = wide // HD
-            counts = [len(pieces) // len(group)] * len(group)
 
             def fn(ins, outs, scratch):
                 me, dpi = lax.axis_index("mp"), lax.axis_index("dp")
-                qkv_ref, p_ref, att_ref, weights, wo, smalls = outs[-6:]
+                if ready:
+                    (weights, wo, smalls), (qkv_ref, p_ref, att_ref) = ins[-3:], outs[-3:]
+                else:
+                    qkv_ref, p_ref, att_ref, weights, wo, smalls = outs[-6:]
                 if first:
                     lens, om, gains, shifts = ins[n_mp : n_mp + 4]
                     x_ref, a1_ref = outs[:2]
@@ -331,15 +361,8 @@
                     a1_ref[...] = (normed * gains[0:1] + shifts[0:1]).astype(BF16)
                 else:
                     lens, om, a1_ref = ins[:3]
-                for j, ps in enumerate(take(ins[-len(pieces) :], counts)):
-                    v = whole(ps, dpi & 1, (dpi >> 1) & 1)
-                    weights[:, j * lane : (j + 1) * lane] = v[:o_at]
-                    for c in range(cols):
-                        wo[j * lane : (j + 1) * lane, c * lane : (c + 1) * lane] = v[
-                            o_at + c * lane : o_at + (c + 1) * lane
-                        ]
-                    parts = v[s_at:].astype(F32)
-                    smalls[j] = parts[:VEC] + parts[VEC : 2 * VEC] + parts[2 * VEC : 3 * VEC]
+                if not ready:
+                    unpack(ins[-len(pieces) :], (weights, wo, smalls), len(group))
                 a1 = a1_ref[...]
                 for t in range(3):
                     y = dot(a1, weights[t * width : (t + 1) * width])
@@ -382,20 +405,19 @@
             return run(
                 "attend",
                 fn,
-                ins + pieces,
+                ins + (list(ready) or pieces),
                 lead
                 + [
                     shape((3, count, wide), BF16),
                     shape((own * heads, slots, slots), BF16),
                     shape((count, wide), BF16),
-                    shape((3 * width, wide), BF16),
-                    shape((wide, width), BF16),
-                    shape((len(group), VEC, lane), F32),
-                ],
+                ]
+                + ([] if ready else unpacked(len(group))),
                 smem=(n_mp if first else 0,),
             )
 
-        x, a1, qkv0, p0, att0, wq0, wo0, small0 = attend(groups[0], True, [bundle, bundle_core])
+        x, a1, qkv0, p0, att0 = attend(groups[0], True, [], near_unpacked)
+        wq0, wo0, small0 = near_unpacked
 
         bundle_x, bundle_z, bundle_xz, (att0,), sends = together(
             bundle_x, bundle_z, bundle_xz, [att0], cot_parts[1:]

time: 117 us -> 117 us (level)
    pallas_call x27 -> x28, Pallas kernels: 37.6 us -> 38 us  [run(): pl.pallas_call(kernel, out_shape=tuple(outs), in_specs=[pl.BlockSpec(memo...]
  transfers between devices with their start and end apart: 52 -> 52, of which waited for: 22 -> 21; matrix products, arithmetic and copies ran while one was open for 0% -> 0% of each run, Pallas kernels for 28% -> 28%
where the time goes in v8:
time: 117 us
  starting transfers between devices  47.2 us (40%)
  Pallas kernels  38 us (32%)
  waiting for transfers between devices  29.5 us (25%)
  local copies, waits for them, and re-layouts  1.18 us (1%)
    ppermute x52, starting transfers between devices, swap(): return lax.ppermute(v, axis, [(i, i ^ bit) for i in range(size)])  47.2 us
    pallas_call x28, Pallas kernels, run(): pl.pallas_call(kernel, out_shape=tuple(outs), in_specs=[pl.BlockSpec(memo...  38 us
    ppermute x52, waiting for transfers between devices, swap(): return lax.ppermute(v, axis, [(i, i ^ bit) for i in range(size)])  29.5 us
  transfers between devices with their start and end apart: 52, of which 21 were waited for; matrix products, arithmetic and copies ran while one was open for 0% of the time, Pallas kernels for 28%

profile of v8, /device:TPU:0, one launch (start us, length us, event | category | flops | bytes accessed | tf_op | source)
XLA Modules:
  0.0 117.0 jit_solution(1220623241463378027)
XLA Ops:
  0.7 3.2 %begin.1 = (bf16[2,64,512]{2,1,0:T(8,128)(2,1)}, bf16[2,64,512]{2,1,0:T(8,128)(2,1)}, bf16[4,64,512]{2,1,0:T(8,128)(2,1)}, bf16[2112,128]{1,0:T(8,128)(2,1)}, bf16[528,128]{1,0:T(8,128)(2,1)}) custom-call(bf16[8,64,512]{2,1,0:T(8,128)(2,1)} %refs_0_.4, bf16[1536,128]{1,0:T(8,128)(2,1)} %bitcast.9, bf16[128,512]{1,0:T(8,128)(2,1)} %refs_2_.3, ...), custom_call_target="tpu_custom_call" | custom-call | flops 1 | bytes 1 | tf_op jit(solution)/shard_map/begin/pallas_call | solution.py:43
  5.0 2.9 %collective-permute-start = (bf16[528,128]{1,0:T(8,128)(2,1)}, bf16[528,128]{1,0:T(8,128)(2,1)S(1)}, u32[]{:S(2)}, u32[]{:S(2)}) collective-permute-start(bf16[528,128]{1,0:T(8,128)(2,1)} %get-tuple-element.159.refs_3_), channel_id=1, source_target_pairs={{0,2},{1,3},{2,0},{3,1},{4,6},{5,7},{6,4},{7,5},{8,10},{9,11},{10,... | collective-permute-start | bytes 405512 | tf_op jit(solution)/shard_map/ppermute | solution.py:21
  8.0 2.8 %collective-permute-start.5 = (bf16[4,64,512]{2,1,0:T(8,128)(2,1)}, bf16[4,64,512]{2,1,0:T(8,128)(2,1)S(1)}, u32[]{:S(2)}, u32[]{:S(2)}) collective-permute-start(bf16[4,64,512]{2,1,0:T(8,128)(2,1)} %get-tuple-element.165), channel_id=1, source_target_pairs={{0,2},{1,3},{2,0},{3,1},{4,6},{5,7},{6,4},{7,5},{8,10},{9,11},{10,... | collective-permute-start | bytes 786440 | tf_op jit(solution)/shard_map/ppermute | solution.py:21
  10.8 1.2 %collective-permute-done.refs_3_ = bf16[528,128]{1,0:T(8,128)(2,1)S(1)} collective-permute-done((bf16[528,128]{1,0:T(8,128)(2,1)}, bf16[528,128]{1,0:T(8,128)(2,1)S(1)}, u32[]{:S(2)}, u32[]{:S(2)}) %collective-permute-start) | collective-permute-done | bytes 135200 | tf_op jit(solution)/shard_map/ppermute | solution.py:21
  12.0 1.8 %collective-permute-start.7 = (bf16[528,128]{1,0:T(8,128)(2,1)S(1)}, bf16[528,128]{1,0:T(8,128)(2,1)S(1)}, u32[]{:S(2)}, u32[]{:S(2)}) collective-permute-start(bf16[528,128]{1,0:T(8,128)(2,1)S(1)} %collective-permute-done.refs_3_), channel_id=1, source_target_pairs={{0,4},{4,0},{8,12},{12,8},{16,20},{20,16},{24,28},{28,24},{1,5},{5... | collective-permute-start | bytes 405512 | tf_op jit(solution)/shard_map/ppermute | solution.py:21
  13.8 2.3 %cut_rest.1 = (bf16[2,64,512]{2,1,0:T(8,128)(2,1)}, bf16[2,64,512]{2,1,0:T(8,128)(2,1)}, bf16[4,64,512]{2,1,0:T(8,128)(2,1)}, bf16[2,256,512]{2,1,0:T(8,128)(2,1)}) custom-call(bf16[8,64,512]{2,1,0:T(8,128)(2,1)} %refs_0_.5, bf16[512,512]{1,0:T(8,128)(2,1)} %refs_7_.5, bf16[512,512]{1,0:T(8,128)(2,1)} %refs_9_.5, bf16[528,128]{1,0:T(8,128)(2,1)} %get-tuple-element.159.refs_3_), custom_call_target="tpu_custom_call" | custom-call | flops 1 | bytes 1 | tf_op jit(solution)/shard_map/cut_rest/pallas_call | solution.py:43
  16.1 1.6 %collective-permute-start.10 = (bf16[2,256,512]{2,1,0:T(8,128)(2,1)}, bf16[2,256,512]{2,1,0:T(8,128)(2,1)S(1)}, u32[]{:S(2)}, u32[]{:S(2)}) collective-permute-start(bf16[2,256,512]{2,1,0:T(8,128)(2,1)} %get-tuple-element.181), channel_id=1, source_target_pairs={{0,2},{1,3},{2,0},{3,1},{4,6},{5,7},{6,4},{7,5},{8,10},{9,11},{10,... | collective-permute-start | bytes 1572872 | tf_op jit(solution)/shard_map/ppermute | solution.py:21
  17.7 1.6 %collective-permute-start.8 = (bf16[528,128]{1,0:T(8,128)(2,1)S(1)}, bf16[528,128]{1,0:T(8,128)(2,1)S(1)}, u32[]{:S(2)}, u32[]{:S(2)}) collective-permute-start(bf16[528,128]{1,0:T(8,128)(2,1)S(1)} %collective-permute-done.refs_3_), channel_id=1, source_target_pairs={{0,8},{4,12},{8,0},{12,4},{16,24},{20,28},{24,16},{28,20},{1,9},{5... | collective-permute-start | bytes 405512 | tf_op jit(solution)/shard_map/ppermute | solution.py:21
  19.7 1.0 copy-done.2
  22.5 3.3 %attend.2 = (bf16[512,512]{1,0:T(8,128)(2,1)S(1)}, bf16[512,512]{1,0:T(8,128)(2,1)S(1)}, bf16[3,512,256]{2,1,0:T(8,128)(2,1)S(1)}, bf16[8,256,256]{2,1,0:T(8,128)(2,1)S(1)}, bf16[512,256]{1,0:T(8,128)(2,1)S(1)}) custom-call(bf16[2,64,512]{2,1,0:T(8,128)(2,1)S(1)} %copy-done.4, bf16[2,64,512]{2,1,0:T(8,128)(2,1)S(1)} %collective-permute-done.2.refs_1_, ...), custom_call_target="tpu_custom_call" | custom-call | flops 1 | bytes 1 | tf_op jit(solution)/shard_map/attend/pallas_call | solution.py:43
  27.7 3.1 %attend.3 = (bf16[3,512,256]{2,1,0:T(8,128)(2,1)S(1)}, bf16[8,256,256]{2,1,0:T(8,128)(2,1)S(1)}, bf16[512,256]{1,0:T(8,128)(2,1)S(1)}, bf16[1536,256]{1,0:T(8,12...) custom-call(s32[8]{0:T(128)S(1)} %copy-done.9, s32[8,256]{1,0:T(8,128)S(1)} %copy-done.6, ...), custom_call_target="tpu_custom_call" | custom-call | flops 1 | bytes 1 | tf_op jit(solution)/shard_map/attend/pallas_call | solution.py:43
  30.9 1.2 %collective-permute-start.19 = (bf16[256,512]{1,0:T(8,128)(2,1)S(1)}, bf16[256,512]{1,0:T(8,128)(2,1)S(1)}, u32[]{:S(2)}, u32[]{:S(2)}) collective-permute-start(bf16[256,512]{1,0:T(8,128)(2,1)S(1)} %get-tuple-element.207.refs_3_.refs_10_), channel_id=1, source_target_pairs={{0,4},{4,0},{8,12},{12,8},{16,20},{20,16},{24,28},{28,24},{1,5},{5... | collective-permute-start | bytes 786440 | tf_op jit(solution)/shard_map/ppermute | solution.py:21
  32.3 0.9 collective-permute-start.21
  33.4 2.7 %mlp_near_forward.1 = (f32[512,512]{1,0:T(8,128)S(1)}, bf16[512,512]{1,0:T(8,128)(2,1)S(1)}, bf16[512,512]{1,0:T(8,128)(2,1)S(1)}, f32[512,512]{1,0:T(8,128)S(1)...) custom-call(bf16[512,512]{1,0:T(8,128)(2,1)S(1)} %get-tuple-element.174.refs_0_.refs_3_, ...), custom_call_target="tpu_custom_call" | custom-call | flops 1 | bytes 1 | tf_op jit(solution)/shard_map/mlp_near_forward/pallas_call | solution.py:43
  36.4 1.1 collective-permute-done.17.refs_6_
  37.5 2.5 %mlp_near_backward.1 = (bf16[512,512]{1,0:T(8,128)(2,1)S(1)}, bf16[512,512]{1,0:T(8,128)(2,1)S(1)}, f32[512,512]{1,0:T(8,128)S(1)}, bf16[1,2,8,64,512]{4,3,2,1,0...) custom-call(bf16[2,512,512]{2,1,0:T(8,128)(2,1)S(1)} %get-tuple-element.198.refs_0_, ...), custom_call_target="tpu_custom_call" | custom-call | flops 1 | bytes 1 | tf_op jit(solution)/shard_map/mlp_near_backward/pallas_call | solution.py:43
  41.3 1.3 %mlp_even_forward.1 = (f32[512,512]{1,0:T(8,128)S(1)}, bf16[1,512,512]{2,1,0:T(8,128)(2,1)S(1)}, f32[1,512,512]{2,1,0:T(8,128)S(1)}) custom-call(bf16[512,512]{1,0:T(8,128)(2,1)S(1)} %get-tuple-element.196.refs_0_.refs_1_, f32[512,512]{1,0:T(8,128)S(1)} %get-tuple-element.205.refs_1_, f32[2,8,128]{2,1,0:T(8,128)S(1)} %get-tuple-element.206.refs_2_.refs_7_, ...), custom_call_target="tpu_custom_call" | custom-call | flops 1 | bytes 1 | tf_op jit(solution)/shard_map/mlp_even_forward/pallas_call | solution.py:43
  42.7 2.2 %mlp_far.2 = (f32[512,512]{1,0:T(8,128)S(1)}, f32[512,512]{1,0:T(8,128)S(1)}, bf16[1,2,8,64,512]{4,3,2,1,0:T(8,128)(2,1)S(1)}, f32[1,1,512]{2,1,0:T(1,128)S(1)}) custom-call(f32[512,512]{1,0:T(8,128)S(1)} %get-tuple-element.193.refs_0_, bf16[512,512]{1,0:T(8,128)(2,1)S(1)} %get-tuple-element.196.refs_0_.refs_1_, ...), custom_call_target="tpu_custom_call" | custom-call | flops 1 | bytes 1 | tf_op jit(solution)/shard_map/mlp_far/pallas_call | solution.py:43
  45.5 2.1 %mlp_far.3 = (bf16[512,512]{1,0:T(8,128)(2,1)S(1)}, f32[512,512]{1,0:T(8,128)S(1)}, bf16[512,512]{1,0:T(8,128)(2,1)S(1)}, f32[4,512]{1,0:T(4,128)S(1)}, bf16[1,2...) custom-call(f32[512,512]{1,0:T(8,128)S(1)} %get-tuple-element.193.refs_0_, ...), custom_call_target="tpu_custom_call" | custom-call | flops 1 | bytes 1 | tf_op jit(solution)/shard_map/mlp_far/pallas_call | solution.py:43
  48.2 1.0 collective-permute-start.27
  49.2 1.0 collective-permute-start.28
  50.3 9.5 %attend_back.1 = (bf16[4,64,512]{2,1,0:T(8,128)(2,1)S(1)}, bf16[4,64,512]{2,1,0:T(8,128)(2,1)S(1)}, bf16[8,64,512]{2,1,0:T(8,128)(2,1)S(1)}, bf16[1,8,272,128]{3...) custom-call(s32[8]{0:T(128)S(1)} %copy-done.9, ...), custom_call_target="tpu_custom_call" | custom-call | flops 1 | bytes 1 | tf_op jit(solution)/shard_map/attend_back/pallas_call | solution.py:43
  60.5 1.0 collective-permute-done.29.refs_1_
  63.3 1.0 collective-permute-start.37
  64.3 1.6 %collective-permute-start.38 = (bf16[4,64,512]{2,1,0:T(8,128)(2,1)S(1)}, bf16[4,64,512]{2,1,0:T(8,128)(2,1)S(1)}, u32[]{:S(2)}, u32[]{:S(2)}) collective-permute-start(bf16[4,64,512]{2,1,0:T(8,128)(2,1)S(1)} %get-tuple-element.267), channel_id=1, source_target_pairs={{0,8},{4,12},{8,0},{12,4},{16,24},{20,28},{24,16},{28,20},{1,9},{5... | collective-permute-start | bytes 786440 | tf_op jit(solution)/shard_map/ppermute | solution.py:21
  65.8 1.1 collective-permute-start.31
  66.9 0.9 collective-permute-start.32
  67.9 4.7 %collective-permute-done.37.refs_1_ = bf16[4,64,512]{2,1,0:T(8,128)(2,1)S(1)} collective-permute-done((bf16[4,64,512]{2,1,0:T(8,128)(2,1)S(1)}, bf16[4,64,512]{2,1,0:T(8,128)(2,1)S(1)}, u32[]{:S(2)}, u32[]{:S(2)}) %collective-permute-start.37) | collective-permute-done | bytes 262176 | tf_op jit(solution)/shard_map/ppermute | solution.py:21
  72.7 1.6 %collective-permute-start.39 = (bf16[2,64,512]{2,1,0:T(8,128)(2,1)S(1)}, bf16[2,64,512]{2,1,0:T(8,128)(2,1)S(1)}, u32[]{:S(2)}, u32[]{:S(2)}) collective-permute-start(bf16[2,64,512]{2,1,0:T(8,128)(2,1)S(1)} %get-tuple-element.269), channel_id=1, source_target_pairs={{0,8},{4,12},{8,0},{12,4},{16,24},{20,28},{24,16},{28,20},{1,9},{5... | collective-permute-start | bytes 393224 | tf_op jit(solution)/shard_map/ppermute | solution.py:21
  75.0 2.8 %collective-permute-done.39.refs_1_ = bf16[2,64,512]{2,1,0:T(8,128)(2,1)S(1)} collective-permute-done((bf16[2,64,512]{2,1,0:T(8,128)(2,1)S(1)}, bf16[2,64,512]{2,1,0:T(8,128)(2,1)S(1)}, u32[]{:S(2)}, u32[]{:S(2)}) %collective-permute-start.39) | collective-permute-done | bytes 131104 | tf_op jit(solution)/shard_map/ppermute | solution.py:21
  77.8 1.6 %collective-permute-done.40.refs_3_ = bf16[2,64,512]{2,1,0:T(8,128)(2,1)S(1)} collective-permute-done((bf16[2,64,512]{2,1,0:T(8,128)(2,1)S(1)}, bf16[2,64,512]{2,1,0:T(8,128)(2,1)S(1)}, u32[]{:S(2)}, u32[]{:S(2)}) %collective-permute-start.40) | collective-permute-done | bytes 131104 | tf_op jit(solution)/shard_map/ppermute | solution.py:21
  79.4 2.7 %collective-permute-start.41 = (bf16[2,2,64,512]{3,2,1,0:T(8,128)(2,1)S(1)}, bf16[2,2,64,512]{3,2,1,0:T(8,128)(2,1)S(1)}, u32[]{:S(2)}, u32[]{:S(2)}) collective-permute-start(bf16[2,2,64,512]{3,2,1,0:T(8,128)(2,1)S(1)} %join.1.refs_0_), channel_id=1, source_target_pairs={{0,16},{4,20},{8,24},{12,28},{16,0},{20,4},{24,8},{28,12},{1,17},{... | collective-permute-start | bytes 786440 | tf_op jit(solution)/shard_map/ppermute | solution.py:21
  82.9 1.3 %collective-permute-start.33 = (bf16[2,272,128]{2,1,0:T(8,128)(2,1)S(1)}, bf16[2,272,128]{2,1,0:T(8,128)(2,1)S(1)}, u32[]{:S(2)}, u32[]{:S(2)}) collective-permute-start(bf16[2,272,128]{2,1,0:T(8,128)(2,1)S(1)} %get-tuple-element.257), channel_id=1, source_target_pairs={{0,4},{4,0},{8,12},{12,8},{16,20},{20,16},{24,28},{28,24},{1,5},{5... | collective-permute-start | bytes 417800 | tf_op jit(solution)/shard_map/ppermute | solution.py:21
  85.0 0.9 collective-permute-start.48
  85.9 2.5 %collective-permute-done.33.refs_1_ = bf16[2,272,128]{2,1,0:T(8,128)(2,1)S(1)} collective-permute-done((bf16[2,272,128]{2,1,0:T(8,128)(2,1)S(1)}, bf16[2,272,128]{2,1,0:T(8,128)(2,1)S(1)}, u32[]{:S(2)}, u32[]{:S(2)}) %collective-permute-start.33) | collective-permute-done | bytes 139296 | tf_op jit(solution)/shard_map/ppermute | solution.py:21
  88.4 1.5 %collective-permute-done.34.refs_2_ = bf16[2,272,128]{2,1,0:T(8,128)(2,1)S(1)} collective-permute-done((bf16[2,272,128]{2,1,0:T(8,128)(2,1)S(1)}, bf16[2,272,128]{2,1,0:T(8,128)(2,1)S(1)}, u32[]{:S(2)}, u32[]{:S(2)}) %collective-permute-start.34) | collective-permute-done | bytes 139296 | tf_op jit(solution)/shard_map/ppermute | solution.py:21
  89.9 1.8 %collective-permute-start.35 = (bf16[1,272,128]{2,1,0:T(8,128)(2,1)S(1)}, bf16[1,272,128]{2,1,0:T(8,128)(2,1)S(1)}, u32[]{:S(2)}, u32[]{:S(2)}) collective-permute-start(bf16[1,272,128]{2,1,0:T(8,128)(2,1)S(1)} %get-tuple-element.260), channel_id=1, source_target_pairs={{0,8},{4,12},{8,0},{12,4},{16,24},{20,28},{24,16},{28,20},{1,9},{5... | collective-permute-start | bytes 208904 | tf_op jit(solution)/shard_map/ppermute | solution.py:21
  92.2 1.8 %collective-permute-start.44 = (bf16[2,64,512]{2,1,0:T(8,128)(2,1)S(1)}, bf16[2,64,512]{2,1,0:T(8,128)(2,1)S(1)}, u32[]{:S(2)}, u32[]{:S(2)}) collective-permute-start(bf16[2,64,512]{2,1,0:T(8,128)(2,1)S(1)} %get-tuple-element.272.refs_3_), channel_id=1, source_target_pairs={{0,8},{4,12},{8,0},{12,4},{16,24},{20,28},{24,16},{28,20},{1,9},{5... | collective-permute-start | bytes 393224 | tf_op jit(solution)/shard_map/ppermute | solution.py:21
  94.0 1.7 %collective-permute-start.46 = (bf16[2,64,512]{2,1,0:T(8,128)(2,1)S(1)}, bf16[2,64,512]{2,1,0:T(8,128)(2,1)S(1)}, u32[]{:S(2)}, u32[]{:S(2)}) collective-permute-start(bf16[2,64,512]{2,1,0:T(8,128)(2,1)S(1)} %get-tuple-element.274), channel_id=1, source_target_pairs={{0,4},{4,0},{8,12},{12,8},{16,20},{20,16},{24,28},{28,24},{1,5},{5... | collective-permute-start | bytes 393224 | tf_op jit(solution)/shard_map/ppermute | solution.py:21
  96.3 3.3 %collective-permute-start.42 = (bf16[2,272,128]{2,1,0:T(8,128)(2,1)S(1)}, bf16[2,272,128]{2,1,0:T(8,128)(2,1)S(1)}, u32[]{:S(2)}, u32[]{:S(2)}) collective-permute-start(bf16[2,272,128]{2,1,0:T(8,128)(2,1)S(1)} %add_parts.5.refs_0_), channel_id=1, source_target_pairs={{0,16},{4,20},{8,24},{12,28},{16,0},{20,4},{24,8},{28,12},{1,17},{... | collective-permute-start | bytes 417800 | tf_op jit(solution)/shard_map/ppermute | solution.py:21
  99.7 1.9 %collective-permute-start.45 = (bf16[4,64,512]{2,1,0:T(8,128)(2,1)S(1)}, bf16[4,64,512]{2,1,0:T(8,128)(2,1)S(1)}, u32[]{:S(2)}, u32[]{:S(2)}) collective-permute-start(bf16[4,64,512]{2,1,0:T(8,128)(2,1)S(1)} %constant_dynamic-update-slice_fusion.refs_0_), channel_id=1, source_target_pairs={{0,4},{4,0},{8,12},{12,8},{16,20},{20,16},{24,28},{28,24},{1,5},{5... | collective-permute-start | bytes 786440 | tf_op jit(solution)/shard_map/ppermute | solution.py:21
  101.6 2.4 %collective-permute-done.42.refs_1_ = bf16[2,272,128]{2,1,0:T(8,128)(2,1)S(1)} collective-permute-done((bf16[2,272,128]{2,1,0:T(8,128)(2,1)S(1)}, bf16[2,272,128]{2,1,0:T(8,128)(2,1)S(1)}, u32[]{:S(2)}, u32[]{:S(2)}) %collective-permute-start.42) | collective-permute-done | bytes 139296 | tf_op jit(solution)/shard_map/ppermute | solution.py:21
  104.5 4.8 %collective-permute-done.43 = bf16[2,272,128]{2,1,0:T(8,128)(2,1)S(1)} collective-permute-done((bf16[2,272,128]{2,1,0:T(8,128)(2,1)S(1)}, bf16[2,272,128]{2,1,0:T(8,128)(2,1)S(1)}, u32[]{:S(2)}, u32[]{:S(2)}) %collective-permute-start.43) | collective-permute-done | bytes 139296 | tf_op jit(solution)/shard_map/ppermute | solution.py:21
  109.3 1.8 %collective-permute-start.51 = (bf16[4,272,128]{2,1,0:T(8,128)(2,1)S(1)}, bf16[4,272,128]{2,1,0:T(8,128)(2,1)S(1)}, u32[]{:S(2)}, u32[]{:S(2)}) collective-permute-start(bf16[4,272,128]{2,1,0:T(8,128)(2,1)S(1)} %pad_maximum_fusion.refs_0_), channel_id=1, source_target_pairs={{0,4},{4,0},{8,12},{12,8},{16,20},{20,16},{24,28},{28,24},{1,5},{5... | collective-permute-start | bytes 835592 | tf_op jit(solution)/shard_map/ppermute | solution.py:21
  111.7 1.7 %finish_mlp.1 = (f32[512,512]{1,0:T(8,128)}, f32[512,512]{1,0:T(8,128)}, f32[8,128]{1,0:T(8,128)S(1)}) custom-call(bf16[4,64,512]{2,1,0:T(8,128)(2,1)S(1)} %constant_dynamic-update-slice_fusion.refs_0_, bf16[4,64,512]{2,1,0:T(8,128)(2,1)S(1)} %collective-permute-done.45.refs_1_, bf16[4,64,512]{2,1,0:T(8,128)(2,1)S(1)} %constant_dynamic-update-slice_fusion.2.refs_2_, ...), custom_call_target="tpu_custom_call" | custom-call | flops 1 | bytes 1 | tf_op jit(solution)/shard_map/finish_mlp/pallas_call | solution.py:43
  113.4 1.2 %gather_rows.1 = (bf16[8,64,512]{2,1,0:T(8,128)(2,1)}, f32[8,64,512]{2,1,0:T(8,128)}, f32[8,128]{1,0:T(8,128)S(1)}) custom-call(bf16[4,64,512]{2,1,0:T(8,128)(2,1)S(1)} %get-tuple-element.278.refs_0_, bf16[4,64,512]{2,1,0:T(8,128)(2,1)S(1)} %collective-permute-done.49.refs_1_, bf16[8,64,512]{2,1,0:T(8,128)(2,1)S(1)} %collective-permute-done.48.refs_2_, ...), custom_call_target="tpu_custom_call" | custom-call | flops 1 | bytes 1 | tf_op jit(solution)/shard_map/gather_rows/pallas_call | solution.py:43
  114.7 1.2 %collective-permute-done.51.refs_1_ = bf16[4,272,128]{2,1,0:T(8,128)(2,1)S(1)} collective-permute-done((bf16[4,272,128]{2,1,0:T(8,128)(2,1)S(1)}, bf16[4,272,128]{2,1,0:T(8,128)(2,1)S(1)}, u32[]{:S(2)}, u32[]{:S(2)}) %collective-permute-start.51) | collective-permute-done | bytes 278560 | tf_op jit(solution)/shard_map/ppermute | solution.py:21
  115.9 1.1 finish_att.1
  (116 shorter events, 15.6 us)
Async XLA Ops:
  3.9 8.1 %collective-permute-start.1 = (bf16[2112,128]{1,0:T(8,128)(2,1)}, bf16[2112,128]{1,0:T(8,128)(2,1)S(1)}, u32[]{:S(2)}, u32[]{:S(2)}) collective-permute-start(bf16[2112,128]{1,0:T(8,128)(2,1)} %get-tuple-element.160.refs_0_), channel_id=1, source_target_pairs={{0,1},{1,0},{2,3},{3,2},{4,5},{5,4},{6,7},{7,6},{8,9},{9,8},{10,11... | collective-permute-start | bytes 1622024 | tf_op jit(solution)/shard_map/ppermute | solution.py:21
  4.4 7.6 %collective-permute-start.3 = (bf16[512,512]{1,0:T(8,128)(2,1)}, bf16[512,512]{1,0:T(8,128)(2,1)S(1)}, u32[]{:S(2)}, u32[]{:S(2)}) collective-permute-start(bf16[512,512]{1,0:T(8,128)(2,1)} %refs_7_.5), channel_id=1, source_target_pairs={{0,1},{1,0},{2,3},{3,2},{4,5},{5,4},{6,7},{7,6},{8,9},{9,8},{10,11... | collective-permute-start | bytes 1572872 | tf_op jit(solution)/shard_map/ppermute | solution.py:21
  4.5 7.5 %collective-permute-start.4 = (bf16[512,512]{1,0:T(8,128)(2,1)}, bf16[512,512]{1,0:T(8,128)(2,1)S(1)}, u32[]{:S(2)}, u32[]{:S(2)}) collective-permute-start(bf16[512,512]{1,0:T(8,128)(2,1)} %refs_9_.5), channel_id=1, source_target_pairs={{0,1},{1,0},{2,3},{3,2},{4,5},{5,4},{6,7},{7,6},{8,9},{9,8},{10,11... | collective-permute-start | bytes 1572872 | tf_op jit(solution)/shard_map/ppermute | solution.py:21
  5.0 3.0 %collective-permute-start.2 = (bf16[2,64,512]{2,1,0:T(8,128)(2,1)}, bf16[2,64,512]{2,1,0:T(8,128)(2,1)S(1)}, u32[]{:S(2)}, u32[]{:S(2)}) collective-permute-start(bf16[2,64,512]{2,1,0:T(8,128)(2,1)} %get-tuple-element.162), channel_id=1, source_target_pairs={{0,1},{1,0},{2,3},{3,2},{4,5},{5,4},{6,7},{7,6},{8,9},{9,8},{10,11... | collective-permute-start | bytes 393224 | tf_op jit(solution)/shard_map/ppermute | solution.py:21
  5.0 7.0 %collective-permute-start = (bf16[528,128]{1,0:T(8,128)(2,1)}, bf16[528,128]{1,0:T(8,128)(2,1)S(1)}, u32[]{:S(2)}, u32[]{:S(2)}) collective-permute-start(bf16[528,128]{1,0:T(8,128)(2,1)} %get-tuple-element.159.refs_3_), channel_id=1, source_target_pairs={{0,2},{1,3},{2,0},{3,1},{4,6},{5,7},{6,4},{7,5},{8,10},{9,11},{10,... | collective-permute-start | bytes 405512 | tf_op jit(solution)/shard_map/ppermute | solution.py:21
  8.0 13.0 %collective-permute-start.5 = (bf16[4,64,512]{2,1,0:T(8,128)(2,1)}, bf16[4,64,512]{2,1,0:T(8,128)(2,1)S(1)}, u32[]{:S(2)}, u32[]{:S(2)}) collective-permute-start(bf16[4,64,512]{2,1,0:T(8,128)(2,1)} %get-tuple-element.165), channel_id=1, source_target_pairs={{0,2},{1,3},{2,0},{3,1},{4,6},{5,7},{6,4},{7,5},{8,10},{9,11},{10,... | collective-permute-start | bytes 786440 | tf_op jit(solution)/shard_map/ppermute | solution.py:21
  12.0 7.2 %collective-permute-start.7 = (bf16[528,128]{1,0:T(8,128)(2,1)S(1)}, bf16[528,128]{1,0:T(8,128)(2,1)S(1)}, u32[]{:S(2)}, u32[]{:S(2)}) collective-permute-start(bf16[528,128]{1,0:T(8,128)(2,1)S(1)} %collective-permute-done.refs_3_), channel_id=1, source_target_pairs={{0,4},{4,0},{8,12},{12,8},{16,20},{20,16},{24,28},{28,24},{1,5},{5... | collective-permute-start | bytes 405512 | tf_op jit(solution)/shard_map/ppermute | solution.py:21
  16.1 14.8 %collective-permute-start.10 = (bf16[2,256,512]{2,1,0:T(8,128)(2,1)}, bf16[2,256,512]{2,1,0:T(8,128)(2,1)S(1)}, u32[]{:S(2)}, u32[]{:S(2)}) collective-permute-start(bf16[2,256,512]{2,1,0:T(8,128)(2,1)} %get-tuple-element.181), channel_id=1, source_target_pairs={{0,2},{1,3},{2,0},{3,1},{4,6},{5,7},{6,4},{7,5},{8,10},{9,11},{10,... | collective-permute-start | bytes 1572872 | tf_op jit(solution)/shard_map/ppermute | solution.py:21
  17.7 8.1 %collective-permute-start.8 = (bf16[528,128]{1,0:T(8,128)(2,1)S(1)}, bf16[528,128]{1,0:T(8,128)(2,1)S(1)}, u32[]{:S(2)}, u32[]{:S(2)}) collective-permute-start(bf16[528,128]{1,0:T(8,128)(2,1)S(1)} %collective-permute-done.refs_3_), channel_id=1, source_target_pairs={{0,8},{4,12},{8,0},{12,4},{16,24},{20,28},{24,16},{28,20},{1,9},{5... | collective-permute-start | bytes 405512 | tf_op jit(solution)/shard_map/ppermute | solution.py:21
  19.3 6.5 %collective-permute-start.9 = (bf16[528,128]{1,0:T(8,128)(2,1)S(1)}, bf16[528,128]{1,0:T(8,128)(2,1)S(1)}, u32[]{:S(2)}, u32[]{:S(2)}) collective-permute-start(bf16[528,128]{1,0:T(8,128)(2,1)S(1)} %collective-permute-done.7.refs_4_), channel_id=1, source_target_pairs={{0,8},{4,12},{8,0},{12,4},{16,24},{20,28},{24,16},{28,20},{1,9},{5... | collective-permute-start | bytes 405512 | tf_op jit(solution)/shard_map/ppermute | solution.py:21
  21.1 5.4 %collective-permute-start.11 = (bf16[528,128]{1,0:T(8,128)(2,1)S(1)}, bf16[528,128]{1,0:T(8,128)(2,1)S(1)}, u32[]{:S(2)}, u32[]{:S(2)}) collective-permute-start(bf16[528,128]{1,0:T(8,128)(2,1)S(1)} %collective-permute-done.refs_3_), channel_id=1, source_target_pairs={{0,1},{1,0},{2,3},{3,2},{4,5},{5,4},{6,7},{7,6},{8,9},{9,8},{10,11... | collective-permute-start | bytes 405512 | tf_op jit(solution)/shard_map/ppermute | solution.py:21
  25.8 1.4 %collective-permute-start.12 = (bf16[528,128]{1,0:T(8,128)(2,1)S(1)}, bf16[528,128]{1,0:T(8,128)(2,1)S(1)}, u32[]{:S(2)}, u32[]{:S(2)}) collective-permute-start(bf16[528,128]{1,0:T(8,128)(2,1)S(1)} %collective-permute-done.7.refs_4_), channel_id=1, source_target_pairs={{0,1},{1,0},{2,3},{3,2},{4,5},{5,4},{6,7},{7,6},{8,9},{9,8},{10,11... | collective-permute-start | bytes 405512 | tf_op jit(solution)/shard_map/ppermute | solution.py:21
  26.5 9.5 %collective-permute-start.16 = (bf16[4,64,512]{2,1,0:T(8,128)(2,1)S(1)}, bf16[4,64,512]{2,1,0:T(8,128)(2,1)S(1)}, u32[]{:S(2)}, u32[]{:S(2)}) collective-permute-start(bf16[4,64,512]{2,1,0:T(8,128)(2,1)S(1)} %copy-done.10), channel_id=1, source_target_pairs={{0,2},{1,3},{2,0},{3,1},{4,6},{5,7},{6,4},{7,5},{8,10},{9,11},{10,... | collective-permute-start | bytes 786440 | tf_op jit(solution)/shard_map/ppermute | solution.py:21
  27.2 3.7 %collective-permute-start.15 = (bf16[2,64,512]{2,1,0:T(8,128)(2,1)S(1)}, bf16[2,64,512]{2,1,0:T(8,128)(2,1)S(1)}, u32[]{:S(2)}, u32[]{:S(2)}) collective-permute-start(bf16[2,64,512]{2,1,0:T(8,128)(2,1)S(1)} %copy-done.11), channel_id=1, source_target_pairs={{0,1},{1,0},{2,3},{3,2},{4,5},{5,4},{6,7},{7,6},{8,9},{9,8},{10,11... | collective-permute-start | bytes 393224 | tf_op jit(solution)/shard_map/ppermute | solution.py:21
  30.9 9.1 %collective-permute-start.19 = (bf16[256,512]{1,0:T(8,128)(2,1)S(1)}, bf16[256,512]{1,0:T(8,128)(2,1)S(1)}, u32[]{:S(2)}, u32[]{:S(2)}) collective-permute-start(bf16[256,512]{1,0:T(8,128)(2,1)S(1)} %get-tuple-element.207.refs_3_.refs_10_), channel_id=1, source_target_pairs={{0,4},{4,0},{8,12},{12,8},{16,20},{20,16},{24,28},{28,24},{1,5},{5... | collective-permute-start | bytes 786440 | tf_op jit(solution)/shard_map/ppermute | solution.py:21
  32.1 7.9 %collective-permute-start.18 = (bf16[256,512]{1,0:T(8,128)(2,1)S(1)}, bf16[256,512]{1,0:T(8,128)(2,1)S(1)}, u32[]{:S(2)}, u32[]{:S(2)}) collective-permute-start(bf16[256,512]{1,0:T(8,128)(2,1)S(1)} %get-tuple-element.207.refs_3_.refs_10_), channel_id=1, source_target_pairs={{0,1},{1,0},{2,3},{3,2},{4,5},{5,4},{6,7},{7,6},{8,9},{9,8},{10,11... | collective-permute-start | bytes 786440 | tf_op jit(solution)/shard_map/ppermute | solution.py:21
  32.3 8.6 %collective-permute-start.21 = (bf16[256,512]{1,0:T(8,128)(2,1)S(1)}, bf16[256,512]{1,0:T(8,128)(2,1)S(1)}, u32[]{:S(2)}, u32[]{:S(2)}) collective-permute-start(bf16[256,512]{1,0:T(8,128)(2,1)S(1)} %get-tuple-element.208.refs_5_.refs_12_), channel_id=1, source_target_pairs={{0,8},{4,12},{8,0},{12,4},{16,24},{20,28},{24,16},{28,20},{1,9},{5... | collective-permute-start | bytes 786440 | tf_op jit(solution)/shard_map/ppermute | solution.py:21
  33.1 7.7 %collective-permute-start.20 = (bf16[256,512]{1,0:T(8,128)(2,1)S(1)}, bf16[256,512]{1,0:T(8,128)(2,1)S(1)}, u32[]{:S(2)}, u32[]{:S(2)}) collective-permute-start(bf16[256,512]{1,0:T(8,128)(2,1)S(1)} %get-tuple-element.208.refs_5_.refs_12_), channel_id=1, source_target_pairs={{0,1},{1,0},{2,3},{3,2},{4,5},{5,4},{6,7},{7,6},{8,9},{9,8},{10,11... | collective-permute-start | bytes 786440 | tf_op jit(solution)/shard_map/ppermute | solution.py:21
  40.8 1.9 %collective-permute-start.22 = (bf16[256,512]{1,0:T(8,128)(2,1)S(1)}, bf16[256,512]{1,0:T(8,128)(2,1)S(1)}, u32[]{:S(2)}, u32[]{:S(2)}) collective-permute-start(bf16[256,512]{1,0:T(8,128)(2,1)S(1)} %collective-permute-done.19.refs_4_.refs_11_), channel_id=1, source_target_pairs={{0,1},{1,0},{2,3},{3,2},{4,5},{5,4},{6,7},{7,6},{8,9},{9,8},{10,11... | collective-permute-start | bytes 786440 | tf_op jit(solution)/shard_map/ppermute | solution.py:21
  40.8 1.9 %collective-permute-start.23 = (bf16[256,512]{1,0:T(8,128)(2,1)S(1)}, bf16[256,512]{1,0:T(8,128)(2,1)S(1)}, u32[]{:S(2)}, u32[]{:S(2)}) collective-permute-start(bf16[256,512]{1,0:T(8,128)(2,1)S(1)} %collective-permute-done.21.refs_6_.refs_13_), channel_id=1, source_target_pairs={{0,1},{1,0},{2,3},{3,2},{4,5},{5,4},{6,7},{7,6},{8,9},{9,8},{10,11... | collective-permute-start | bytes 786440 | tf_op jit(solution)/shard_map/ppermute | solution.py:21
  41.3 6.2 %collective-permute-start.24 = (bf16[1,2,8,64,512]{4,3,2,1,0:T(8,128)(2,1)S(1)}, bf16[1,2,8,64,512]{4,3,2,1,0:T(8,128)(2,1)S(1)}, u32[]{:S(2)}, u32[]{:S(2)}) collective-permute-start(bf16[1,2,8,64,512]{4,3,2,1,0:T(8,128)(2,1)S(1)} %get-tuple-element.224), channel_id=1, source_target_pairs={{0,1},{1,0},{2,3},{3,2},{4,5},{5,4},{6,7},{7,6},{8,9},{9,8},{10,11... | collective-permute-start | bytes 3145736 | tf_op jit(solution)/shard_map/ppermute | solution.py:21
  44.9 2.8 %collective-permute-start.25 = (bf16[1,2,8,64,512]{4,3,2,1,0:T(8,128)(2,1)S(1)}, bf16[1,2,8,64,512]{4,3,2,1,0:T(8,128)(2,1)S(1)}, u32[]{:S(2)}, u32[]{:S(2)}) collective-permute-start(bf16[1,2,8,64,512]{4,3,2,1,0:T(8,128)(2,1)S(1)} %get-tuple-element.226), channel_id=1, source_target_pairs={{0,1},{1,0},{2,3},{3,2},{4,5},{5,4},{6,7},{7,6},{8,9},{9,8},{10,11... | collective-permute-start | bytes 3145736 | tf_op jit(solution)/shard_map/ppermute | solution.py:21
  48.2 14.3 %collective-permute-start.27 = (bf16[2,4,64,512]{3,2,1,0:T(8,128)(2,1)S(1)}, bf16[2,4,64,512]{3,2,1,0:T(8,128)(2,1)S(1)}, u32[]{:S(2)}, u32[]{:S(2)}) collective-permute-start(bf16[2,4,64,512]{3,2,1,0:T(8,128)(2,1)S(1)} %get-tuple-element.244), channel_id=1, source_target_pairs={{0,4},{4,0},{8,12},{12,8},{16,20},{20,16},{24,28},{28,24},{1,5},{5... | collective-permute-start | bytes 1572872 | tf_op jit(solution)/shard_map/ppermute | solution.py:21
  49.2 13.9 %collective-permute-start.28 = (bf16[8,64,512]{2,1,0:T(8,128)(2,1)S(1)}, bf16[8,64,512]{2,1,0:T(8,128)(2,1)S(1)}, u32[]{:S(2)}, u32[]{:S(2)}) collective-permute-start(bf16[8,64,512]{2,1,0:T(8,128)(2,1)S(1)} %get-tuple-element.247), channel_id=1, source_target_pairs={{0,2},{1,3},{2,0},{3,1},{4,6},{5,7},{6,4},{7,5},{8,10},{9,11},{10,... | collective-permute-start | bytes 1572872 | tf_op jit(solution)/shard_map/ppermute | solution.py:21
  59.8 1.6 %collective-permute-start.29 = (bf16[1,4,272,128]{3,2,1,0:T(8,128)(2,1)S(1)}, bf16[1,4,272,128]{3,2,1,0:T(8,128)(2,1)S(1)}, u32[]{:S(2)}, u32[]{:S(2)}) collective-permute-start(bf16[1,4,272,128]{3,2,1,0:T(8,128)(2,1)S(1)} %get-tuple-element.250), channel_id=1, source_target_pairs={{0,1},{1,0},{2,3},{3,2},{4,5},{5,4},{6,7},{7,6},{8,9},{9,8},{10,11... | collective-permute-start | bytes 835592 | tf_op jit(solution)/shard_map/ppermute | solution.py:21
  59.9 1.9 %collective-permute-start.30 = (bf16[1,4,272,128]{3,2,1,0:T(8,128)(2,1)S(1)}, bf16[1,4,272,128]{3,2,1,0:T(8,128)(2,1)S(1)}, u32[]{:S(2)}, u32[]{:S(2)}) collective-permute-start(bf16[1,4,272,128]{3,2,1,0:T(8,128)(2,1)S(1)} %get-tuple-element.251), channel_id=1, source_target_pairs={{0,1},{1,0},{2,3},{3,2},{4,5},{5,4},{6,7},{7,6},{8,9},{9,8},{10,11... | collective-permute-start | bytes 835592 | tf_op jit(solution)/shard_map/ppermute | solution.py:21
  60.4 21.7 %collective-permute-start.26 = (bf16[1,8,272,128]{3,2,1,0:T(8,128)(2,1)S(1)}, bf16[1,8,272,128]{3,2,1,0:T(8,128)(2,1)S(1)}, u32[]{:S(2)}, u32[]{:S(2)}) collective-permute-start(bf16[1,8,272,128]{3,2,1,0:T(8,128)(2,1)S(1)} %get-tuple-element.242), channel_id=1, source_target_pairs={{0,1},{1,0},{2,3},{3,2},{4,5},{5,4},{6,7},{7,6},{8,9},{9,8},{10,11... | collective-permute-start | bytes 1671176 | tf_op jit(solution)/shard_map/ppermute | solution.py:21
  63.3 9.3 %collective-permute-start.37 = (bf16[4,64,512]{2,1,0:T(8,128)(2,1)S(1)}, bf16[4,64,512]{2,1,0:T(8,128)(2,1)S(1)}, u32[]{:S(2)}, u32[]{:S(2)}) collective-permute-start(bf16[4,64,512]{2,1,0:T(8,128)(2,1)S(1)} %get-tuple-element.263), channel_id=1, source_target_pairs={{0,2},{1,3},{2,0},{3,1},{4,6},{5,7},{6,4},{7,5},{8,10},{9,11},{10,... | collective-permute-start | bytes 786440 | tf_op jit(solution)/shard_map/ppermute | solution.py:21
  64.3 8.4 %collective-permute-start.38 = (bf16[4,64,512]{2,1,0:T(8,128)(2,1)S(1)}, bf16[4,64,512]{2,1,0:T(8,128)(2,1)S(1)}, u32[]{:S(2)}, u32[]{:S(2)}) collective-permute-start(bf16[4,64,512]{2,1,0:T(8,128)(2,1)S(1)} %get-tuple-element.267), channel_id=1, source_target_pairs={{0,8},{4,12},{8,0},{12,4},{16,24},{20,28},{24,16},{28,20},{1,9},{5... | collective-permute-start | bytes 786440 | tf_op jit(solution)/shard_map/ppermute | solution.py:21
  65.8 16.2 %collective-permute-start.31 = (bf16[4,272,128]{2,1,0:T(8,128)(2,1)S(1)}, bf16[4,272,128]{2,1,0:T(8,128)(2,1)S(1)}, u32[]{:S(2)}, u32[]{:S(2)}) collective-permute-start(bf16[4,272,128]{2,1,0:T(8,128)(2,1)S(1)} %get-tuple-element.254), channel_id=1, source_target_pairs={{0,2},{1,3},{2,0},{3,1},{4,6},{5,7},{6,4},{7,5},{8,10},{9,11},{10,... | collective-permute-start | bytes 835592 | tf_op jit(solution)/shard_map/ppermute | solution.py:21
  66.9 15.8 %collective-permute-start.32 = (bf16[4,272,128]{2,1,0:T(8,128)(2,1)S(1)}, bf16[4,272,128]{2,1,0:T(8,128)(2,1)S(1)}, u32[]{:S(2)}, u32[]{:S(2)}) collective-permute-start(bf16[4,272,128]{2,1,0:T(8,128)(2,1)S(1)} %get-tuple-element.255), channel_id=1, source_target_pairs={{0,2},{1,3},{2,0},{3,1},{4,6},{5,7},{6,4},{7,5},{8,10},{9,11},{10,... | collective-permute-start | bytes 835592 | tf_op jit(solution)/shard_map/ppermute | solution.py:21
  72.7 5.0 %collective-permute-start.39 = (bf16[2,64,512]{2,1,0:T(8,128)(2,1)S(1)}, bf16[2,64,512]{2,1,0:T(8,128)(2,1)S(1)}, u32[]{:S(2)}, u32[]{:S(2)}) collective-permute-start(bf16[2,64,512]{2,1,0:T(8,128)(2,1)S(1)} %get-tuple-element.269), channel_id=1, source_target_pairs={{0,8},{4,12},{8,0},{12,4},{16,24},{20,28},{24,16},{28,20},{1,9},{5... | collective-permute-start | bytes 393224 | tf_op jit(solution)/shard_map/ppermute | solution.py:21
  74.4 5.0 %collective-permute-start.40 = (bf16[2,64,512]{2,1,0:T(8,128)(2,1)S(1)}, bf16[2,64,512]{2,1,0:T(8,128)(2,1)S(1)}, u32[]{:S(2)}, u32[]{:S(2)}) collective-permute-start(bf16[2,64,512]{2,1,0:T(8,128)(2,1)S(1)} %get-tuple-element.271), channel_id=1, source_target_pairs={{0,4},{4,0},{8,12},{12,8},{16,20},{20,16},{24,28},{28,24},{1,5},{5... | collective-permute-start | bytes 393224 | tf_op jit(solution)/shard_map/ppermute | solution.py:21
  79.4 12.4 %collective-permute-start.41 = (bf16[2,2,64,512]{3,2,1,0:T(8,128)(2,1)S(1)}, bf16[2,2,64,512]{3,2,1,0:T(8,128)(2,1)S(1)}, u32[]{:S(2)}, u32[]{:S(2)}) collective-permute-start(bf16[2,2,64,512]{3,2,1,0:T(8,128)(2,1)S(1)} %join.1.refs_0_), channel_id=1, source_target_pairs={{0,16},{4,20},{8,24},{12,28},{16,0},{20,4},{24,8},{28,12},{1,17},{... | collective-permute-start | bytes 786440 | tf_op jit(solution)/shard_map/ppermute | solution.py:21
  82.9 5.5 %collective-permute-start.33 = (bf16[2,272,128]{2,1,0:T(8,128)(2,1)S(1)}, bf16[2,272,128]{2,1,0:T(8,128)(2,1)S(1)}, u32[]{:S(2)}, u32[]{:S(2)}) collective-permute-start(bf16[2,272,128]{2,1,0:T(8,128)(2,1)S(1)} %get-tuple-element.257), channel_id=1, source_target_pairs={{0,4},{4,0},{8,12},{12,8},{16,20},{20,16},{24,28},{28,24},{1,5},{5... | collective-permute-start | bytes 417800 | tf_op jit(solution)/shard_map/ppermute | solution.py:21
  84.2 5.6 %collective-permute-start.34 = (bf16[2,272,128]{2,1,0:T(8,128)(2,1)S(1)}, bf16[2,272,128]{2,1,0:T(8,128)(2,1)S(1)}, u32[]{:S(2)}, u32[]{:S(2)}) collective-permute-start(bf16[2,272,128]{2,1,0:T(8,128)(2,1)S(1)} %get-tuple-element.258), channel_id=1, source_target_pairs={{0,4},{4,0},{8,12},{12,8},{16,20},{20,16},{24,28},{28,24},{1,5},{5... | collective-permute-start | bytes 417800 | tf_op jit(solution)/shard_map/ppermute | solution.py:21
  85.0 24.2 %collective-permute-start.48 = (bf16[8,64,512]{2,1,0:T(8,128)(2,1)S(1)}, bf16[8,64,512]{2,1,0:T(8,128)(2,1)S(1)}, u32[]{:S(2)}, u32[]{:S(2)}) collective-permute-start(bf16[8,64,512]{2,1,0:T(8,128)(2,1)S(1)} %get-tuple-element.277), channel_id=1, source_target_pairs={{0,2},{1,3},{2,0},{3,1},{4,6},{5,7},{6,4},{7,5},{8,10},{9,11},{10,... | collective-permute-start | bytes 1572872 | tf_op jit(solution)/shard_map/ppermute | solution.py:21
  89.9 5.9 %collective-permute-start.35 = (bf16[1,272,128]{2,1,0:T(8,128)(2,1)S(1)}, bf16[1,272,128]{2,1,0:T(8,128)(2,1)S(1)}, u32[]{:S(2)}, u32[]{:S(2)}) collective-permute-start(bf16[1,272,128]{2,1,0:T(8,128)(2,1)S(1)} %get-tuple-element.260), channel_id=1, source_target_pairs={{0,8},{4,12},{8,0},{12,4},{16,24},{20,28},{24,16},{28,20},{1,9},{5... | collective-permute-start | bytes 208904 | tf_op jit(solution)/shard_map/ppermute | solution.py:21
  91.8 4.4 %collective-permute-start.36 = (bf16[1,272,128]{2,1,0:T(8,128)(2,1)S(1)}, bf16[1,272,128]{2,1,0:T(8,128)(2,1)S(1)}, u32[]{:S(2)}, u32[]{:S(2)}) collective-permute-start(bf16[1,272,128]{2,1,0:T(8,128)(2,1)S(1)} %get-tuple-element.261), channel_id=1, source_target_pairs={{0,8},{4,12},{8,0},{12,4},{16,24},{20,28},{24,16},{28,20},{1,9},{5... | collective-permute-start | bytes 208904 | tf_op jit(solution)/shard_map/ppermute | solution.py:21
  92.2 7.5 %collective-permute-start.44 = (bf16[2,64,512]{2,1,0:T(8,128)(2,1)S(1)}, bf16[2,64,512]{2,1,0:T(8,128)(2,1)S(1)}, u32[]{:S(2)}, u32[]{:S(2)}) collective-permute-start(bf16[2,64,512]{2,1,0:T(8,128)(2,1)S(1)} %get-tuple-element.272.refs_3_), channel_id=1, source_target_pairs={{0,8},{4,12},{8,0},{12,4},{16,24},{20,28},{24,16},{28,20},{1,9},{5... | collective-permute-start | bytes 393224 | tf_op jit(solution)/shard_map/ppermute | solution.py:21
  94.0 5.6 %collective-permute-start.46 = (bf16[2,64,512]{2,1,0:T(8,128)(2,1)S(1)}, bf16[2,64,512]{2,1,0:T(8,128)(2,1)S(1)}, u32[]{:S(2)}, u32[]{:S(2)}) collective-permute-start(bf16[2,64,512]{2,1,0:T(8,128)(2,1)S(1)} %get-tuple-element.274), channel_id=1, source_target_pairs={{0,4},{4,0},{8,12},{12,8},{16,20},{20,16},{24,28},{28,24},{1,5},{5... | collective-permute-start | bytes 393224 | tf_op jit(solution)/shard_map/ppermute | solution.py:21
  96.3 7.8 %collective-permute-start.42 = (bf16[2,272,128]{2,1,0:T(8,128)(2,1)S(1)}, bf16[2,272,128]{2,1,0:T(8,128)(2,1)S(1)}, u32[]{:S(2)}, u32[]{:S(2)}) collective-permute-start(bf16[2,272,128]{2,1,0:T(8,128)(2,1)S(1)} %add_parts.5.refs_0_), channel_id=1, source_target_pairs={{0,16},{4,20},{8,24},{12,28},{16,0},{20,4},{24,8},{28,12},{1,17},{... | collective-permute-start | bytes 417800 | tf_op jit(solution)/shard_map/ppermute | solution.py:21
  99.6 9.7 %collective-permute-start.47 = (bf16[4,64,512]{2,1,0:T(8,128)(2,1)S(1)}, bf16[4,64,512]{2,1,0:T(8,128)(2,1)S(1)}, u32[]{:S(2)}, u32[]{:S(2)}) collective-permute-start(bf16[4,64,512]{2,1,0:T(8,128)(2,1)S(1)} %constant_dynamic-update-slice_fusion.2.refs_2_), channel_id=1, source_target_pairs={{0,8},{4,12},{8,0},{12,4},{16,24},{20,28},{24,16},{28,20},{1,9},{5... | collective-permute-start | bytes 786440 | tf_op jit(solution)/shard_map/ppermute | solution.py:21
  99.7 9.6 %collective-permute-start.45 = (bf16[4,64,512]{2,1,0:T(8,128)(2,1)S(1)}, bf16[4,64,512]{2,1,0:T(8,128)(2,1)S(1)}, u32[]{:S(2)}, u32[]{:S(2)}) collective-permute-start(bf16[4,64,512]{2,1,0:T(8,128)(2,1)S(1)} %constant_dynamic-update-slice_fusion.refs_0_), channel_id=1, source_target_pairs={{0,4},{4,0},{8,12},{12,8},{16,20},{20,16},{24,28},{28,24},{1,5},{5... | collective-permute-start | bytes 786440 | tf_op jit(solution)/shard_map/ppermute | solution.py:21
  104.1 5.1 %collective-permute-start.43 = (bf16[2,272,128]{2,1,0:T(8,128)(2,1)S(1)}, bf16[2,272,128]{2,1,0:T(8,128)(2,1)S(1)}, u32[]{:S(2)}, u32[]{:S(2)}) collective-permute-start(bf16[2,272,128]{2,1,0:T(8,128)(2,1)S(1)} %meet.3), channel_id=1, source_target_pairs={{0,8},{4,12},{8,0},{12,4},{16,24},{20,28},{24,16},{28,20},{1,9},{5... | collective-permute-start | bytes 417800 | tf_op jit(solution)/shard_map/ppermute | solution.py:21
  109.3 6.6 %collective-permute-start.51 = (bf16[4,272,128]{2,1,0:T(8,128)(2,1)S(1)}, bf16[4,272,128]{2,1,0:T(8,128)(2,1)S(1)}, u32[]{:S(2)}, u32[]{:S(2)}) collective-permute-start(bf16[4,272,128]{2,1,0:T(8,128)(2,1)S(1)} %pad_maximum_fusion.refs_0_), channel_id=1, source_target_pairs={{0,4},{4,0},{8,12},{12,8},{16,20},{20,16},{24,28},{28,24},{1,5},{5... | collective-permute-start | bytes 835592 | tf_op jit(solution)/shard_map/ppermute | solution.py:21
  111.1 2.3 %collective-permute-start.50 = (bf16[4,64,512]{2,1,0:T(8,128)(2,1)S(1)}, bf16[4,64,512]{2,1,0:T(8,128)(2,1)S(1)}, u32[]{:S(2)}, u32[]{:S(2)}) collective-permute-start(bf16[4,64,512]{2,1,0:T(8,128)(2,1)S(1)} %slice.11), channel_id=1, source_target_pairs={{0,1},{1,0},{2,3},{3,2},{4,5},{5,4},{6,7},{7,6},{8,9},{9,8},{10,11... | collective-permute-start | bytes 786440 | tf_op jit(solution)/shard_map/ppermute | solution.py:21
  111.2 2.2 %collective-permute-start.49 = (bf16[4,64,512]{2,1,0:T(8,128)(2,1)S(1)}, bf16[4,64,512]{2,1,0:T(8,128)(2,1)S(1)}, u32[]{:S(2)}, u32[]{:S(2)}) collective-permute-start(bf16[4,64,512]{2,1,0:T(8,128)(2,1)S(1)} %get-tuple-element.279), channel_id=1, source_target_pairs={{0,1},{1,0},{2,3},{3,2},{4,5},{5,4},{6,7},{7,6},{8,9},{9,8},{10,11... | collective-permute-start | bytes 786440 | tf_op jit(solution)/shard_map/ppermute | solution.py:21
  (16 other events, 168.1 us)
